TPU v7x, 32 devices: a whole 2x2x4 slice. The times are simulated.
32 devices in a mesh: dom: 8 (over z, x), snap: 4 (over y, core).
Axes of the slice: x: 2, y: 2, z: 4, core: 2. Of those that a mesh axis runs over, the one named last changes fastest.
Arguments:
- feat: bfloat16 [4, 1024, 512], P('snap', 'dom'), may hold values from -6 to 6
- w_struct: bfloat16 [512, 1536], replicated, may hold values from -0.25 to 0.25
- w_temp: bfloat16 [512, 1536], replicated, may hold values from -0.25 to 0.25
- pos_embed: bfloat16 [4, 512], replicated, may hold values from -3 to 3
- rel_bias: float32 [4, 8], replicated, may hold values from -1.5 to 1.5
- nbr: int32 [4, 1024, 8], P('snap', 'dom'), may hold values from 0 to 191
- rel_type: int32 [4, 1024, 8], P('snap', 'dom'), may hold values from 0 to 3
- send_idx: int32 [4, 8, 8, 8], P('snap', 'dom'), may hold values from 0 to 127
- active: int32 [4, 1024], P(None, ('dom', 'snap')), may hold values 0 or 1
- cotangent: bfloat16 [4, 1024, 512], P(None, ('dom', 'snap')), may hold values from -6 to 6
Outputs:
- grad_feat: bfloat16 [4, 1024, 512], P('snap', 'dom')
- grad_wtemp: float32 [512, 1536], P('snap')
Inputs may be any that keep to these rules, and one draw needn't show every extreme that they name: `nbr`: rows of the partition's key table: its 128 own entities first, then 8 halo rows from each partition in order.
All inputs are finite; a program needn't handle non-finite values. No bound on the sum of `active` on one device may be relied on, other than what follows from the above.
Results may differ from a plain program's by a relative error of at most 0.024.
Values may be sent and summed in bfloat16 or wider, within the bound.
No kernel may reach another device: no remote copies, remote signals or barrier semaphores. Data moves between devices by JAX's collectives and lax.ppermute only.
A program may use at most 64 MiB of HBM per device.

v0:
```python
import jax
import jax.numpy as jnp
from jax import lax
from jax.sharding import PartitionSpec as P

HEADS = 8


def edge_scores(rel_ids, rel_bias):
    onehot = (rel_ids[..., None] == jnp.arange(rel_bias.shape[0], dtype=jnp.int32)).astype(
        jnp.float32
    )
    return jnp.einsum("rek,kh->reh", onehot, rel_bias, precision=lax.Precision.HIGHEST)


def struct_core(query, key_tab, val_tab, links, edge_add):
    row_count, width = query.shape
    slots = links.shape[1]
    head_dim = width // HEADS
    keys_g = key_tab[links].reshape(row_count, slots, HEADS, head_dim)
    vals_g = val_tab[links].reshape(row_count, slots, HEADS, head_dim)
    query_h = query.reshape(row_count, HEADS, head_dim)
    scores = jnp.einsum("rhc,rehc->reh", query_h, keys_g) * head_dim ** (-0.5) + edge_add
    weights = jax.nn.softmax(scores, axis=1)
    rounded = lax.optimization_barrier(weights.astype(jnp.bfloat16)).astype(jnp.float32)
    return jnp.einsum("reh,rehc->rhc", rounded, vals_g).reshape(row_count, width)


def temp_allowed(active_blk):
    snaps = active_blk.shape[0]
    later = jnp.arange(snaps, dtype=jnp.int32)[:, None]
    earlier = jnp.arange(snaps, dtype=jnp.int32)[None, :]
    causal = (earlier <= later)[..., None]
    itself = (earlier == later)[..., None]
    return causal & (itself | (active_blk[None, :, :] == 1))


def temp_core(t_query, t_key, t_value, allowed):
    snaps, count, width = t_query.shape
    head_dim = width // HEADS
    query_h = t_query.reshape(snaps, count, HEADS, head_dim)
    key_h = t_key.reshape(snaps, count, HEADS, head_dim)
    value_h = t_value.reshape(snaps, count, HEADS, head_dim)
    scores = jnp.einsum("tmhc,umhc->tumh", query_h, key_h) * head_dim ** (-0.5)
    scores = jnp.where(allowed[..., None], scores, -1e30)
    weights = jax.nn.softmax(scores, axis=1)
    rounded = lax.optimization_barrier(weights.astype(jnp.bfloat16)).astype(jnp.float32)
    return jnp.einsum("tumh,umhc->tmhc", rounded, value_h).reshape(snaps, count, width)


def per_device(
    feat, w_struct, w_temp, pos_embed, rel_bias, nbr, rel_type, send_idx, active, cotangent
):
    x_rows = feat[0]
    local_count, width = x_rows.shape
    dom_count = lax.axis_size("dom")
    route = send_idx[0, 0]
    halo_per = route.shape[1]
    route_flat = route.reshape(-1)
    projected = jnp.dot(x_rows, w_struct, preferred_element_type=jnp.float32).astype(jnp.bfloat16)
    pair_cols = projected[:, width:]
    tiles = pair_cols[route_flat].reshape(dom_count, halo_per, 2 * width)
    arrived = lax.all_to_all(tiles, "dom", split_axis=0, concat_axis=0, tiled=True).reshape(
        -1, 2 * width
    )
    query_f = projected[:, :width].astype(jnp.float32)
    table = jnp.concatenate([pair_cols, arrived], axis=0).astype(jnp.float32)
    edge_add = edge_scores(rel_type[0], rel_bias)
    links = nbr[0]
    summed = struct_core(query_f, table[:, :width], table[:, width:], links, edge_add)
    hidden = (x_rows.astype(jnp.float32) + jax.nn.elu(summed)).astype(jnp.bfloat16)
    by_entity = lax.all_to_all(hidden[None], "snap", split_axis=1, concat_axis=0, tiled=True)
    snaps = by_entity.shape[0]
    z_in = (by_entity.astype(jnp.float32) + pos_embed.astype(jnp.float32)[:, None, :]).astype(
        jnp.bfloat16
    )
    z_flat = z_in.reshape(-1, width)
    t_proj = jnp.dot(z_flat, w_temp, preferred_element_type=jnp.float32).astype(jnp.bfloat16)
    t_proj = t_proj.reshape(snaps, -1, 3 * width).astype(jnp.float32)
    allowed = temp_allowed(active)
    cot_f = cotangent.astype(jnp.float32)
    _, pull = jax.vjp(
        lambda a_in, b_in, c_in: temp_core(a_in, b_in, c_in, allowed),
        t_proj[..., :width],
        t_proj[..., width : 2 * width],
        t_proj[..., 2 * width :],
    )
    grads_t = pull(cot_f)
    dt_proj = jnp.concatenate(grads_t, axis=-1).astype(jnp.bfloat16).reshape(-1, 3 * width)
    terms = lax.dot_general(
        z_flat, dt_proj, (((0,), (0,)), ((), ())), preferred_element_type=jnp.float32
    )
    share = lax.psum_scatter(terms.astype(jnp.bfloat16), "snap", scatter_dimension=0, tiled=True)
    grad_wtemp = lax.psum(share, "dom").astype(jnp.float32)
    d_z = cot_f + jnp.dot(dt_proj, w_temp.T, preferred_element_type=jnp.float32).reshape(
        snaps, -1, width
    )
    returned = lax.all_to_all(
        d_z.astype(jnp.bfloat16), "snap", split_axis=0, concat_axis=1, tiled=True
    )[0]
    dh_f = returned.astype(jnp.float32)
    d_agg = dh_f * jnp.where(summed > 0, 1.0, jnp.exp(summed))
    _, pull_s = jax.vjp(
        lambda a_in, b_in, c_in: struct_core(a_in, b_in, c_in, links, edge_add),
        query_f,
        table[:, :width],
        table[:, width:],
    )
    d_query, d_key, d_val = pull_s(d_agg)
    halo_back = jnp.concatenate([d_key[local_count:], d_val[local_count:]], axis=-1)
    halo_back = halo_back.reshape(dom_count, halo_per, 2 * width)
    came_back = (
        lax.all_to_all(
            halo_back.astype(jnp.bfloat16), "dom", split_axis=0, concat_axis=0, tiled=True
        )
        .astype(halo_back.dtype)
        .reshape(-1, 2 * width)
    )
    owned = jnp.concatenate([d_key[:local_count], d_val[:local_count]], axis=-1)
    owned = owned.at[route_flat].add(came_back)
    d_proj = jnp.concatenate([d_query, owned], axis=-1).astype(jnp.bfloat16)
    grad_rows = (dh_f + jnp.dot(d_proj, w_struct.T, preferred_element_type=jnp.float32)).astype(
        jnp.bfloat16
    )
    return (grad_rows[None], grad_wtemp)


def solution(mesh):
    return jax.shard_map(
        per_device,
        mesh=mesh,
        in_specs=(
            P("snap", "dom", None),
            P(),
            P(),
            P(),
            P(),
            P("snap", "dom", None),
            P("snap", "dom", None),
            P("snap", "dom", None, None),
            P(None, ("dom", "snap")),
            P(None, ("dom", "snap"), None),
        ),
        out_specs=(P("snap", "dom", None), P("snap", None)),
        check_vma=False,
    )
```

profile of v0, /device:TPU:0, one launch (start us, length us, event | category | flops | bytes accessed | tf_op | source)
XLA Modules:
  0.0 214.9 jit_solution(6174571612529438990)
XLA Ops:
  7.2 2.0 convolution_convert_fusion.1
  9.6 1.4 gather_fusion
  10.9 7.3 %all-to-all-start = ((bf16[8,8,1024]{2,1,0:T(8,128)(2,1)}), bf16[8,8,1024]{2,1,0:T(8,128)(2,1)S(1)}, u32[]{:S(2)}, u32[]{:S(2)}) async-start(bf16[8,8,1024]{2,1,0:T(8,128)(2,1)} %bitcast.7), calls=%async_computation | async-start | bytes 262144 | tf_op jit(solution)/shard_map/all_to_all | solution.py:63
  18.8 6.7 %all-to-all-done = bf16[8,8,1024]{2,1,0:T(8,128)(2,1)S(1)} async-done(((bf16[8,8,1024]{2,1,0:T(8,128)(2,1)}), bf16[8,8,1024]{2,1,0:T(8,128)(2,1)S(1)}, u32[]{:S(2)}, u32[]{:S(2)}) %all-to-all-start) | async-done | bytes 131104 | tf_op jit(solution)/shard_map/all_to_all | solution.py:63
  25.6 5.1 %gather_fusion.1 = bf16[1024,512]{1,0:T(8,128)(2,1)} fusion(bf16[192,512]{1,0:T(8,128)(2,1)S(1)} %get-tuple-element.12, s32[1024]{0:T(1024)S(1)} %get-tuple-element.22), kind=kCustom, calls=%fused_computation.1 | custom fusion | bytes 2101248 | tf_op jit(solution)/shard_map/gather | solution.py:20
  30.6 3.9 %reshape.244 = bf16[128,8,8,64]{3,2,1,0:T(8,128)(2,1)} reshape(bf16[1024,512]{1,0:T(8,128)(2,1)} %gather_fusion.1) | data formatting | bytes 2097152 | tf_op jit(solution)/shard_map/reshape | solution.py:20
  34.5 2.8 %multiply_reduce_fusion.3 = f32[128,8,8]{1,2,0:T(8,128)S(1)} fusion(f32[128,8,64]{2,1,0:T(8,128)S(1)} %copy.115, bf16[128,8,8,64]{3,2,1,0:T(8,128)(2,1)} %reshape.244), kind=kLoop, calls=%fused_computation.10 | loop fusion | flops 1564672 | bytes 1343488
  38.7 5.1 %gather_fusion.2 = bf16[1024,512]{1,0:T(8,128)(2,1)} fusion(bf16[192,512]{1,0:T(8,128)(2,1)S(1)} %get-tuple-element.11, s32[1024]{0:T(1024)S(1)} %get-tuple-element.22), kind=kCustom, calls=%fused_computation.2 | custom fusion | bytes 2101248 | tf_op jit(solution)/shard_map/gather | solution.py:21
  43.8 3.9 %reshape.246 = bf16[128,8,8,64]{3,2,1,0:T(8,128)(2,1)} reshape(bf16[1024,512]{1,0:T(8,128)(2,1)} %gather_fusion.2) | data formatting | bytes 2097152 | tf_op jit(solution)/shard_map/reshape | solution.py:21
  47.6 3.4 %multiply_reduce_fusion.2 = f32[128,8,64]{2,1,0:T(8,128)} fusion(f32[128,8,8]{1,2,0:T(8,128)S(1)} %copy.116, bf16[128,8,8,64]{3,2,1,0:T(8,128)(2,1)} %reshape.246), kind=kLoop, calls=%fused_computation.9 | loop fusion | flops 1507328 | bytes 1343488
  51.1 1.3 copy.100
  53.2 1.4 reduce.8
  55.3 3.3 %all-to-all-start.1 = ((bf16[4,2,8192]{2,1,0:T(2,128)(2,1)}), bf16[4,2,8192]{2,1,0:T(2,128)(2,1)S(1)}, u32[]{:S(2)}, u32[]{:S(2)}) async-start(bf16[4,2,8192]{2,1,0:T(2,128)(2,1)} %reshape.337), calls=%async_computation.1 | async-start | bytes 262144 | tf_op jit(solution)/shard_map/all_to_all | solution.py:72
  59.8 3.4 %all-to-all-done.1 = bf16[4,2,8192]{2,1,0:T(2,128)(2,1)S(1)} async-done(((bf16[4,2,8192]{2,1,0:T(2,128)(2,1)}), bf16[4,2,8192]{2,1,0:T(2,128)(2,1)S(1)}, u32[]{:S(2)}, u32[]{:S(2)}) %all-to-all-start.1) | async-done | bytes 131104 | tf_op jit(solution)/shard_map/all_to_all | solution.py:72
  66.3 2.1 fusion.65
  74.4 1.4 fusion.11
  76.1 2.8 %fusion.1 = bf16[512,1536]{1,0:T(8,128)(2,1)} fusion(bf16[4,32,1536]{2,1,0:T(8,128)(2,1)S(1)} %constant_dynamic-update-slice_fusion, f32[4,32,512]{2,1,0:T(8,128)} %bitcast.127, f32[4,512]{1,0:T(4,128)S(1)} %convert_element_type.110), kind=kOutput, calls=%fused_computation.14 | convolution fusion | flops 202244096 | bytes 2236416 | tf_op jit(solution)/shard_map/dot_general | solution.py:90
  78.9 1.3 fusion.16
  80.2 3.5 %all-to-all-start.2 = ((bf16[4,32,512]{2,1,0:T(8,128)(2,1)}), bf16[4,32,512]{2,1,0:T(8,128)(2,1)S(1)}, u32[]{:S(2)}, u32[]{:S(2)}) async-start(bf16[4,32,512]{2,1,0:T(8,128)(2,1)} %fusion.16), calls=%async_computation.2 | async-start | bytes 262144 | tf_op jit(solution)/shard_map/all_to_all | solution.py:98
  84.8 3.4 %all-to-all-done.2 = bf16[4,32,512]{2,1,0:T(8,128)(2,1)S(1)} async-done(((bf16[4,32,512]{2,1,0:T(8,128)(2,1)}), bf16[4,32,512]{2,1,0:T(8,128)(2,1)S(1)}, u32[]{:S(2)}, u32[]{:S(2)}) %all-to-all-start.2) | async-done | bytes 131104 | tf_op jit(solution)/shard_map/all_to_all | solution.py:98
  89.1 5.6 %multiply_reduce_fusion.1 = (bf16[128,8,8]{1,2,0:T(8,128)(2,1)S(1)}, f32[128,8,8,64]{3,2,1,0:T(8,128)}) fusion(f32[128,8,64]{2,1,0:T(8,128)S(1)} %copy.117, bf16[128,8,8,64]{3,2,1,0:T(8,128)(2,1)} %reshape.246, f32[128,8,8]{1,2,0:T(8,128)} %copy.85), kind=kLoop, calls=%fused_computation.8 | loop fusion | flops 2088960 | bytes 3457024
  94.7 4.8 %reshape.300 = f32[1024,512]{1,0:T(8,128)} reshape(f32[128,8,8,64]{3,2,1,0:T(8,128)} %get-tuple-element.5) | data formatting | bytes 4194304 | tf_op jit(solution)/shard_map/transpose(jvp())/reshape | solution.py:21
  100.0 5.6 %multiply_reduce_fusion = (bf16[128,8,64]{2,1,0:T(8,128)(2,1)}, f32[128,8,8,64]{3,2,1,0:T(8,128)}) fusion(f32[128,8,8]{1,2,0:T(8,128)S(1)} %copy.118, bf16[128,8,8,64]{3,2,1,0:T(8,128)(2,1)} %reshape.244, f32[128,8,64]{2,1,0:T(8,128)S(1)} %copy.115), kind=kLoop, calls=%fused_computation.7 | loop fusion | flops 2031616 | bytes 3571712
  105.7 4.8 %reshape.292 = f32[1024,512]{1,0:T(8,128)} reshape(f32[128,8,8,64]{3,2,1,0:T(8,128)} %get-tuple-element.3) | data formatting | bytes 4194304 | tf_op jit(solution)/shard_map/transpose(jvp())/reshape | solution.py:20
  110.5 7.3 %scatter_custom_fusion.1 = f32[192,512]{1,0:T(8,128)S(1)} fusion(s32[1024]{0:T(1024)} %copy-done.13, f32[1024,512]{1,0:T(8,128)} %reshape.300, f32[]{:T(128)} %constant.15.clone.1), kind=kCustom, calls=%fused_computation.76 | custom fusion | flops 524288 | bytes 393728 | tf_op jit(solution)/shard_map/transpose(jvp())/scatter-add | solution.py:21
  117.8 7.4 %scatter_custom_fusion = f32[192,512]{1,0:T(8,128)S(1)} fusion(s32[1024]{0:T(1024)} %copy-done.13, f32[1024,512]{1,0:T(8,128)} %reshape.292, f32[]{:T(128)} %constant.15.clone.1), kind=kCustom, calls=%fused_computation.78 | custom fusion | flops 524288 | bytes 393728 | tf_op jit(solution)/shard_map/transpose(jvp())/scatter-add | solution.py:20
  125.9 4.0 %all-to-all-start.3 = ((bf16[8,8,1024]{2,1,0:T(8,128)(2,1)}), bf16[8,8,1024]{2,1,0:T(8,128)(2,1)}, u32[]{:S(2)}, u32[]{:S(2)}) async-start(bf16[8,8,1024]{2,1,0:T(8,128)(2,1)} %maximum_bitcast_fusion), calls=%async_computation.3 | async-start | bytes 262144 | tf_op jit(solution)/shard_map/all_to_all | solution.py:113
  134.2 1.9 pad_maximum_fusion
  137.2 3.3 %scatter_custom_fusion.2 = f32[128,1024]{1,0:T(8,128)} fusion(f32[128,1024]{1,0:T(8,128)} %pad_maximum_fusion, s32[64]{0:T(128)} %copy-done.20, bf16[8,8,1024]{2,1,0:T(8,128)(2,1)} %all-to-all-done.3), kind=kCustom, calls=%fused_computation.59 | custom fusion | flops 131072 | bytes 655360 | tf_op jit(solution)/shard_map/scatter-add | solution.py:120
  141.6 1.3 fusion.19
  142.9 63.2 %all-reduce.2.cloned.1.call-done = bf16[128,1536]{1,0:T(8,128)(2,1)} async-done(((bf16[128,1536]{1,0:T(8,128)(2,1)}), bf16[128,1536]{1,0:T(8,128)(2,1)}) %all-reduce.2.cloned.1.call-update) | async-done | bytes 393232 | tf_op jit(solution)/shard_map/psum | solution.py:94
  206.1 2.0 convert_element_type.131
  (121 shorter events, 23.7 us)
Async XLA Ops:
  7.2 56.3 %copy-start = (bf16[512,1536]{1,0:T(8,128)(2,1)S(1)}, bf16[512,1536]{1,0:T(8,128)(2,1)}, u32[]{:S(2)}) copy-start(bf16[512,1536]{1,0:T(8,128)(2,1)} %param.12) | copy-start | bytes 4718596
  7.2 11.0 %copy-start.7 = (bf16[1,128,512]{2,1,0:T(8,128)(2,1)S(1)}, bf16[1,128,512]{2,1,0:T(8,128)(2,1)}, u32[]{:S(2)}) copy-start(bf16[1,128,512]{2,1,0:T(8,128)(2,1)} %param.10) | copy-start | bytes 393220
  7.2 2.0 copy-start.16
  7.2 2.1 copy-start.17
  7.2 11.1 %copy-start.19 = (s32[4,32]{1,0:T(4,128)S(1)}, s32[4,32]{1,0:T(4,128)}, u32[]{:S(2)}) copy-start(s32[4,32]{1,0:T(4,128)} %param.18) | copy-start | bytes 1540
  9.3 1.6 copy-start.20
  9.5 1.4 copy-start.13
  10.9 14.6 %all-to-all-start = ((bf16[8,8,1024]{2,1,0:T(8,128)(2,1)}), bf16[8,8,1024]{2,1,0:T(8,128)(2,1)S(1)}, u32[]{:S(2)}, u32[]{:S(2)}) async-start(bf16[8,8,1024]{2,1,0:T(8,128)(2,1)} %bitcast.7), calls=%async_computation | async-start | bytes 262144 | tf_op jit(solution)/shard_map/all_to_all | solution.py:63
  34.5 3.0 %copy-start.14 = (s32[1,128,8]{1,2,0:T(8,128)S(1)}, s32[1,128,8]{1,2,0:T(8,128)}, u32[]{:S(2)}) copy-start(s32[1,128,8]{1,2,0:T(8,128)} %param.16) | copy-start | bytes 12292
  34.5 3.0 %copy-start.18 = (f32[4,8]{1,0:T(4,128)S(1)}, f32[4,8]{1,0:T(4,128)}, u32[]{:S(2)}) copy-start(f32[4,8]{1,0:T(4,128)} %param.14) | copy-start | bytes 388
  37.8 6.0 %copy-start.3 = (f32[128,8,8]{0,2,1:T(8,128)}, f32[128,8,8]{0,2,1:T(8,128)S(1)}, u32[]{:S(2)}) copy-start(f32[128,8,8]{0,2,1:T(8,128)S(1)} %get-tuple-element.16) | copy-start | bytes 98308
  51.1 8.5 %copy-start.15 = (bf16[4,512]{1,0:T(4,128)(2,1)S(1)}, bf16[4,512]{1,0:T(4,128)(2,1)}, u32[]{:S(2)}) copy-start(bf16[4,512]{1,0:T(4,128)(2,1)} %param.13) | copy-start | bytes 12292
  51.1 8.5 %copy-start.5 = (bf16[4,32,512]{2,1,0:T(8,128)(2,1)S(1)}, bf16[4,32,512]{2,1,0:T(8,128)(2,1)}, u32[]{:S(2)}) copy-start(bf16[4,32,512]{2,1,0:T(8,128)(2,1)} %param.19) | copy-start | bytes 393220
  55.3 7.9 %all-to-all-start.1 = ((bf16[4,2,8192]{2,1,0:T(2,128)(2,1)}), bf16[4,2,8192]{2,1,0:T(2,128)(2,1)S(1)}, u32[]{:S(2)}, u32[]{:S(2)}) async-start(bf16[4,2,8192]{2,1,0:T(2,128)(2,1)} %reshape.337), calls=%async_computation.1 | async-start | bytes 262144 | tf_op jit(solution)/shard_map/all_to_all | solution.py:72
  58.7 71.3 %reduce-scatter.2.cloned.1.call-start = ((), (), s32[]{:S(2)}) async-start(), calls=%async_computation.5 | async-start | bytes 1966080 | tf_op jit(solution)/shard_map/reduce_scatter | solution.py:93
  59.8 6.0 %copy-start.8 = (bf16[4,32,8,64]{3,2,1,0:T(8,128)(2,1)}, bf16[4,32,8,64]{3,2,1,0:T(8,128)(2,1)S(1)}, u32[]{:S(2)}) copy-start(bf16[4,32,8,64]{3,2,1,0:T(8,128)(2,1)S(1)} %reshape.250) | copy-start | bytes 393220
  68.4 2.2 %copy-start.11 = (bf16[4,32,8,64]{3,2,1,0:T(8,128)(2,1)S(1)}, bf16[4,32,8,64]{3,2,1,0:T(8,128)(2,1)}, u32[]{:S(2)}) copy-start(bf16[4,32,8,64]{3,2,1,0:T(8,128)(2,1)} %reshape.251) | copy-start | bytes 393220
  68.4 2.6 %copy-start.10 = (bf16[4,32,8,64]{3,2,1,0:T(8,128)(2,1)S(1)}, bf16[4,32,8,64]{3,2,1,0:T(8,128)(2,1)}, u32[]{:S(2)}) copy-start(bf16[4,32,8,64]{3,2,1,0:T(8,128)(2,1)} %reshape.252) | copy-start | bytes 393220
  71.0 3.3 %copy-start.9 = (bf16[4,32,8,64]{3,2,1,0:T(8,128)(2,1)S(1)}, bf16[4,32,8,64]{3,2,1,0:T(8,128)(2,1)}, u32[]{:S(2)}) copy-start(bf16[4,32,8,64]{3,2,1,0:T(8,128)(2,1)} %copy-done.8) | copy-start | bytes 393220
  76.0 2.9 %copy-start.6 = (bf16[4,32,512]{2,1,0:T(8,128)(2,1)S(1)}, bf16[4,32,512]{2,1,0:T(8,128)(2,1)}, u32[]{:S(2)}) copy-start(bf16[4,32,512]{2,1,0:T(8,128)(2,1)} %param.19) | copy-start | bytes 393220
  78.9 4.9 %copy-start.12 = (f32[128,8,8]{0,1,2:T(8,128)S(1)}, f32[128,8,8]{0,1,2:T(8,128)}, u32[]{:S(2)}) copy-start(f32[128,8,8]{0,1,2:T(8,128)} %get-tuple-element.13) | copy-start | bytes 98308
  80.2 7.9 %all-to-all-start.2 = ((bf16[4,32,512]{2,1,0:T(8,128)(2,1)}), bf16[4,32,512]{2,1,0:T(8,128)(2,1)S(1)}, u32[]{:S(2)}, u32[]{:S(2)}) async-start(bf16[4,32,512]{2,1,0:T(8,128)(2,1)} %fusion.16), calls=%async_computation.2 | async-start | bytes 262144 | tf_op jit(solution)/shard_map/all_to_all | solution.py:98
  88.1 0.7 copy-start.2
  94.7 5.0 %copy-start.4 = (f32[128,8,8]{0,2,1:T(8,128)S(1)}, f32[128,8,8]{0,2,1:T(8,128)}, u32[]{:S(2)}) copy-start(f32[128,8,8]{0,2,1:T(8,128)} %copy-done.3) | copy-start | bytes 98308
  125.9 11.4 %all-to-all-start.3 = ((bf16[8,8,1024]{2,1,0:T(8,128)(2,1)}), bf16[8,8,1024]{2,1,0:T(8,128)(2,1)}, u32[]{:S(2)}, u32[]{:S(2)}) async-start(bf16[8,8,1024]{2,1,0:T(8,128)(2,1)} %maximum_bitcast_fusion), calls=%async_computation.3 | async-start | bytes 262144 | tf_op jit(solution)/shard_map/all_to_all | solution.py:113
  129.9 76.3 %all-reduce.2.cloned.1.call-start = ((), (), s32[]{:S(2)}) async-start(), calls=%async_computation.6 | async-start | bytes 786432 | tf_op jit(solution)/shard_map/psum | solution.py:94
  131.3 10.2 %copy-start.1 = (bf16[512,1536]{1,0:T(8,128)(2,1)S(1)}, bf16[512,1536]{1,0:T(8,128)(2,1)}, u32[]{:S(2)}) copy-start(bf16[512,1536]{1,0:T(8,128)(2,1)} %param.11) | copy-start | bytes 4718596
Sparse Core Ops, SparseCore 0:
  79.0 25.0 reduce-scatter.1
  134.4 71.6 all-reduce.1
where the time goes:
time: 216 us; the launch traced here: 215 us
  waiting for transfers between devices  78.6 us (36%)
  other arithmetic  47.8 us (22%)
  local copies, waits for them, and re-layouts  42 us (19%)
  starting transfers between devices  18.4 us (9%)
  between operations  14.7 us (7%)
  matrix products  13.5 us (6%)
    psum x1, waiting for transfers between devices, per_device(): grad_wtemp = lax.psum(share, 'dom').astype(jnp.float32)  63.2 us
    unnamed x5, other arithmetic  18.9 us
    reshape x2, local copies, waits for them, and re-layouts, struct_core(): keys_g = key_tab[links].reshape(row_count, slots, HEADS, head_dim)  8.7 us
    reshape x2, local copies, waits for them, and re-layouts, struct_core(): vals_g = val_tab[links].reshape(row_count, slots, HEADS, head_dim)  8.7 us
    scatter-add x1, other arithmetic, struct_core(): keys_g = key_tab[links].reshape(row_count, slots, HEADS, head_dim)  7.36 us
    scatter-add x1, other arithmetic, struct_core(): vals_g = val_tab[links].reshape(row_count, slots, HEADS, head_dim)  7.35 us
    all_to_all x1, starting transfers between devices, per_device(): lax.all_to_all(tiles, 'dom', split_axis=0, concat_axis=0, tiled=True)  7.26 us
    all_to_all x1, waiting for transfers between devices, per_device(): lax.all_to_all(tiles, 'dom', split_axis=0, concat_axis=0, tiled=True)  6.73 us
  transfers between devices with their start and end apart: 6, of which 5 were waited for; matrix products, arithmetic and copies ran while one was open for 24% of the time, Pallas kernels for 0%

commit v1 on v0

v1 whole, which is shorter than its diff:
```python
import functools

import jax
import jax.numpy as jnp
from jax import lax
from jax.experimental import pallas as pl
from jax.experimental.pallas import tpu as pltpu
from jax.sharding import PartitionSpec as P

F32 = jnp.float32
BF16 = jnp.bfloat16
LANES = 128
NEG = -1e30
VMEM = pl.BlockSpec(memory_space=pltpu.VMEM)
SMEM = pl.BlockSpec(memory_space=pltpu.SMEM)


def dot_nn(a, b):
    return lax.dot_general(a, b, (((1,), (0,)), ((), ())), preferred_element_type=F32)


def dot_nt(a, b):
    return lax.dot_general(a, b, (((1,), (1,)), ((), ())), preferred_element_type=F32)


def dot_tn(a, b):
    return lax.dot_general(a, b, (((0,), (0,)), ((), ())), preferred_element_type=F32)


def stack_heads(block, head_dim):
    rows, lanes = block.shape
    head = lax.broadcasted_iota(jnp.int32, (rows, lanes), 1) // head_dim
    zero = jnp.zeros_like(block)
    return jnp.concatenate(
        [jnp.where(head == g, block, zero) for g in range(lanes // head_dim)], axis=0
    )


def unstack_heads(stacked, head_dim):
    lanes = stacked.shape[1]
    groups = lanes // head_dim
    rows = stacked.shape[0] // groups
    head = lax.broadcasted_iota(jnp.int32, (rows, lanes), 1) // head_dim
    out = stacked[:rows]
    for g in range(1, groups):
        out = jnp.where(head == g, stacked[g * rows : (g + 1) * rows], out)
    return out


def own_kernel(heads, x_ref, w_ref, nbr_ref, rel_ref, bias_ref, proj_ref, weight_ref):
    rows, width = x_ref.shape
    keys = weight_ref.shape[2]
    kinds = bias_ref.shape[0]
    slots = nbr_ref.shape[1]
    scale = (width // heads) ** (-0.5)
    x = x_ref[...]
    for part in range(3):
        cols = slice(part * width, (part + 1) * width)
        out = dot_nn(x, w_ref[:, cols]).astype(BF16)
        if part == 0:
            out = (out.astype(F32) * scale).astype(BF16)
        proj_ref[:, cols] = out
    code = nbr_ref[...] * kinds + rel_ref[...]
    spot = lax.broadcasted_iota(jnp.int32, (rows, keys), 1) * kinds
    gain = jnp.exp(bias_ref[...])
    counts = []
    for r in range(kinds):
        here = spot + r
        count = jnp.zeros((rows, keys), F32)
        for k in range(slots):
            count = count + jnp.where(code[:, k : k + 1] == here, 1.0, 0.0)
        counts.append(count)
    for h in range(heads):
        total = counts[0] * gain[0:1, h : h + 1]
        for r in range(1, kinds):
            total = total + counts[r] * gain[r : r + 1, h : h + 1]
        weight_ref[h] = total


def forward_kernel(
    heads, x_ref, halo_ref, w_ref, proj_ref, weight_ref, hidden_ref, agg_ref, tab_ref, attn_ref
):
    rows, width = x_ref.shape
    keys = weight_ref.shape[2]
    halo_rows = halo_ref.shape[0]
    head_dim = width // heads
    group = LANES // head_dim
    tab_ref[:rows, :] = proj_ref[:, width:]
    tab_ref[rows : rows + halo_rows, :] = dot_nn(halo_ref[...], w_ref[:, width:]).astype(BF16)
    if keys > rows + halo_rows:
        tab_ref[rows + halo_rows :, :] = jnp.zeros((keys - rows - halo_rows, 2 * width), BF16)
    for p in range(width // LANES):
        cols = slice(p * LANES, (p + 1) * LANES)
        vcols = slice(width + p * LANES, width + (p + 1) * LANES)
        kk = stack_heads(tab_ref[:, cols], head_dim)
        vv = stack_heads(tab_ref[:, vcols], head_dim)
        score = dot_nt(proj_ref[:, cols], kk)
        parts = []
        for g in range(group):
            wt = weight_ref[p * group + g]
            s = jnp.where(wt > 0, score[:, g * keys : (g + 1) * keys], NEG)
            top = jnp.max(s, axis=1, keepdims=True)
            e = jnp.exp(s - top) * wt
            parts.append((e * (1.0 / jnp.sum(e, axis=1, keepdims=True))).astype(BF16))
        attn = jnp.concatenate(parts, axis=1)
        attn_ref[p] = attn
        agg = dot_nn(attn, vv)
        agg_ref[:, cols] = agg
        elu = jnp.where(agg > 0, agg, jnp.exp(jnp.minimum(agg, 0.0)) - 1.0)
        hidden_ref[:, cols] = (x_ref[:, cols].astype(F32) + elu).astype(BF16)


def temporal_kernel(snaps, heads, me_ref, pos_ref, w_ref, *refs):
    hid = refs[:snaps]
    cot = refs[snaps : 2 * snaps]
    terms_ref, dt_own_ref, cot_own_ref, z_s, tp_s, dt_s, *wide = refs[2 * snaps :]
    local, width = hid[0].shape
    ents = local // snaps
    rows = snaps * ents
    head_dim = width // heads
    group = LANES // head_dim
    scale = head_dim ** (-0.5)
    me = me_ref[0]
    cot_rows = [cot[m].at[:rows, :] for m in range(snaps)]
    if wide:
        for m in range(snaps):
            wide[0][m] = hid[m][...].astype(F32)
            wide[1][m] = cot[m][:rows, :].astype(F32)
        hid = [wide[0].at[m] for m in range(snaps)]
        cot_rows = [wide[1].at[m] for m in range(snaps)]
    pos = pos_ref[...].astype(F32)
    which = lax.broadcasted_iota(jnp.int32, pos.shape, 0)
    for n in range(snaps):
        t = lax.bitwise_xor(me, n)
        shift = jnp.sum(jnp.where(which == t, pos, 0.0), axis=0, keepdims=True)
        for m in range(snaps):
            b = lax.bitwise_xor(me, m)
            src = pl.ds(pl.multiple_of(b * ents, ents), ents)
            dst = pl.ds(pl.multiple_of(m * rows + t * ents, ents), ents)
            z_s[dst, :] = (hid[n][src, :].astype(F32) + shift).astype(z_s.dtype)
    z = z_s[...].astype(BF16)
    for part in range(3):
        cols = slice(part * width, (part + 1) * width)
        out = dot_nn(z, w_ref[:, cols]).astype(BF16)
        if part == 0:
            out = (out.astype(F32) * scale).astype(BF16)
        tp_s[:, cols] = out
    later = lax.broadcasted_iota(jnp.int32, (rows, rows), 0)
    early = lax.broadcasted_iota(jnp.int32, (rows, rows), 1)
    same = (later % ents) == (early % ents)
    past = same & (early < later)
    itself = early == later
    for m in range(snaps):
        blk = slice(m * rows, (m + 1) * rows)
        act = cot[m][rows : rows + 16, :rows].astype(F32)[0:1]
        allowed = itself | (past & (act > 0.5))
        for p in range(width // LANES):
            c0 = p * LANES
            q = tp_s[blk, c0 : c0 + LANES]
            kk = stack_heads(tp_s[blk, width + c0 : width + c0 + LANES], head_dim)
            vv = stack_heads(tp_s[blk, 2 * width + c0 : 2 * width + c0 + LANES], head_dim)
            ct = cot[m][:rows, c0 : c0 + LANES]
            score = dot_nt(q, kk)
            dattn = dot_nt(ct, vv).astype(BF16).astype(F32)
            attn_b, ds = [], []
            for g in range(group):
                s = jnp.where(allowed, score[:, g * rows : (g + 1) * rows], NEG)
                e = jnp.exp(s - jnp.max(s, axis=1, keepdims=True))
                a = e * (1.0 / jnp.sum(e, axis=1, keepdims=True))
                attn_b.append(a.astype(BF16))
                d = dattn[:, g * rows : (g + 1) * rows]
                ad = a * d
                ds.append((ad - a * jnp.sum(ad, axis=1, keepdims=True)).astype(BF16))
            ds = jnp.concatenate(ds, axis=1)
            attn_b = jnp.concatenate(attn_b, axis=1)
            dq = dot_nn(ds, kk) * scale
            dk = unstack_heads(dot_tn(ds, q), head_dim)
            dv = unstack_heads(dot_tn(attn_b, ct), head_dim)
            dt_s[blk, c0 : c0 + LANES] = dq.astype(BF16).astype(dt_s.dtype)
            dt_s[blk, width + c0 : width + c0 + LANES] = dk.astype(BF16).astype(dt_s.dtype)
            dt_s[blk, 2 * width + c0 : 2 * width + c0 + LANES] = dv.astype(BF16).astype(dt_s.dtype)
    share = width // snaps
    pick = (
        lax.broadcasted_iota(jnp.int32, (width, share), 0)
        == lax.broadcasted_iota(jnp.int32, (width, share), 1) + me * share
    )
    z_mine = dot_nn(z, jnp.where(pick, 1.0, 0.0).astype(BF16)).astype(BF16)
    for part in range(3):
        cols = slice(part * width, (part + 1) * width)
        terms_ref[:, cols] = dot_tn(z_mine, dt_s[:, cols].astype(BF16)).astype(BF16)
    for m in range(snaps):
        b = lax.bitwise_xor(me, m)
        dst = pl.ds(pl.multiple_of(b * ents, ents), ents)
        mine = pl.multiple_of(me * ents, ents)
        dt_own_ref[dst, :] = dt_s[pl.ds(m * rows + mine, ents), :]
        cot_own_ref[dst, :] = cot_rows[m][pl.ds(mine, ents), :]


def backward_kernel(
    heads,
    halo_rows,
    dt_ref,
    cot_ref,
    wt_ref,
    ws_ref,
    proj_ref,
    agg_ref,
    tab_ref,
    attn_ref,
    halo_ref,
    part_ref,
    dq_s,
    dtab_s,
):
    rows, width = cot_ref.shape
    keys = tab_ref.shape[0]
    head_dim = width // heads
    group = LANES // head_dim
    scale = head_dim ** (-0.5)
    dh = cot_ref[...].astype(F32) + dot_nt(dt_ref[...].astype(BF16), wt_ref[...])
    dh = dh.astype(BF16).astype(F32)
    part_ref[...] = dh
    agg = agg_ref[...]
    dagg = (dh * jnp.where(agg > 0, 1.0, jnp.exp(jnp.minimum(agg, 0.0)))).astype(BF16)
    for p in range(width // LANES):
        cols = slice(p * LANES, (p + 1) * LANES)
        vcols = slice(width + p * LANES, width + (p + 1) * LANES)
        kk = stack_heads(tab_ref[:, cols], head_dim)
        vv = stack_heads(tab_ref[:, vcols], head_dim)
        da = dagg[:, cols]
        dattn = dot_nt(da, vv).astype(BF16).astype(F32)
        attn_b = attn_ref[p]
        attn = attn_b.astype(F32)
        ad = attn * dattn
        ds = []
        for g in range(group):
            span = slice(g * keys, (g + 1) * keys)
            tot = jnp.sum(ad[:, span], axis=1, keepdims=True)
            ds.append((ad[:, span] - attn[:, span] * tot).astype(BF16))
        ds = jnp.concatenate(ds, axis=1)
        dq_s[:, cols] = (dot_nn(ds, kk) * scale).astype(BF16)
        dtab_s[:, cols] = unstack_heads(dot_tn(ds, proj_ref[:, cols]), head_dim).astype(BF16)
        dtab_s[:, vcols] = unstack_heads(dot_tn(attn_b, da), head_dim).astype(BF16)
    halo_ref[...] = dot_nt(dtab_s[rows : rows + halo_rows, :], ws_ref[:, width:]).astype(BF16)
    part_ref[...] += dot_nt(dq_s[...], ws_ref[:, :width]) + dot_nt(
        dtab_s[:rows, :], ws_ref[:, width:]
    )


def params(mib):
    return pltpu.CompilerParams(vmem_limit_bytes=mib * 1024 * 1024)


def gather_blocks(block, axis):
    count = lax.axis_size(axis)
    held = {0: block}
    bit = count // 2
    while bit:
        for m in sorted(held):
            pairs = [(i, i ^ bit) for i in range(count)]
            held[m ^ bit] = lax.ppermute(held[m], axis, pairs)
        bit //= 2
    return [held[m] for m in range(count)]


def per_device(
    feat, w_struct, w_temp, pos_embed, rel_bias, nbr, rel_type, send_idx, active, cotangent
):
    x = feat[0]
    local, width = x.shape
    heads = rel_bias.shape[1]
    doms = lax.axis_size("dom")
    snaps = lax.axis_size("snap")
    ents = local // snaps
    rows = snaps * ents
    route = send_idx[0, 0]
    halo_per = route.shape[1]
    halo_rows = doms * halo_per
    keys = -(-(local + halo_rows) // LANES) * LANES
    route_flat = route.reshape(-1)
    picks = (route_flat[:, None] == jnp.arange(local, dtype=jnp.int32)).astype(BF16)
    tiles = jnp.dot(picks, x, preferred_element_type=F32).astype(BF16)
    halo = lax.all_to_all(
        tiles.reshape(doms, halo_per, width), "dom", split_axis=0, concat_axis=0, tiled=True
    ).reshape(halo_rows, width)

    act_row = jnp.pad(active.astype(BF16).reshape(1, rows), ((0, 15), (0, width - rows)))
    cots = gather_blocks(
        jnp.concatenate([cotangent.reshape(rows, width), act_row], axis=0), "snap"
    )

    proj, weight = pl.pallas_call(
        functools.partial(own_kernel, heads),
        out_shape=(
            jax.ShapeDtypeStruct((local, 3 * width), BF16),
            jax.ShapeDtypeStruct((heads, local, keys), F32),
        ),
        in_specs=[VMEM] * 5,
        out_specs=(VMEM, VMEM),
        compiler_params=params(16),
        name="own_rows",
    )(x, w_struct, nbr[0], rel_type[0], rel_bias)

    lane_groups = width // LANES
    group = heads // lane_groups
    hidden, agg, tab, attn = pl.pallas_call(
        functools.partial(forward_kernel, heads),
        out_shape=(
            jax.ShapeDtypeStruct((local, width), BF16),
            jax.ShapeDtypeStruct((local, width), F32),
            jax.ShapeDtypeStruct((keys, 2 * width), BF16),
            jax.ShapeDtypeStruct((lane_groups, local, group * keys), BF16),
        ),
        in_specs=[VMEM] * 5,
        out_specs=(VMEM,) * 4,
        compiler_params=params(16),
        name="struct_forward",
    )(x, halo, w_struct, proj, weight)

    hids = gather_blocks(hidden, "snap")
    me = lax.axis_index("snap").astype(jnp.int32).reshape(1)
    share = width // snaps
    hold = F32 if ents % 16 else BF16
    terms, dt_own, cot_own = pl.pallas_call(
        functools.partial(temporal_kernel, snaps, heads),
        out_shape=(
            jax.ShapeDtypeStruct((share, 3 * width), BF16),
            jax.ShapeDtypeStruct((local, 3 * width), hold),
            jax.ShapeDtypeStruct((local, width), hold),
        ),
        in_specs=[SMEM, VMEM, VMEM] + [VMEM] * (2 * snaps),
        out_specs=(VMEM,) * 3,
        scratch_shapes=[
            pltpu.VMEM((snaps * rows, width), hold),
            pltpu.VMEM((snaps * rows, 3 * width), BF16),
            pltpu.VMEM((snaps * rows, 3 * width), hold),
        ]
        + ([] if hold == BF16 else [pltpu.VMEM((snaps, rows, width), F32)] * 2),
        compiler_params=params(32 if hold == BF16 else 56),
        name="temporal",
    )(me, pos_embed, w_temp, *hids, *cots)

    parts = lax.all_to_all(
        terms.reshape(doms, share // doms, 3 * width),
        "dom",
        split_axis=0,
        concat_axis=0,
        tiled=True,
    )
    halo_back, partial = pl.pallas_call(
        functools.partial(backward_kernel, heads, halo_rows),
        out_shape=(
            jax.ShapeDtypeStruct((halo_rows, width), BF16),
            jax.ShapeDtypeStruct((local, width), F32),
        ),
        in_specs=[VMEM] * 8,
        out_specs=(VMEM, VMEM),
        scratch_shapes=[
            pltpu.VMEM((local, width), BF16),
            pltpu.VMEM((keys, 2 * width), BF16),
        ],
        compiler_params=params(32),
        name="struct_backward",
    )(dt_own, cot_own, w_temp, w_struct, proj, agg, tab, attn)
    came = lax.all_to_all(
        halo_back.reshape(doms, halo_per, width), "dom", split_axis=0, concat_axis=0, tiled=True
    ).reshape(halo_rows, width)
    piece = jnp.sum(parts.astype(F32), axis=0).astype(BF16)
    whole = lax.all_to_all(
        jnp.broadcast_to(piece[None], (doms,) + piece.shape),
        "dom",
        split_axis=0,
        concat_axis=0,
        tiled=True,
    )
    grad_wtemp = whole.astype(F32).reshape(share, 3 * width)
    back = lax.dot_general(picks, came, (((0,), (0,)), ((), ())), preferred_element_type=F32)
    grad_feat = (partial + back).astype(BF16)
    return (grad_feat[None], grad_wtemp)


def solution(mesh):
    return jax.shard_map(
        per_device,
        mesh=mesh,
        in_specs=(
            P("snap", "dom", None),
            P(),
            P(),
            P(),
            P(),
            P("snap", "dom", None),
            P("snap", "dom", None),
            P("snap", "dom", None, None),
            P(None, ("dom", "snap")),
            P(None, ("dom", "snap"), None),
        ),
        out_specs=(P("snap", "dom", None), P("snap", None)),
        check_vma=False,
    )
```

time: 216 us -> 95 us (0.44)
  waiting for transfers between devices: 78.6 us -> 24.3 us
  other arithmetic: 47.8 us -> 4.99 us
  local copies, waits for them, and re-layouts: 42 us -> 21.5 us
  Pallas kernels: 0 us -> 17.3 us
  between operations: 14.7 us -> 0.76 us
  matrix products: 13.5 us -> 2.04 us
  starting transfers between devices: 18.4 us -> 23 us
    psum x1 -> x0, waiting for transfers between devices: 63.2 us -> none  [per_device(): grad_wtemp = lax.psum(share, 'dom').astype(jnp.float32)]
    reshape x9 -> x1, local copies, waits for them, and re-layouts: 19.7 us -> 0.09 us  [per_device(): active.astype(BF16).reshape(1, rows)]
    unnamed x5 -> x0, other arithmetic: 18.9 us -> none
    scatter-add x3 -> x0, other arithmetic: 18 us -> none  [the longest x1 7.36 us: struct_core(): keys_g = key_tab[links].reshape(row_count, slots, HEADS, head_dim)]
    pallas_call x0 -> x4, Pallas kernels: none -> 17.3 us  [the longest x1 11 us: per_device(): pl.pallas_call(functools.partial(temporal_kernel, snaps, heads), out_shap...]
    unnamed x52, local copies, waits for them, and re-layouts: 2.83 us -> 19.9 us
    gather x3 -> x0, local copies, waits for them, and re-layouts: 11.5 us -> none  [the longest x1 5.07 us: struct_core(): keys_g = key_tab[links].reshape(row_count, slots, HEADS, head_dim)]
    dot_general x10 -> x2, matrix products: 11.4 us -> 2.04 us  [the longest x1 1.75 us: per_device(): tiles = jnp.dot(picks, x, preferred_element_type=F32).astype(BF16)]
  transfers between devices with their start and end apart: 6 -> 10, of which waited for: 5 -> 5; matrix products, arithmetic and copies ran while one was open for 24% -> 6% of each run, Pallas kernels for 0% -> 7%
where the time goes in v1:
time: 95 us; the launch traced here: 94 us
  waiting for transfers between devices  24.3 us (26%)
  starting transfers between devices  23 us (24%)
  local copies, waits for them, and re-layouts  21.5 us (23%)
  Pallas kernels  17.3 us (18%)
  other arithmetic  4.99 us (5%)
  matrix products  2.04 us (2%)
    unnamed x52, local copies, waits for them, and re-layouts  19.9 us
    pallas_call x1, Pallas kernels, per_device(): pl.pallas_call(functools.partial(temporal_kernel, snaps, heads), out_shap...  11 us
    all_to_all x1, waiting for transfers between devices, per_device(): lax.all_to_all(jnp.broadcast_to(piece[None], (doms,) + piece.shape), 'dom...  9.73 us
    all_to_all x1, starting transfers between devices, per_device(): lax.all_to_all(tiles.reshape(doms, halo_per, width), 'dom', split_axis=0,...  7.25 us
    all_to_all x1, starting transfers between devices, per_device(): lax.all_to_all(terms.reshape(doms, share // doms, 3 * width), 'dom', spli...  6 us
    ppermute x6, waiting for transfers between devices, gather_blocks(): held[m ^ bit] = lax.ppermute(held[m], axis, pairs)  5.93 us
    all_to_all x1, waiting for transfers between devices, per_device(): lax.all_to_all(halo_back.reshape(doms, halo_per, width), 'dom', split_axi...  5.85 us
    all_to_all x1, starting transfers between devices, per_device(): lax.all_to_all(halo_back.reshape(doms, halo_per, width), 'dom', split_axi...  3.77 us
  transfers between devices with their start and end apart: 10, of which 5 were waited for; matrix products, arithmetic and copies ran while one was open for 6% of the time, Pallas kernels for 7%

profile of v1, /device:TPU:0, one launch (start us, length us, event | category | flops | bytes accessed | tf_op | source)
XLA Modules:
  0.0 94.0 jit_solution(11287726550512800340)
XLA Ops:
  1.4 1.7 %fusion = bf16[8,8,512]{2,1,0:T(8,128)(2,1)} fusion(s32[64]{0:T(128)S(1)} %eq.15, bf16[1,128,512]{2,1,0:T(8,128)(2,1)} %param.10), kind=kOutput, calls=%fused_computation.1 | convolution fusion | flops 8429568 | bytes 196864 | tf_op jit(solution)/shard_map/dot_general | solution.py:282
  3.1 7.2 %all-to-all-start = ((bf16[8,8,512]{2,1,0:T(8,128)(2,1)}), bf16[8,8,512]{2,1,0:T(8,128)(2,1)S(1)}, u32[]{:S(2)}, u32[]{:S(2)}) async-start(bf16[8,8,512]{2,1,0:T(8,128)(2,1)} %fusion), calls=%async_computation | async-start | bytes 131072 | tf_op jit(solution)/shard_map/all_to_all | solution.py:283
  11.2 1.6 %fusion.2.refs_4_ = bf16[144,512]{1,0:T(8,128)(2,1)} fusion(bf16[1,128]{1,0:T(2,128)(2,1)S(1)} %reshape.40, bf16[128,512]{1,0:T(8,128)(2,1)} %bitcast.29), kind=kLoop, calls=%fused_computation.6 | loop fusion | flops 442368 | bytes 278784 | tf_op jit(solution)/shard_map/concatenate | solution.py:289
  12.7 1.5 %collective-permute-start.4 = (bf16[144,512]{1,0:T(8,128)(2,1)}, bf16[144,512]{1,0:T(8,128)(2,1)}, u32[]{:S(2)}, u32[]{:S(2)}) collective-permute-start(bf16[144,512]{1,0:T(8,128)(2,1)} %fusion.2.refs_4_), channel_id=1, source_target_pairs={{0,2},{1,3},{2,0},{3,1},{4,6},{5,7},{6,4},{7,5},{8,10},{9,11},{10,... | collective-permute-start | bytes 442376 | tf_op jit(solution)/shard_map/ppermute | solution.py:261
  14.3 0.8 copy.12
  15.8 1.4 %copy-done = bf16[512,1536]{1,0:T(8,128)(2,1)S(1)} copy-done((bf16[512,1536]{1,0:T(8,128)(2,1)S(1)}, bf16[512,1536]{1,0:T(8,128)(2,1)}, u32[]{:S(2)}) %copy-start) | copy-done | bytes 1572888
  17.2 0.9 copy-done.3
  18.8 0.9 own_rows.1
  19.8 1.0 %copy-done.5 = f32[8,128,256]{2,1,0:T(8,128)} copy-done((f32[8,128,256]{2,1,0:T(8,128)}, f32[8,128,256]{2,1,0:T(8,128)S(1)}, u32[]{:S(2)}) %copy-start.5) | copy-done | bytes 1048600
  21.4 0.9 copy-done.4
  22.3 1.2 %copy-done.6 = f32[8,128,256]{2,1,0:T(8,128)S(1)} copy-done((f32[8,128,256]{2,1,0:T(8,128)S(1)}, f32[8,128,256]{2,1,0:T(8,128)}, u32[]{:S(2)}) %copy-start.6) | copy-done | bytes 1048600
  23.5 0.8 copy-done.15
  24.4 2.4 %struct_forward.1 = (bf16[128,512]{1,0:T(8,128)(2,1)}, f32[128,512]{1,0:T(8,128)S(1)}, bf16[256,1024]{1,0:T(8,128)(2,1)S(1)}, bf16[4,128,512]{2,1,0:T(8,128)(2,1)S(1)}) custom-call(bf16[128,512]{1,0:T(8,128)(2,1)S(1)} %bitcast.23, bf16[64,512]{1,0:T(8,128)(2,1)S(1)} %bitcast.25, bf16[512,1536]{1,0:T(8,128)(2,1)S(1)} %copy-done.1, ...), custom_call_target="tpu_custom_call" | custom-call | tf_op jit(solution)/shard_map/struct_forward/pallas_call | solution.py:306
  26.8 0.8 copy-done.7
  27.6 0.8 copy-done.9
  30.1 4.3 %collective-permute-done.1.refs_2_ = bf16[128,512]{1,0:T(8,128)(2,1)} collective-permute-done((bf16[128,512]{1,0:T(8,128)(2,1)}, bf16[128,512]{1,0:T(8,128)(2,1)}, u32[]{:S(2)}, u32[]{:S(2)}) %collective-permute-start.1) | collective-permute-done | bytes 131104 | tf_op jit(solution)/shard_map/ppermute | solution.py:261
  34.4 1.7 %collective-permute-done.2.refs_3_ = bf16[128,512]{1,0:T(8,128)(2,1)} collective-permute-done((bf16[128,512]{1,0:T(8,128)(2,1)}, bf16[128,512]{1,0:T(8,128)(2,1)}, u32[]{:S(2)}, u32[]{:S(2)}) %collective-permute-start.2) | collective-permute-done | bytes 131104 | tf_op jit(solution)/shard_map/ppermute | solution.py:261
  36.1 11.0 %temporal.1 = (bf16[128,1536]{1,0:T(8,128)(2,1)S(1)}, bf16[128,1536]{1,0:T(8,128)(2,1)S(1)}, bf16[128,512]{1,0:T(8,128)(2,1)S(1)}) custom-call(s32[1]{0:T(128)} %bitcast.me_ref, bf16[4,512]{1,0:T(4,128)(2,1)S(1)} %copy-done.23, bf16[512,1536]{1,0:T(8,128)(2,1)S(1)} %copy-done.2, bf16[128,512]{1,0:T(8,128)(2,1)} %get-tuple-element.15.refs_0_, ...), custom_call_target="tpu_custom_call" | custom-call | tf_op jit(solution)/shard_map/temporal/pallas_call | solution.py:324
  49.3 6.0 %all-to-all-start.2 = ((bf16[8,16,1536]{2,1,0:T(8,128)(2,1)}), bf16[8,16,1536]{2,1,0:T(8,128)(2,1)}, u32[]{:S(2)}, u32[]{:S(2)}) async-start(bf16[8,16,1536]{2,1,0:T(8,128)(2,1)} %bitcast.24), calls=%async_computation.2 | async-start | bytes 786432 | tf_op jit(solution)/shard_map/all_to_all | solution.py:343
  55.3 1.0 %copy-done.8 = bf16[256,1024]{1,0:T(8,128)(2,1)S(1)} copy-done((bf16[256,1024]{1,0:T(8,128)(2,1)S(1)}, bf16[256,1024]{1,0:T(8,128)(2,1)}, u32[]{:S(2)}) %copy-start.8) | copy-done | bytes 524312
  56.3 1.0 %copy-done.10 = bf16[4,128,512]{2,1,0:T(8,128)(2,1)S(1)} copy-done((bf16[4,128,512]{2,1,0:T(8,128)(2,1)S(1)}, bf16[4,128,512]{2,1,0:T(8,128)(2,1)}, u32[]{:S(2)}) %copy-start.10) | copy-done | bytes 524312
  57.4 1.0 %copy-done.13 = bf16[128,1536]{1,0:T(8,128)(2,1)S(1)} copy-done((bf16[128,1536]{1,0:T(8,128)(2,1)S(1)}, bf16[128,1536]{1,0:T(8,128)(2,1)}, u32[]{:S(2)}) %copy-start.13) | copy-done | bytes 393240
  58.3 0.9 %copy-done.19 = f32[128,512]{1,0:T(8,128)S(1)} copy-done((f32[128,512]{1,0:T(8,128)S(1)}, f32[128,512]{1,0:T(8,128)}, u32[]{:S(2)}) %copy-start.19) | copy-done | bytes 262168
  59.3 0.9 copy-done.21
  60.2 3.0 %struct_backward.1 = (bf16[64,512]{1,0:T(8,128)(2,1)S(1)}, f32[128,512]{1,0:T(8,128)S(1)}) custom-call(bf16[128,1536]{1,0:T(8,128)(2,1)S(1)} %copy-done.13, bf16[128,512]{1,0:T(8,128)(2,1)S(1)} %copy-done.21, bf16[512,1536]{1,0:T(8,128)(2,1)S(1)} %copy-done.2, bf16[512,1536]{1,0:T(8,128)(2,1)S(1)} %copy-done.1, ...), custom_call_target="tpu_custom_call" | custom-call | tf_op jit(solution)/shard_map/struct_backward/pallas_call | solution.py:350
  64.5 2.8 %all-to-all-done.2 = bf16[8,16,1536]{2,1,0:T(8,128)(2,1)} async-done(((bf16[8,16,1536]{2,1,0:T(8,128)(2,1)}), bf16[8,16,1536]{2,1,0:T(8,128)(2,1)}, u32[]{:S(2)}, u32[]{:S(2)}) %all-to-all-start.2) | async-done | bytes 393248 | tf_op jit(solution)/shard_map/all_to_all | solution.py:343
  67.4 3.8 %all-to-all-start.1 = ((bf16[8,8,512]{2,1,0:T(8,128)(2,1)}), bf16[8,8,512]{2,1,0:T(8,128)(2,1)S(1)}, u32[]{:S(2)}, u32[]{:S(2)}) async-start(bf16[8,8,512]{2,1,0:T(8,128)(2,1)} %bitcast.28), calls=%async_computation.1 | async-start | bytes 131072 | tf_op jit(solution)/shard_map/all_to_all | solution.py:365
  71.1 1.1 %reduce_sum.12 = bf16[16,1536]{1,0:T(8,128)(2,1)S(1)} reduce(bf16[8,16,1536]{2,1,0:T(8,128)(2,1)} %all-to-all-done.2, bf16[]{:T(256)} %constant.8.clone.1), dimensions={0}, to_apply=%region_0.1 | reduce | flops 172032 | bytes 442370 | tf_op jit(solution)/shard_map/reduce_sum | solution.py:368
  72.2 5.8 %all-to-all-done.1 = bf16[8,8,512]{2,1,0:T(8,128)(2,1)S(1)} async-done(((bf16[8,8,512]{2,1,0:T(8,128)(2,1)}), bf16[8,8,512]{2,1,0:T(8,128)(2,1)S(1)}, u32[]{:S(2)}, u32[]{:S(2)}) %all-to-all-start.1) | async-done | bytes 65568 | tf_op jit(solution)/shard_map/all_to_all | solution.py:365
  78.8 3.5 %all-to-all-start.3 = ((bf16[8,16,1536]{2,1,0:T(8,128)(2,1)}), bf16[8,16,1536]{2,1,0:T(8,128)(2,1)S(1)}, u32[]{:S(2)}, u32[]{:S(2)}) async-start(bf16[8,16,1536]{2,1,0:T(8,128)(2,1)} %broadcast_in_dim.5), calls=%async_computation.3 | async-start | bytes 786432 | tf_op jit(solution)/shard_map/all_to_all | solution.py:369
  83.3 9.7 %all-to-all-done.3 = bf16[8,16,1536]{2,1,0:T(8,128)(2,1)S(1)} async-done(((bf16[8,16,1536]{2,1,0:T(8,128)(2,1)}), bf16[8,16,1536]{2,1,0:T(8,128)(2,1)S(1)}, u32[]{:S(2)}, u32[]{:S(2)}) %all-to-all-start.3) | async-done | bytes 393248 | tf_op jit(solution)/shard_map/all_to_all | solution.py:369
  93.0 1.0 %bitcast_convert_fusion = f32[128,1536]{1,0:T(8,128)} fusion(bf16[8,16,1536]{2,1,0:T(8,128)(2,1)S(1)} %all-to-all-done.3), kind=kLoop, calls=%fused_computation.2 | loop fusion | flops 196608 | bytes 1179648 | tf_op jit(solution)/shard_map/reshape | solution.py:376
  (54 shorter events, 10.7 us)
Async XLA Ops:
  3.1 17.6 %all-to-all-start = ((bf16[8,8,512]{2,1,0:T(8,128)(2,1)}), bf16[8,8,512]{2,1,0:T(8,128)(2,1)S(1)}, u32[]{:S(2)}, u32[]{:S(2)}) async-start(bf16[8,8,512]{2,1,0:T(8,128)(2,1)} %fusion), calls=%async_computation | async-start | bytes 131072 | tf_op jit(solution)/shard_map/all_to_all | solution.py:283
  12.7 16.9 %collective-permute-start.4 = (bf16[144,512]{1,0:T(8,128)(2,1)}, bf16[144,512]{1,0:T(8,128)(2,1)}, u32[]{:S(2)}, u32[]{:S(2)}) collective-permute-start(bf16[144,512]{1,0:T(8,128)(2,1)} %fusion.2.refs_4_), channel_id=1, source_target_pairs={{0,2},{1,3},{2,0},{3,1},{4,6},{5,7},{6,4},{7,5},{8,10},{9,11},{10,... | collective-permute-start | bytes 442376 | tf_op jit(solution)/shard_map/ppermute | solution.py:261
  15.8 1.4 %copy-start = (bf16[512,1536]{1,0:T(8,128)(2,1)S(1)}, bf16[512,1536]{1,0:T(8,128)(2,1)}, u32[]{:S(2)}) copy-start(bf16[512,1536]{1,0:T(8,128)(2,1)} %ws_ref.1) | copy-start | bytes 4718596
  17.2 0.9 copy-start.3
  18.1 0.7 copy-start.24
  18.8 2.6 %copy-start.1 = (bf16[512,1536]{1,0:T(8,128)(2,1)S(1)}, bf16[512,1536]{1,0:T(8,128)(2,1)}, u32[]{:S(2)}) copy-start(bf16[512,1536]{1,0:T(8,128)(2,1)} %ws_ref.1) | copy-start | bytes 4718596
  19.8 1.0 %copy-start.5 = (f32[8,128,256]{2,1,0:T(8,128)}, f32[8,128,256]{2,1,0:T(8,128)S(1)}, u32[]{:S(2)}) copy-start(f32[8,128,256]{2,1,0:T(8,128)S(1)} %get-tuple-element.14.weight_ref) | copy-start | bytes 3145732
  21.4 0.9 copy-start.4
  22.3 1.2 %copy-start.6 = (f32[8,128,256]{2,1,0:T(8,128)S(1)}, f32[8,128,256]{2,1,0:T(8,128)}, u32[]{:S(2)}) copy-start(f32[8,128,256]{2,1,0:T(8,128)} %copy-done.5) | copy-start | bytes 3145732
  23.5 0.8 copy-start.15
  24.4 11.7 %copy-start.2 = (bf16[512,1536]{1,0:T(8,128)(2,1)S(1)}, bf16[512,1536]{1,0:T(8,128)(2,1)}, u32[]{:S(2)}) copy-start(bf16[512,1536]{1,0:T(8,128)(2,1)} %wt_ref.1) | copy-start | bytes 4718596
  24.4 11.7 %copy-start.23 = (bf16[4,512]{1,0:T(4,128)(2,1)S(1)}, bf16[4,512]{1,0:T(4,128)(2,1)}, u32[]{:S(2)}) copy-start(bf16[4,512]{1,0:T(4,128)(2,1)} %pos_ref.1) | copy-start | bytes 12292
  26.8 0.8 copy-start.7
  27.6 0.8 copy-start.9
  28.4 0.7 copy-start.18
  29.1 5.3 %collective-permute-start.1 = (bf16[128,512]{1,0:T(8,128)(2,1)}, bf16[128,512]{1,0:T(8,128)(2,1)}, u32[]{:S(2)}, u32[]{:S(2)}) collective-permute-start(bf16[128,512]{1,0:T(8,128)(2,1)} %get-tuple-element.15.refs_0_), channel_id=1, source_target_pairs={{0,2},{1,3},{2,0},{3,1},{4,6},{5,7},{6,4},{7,5},{8,10},{9,11},{10,... | collective-permute-start | bytes 393224 | tf_op jit(solution)/shard_map/ppermute | solution.py:261
  29.6 4.8 %collective-permute-start.3 = (bf16[144,512]{1,0:T(8,128)(2,1)}, bf16[144,512]{1,0:T(8,128)(2,1)}, u32[]{:S(2)}, u32[]{:S(2)}) collective-permute-start(bf16[144,512]{1,0:T(8,128)(2,1)} %fusion.2.refs_4_), channel_id=1, source_target_pairs={{0,1},{1,0},{2,3},{3,2},{4,5},{5,4},{6,7},{7,6},{8,9},{9,8},{10,11... | collective-permute-start | bytes 442376 | tf_op jit(solution)/shard_map/ppermute | solution.py:261
  29.6 4.8 %collective-permute-start.5 = (bf16[144,512]{1,0:T(8,128)(2,1)}, bf16[144,512]{1,0:T(8,128)(2,1)}, u32[]{:S(2)}, u32[]{:S(2)}) collective-permute-start(bf16[144,512]{1,0:T(8,128)(2,1)} %collective-permute-done.4.refs_6_), channel_id=1, source_target_pairs={{0,1},{1,0},{2,3},{3,2},{4,5},{5,4},{6,7},{7,6},{8,9},{9,8},{10,11... | collective-permute-start | bytes 442376 | tf_op jit(solution)/shard_map/ppermute | solution.py:261
  30.1 4.3 %collective-permute-start = (bf16[128,512]{1,0:T(8,128)(2,1)}, bf16[128,512]{1,0:T(8,128)(2,1)}, u32[]{:S(2)}, u32[]{:S(2)}) collective-permute-start(bf16[128,512]{1,0:T(8,128)(2,1)} %get-tuple-element.15.refs_0_), channel_id=1, source_target_pairs={{0,1},{1,0},{2,3},{3,2},{4,5},{5,4},{6,7},{7,6},{8,9},{9,8},{10,11... | collective-permute-start | bytes 393224 | tf_op jit(solution)/shard_map/ppermute | solution.py:261
  34.4 1.7 %collective-permute-start.2 = (bf16[128,512]{1,0:T(8,128)(2,1)}, bf16[128,512]{1,0:T(8,128)(2,1)}, u32[]{:S(2)}, u32[]{:S(2)}) collective-permute-start(bf16[128,512]{1,0:T(8,128)(2,1)} %collective-permute-done.1.refs_2_), channel_id=1, source_target_pairs={{0,1},{1,0},{2,3},{3,2},{4,5},{5,4},{6,7},{7,6},{8,9},{9,8},{10,11... | collective-permute-start | bytes 393224 | tf_op jit(solution)/shard_map/ppermute | solution.py:261
  47.1 0.8 copy-start.11
  47.8 0.8 copy-start.12
  49.3 18.1 %all-to-all-start.2 = ((bf16[8,16,1536]{2,1,0:T(8,128)(2,1)}), bf16[8,16,1536]{2,1,0:T(8,128)(2,1)}, u32[]{:S(2)}, u32[]{:S(2)}) async-start(bf16[8,16,1536]{2,1,0:T(8,128)(2,1)} %bitcast.24), calls=%async_computation.2 | async-start | bytes 786432 | tf_op jit(solution)/shard_map/all_to_all | solution.py:343
  55.3 1.0 %copy-start.8 = (bf16[256,1024]{1,0:T(8,128)(2,1)S(1)}, bf16[256,1024]{1,0:T(8,128)(2,1)}, u32[]{:S(2)}) copy-start(bf16[256,1024]{1,0:T(8,128)(2,1)} %copy-done.7) | copy-start | bytes 1572868
  56.3 1.0 %copy-start.10 = (bf16[4,128,512]{2,1,0:T(8,128)(2,1)S(1)}, bf16[4,128,512]{2,1,0:T(8,128)(2,1)}, u32[]{:S(2)}) copy-start(bf16[4,128,512]{2,1,0:T(8,128)(2,1)} %copy-done.9) | copy-start | bytes 1572868
  57.3 1.0 %copy-start.13 = (bf16[128,1536]{1,0:T(8,128)(2,1)S(1)}, bf16[128,1536]{1,0:T(8,128)(2,1)}, u32[]{:S(2)}) copy-start(bf16[128,1536]{1,0:T(8,128)(2,1)} %copy-done.12) | copy-start | bytes 1179652
  58.3 0.9 %copy-start.19 = (f32[128,512]{1,0:T(8,128)S(1)}, f32[128,512]{1,0:T(8,128)}, u32[]{:S(2)}) copy-start(f32[128,512]{1,0:T(8,128)} %copy-done.18) | copy-start | bytes 786436
  59.3 0.9 copy-start.21
  63.2 0.7 copy-start.16
  67.4 15.2 %copy-start.17 = (f32[128,512]{1,0:T(8,128)S(1)}, f32[128,512]{1,0:T(8,128)}, u32[]{:S(2)}) copy-start(f32[128,512]{1,0:T(8,128)} %copy-done.16) | copy-start | bytes 786436
  67.4 10.7 %all-to-all-start.1 = ((bf16[8,8,512]{2,1,0:T(8,128)(2,1)}), bf16[8,8,512]{2,1,0:T(8,128)(2,1)S(1)}, u32[]{:S(2)}, u32[]{:S(2)}) async-start(bf16[8,8,512]{2,1,0:T(8,128)(2,1)} %bitcast.28), calls=%async_computation.1 | async-start | bytes 131072 | tf_op jit(solution)/shard_map/all_to_all | solution.py:365
  78.8 14.2 %all-to-all-start.3 = ((bf16[8,16,1536]{2,1,0:T(8,128)(2,1)}), bf16[8,16,1536]{2,1,0:T(8,128)(2,1)S(1)}, u32[]{:S(2)}, u32[]{:S(2)}) async-start(bf16[8,16,1536]{2,1,0:T(8,128)(2,1)} %broadcast_in_dim.5), calls=%async_computation.3 | async-start | bytes 786432 | tf_op jit(solution)/shard_map/all_to_all | solution.py:369
  (3 other events, 1.9 us)

commit v2 on v0

v2 whole, which is shorter than its diff:
```python
import functools

import jax
import jax.numpy as jnp
from jax import lax
from jax.experimental import pallas as pl
from jax.experimental.pallas import tpu as pltpu
from jax.sharding import PartitionSpec as P

F32 = jnp.float32
BF16 = jnp.bfloat16
LANES = 128
NEG = -1e30
VMEM = pl.BlockSpec(memory_space=pltpu.VMEM)
SMEM = pl.BlockSpec(memory_space=pltpu.SMEM)
ANY = pl.BlockSpec(memory_space=pl.ANY)


def dot_nn(a, b):
    return lax.dot_general(a, b, (((1,), (0,)), ((), ())), preferred_element_type=F32)


def dot_nt(a, b):
    return lax.dot_general(a, b, (((1,), (1,)), ((), ())), preferred_element_type=F32)


def dot_tn(a, b):
    return lax.dot_general(a, b, (((0,), (0,)), ((), ())), preferred_element_type=F32)


def stack_heads(block, head_dim):
    rows, lanes = block.shape
    head = lax.broadcasted_iota(jnp.int32, (rows, lanes), 1) // head_dim
    zero = jnp.zeros_like(block)
    return jnp.concatenate(
        [jnp.where(head == g, block, zero) for g in range(lanes // head_dim)], axis=0
    )


def unstack_heads(stacked, head_dim):
    lanes = stacked.shape[1]
    groups = lanes // head_dim
    rows = stacked.shape[0] // groups
    head = lax.broadcasted_iota(jnp.int32, (rows, lanes), 1) // head_dim
    out = stacked[:rows]
    for g in range(1, groups):
        out = jnp.where(head == g, stacked[g * rows : (g + 1) * rows], out)
    return out


class Fetch:

    def __init__(self, sems, *pairs):
        self.copies = [
            pltpu.make_async_copy(src, dst, sems.at[i]) for i, (src, dst) in enumerate(pairs)
        ]
        for copy in self.copies:
            copy.start()

    def wait(self, *which):
        for i in which:
            self.copies[i].wait()


def pick_rows(route_ref, local):
    doms, per = route_ref.shape
    lane = lax.broadcasted_iota(jnp.int32, (per, local), 1)
    sub = lax.broadcasted_iota(jnp.int32, (per, local), 0)
    tiles = []
    for r in range(doms):
        spot = jnp.zeros((per, local), jnp.int32)
        for j in range(per):
            spot = jnp.where(sub == j, route_ref[r, j], spot)
        tiles.append(jnp.where(lane == spot, 1.0, 0.0))
    return jnp.concatenate(tiles, axis=0).astype(BF16)


def tiles_kernel(route_ref, x_ref, out_ref):
    out_ref[...] = dot_nn(pick_rows(route_ref, x_ref.shape[0]), x_ref[...]).astype(BF16)


def own_kernel(x_ref, w_hbm, nbr_ref, rel_ref, act_ref, cot_ref, proj_ref, count_ref, load_ref, w_s, sems):
    rows, width = x_ref.shape
    kinds, _, keys = count_ref.shape
    slots = nbr_ref.shape[0]
    snaps, ents, _ = cot_ref.shape
    fetch = Fetch(sems, (w_hbm, w_s))
    for t in range(snaps):
        load_ref[t] = cot_ref[t]
    row = lax.broadcasted_iota(jnp.int32, (ents, ents), 0)
    col = lax.broadcasted_iota(jnp.int32, (ents, ents), 1)
    lane = lax.broadcasted_iota(jnp.int32, (ents, width), 1)
    flags = jnp.zeros((ents, width), F32)
    act = act_ref[...].astype(F32)
    for t in range(snaps):
        column = jnp.sum(jnp.where(row == col, act[t : t + 1, :], 0.0), axis=1, keepdims=True)
        flags = jnp.where(lane == t, column, flags)
    load_ref[snaps] = flags.astype(BF16)
    code = jnp.transpose((nbr_ref[...] * kinds + rel_ref[...]).astype(F32))
    spot = (lax.broadcasted_iota(jnp.int32, (rows, keys), 1) * kinds).astype(F32)
    for r in range(kinds):
        here = spot + float(r)
        count = jnp.zeros((rows, keys), F32)
        for k in range(slots):
            count = count + jnp.where(code[:, k : k + 1] == here, 1.0, 0.0)
        count_ref[r] = count.astype(BF16)
    fetch.wait(0)
    x = x_ref[...]
    for part in range(3):
        cols = slice(part * width, (part + 1) * width)
        proj_ref[:, cols] = dot_nn(x, w_s[:, cols]).astype(BF16)


def fill_table(tab_s, proj, halo, w_kv):
    rows, width = proj.shape[0], halo.shape[1]
    used = rows + halo.shape[0]
    tab_s[:rows, :] = proj[:, width:]
    for part in range(2):
        cols = slice(part * width, (part + 1) * width)
        tab_s[rows:used, cols] = dot_nn(halo[...], w_kv[:, cols]).astype(BF16)
    if tab_s.shape[0] > used:
        tab_s[used:, :] = jnp.zeros((tab_s.shape[0] - used, 2 * width), BF16)


def edge_attention(p, heads, proj, count, bias, tab_s, width):
    keys = tab_s.shape[0]
    head_dim = width // heads
    group = LANES // head_dim
    cols = slice(p * LANES, (p + 1) * LANES)
    kk = stack_heads(tab_s[:, cols], head_dim)
    score = dot_nt(proj[:, cols], kk) * head_dim ** (-0.5)
    gain = jnp.exp(bias[...])
    parts = []
    for g in range(group):
        h = p * group + g
        wt = count[0].astype(F32) * gain[0:1, h : h + 1]
        for r in range(1, count.shape[0]):
            wt = wt + count[r].astype(F32) * gain[r : r + 1, h : h + 1]
        s = jnp.where(wt > 0, score[:, g * keys : (g + 1) * keys], NEG)
        e = jnp.exp(s - jnp.max(s, axis=1, keepdims=True)) * wt
        parts.append(e * (1.0 / jnp.sum(e, axis=1, keepdims=True)))
    return kk, parts


def forward_kernel(
    heads, x_ref, bias_ref, halo_hbm, proj_hbm, count_hbm, w_hbm, hidden_ref,
    halo, proj, count, w_kv, tab_s, sems,
):
    width = x_ref.shape[1]
    head_dim = width // heads
    fetch = Fetch(
        sems,
        (halo_hbm, halo),
        (w_hbm.at[:, width:], w_kv),
        (proj_hbm, proj),
        (count_hbm, count),
    )
    fetch.wait(0, 1, 2, 3)
    fill_table(tab_s, proj, halo, w_kv)
    for p in range(width // LANES):
        cols = slice(p * LANES, (p + 1) * LANES)
        vcols = slice(width + p * LANES, width + (p + 1) * LANES)
        _, attn = edge_attention(p, heads, proj, count, bias_ref, tab_s, width)
        vv = stack_heads(tab_s[:, vcols], head_dim)
        agg = dot_nn(jnp.concatenate([a.astype(BF16) for a in attn], axis=1), vv)
        elu = jnp.where(agg > 0, agg, jnp.exp(jnp.minimum(agg, 0.0)) - 1.0)
        hidden_ref[:, cols] = (x_ref[:, cols].astype(F32) + elu).astype(BF16)


def each(lo, hi, unroll, body):
    if unroll:
        for i in range(lo, hi):
            body(i)
    else:
        lax.fori_loop(lo, hi, lambda i, c: (body(i), c)[1], 0)


def temporal_kernel(snaps, heads, me_ref, pos_ref, w_hbm, *refs):
    hid_hbm = refs[:snaps]
    cot_hbm = refs[snaps : 2 * snaps]
    (
        terms_ref, dt_own_ref, cot_own_ref,
        w_s, hid, cot, z_s, ct_s, tp_s, dt_s, act_s, s_s, d_s, a_s, ds_s, dk_s, dv_s, sems,
    ) = refs[2 * snaps :]
    _, local, width = hid.shape
    ents = cot.shape[2]
    head_dim = width // heads
    scale = head_dim ** (-0.5)
    unroll = snaps <= 4
    me = me_ref[0]
    fetch = Fetch(
        sems,
        *[(hid_hbm[n], hid.at[n]) for n in range(snaps)],
        (w_hbm, w_s),
        *[(cot_hbm[n], cot.at[n]) for n in range(snaps)],
    )
    pos = pos_ref[...].astype(F32)
    which = lax.broadcasted_iota(jnp.int32, pos.shape, 0)

    def rows_of(t):
        return pl.ds(t * local if isinstance(t, int) else pl.multiple_of(t * local, local), local)

    for n in range(snaps):
        t = lax.bitwise_xor(me, n)
        shift = jnp.sum(jnp.where(which == t, pos, 0.0), axis=0, keepdims=True)
        fetch.wait(n)
        z_s[rows_of(t), :] = (hid[n].astype(F32) + shift).astype(BF16)
    fetch.wait(snaps)
    for part in range(3):
        cols = slice(part * width, (part + 1) * width)
        tp_s[:, cols] = dot_nn(z_s[...], w_s[:, cols]).astype(BF16)
    fetch.wait(*range(snaps + 1, 2 * snaps + 1))
    for m in range(snaps):
        at = pl.multiple_of(lax.bitwise_xor(me, m) * ents, ents)
        for t in range(snaps):
            ct_s[pl.ds(t * local + at, ents), :] = cot[m, t].astype(ct_s.dtype)
        act_s[pl.ds(at, ents), :] = cot[m, snaps][:, :LANES].astype(F32)
    lane_head = lax.broadcasted_iota(jnp.int32, (width, LANES), 0) // head_dim
    fold = (lane_head == lax.broadcasted_iota(jnp.int32, (width, LANES), 1)).astype(F32).astype(BF16)
    head_lane = lax.broadcasted_iota(jnp.int32, (LANES, width), 1) // head_dim
    spread = (head_lane == lax.broadcasted_iota(jnp.int32, (LANES, width), 0)).astype(F32).astype(BF16)
    spread_scaled = (spread.astype(F32) * scale).astype(BF16)
    act = act_s[...]
    snap_lane = lax.broadcasted_iota(jnp.int32, act.shape, 1)
    dk_s[...] = jnp.zeros_like(dk_s)
    dv_s[...] = jnp.zeros_like(dv_s)

    def scores(t):
        def pair(u):
            q, k, v = (
                tp_s[rows_of(i), part * width : (part + 1) * width]
                for part, i in ((0, t), (1, u), (2, u))
            )
            s = dot_nn(q * k, fold) * scale
            on = jnp.sum(jnp.where(snap_lane == u, act, 0.0), axis=1, keepdims=True)
            s_s[u] = jnp.where((on > 0.5) | (u == t), s, NEG)
            d = dot_nn(ct_s[rows_of(t), :].astype(BF16) * v, fold)
            d_s[u] = d.astype(BF16).astype(F32)

        each(0, t + 1, unroll, pair)
        top = s_s[0]
        if unroll:
            for u in range(1, t + 1):
                top = jnp.maximum(top, s_s[u])
        else:
            top = lax.fori_loop(1, t + 1, lambda u, c: jnp.maximum(c, s_s[u]), top)
        zero = jnp.zeros_like(top)

        def expo(u, total):
            e = jnp.exp(s_s[u] - top)
            s_s[u] = e
            return total + e

        total = zero
        if unroll:
            for u in range(t + 1):
                total = expo(u, total)
        else:
            total = lax.fori_loop(0, t + 1, expo, total)
        inv = 1.0 / total

        def weigh(u, dot):
            a = s_s[u] * inv
            s_s[u] = a
            return dot + a * d_s[u]

        dot = zero
        if unroll:
            for u in range(t + 1):
                dot = weigh(u, dot)
        else:
            dot = lax.fori_loop(0, t + 1, weigh, dot)

        def keep(u):
            a = s_s[u]
            a_s[u] = a.astype(BF16)
            ds_s[u] = (a * (d_s[u] - dot)).astype(BF16)

        each(0, t + 1, unroll, keep)

        for p in range(width // LANES):
            c0 = p * LANES
            cols = slice(c0, c0 + LANES)
            q = tp_s[rows_of(t), cols].astype(F32)
            ct = ct_s[rows_of(t), cols].astype(F32)

            def back(u, dq):
                k = tp_s[rows_of(u), width + c0 : width + c0 + LANES].astype(F32)
                wide_ds = dot_nn(ds_s[u], spread_scaled[:, cols])
                wide_a = dot_nn(a_s[u], spread[:, cols])
                dk_s[rows_of(u), cols] += wide_ds * q
                dv_s[rows_of(u), cols] += wide_a * ct
                return dq + wide_ds * k

            dq = jnp.zeros_like(q)
            if unroll:
                for u in range(t + 1):
                    dq = back(u, dq)
            else:
                dq = lax.fori_loop(0, t + 1, back, dq)
            dt_s[rows_of(t), cols] = dq.astype(BF16)

    each(0, snaps, unroll, scores)
    dt_s[:, width : 2 * width] = dk_s[...].astype(BF16)
    dt_s[:, 2 * width :] = dv_s[...].astype(BF16)
    share = width // snaps
    pick = (
        lax.broadcasted_iota(jnp.int32, (width, share), 0)
        == lax.broadcasted_iota(jnp.int32, (width, share), 1) + me * share
    )
    z_mine = dot_nn(z_s[...], jnp.where(pick, 1.0, 0.0).astype(BF16)).astype(BF16)
    for part in range(3):
        cols = slice(part * width, (part + 1) * width)
        terms_ref[:, cols] = dot_tn(z_mine, dt_s[:, cols]).astype(BF16)
    dt_own_ref[...] = dt_s[rows_of(me), :]
    cot_own_ref[...] = ct_s[rows_of(me), :].astype(BF16)


def backward_kernel(
    heads, bias_ref, halo_hbm, proj_hbm, count_hbm, ws_hbm, wt_hbm, dt_hbm, cot_hbm, back_ref, part_ref,
    halo, proj, count, ws, wt, dt, cot, tab_s, dq_s, dtab_s, sems,
):
    rows, width = cot.shape
    halo_rows = halo.shape[0]
    keys = tab_s.shape[0]
    head_dim = width // heads
    group = LANES // head_dim
    scale = head_dim ** (-0.5)
    fetch = Fetch(
        sems,
        (halo_hbm, halo),
        (ws_hbm, ws),
        (proj_hbm, proj),
        (count_hbm, count),
        (dt_hbm, dt),
        (cot_hbm, cot),
        (wt_hbm, wt),
    )
    fetch.wait(*range(7))
    fill_table(tab_s, proj, halo, ws.at[:, width:])
    dh = cot[...].astype(F32) + dot_nt(dt[...], wt[...])
    part_ref[...] = dh.astype(BF16).astype(F32)
    for p in range(width // LANES):
        cols = slice(p * LANES, (p + 1) * LANES)
        vcols = slice(width + p * LANES, width + (p + 1) * LANES)
        kk, attn = edge_attention(p, heads, proj, count, bias_ref, tab_s, width)
        vv = stack_heads(tab_s[:, vcols], head_dim)
        attn_b = jnp.concatenate([a.astype(BF16) for a in attn], axis=1)
        agg = dot_nn(attn_b, vv)
        da = part_ref[:, cols] * jnp.where(agg > 0, 1.0, jnp.exp(jnp.minimum(agg, 0.0)))
        da = da.astype(BF16)
        dattn = dot_nt(da, vv).astype(BF16).astype(F32)
        ds = []
        for g in range(group):
            ad = attn[g] * dattn[:, g * keys : (g + 1) * keys]
            ds.append((ad - attn[g] * jnp.sum(ad, axis=1, keepdims=True)).astype(BF16))
        ds = jnp.concatenate(ds, axis=1)
        dq_s[:, cols] = (dot_nn(ds, kk) * scale).astype(BF16)
        dtab_s[:, cols] = (unstack_heads(dot_tn(ds, proj[:, cols]), head_dim) * scale).astype(BF16)
        dtab_s[:, vcols] = unstack_heads(dot_tn(attn_b, da), head_dim).astype(BF16)
    back_ref[...] = dot_nt(dtab_s[rows : rows + halo_rows, :], ws[:, width:])
    part_ref[...] += dot_nt(dq_s[...], ws[:, :width]) + dot_nt(dtab_s[:rows, :], ws[:, width:])


def sum_kernel(parts_ref, back_ref, out_ref):
    doms, rows, wide = parts_ref.shape
    per = back_ref.shape[0] // doms
    half = back_ref.shape[1] * per // rows
    total = parts_ref[0].astype(F32)
    for d in range(1, doms):
        total = total + parts_ref[d].astype(F32)
    total = total.astype(BF16)
    for d in range(doms):
        out_ref[d, :, :wide] = total
        tile = back_ref[d * per : (d + 1) * per, :]
        folded = [tile[:, i * half : (i + 1) * half] for i in range(rows // per)]
        out_ref[d, :, wide:] = jnp.concatenate(folded, axis=0).astype(BF16)


def last_kernel(route_ref, got_ref, part_ref, feat_ref, wtemp_ref, came_s):
    doms, rows, wide = got_ref.shape
    per = came_s.shape[0] // doms
    half = came_s.shape[1] * per // rows
    wide -= half
    for d in range(doms):
        wtemp_ref[d * rows : (d + 1) * rows, :] = got_ref[d, :, :wide].astype(F32)
        folded = got_ref[d, :, wide:].astype(F32)
        for i in range(rows // per):
            came_s[d * per : (d + 1) * per, i * half : (i + 1) * half] = folded[
                i * per : (i + 1) * per
            ]
    picks = pick_rows(route_ref, part_ref.shape[0])
    back = dot_tn(picks, came_s[...].astype(BF16))
    feat_ref[...] = (part_ref[...] + back).astype(BF16)


def params(mib):
    return pltpu.CompilerParams(vmem_limit_bytes=mib * 1024 * 1024)


def gather_blocks(block, axis):
    count = lax.axis_size(axis)
    held = {0: block}
    bit = count // 2
    while bit:
        for m in sorted(held):
            pairs = [(i, i ^ bit) for i in range(count)]
            held[m ^ bit] = lax.ppermute(held[m], axis, pairs)
        bit //= 2
    return [held[m] for m in range(count)]


def exchange(tiles, axis):
    return lax.all_to_all(tiles, axis, split_axis=0, concat_axis=0, tiled=True)


def per_device(
    feat, w_struct, w_temp, pos_embed, rel_bias, nbr, rel_type, send_idx, active, cotangent
):
    x = feat[0]
    local, width = x.shape
    kinds, heads = rel_bias.shape
    slots = nbr.shape[2]
    doms = lax.axis_size("dom")
    snaps = lax.axis_size("snap")
    ents = local // snaps
    route = send_idx[0, 0]
    halo_per = route.shape[1]
    halo_rows = doms * halo_per
    keys = -(-(local + halo_rows) // LANES) * LANES
    share = width // snaps
    piece = share // doms
    me = lax.axis_index("snap").astype(jnp.int32).reshape(1)

    def shape(*dims, dtype=BF16):
        return jax.ShapeDtypeStruct(dims, dtype)

    tiles = pl.pallas_call(
        tiles_kernel,
        out_shape=shape(halo_rows, width),
        in_specs=[SMEM, VMEM],
        out_specs=VMEM,
        compiler_params=params(8),
        name="halo_tiles",
    )(route, x)
    halo = exchange(tiles.reshape(doms, halo_per, width), "dom").reshape(halo_rows, width)

    proj, count, load = pl.pallas_call(
        own_kernel,
        out_shape=(
            shape(local, 3 * width),
            shape(kinds, local, keys),
            shape(snaps + 1, ents, width),
        ),
        in_specs=[VMEM, ANY, VMEM, VMEM, VMEM, VMEM],
        out_specs=(VMEM,) * 3,
        scratch_shapes=[pltpu.VMEM(w_struct.shape, BF16), pltpu.SemaphoreType.DMA((1,))],
        compiler_params=params(16),
        cost_estimate=pl.CostEstimate(flops=10**9, bytes_accessed=4 * 10**6, transcendentals=0),
        name="own_rows",
    )(x, w_struct, nbr[0].T, rel_type[0].T, active, cotangent)
    cots = gather_blocks(load, "snap")

    hidden = pl.pallas_call(
        functools.partial(forward_kernel, heads),
        out_shape=shape(local, width),
        in_specs=[VMEM, VMEM] + [ANY] * 4,
        out_specs=VMEM,
        scratch_shapes=[
            pltpu.VMEM((halo_rows, width), BF16),
            pltpu.VMEM((local, 3 * width), BF16),
            pltpu.VMEM((kinds, local, keys), BF16),
            pltpu.VMEM((width, 2 * width), BF16),
            pltpu.VMEM((keys, 2 * width), BF16),
            pltpu.SemaphoreType.DMA((4,)),
        ],
        compiler_params=params(16),
        name="struct_forward",
    )(x, rel_bias, halo, proj, count, w_struct)

    hids = gather_blocks(hidden, "snap")
    every = snaps * local
    terms, dt_own, cot_own = pl.pallas_call(
        functools.partial(temporal_kernel, snaps, heads),
        out_shape=(shape(share, 3 * width), shape(local, 3 * width), shape(local, width)),
        in_specs=[SMEM, VMEM] + [ANY] * (1 + 2 * snaps),
        out_specs=(VMEM,) * 3,
        scratch_shapes=[
            pltpu.VMEM(w_temp.shape, BF16),
            pltpu.VMEM((snaps, local, width), BF16),
            pltpu.VMEM((snaps, snaps + 1, ents, width), BF16),
            pltpu.VMEM((every, width), BF16),
            pltpu.VMEM((every, width), F32 if ents % 16 else BF16),
            pltpu.VMEM((every, 3 * width), BF16),
            pltpu.VMEM((every, 3 * width), BF16),
            pltpu.VMEM((local, LANES), F32),
            pltpu.VMEM((snaps, local, LANES), F32),
            pltpu.VMEM((snaps, local, LANES), F32),
            pltpu.VMEM((snaps, local, LANES), BF16),
            pltpu.VMEM((snaps, local, LANES), BF16),
            pltpu.VMEM((every, width), F32),
            pltpu.VMEM((every, width), F32),
            pltpu.SemaphoreType.DMA((2 * snaps + 1,)),
        ],
        compiler_params=params(24 if snaps <= 4 else 56),
        name="temporal",
    )(me, pos_embed, w_temp, *hids, *cots)

    parts = exchange(terms.reshape(doms, piece, 3 * width), "dom")
    back, partial = pl.pallas_call(
        functools.partial(backward_kernel, heads),
        out_shape=(shape(halo_rows, width, dtype=F32), shape(local, width, dtype=F32)),
        in_specs=[VMEM] + [ANY] * 7,
        out_specs=(VMEM, VMEM),
        scratch_shapes=[
            pltpu.VMEM((halo_rows, width), BF16),
            pltpu.VMEM((local, 3 * width), BF16),
            pltpu.VMEM((kinds, local, keys), BF16),
            pltpu.VMEM(w_struct.shape, BF16),
            pltpu.VMEM(w_temp.shape, BF16),
            pltpu.VMEM((local, 3 * width), BF16),
            pltpu.VMEM((local, width), BF16),
            pltpu.VMEM((keys, 2 * width), BF16),
            pltpu.VMEM((local, width), BF16),
            pltpu.VMEM((keys, 2 * width), BF16),
            pltpu.SemaphoreType.DMA((7,)),
        ],
        compiler_params=params(24),
        cost_estimate=pl.CostEstimate(flops=2 * 10**9, bytes_accessed=8 * 10**6, transcendentals=0),
        name="struct_backward",
    )(rel_bias, halo, proj, count, w_struct, w_temp, dt_own, cot_own)

    if piece % 16 == 0 and (halo_per * width) % (piece * LANES) == 0:
        side = halo_per * width // piece
        mixed = pl.pallas_call(
            sum_kernel,
            out_shape=shape(doms, piece, 3 * width + side),
            in_specs=[VMEM, VMEM],
            out_specs=VMEM,
            compiler_params=params(8),
            name="sum_parts",
        )(parts, back)
        got = exchange(mixed, "dom")
        grad_feat, grad_wtemp = pl.pallas_call(
            last_kernel,
            out_shape=(shape(local, width), shape(share, 3 * width, dtype=F32)),
            in_specs=[SMEM, VMEM, VMEM],
            out_specs=(VMEM, VMEM),
            scratch_shapes=[pltpu.VMEM((halo_rows, width), F32)],
            compiler_params=params(8),
            name="last_sums",
        )(route, got, partial)
        return (grad_feat[None], grad_wtemp)
    total = jnp.sum(parts.astype(F32), axis=0).astype(BF16)
    got = exchange(jnp.broadcast_to(total[None], (doms,) + total.shape), "dom")
    grad_wtemp = got.astype(F32).reshape(share, 3 * width)
    came = exchange(back.astype(BF16).reshape(doms, halo_per, width), "dom")
    picks = (route.reshape(-1)[:, None] == jnp.arange(local, dtype=jnp.int32)).astype(BF16)
    sums = dot_tn(picks, came.reshape(halo_rows, width))
    return ((partial + sums).astype(BF16)[None], grad_wtemp)


def solution(mesh):
    return jax.shard_map(
        per_device,
        mesh=mesh,
        in_specs=(
            P("snap", "dom", None),
            P(),
            P(),
            P(),
            P(),
            P("snap", "dom", None),
            P("snap", "dom", None),
            P("snap", "dom", None, None),
            P(None, ("dom", "snap")),
            P(None, ("dom", "snap"), None),
        ),
        out_specs=(P("snap", "dom", None), P("snap", None)),
        check_vma=False,
    )
```

time: 216 us -> 79.4 us (0.37)
  waiting for transfers between devices: 78.6 us -> 5.5 us
  other arithmetic: 47.8 us -> 0 us
  local copies, waits for them, and re-layouts: 42 us -> 19.4 us
  blocking collectives: 0 us -> 18.7 us
  Pallas kernels: 0 us -> 18.3 us
  between operations: 14.7 us -> 0.78 us
  matrix products: 13.5 us -> 0 us
  starting transfers between devices: 18.4 us -> 15.9 us
    psum x1 -> x0, waiting for transfers between devices: 63.2 us -> none  [per_device(): grad_wtemp = lax.psum(share, 'dom').astype(jnp.float32)]
    reshape x9 -> x0, local copies, waits for them, and re-layouts: 19.7 us -> none  [the longest x2 8.7 us: struct_core(): keys_g = key_tab[links].reshape(row_count, slots, HEADS, head_dim)]
    unnamed x5 -> x0, other arithmetic: 18.9 us -> none
    all_to_all x0 -> x1, blocking collectives: none -> 18.7 us  [exchange(): return lax.all_to_all(tiles, axis, split_axis=0, concat_axis=0, tiled=True)]
    pallas_call x0 -> x7, Pallas kernels: none -> 18.3 us  [the longest x1 5.83 us: per_device(): pl.pallas_call(functools.partial(backward_kernel, heads), out_shape=(shap...]
    scatter-add x3 -> x0, other arithmetic: 18 us -> none  [the longest x1 7.36 us: struct_core(): keys_g = key_tab[links].reshape(row_count, slots, HEADS, head_dim)]
    unnamed x52 -> x62, local copies, waits for them, and re-layouts: 2.83 us -> 19.4 us
    all_to_all x4 -> x2, waiting for transfers between devices: 14.7 us -> 0.09 us  [exchange(): return lax.all_to_all(tiles, axis, split_axis=0, concat_axis=0, tiled=True)]
  transfers between devices with their start and end apart: 6 -> 8, of which waited for: 5 -> 3; matrix products, arithmetic and copies ran while one was open for 24% -> 0% of each run, Pallas kernels for 0% -> 12%
where the time goes in v2:
time: 79.4 us; the launch traced here: 78.6 us
  local copies, waits for them, and re-layouts  19.4 us (24%)
  blocking collectives  18.7 us (24%)
  Pallas kernels  18.3 us (23%)
  starting transfers between devices  15.9 us (20%)
  waiting for transfers between devices  5.5 us (7%)
    unnamed x62, local copies, waits for them, and re-layouts  19.4 us
    all_to_all x1, blocking collectives, exchange(): return lax.all_to_all(tiles, axis, split_axis=0, concat_axis=0, tiled=True)  18.7 us
    all_to_all x2, starting transfers between devices, exchange(): return lax.all_to_all(tiles, axis, split_axis=0, concat_axis=0, tiled=True)  13.3 us
    pallas_call x1, Pallas kernels, per_device(): pl.pallas_call(functools.partial(backward_kernel, heads), out_shape=(shap...  5.83 us
    pallas_call x1, Pallas kernels, per_device(): pl.pallas_call(functools.partial(temporal_kernel, snaps, heads), out_shap...  5.55 us
    ppermute x6, waiting for transfers between devices, gather_blocks(): held[m ^ bit] = lax.ppermute(held[m], axis, pairs)  5.41 us
    ppermute x6, starting transfers between devices, gather_blocks(): held[m ^ bit] = lax.ppermute(held[m], axis, pairs)  2.61 us
    pallas_call x1, Pallas kernels, per_device(): pl.pallas_call(functools.partial(forward_kernel, heads), out_shape=shape(...  2.35 us
  transfers between devices with their start and end apart: 8, of which 3 were waited for; matrix products, arithmetic and copies ran while one was open for 0% of the time, Pallas kernels for 12%

profile of v2, /device:TPU:0, one launch (start us, length us, event | category | flops | bytes accessed | tf_op | source)
XLA Modules:
  0.0 78.6 jit_solution(3816726268856081887)
XLA Ops:
  0.6 0.9 %copy-done.3 = bf16[1,128,512]{2,1,0:T(8,128)(2,1)S(1)} copy-done((bf16[1,128,512]{2,1,0:T(8,128)(2,1)S(1)}, bf16[1,128,512]{2,1,0:T(8,128)(2,1)}, u32[]{:S(2)}) %copy-start.3) | copy-done | bytes 131096
  1.5 0.7 copy-done.19
  2.2 1.4 %halo_tiles.1 = bf16[64,512]{1,0:T(8,128)(2,1)} custom-call(s32[8,8]{1,0:T(8,128)S(1)} %bitcast.19, bf16[128,512]{1,0:T(8,128)(2,1)S(1)} %bitcast.13), custom_call_target="tpu_custom_call" | custom-call | tf_op jit(solution)/shard_map/halo_tiles/pallas_call | solution.py:438
  3.6 7.3 %all-to-all-start = ((bf16[8,8,512]{2,1,0:T(8,128)(2,1)}), bf16[8,8,512]{2,1,0:T(8,128)(2,1)S(1)}, u32[]{:S(2)}, u32[]{:S(2)}) async-start(bf16[8,8,512]{2,1,0:T(8,128)(2,1)} %bitcast.3), calls=%async_computation | async-start | bytes 131072 | tf_op jit(solution)/shard_map/all_to_all | solution.py:414
  10.9 1.4 %copy-done.1 = bf16[512,1536]{1,0:T(8,128)(2,1)S(1)} copy-done((bf16[512,1536]{1,0:T(8,128)(2,1)S(1)}, bf16[512,1536]{1,0:T(8,128)(2,1)}, u32[]{:S(2)}) %copy-start.1) | copy-done | bytes 1572888
  12.3 0.9 %copy-done.4 = bf16[1,128,512]{2,1,0:T(8,128)(2,1)S(1)} copy-done((bf16[1,128,512]{2,1,0:T(8,128)(2,1)S(1)}, bf16[1,128,512]{2,1,0:T(8,128)(2,1)}, u32[]{:S(2)}) %copy-start.4) | copy-done | bytes 131096
  13.2 0.9 %copy-done.25 = bf16[4,32,512]{2,1,0:T(8,128)(2,1)S(1)} copy-done((bf16[4,32,512]{2,1,0:T(8,128)(2,1)S(1)}, bf16[4,32,512]{2,1,0:T(8,128)(2,1)}, u32[]{:S(2)}) %copy-start.25) | copy-done | bytes 131096
  14.1 0.7 copy-done.28
  14.8 0.7 copy-done.29
  16.1 1.5 %own_rows.1 = (bf16[128,1536]{1,0:T(8,128)(2,1)S(1)}, bf16[4,128,256]{2,1,0:T(8,128)(2,1)S(1)}, bf16[5,32,512]{2,1,0:T(8,128)(2,1)}) custom-call(bf16[128,512]{1,0:T(8,128)(2,1)S(1)} %bitcast.14, bf16[512,1536]{1,0:T(8,128)(2,1)S(1)} %copy-done.1, s32[8,128]{1,0:T(8,128)S(1)} %bitcast.21, s32[8,128]{1,0:T(8,128)S(1)} %bitcast.22, s32[4,32]{1,0:T(4,128)S(1)} %copy-done.30, ...), custom_call_target="tpu_custom_call" | custom-call | flops 1000000000 | bytes 4000000 | tf_op jit(solution)/shard_map/own_rows/pallas_call | solution.py:448
  17.6 0.7 copy-done.7
  18.4 0.7 copy-done.10
  19.1 1.5 %collective-permute-start.4 = (bf16[5,32,512]{2,1,0:T(8,128)(2,1)}, bf16[5,32,512]{2,1,0:T(8,128)(2,1)}, u32[]{:S(2)}, u32[]{:S(2)}) collective-permute-start(bf16[5,32,512]{2,1,0:T(8,128)(2,1)} %get-tuple-element.14.refs_4_), channel_id=1, source_target_pairs={{0,2},{1,3},{2,0},{3,1},{4,6},{5,7},{6,4},{7,5},{8,10},{9,11},{10,... | collective-permute-start | bytes 491528 | tf_op jit(solution)/shard_map/ppermute | solution.py:408
  20.6 1.0 %copy-done.8 = bf16[128,1536]{1,0:T(8,128)(2,1)S(1)} copy-done((bf16[128,1536]{1,0:T(8,128)(2,1)S(1)}, bf16[128,1536]{1,0:T(8,128)(2,1)}, u32[]{:S(2)}) %copy-start.8) | copy-done | bytes 393240
  21.7 0.9 %copy-done.11 = bf16[4,128,256]{2,1,0:T(8,128)(2,1)S(1)} copy-done((bf16[4,128,256]{2,1,0:T(8,128)(2,1)S(1)}, bf16[4,128,256]{2,1,0:T(8,128)(2,1)}, u32[]{:S(2)}) %copy-start.11) | copy-done | bytes 262168
  22.6 2.4 %struct_forward.1.refs_0_ = bf16[128,512]{1,0:T(8,128)(2,1)S(1)} custom-call(bf16[128,512]{1,0:T(8,128)(2,1)S(1)} %bitcast.15, f32[4,8]{1,0:T(4,128)S(1)} %copy-done.22, bf16[64,512]{1,0:T(8,128)(2,1)S(1)} %bitcast.17, bf16[128,1536]{1,0:T(8,128)(2,1)S(1)} %copy-done.8, bf16[4,128,256]{2,1,0:T(8,128)(2,1)S(1)} %copy-done.11, bf16[512,1536]{1,0:T(8,128)(2,1)S(1)} %copy-done.2), custom_call_target="tpu_custom_call" | custom-call | tf_op jit(solution)/shard_map/struct_forward/pallas_call | solution.py:464
  26.1 3.9 %collective-permute-done.1.refs_2_ = bf16[128,512]{1,0:T(8,128)(2,1)S(1)} collective-permute-done((bf16[128,512]{1,0:T(8,128)(2,1)S(1)}, bf16[128,512]{1,0:T(8,128)(2,1)S(1)}, u32[]{:S(2)}, u32[]{:S(2)}) %collective-permute-start.1) | collective-permute-done | bytes 131104 | tf_op jit(solution)/shard_map/ppermute | solution.py:408
  30.0 1.5 %collective-permute-done.2.refs_3_ = bf16[128,512]{1,0:T(8,128)(2,1)} collective-permute-done((bf16[128,512]{1,0:T(8,128)(2,1)S(1)}, bf16[128,512]{1,0:T(8,128)(2,1)}, u32[]{:S(2)}, u32[]{:S(2)}) %collective-permute-start.2) | collective-permute-done | bytes 131104 | tf_op jit(solution)/shard_map/ppermute | solution.py:408
  31.5 5.5 %temporal.1 = (bf16[128,1536]{1,0:T(8,128)(2,1)S(1)}, bf16[128,1536]{1,0:T(8,128)(2,1)S(1)}, bf16[128,512]{1,0:T(8,128)(2,1)S(1)}) custom-call(s32[1]{0:T(128)} %bitcast.1.me_ref, bf16[4,512]{1,0:T(4,128)(2,1)S(1)} %copy-done.21, bf16[512,1536]{1,0:T(8,128)(2,1)S(1)} %copy-done, bf16[128,512]{1,0:T(8,128)(2,1)S(1)} %struct_forward.1.refs_0_, ...), custom_call_target="tpu_custom_call" | custom-call | tf_op jit(solution)/shard_map/temporal/pallas_call | solution.py:483
  37.1 0.7 copy-done.6
  37.8 0.8 copy-done.23
  39.2 6.0 %all-to-all-start.1 = ((bf16[8,16,1536]{2,1,0:T(8,128)(2,1)}), bf16[8,16,1536]{2,1,0:T(8,128)(2,1)S(1)}, u32[]{:S(2)}, u32[]{:S(2)}) async-start(bf16[8,16,1536]{2,1,0:T(8,128)(2,1)} %bitcast.16), calls=%async_computation.1 | async-start | bytes 786432 | tf_op jit(solution)/shard_map/all_to_all | solution.py:414
  45.2 1.0 %copy-done.9 = bf16[128,1536]{1,0:T(8,128)(2,1)S(1)} copy-done((bf16[128,1536]{1,0:T(8,128)(2,1)S(1)}, bf16[128,1536]{1,0:T(8,128)(2,1)}, u32[]{:S(2)}) %copy-start.9) | copy-done | bytes 393240
  46.2 0.9 %copy-done.12 = bf16[4,128,256]{2,1,0:T(8,128)(2,1)S(1)} copy-done((bf16[4,128,256]{2,1,0:T(8,128)(2,1)S(1)}, bf16[4,128,256]{2,1,0:T(8,128)(2,1)}, u32[]{:S(2)}) %copy-start.12) | copy-done | bytes 262168
  47.2 0.8 %copy-done.14 = bf16[8,8,512]{2,1,0:T(8,128)(2,1)S(1)} copy-done((bf16[8,8,512]{2,1,0:T(8,128)(2,1)S(1)}, bf16[8,8,512]{2,1,0:T(8,128)(2,1)}, u32[]{:S(2)}) %copy-start.14) | copy-done | bytes 65560
  48.0 1.0 %copy-done.24 = bf16[128,1536]{1,0:T(8,128)(2,1)S(1)} copy-done((bf16[128,1536]{1,0:T(8,128)(2,1)S(1)}, bf16[128,1536]{1,0:T(8,128)(2,1)}, u32[]{:S(2)}) %copy-start.24) | copy-done | bytes 393240
  49.0 0.9 %copy-done.27 = bf16[128,512]{1,0:T(8,128)(2,1)S(1)} copy-done((bf16[128,512]{1,0:T(8,128)(2,1)S(1)}, bf16[128,512]{1,0:T(8,128)(2,1)}, u32[]{:S(2)}) %copy-start.27) | copy-done | bytes 131096
  49.9 5.8 %struct_backward.1 = (f32[64,512]{1,0:T(8,128)S(1)}, f32[128,512]{1,0:T(8,128)S(1)}) custom-call(f32[4,8]{1,0:T(4,128)S(1)} %copy-done.22, bf16[64,512]{1,0:T(8,128)(2,1)S(1)} %bitcast.18, bf16[128,1536]{1,0:T(8,128)(2,1)S(1)} %copy-done.9, bf16[4,128,256]{2,1,0:T(8,128)(2,1)S(1)} %copy-done.12, bf16[512,1536]{1,0:T(8,128)(2,1)S(1)} %copy-done.2, ...), custom_call_target="tpu_custom_call" | custom-call | flops 2000000000 | bytes 8000000 | tf_op jit(solution)/shard_map/struct_backward/pallas_call | solution.py:510
  55.8 0.7 copy-done.15
  57.2 0.9 %copy-done.18 = f32[64,512]{1,0:T(8,128)S(1)} copy-done((f32[64,512]{1,0:T(8,128)S(1)}, f32[64,512]{1,0:T(8,128)}, u32[]{:S(2)}) %copy-start.18) | copy-done | bytes 131096
  58.2 18.7 %all_to_all.15.got_ref = bf16[8,16,1792]{2,1,0:T(8,128)(2,1)S(1)} all-to-all(bf16[8,16,1792]{2,1,0:T(8,128)(2,1)S(1)} %sum_parts.1), channel_id=1, replica_groups=mesh['dom'=8,'snap'=4] {'dom'}, dimensions={0} | all-to-all | bytes 917504 | tf_op jit(solution)/shard_map/all_to_all | solution.py:414
  76.9 1.6 %last_sums.1 = (bf16[128,512]{1,0:T(8,128)(2,1)}, f32[128,1536]{1,0:T(8,128)}) custom-call(s32[8,8]{1,0:T(8,128)S(1)} %bitcast.20, bf16[8,16,1792]{2,1,0:T(8,128)(2,1)S(1)} %all_to_all.15.got_ref, f32[128,512]{1,0:T(8,128)S(1)} %copy-done.16), custom_call_target="tpu_custom_call" | custom-call | tf_op jit(solution)/shard_map/last_sums/pallas_call | solution.py:544
  (54 shorter events, 3.3 us)
Async XLA Ops:
  0.6 0.9 %copy-start.3 = (bf16[1,128,512]{2,1,0:T(8,128)(2,1)S(1)}, bf16[1,128,512]{2,1,0:T(8,128)(2,1)}, u32[]{:S(2)}) copy-start(bf16[1,128,512]{2,1,0:T(8,128)(2,1)} %param.10) | copy-start | bytes 393220
  3.6 17.0 %all-to-all-start = ((bf16[8,8,512]{2,1,0:T(8,128)(2,1)}), bf16[8,8,512]{2,1,0:T(8,128)(2,1)S(1)}, u32[]{:S(2)}, u32[]{:S(2)}) async-start(bf16[8,8,512]{2,1,0:T(8,128)(2,1)} %bitcast.3), calls=%async_computation | async-start | bytes 131072 | tf_op jit(solution)/shard_map/all_to_all | solution.py:414
  10.9 1.4 %copy-start.1 = (bf16[512,1536]{1,0:T(8,128)(2,1)S(1)}, bf16[512,1536]{1,0:T(8,128)(2,1)}, u32[]{:S(2)}) copy-start(bf16[512,1536]{1,0:T(8,128)(2,1)} %ws_hbm.1) | copy-start | bytes 4718596
  12.3 0.9 %copy-start.4 = (bf16[1,128,512]{2,1,0:T(8,128)(2,1)S(1)}, bf16[1,128,512]{2,1,0:T(8,128)(2,1)}, u32[]{:S(2)}) copy-start(bf16[1,128,512]{2,1,0:T(8,128)(2,1)} %param.10) | copy-start | bytes 393220
  13.2 0.9 %copy-start.25 = (bf16[4,32,512]{2,1,0:T(8,128)(2,1)S(1)}, bf16[4,32,512]{2,1,0:T(8,128)(2,1)}, u32[]{:S(2)}) copy-start(bf16[4,32,512]{2,1,0:T(8,128)(2,1)} %cot_ref.1) | copy-start | bytes 393220
  16.1 4.5 %copy-start.2 = (bf16[512,1536]{1,0:T(8,128)(2,1)S(1)}, bf16[512,1536]{1,0:T(8,128)(2,1)}, u32[]{:S(2)}) copy-start(bf16[512,1536]{1,0:T(8,128)(2,1)} %ws_hbm.1) | copy-start | bytes 4718596
  16.1 4.5 %copy-start.5 = (bf16[1,128,512]{2,1,0:T(8,128)(2,1)S(1)}, bf16[1,128,512]{2,1,0:T(8,128)(2,1)}, u32[]{:S(2)}) copy-start(bf16[1,128,512]{2,1,0:T(8,128)(2,1)} %param.10) | copy-start | bytes 393220
  16.1 4.5 %copy-start.22 = (f32[4,8]{1,0:T(4,128)S(1)}, f32[4,8]{1,0:T(4,128)}, u32[]{:S(2)}) copy-start(f32[4,8]{1,0:T(4,128)} %bias_ref.3) | copy-start | bytes 388
  16.1 15.3 %copy-start.21 = (bf16[4,512]{1,0:T(4,128)(2,1)S(1)}, bf16[4,512]{1,0:T(4,128)(2,1)}, u32[]{:S(2)}) copy-start(bf16[4,512]{1,0:T(4,128)(2,1)} %pos_ref.1) | copy-start | bytes 12292
  17.6 0.7 copy-start.7
  19.1 12.4 %copy-start = (bf16[512,1536]{1,0:T(8,128)(2,1)S(1)}, bf16[512,1536]{1,0:T(8,128)(2,1)}, u32[]{:S(2)}) copy-start(bf16[512,1536]{1,0:T(8,128)(2,1)} %wt_hbm.1) | copy-start | bytes 4718596
  19.1 6.5 %collective-permute-start.4 = (bf16[5,32,512]{2,1,0:T(8,128)(2,1)}, bf16[5,32,512]{2,1,0:T(8,128)(2,1)}, u32[]{:S(2)}, u32[]{:S(2)}) collective-permute-start(bf16[5,32,512]{2,1,0:T(8,128)(2,1)} %get-tuple-element.14.refs_4_), channel_id=1, source_target_pairs={{0,2},{1,3},{2,0},{3,1},{4,6},{5,7},{6,4},{7,5},{8,10},{9,11},{10,... | collective-permute-start | bytes 491528 | tf_op jit(solution)/shard_map/ppermute | solution.py:408
  20.6 16.4 %copy-start.13 = (bf16[8,8,512]{2,1,0:T(8,128)(2,1)}, bf16[8,8,512]{2,1,0:T(8,128)(2,1)S(1)}, u32[]{:S(2)}) copy-start(bf16[8,8,512]{2,1,0:T(8,128)(2,1)S(1)} %all-to-all-done) | copy-start | bytes 196612
  20.6 1.0 %copy-start.8 = (bf16[128,1536]{1,0:T(8,128)(2,1)S(1)}, bf16[128,1536]{1,0:T(8,128)(2,1)}, u32[]{:S(2)}) copy-start(bf16[128,1536]{1,0:T(8,128)(2,1)} %copy-done.7) | copy-start | bytes 1179652
  21.7 0.9 %copy-start.11 = (bf16[4,128,256]{2,1,0:T(8,128)(2,1)S(1)}, bf16[4,128,256]{2,1,0:T(8,128)(2,1)}, u32[]{:S(2)}) copy-start(bf16[4,128,256]{2,1,0:T(8,128)(2,1)} %copy-done.10) | copy-start | bytes 786436
  25.0 5.0 %collective-permute-start.1 = (bf16[128,512]{1,0:T(8,128)(2,1)S(1)}, bf16[128,512]{1,0:T(8,128)(2,1)S(1)}, u32[]{:S(2)}, u32[]{:S(2)}) collective-permute-start(bf16[128,512]{1,0:T(8,128)(2,1)S(1)} %struct_forward.1.refs_0_), channel_id=1, source_target_pairs={{0,2},{1,3},{2,0},{3,1},{4,6},{5,7},{6,4},{7,5},{8,10},{9,11},{10,... | collective-permute-start | bytes 393224 | tf_op jit(solution)/shard_map/ppermute | solution.py:408
  25.5 4.5 %collective-permute-start.3 = (bf16[5,32,512]{2,1,0:T(8,128)(2,1)}, bf16[5,32,512]{2,1,0:T(8,128)(2,1)}, u32[]{:S(2)}, u32[]{:S(2)}) collective-permute-start(bf16[5,32,512]{2,1,0:T(8,128)(2,1)} %get-tuple-element.14.refs_4_), channel_id=1, source_target_pairs={{0,1},{1,0},{2,3},{3,2},{4,5},{5,4},{6,7},{7,6},{8,9},{9,8},{10,11... | collective-permute-start | bytes 491528 | tf_op jit(solution)/shard_map/ppermute | solution.py:408
  25.5 4.5 %collective-permute-start.5 = (bf16[5,32,512]{2,1,0:T(8,128)(2,1)}, bf16[5,32,512]{2,1,0:T(8,128)(2,1)}, u32[]{:S(2)}, u32[]{:S(2)}) collective-permute-start(bf16[5,32,512]{2,1,0:T(8,128)(2,1)} %collective-permute-done.4.refs_6_), channel_id=1, source_target_pairs={{0,1},{1,0},{2,3},{3,2},{4,5},{5,4},{6,7},{7,6},{8,9},{9,8},{10,11... | collective-permute-start | bytes 491528 | tf_op jit(solution)/shard_map/ppermute | solution.py:408
  26.1 4.0 %collective-permute-start = (bf16[128,512]{1,0:T(8,128)(2,1)S(1)}, bf16[128,512]{1,0:T(8,128)(2,1)}, u32[]{:S(2)}, u32[]{:S(2)}) collective-permute-start(bf16[128,512]{1,0:T(8,128)(2,1)S(1)} %struct_forward.1.refs_0_), channel_id=1, source_target_pairs={{0,1},{1,0},{2,3},{3,2},{4,5},{5,4},{6,7},{7,6},{8,9},{9,8},{10,11... | collective-permute-start | bytes 393224 | tf_op jit(solution)/shard_map/ppermute | solution.py:408
  30.0 1.5 %collective-permute-start.2 = (bf16[128,512]{1,0:T(8,128)(2,1)S(1)}, bf16[128,512]{1,0:T(8,128)(2,1)}, u32[]{:S(2)}, u32[]{:S(2)}) collective-permute-start(bf16[128,512]{1,0:T(8,128)(2,1)S(1)} %collective-permute-done.1.refs_2_), channel_id=1, source_target_pairs={{0,1},{1,0},{2,3},{3,2},{4,5},{5,4},{6,7},{7,6},{8,9},{9,8},{10,11... | collective-permute-start | bytes 393224 | tf_op jit(solution)/shard_map/ppermute | solution.py:408
  37.1 0.7 copy-start.6
  37.8 0.8 copy-start.23
  39.2 18.0 %all-to-all-start.1 = ((bf16[8,16,1536]{2,1,0:T(8,128)(2,1)}), bf16[8,16,1536]{2,1,0:T(8,128)(2,1)S(1)}, u32[]{:S(2)}, u32[]{:S(2)}) async-start(bf16[8,16,1536]{2,1,0:T(8,128)(2,1)} %bitcast.16), calls=%async_computation.1 | async-start | bytes 786432 | tf_op jit(solution)/shard_map/all_to_all | solution.py:414
  45.2 1.0 %copy-start.9 = (bf16[128,1536]{1,0:T(8,128)(2,1)S(1)}, bf16[128,1536]{1,0:T(8,128)(2,1)}, u32[]{:S(2)}) copy-start(bf16[128,1536]{1,0:T(8,128)(2,1)} %copy-done.7) | copy-start | bytes 1179652
  46.2 0.9 %copy-start.12 = (bf16[4,128,256]{2,1,0:T(8,128)(2,1)S(1)}, bf16[4,128,256]{2,1,0:T(8,128)(2,1)}, u32[]{:S(2)}) copy-start(bf16[4,128,256]{2,1,0:T(8,128)(2,1)} %copy-done.10) | copy-start | bytes 786436
  47.2 0.8 %copy-start.14 = (bf16[8,8,512]{2,1,0:T(8,128)(2,1)S(1)}, bf16[8,8,512]{2,1,0:T(8,128)(2,1)}, u32[]{:S(2)}) copy-start(bf16[8,8,512]{2,1,0:T(8,128)(2,1)} %copy-done.13) | copy-start | bytes 196612
  48.0 1.0 %copy-start.24 = (bf16[128,1536]{1,0:T(8,128)(2,1)S(1)}, bf16[128,1536]{1,0:T(8,128)(2,1)}, u32[]{:S(2)}) copy-start(bf16[128,1536]{1,0:T(8,128)(2,1)} %copy-done.23) | copy-start | bytes 1179652
  49.0 0.9 %copy-start.27 = (bf16[128,512]{1,0:T(8,128)(2,1)S(1)}, bf16[128,512]{1,0:T(8,128)(2,1)}, u32[]{:S(2)}) copy-start(bf16[128,512]{1,0:T(8,128)(2,1)} %copy-done.26) | copy-start | bytes 393220
  49.9 27.0 %copy-start.20 = (s32[1,1,8,8]{3,2,1,0:T(8,128)S(1)}, s32[1,1,8,8]{3,2,1,0:T(8,128)}, u32[]{:S(2)}) copy-start(s32[1,1,8,8]{3,2,1,0:T(8,128)} %param.17) | copy-start | bytes 772
  55.7 0.7 copy-start.15
  57.2 19.7 %copy-start.16 = (f32[128,512]{1,0:T(8,128)S(1)}, f32[128,512]{1,0:T(8,128)}, u32[]{:S(2)}) copy-start(f32[128,512]{1,0:T(8,128)} %copy-done.15) | copy-start | bytes 786436
  57.2 0.9 %copy-start.18 = (f32[64,512]{1,0:T(8,128)S(1)}, f32[64,512]{1,0:T(8,128)}, u32[]{:S(2)}) copy-start(f32[64,512]{1,0:T(8,128)} %copy-done.17) | copy-start | bytes 393220
  (7 other events, 4.8 us)

commit v3 on v2

--- a/solution.py
+++ b/solution.py
@@ -13,7 +13,7 @@
 NEG = -1e30
 VMEM = pl.BlockSpec(memory_space=pltpu.VMEM)
 SMEM = pl.BlockSpec(memory_space=pltpu.SMEM)
-ANY = pl.BlockSpec(memory_space=pl.ANY)
+HBM = pl.BlockSpec(memory_space=pltpu.HBM)
 
 
 def dot_nn(a, b):
@@ -75,40 +75,56 @@
     return jnp.concatenate(tiles, axis=0).astype(BF16)
 
 
-def tiles_kernel(route_ref, x_ref, out_ref):
-    out_ref[...] = dot_nn(pick_rows(route_ref, x_ref.shape[0]), x_ref[...]).astype(BF16)
-
-
-def own_kernel(x_ref, w_hbm, nbr_ref, rel_ref, act_ref, cot_ref, proj_ref, count_ref, load_ref, w_s, sems):
-    rows, width = x_ref.shape
-    kinds, _, keys = count_ref.shape
-    slots = nbr_ref.shape[0]
-    snaps, ents, _ = cot_ref.shape
-    fetch = Fetch(sems, (w_hbm, w_s))
-    for t in range(snaps):
-        load_ref[t] = cot_ref[t]
+def tiles_kernel(route_hbm, x_hbm, out_ref, route, x, sems):
+    fetch = Fetch(sems, (route_hbm, route), (x_hbm, x))
+    fetch.wait(0, 1)
+    out_ref[...] = dot_nn(pick_rows(route, x.shape[0]), x[...]).astype(BF16)
+
+
+def own_kernel(
+    x_hbm, w_hbm, nbr_hbm, rel_hbm, act_hbm, cot_hbm, proj_hbm, count_hbm, load_hbm,
+    x, w, nbr, rel, act, proj, count, flags_s, sems,
+):
+    rows, width = x.shape
+    kinds, _, keys = count.shape
+    slots = nbr.shape[0]
+    snaps, ents = act.shape
+    fetch = Fetch(
+        sems,
+        (nbr_hbm, nbr),
+        (rel_hbm, rel),
+        (act_hbm, act),
+        (cot_hbm, load_hbm.at[:snaps]),
+        (x_hbm, x),
+        (w_hbm, w),
+    )
     row = lax.broadcasted_iota(jnp.int32, (ents, ents), 0)
     col = lax.broadcasted_iota(jnp.int32, (ents, ents), 1)
     lane = lax.broadcasted_iota(jnp.int32, (ents, width), 1)
     flags = jnp.zeros((ents, width), F32)
-    act = act_ref[...].astype(F32)
+    fetch.wait(0, 1, 2)
+    on = act[...].astype(F32)
     for t in range(snaps):
-        column = jnp.sum(jnp.where(row == col, act[t : t + 1, :], 0.0), axis=1, keepdims=True)
+        column = jnp.sum(jnp.where(row == col, on[t : t + 1, :], 0.0), axis=1, keepdims=True)
         flags = jnp.where(lane == t, column, flags)
-    load_ref[snaps] = flags.astype(BF16)
-    code = jnp.transpose((nbr_ref[...] * kinds + rel_ref[...]).astype(F32))
+    flags_s[...] = flags.astype(BF16)
+    code = jnp.transpose((nbr[...] * kinds + rel[...]).astype(F32))
     spot = (lax.broadcasted_iota(jnp.int32, (rows, keys), 1) * kinds).astype(F32)
     for r in range(kinds):
         here = spot + float(r)
-        count = jnp.zeros((rows, keys), F32)
+        total = jnp.zeros((rows, keys), F32)
         for k in range(slots):
-            count = count + jnp.where(code[:, k : k + 1] == here, 1.0, 0.0)
-        count_ref[r] = count.astype(BF16)
-    fetch.wait(0)
-    x = x_ref[...]
+            total = total + jnp.where(code[:, k : k + 1] == here, 1.0, 0.0)
+        count[r] = total.astype(BF16)
+    store = Fetch(sems.at[6:], (flags_s, load_hbm.at[snaps]), (count, count_hbm))
+    fetch.wait(4, 5)
     for part in range(3):
         cols = slice(part * width, (part + 1) * width)
-        proj_ref[:, cols] = dot_nn(x, w_s[:, cols]).astype(BF16)
+        proj[:, cols] = dot_nn(x[...], w[:, cols]).astype(BF16)
+    last = Fetch(sems.at[8:], (proj, proj_hbm))
+    fetch.wait(3)
+    store.wait(0, 1)
+    last.wait(0)
 
 
 def fill_table(tab_s, proj, halo, w_kv):
@@ -142,29 +158,23 @@
     return kk, parts
 
 
-def forward_kernel(
-    heads, x_ref, bias_ref, halo_hbm, proj_hbm, count_hbm, w_hbm, hidden_ref,
-    halo, proj, count, w_kv, tab_s, sems,
-):
-    width = x_ref.shape[1]
+def forward_kernel(heads, x, bias, halo, w, count_hbm, hidden_ref, count, proj, tab_s, sems):
+    width = x.shape[1]
     head_dim = width // heads
-    fetch = Fetch(
-        sems,
-        (halo_hbm, halo),
-        (w_hbm.at[:, width:], w_kv),
-        (proj_hbm, proj),
-        (count_hbm, count),
-    )
-    fetch.wait(0, 1, 2, 3)
-    fill_table(tab_s, proj, halo, w_kv)
+    fetch = Fetch(sems, (count_hbm, count))
+    for part in range(3):
+        cols = slice(part * width, (part + 1) * width)
+        proj[:, cols] = dot_nn(x[...], w[:, cols]).astype(BF16)
+    fill_table(tab_s, proj, halo, w.at[:, width:])
+    fetch.wait(0)
     for p in range(width // LANES):
         cols = slice(p * LANES, (p + 1) * LANES)
         vcols = slice(width + p * LANES, width + (p + 1) * LANES)
-        _, attn = edge_attention(p, heads, proj, count, bias_ref, tab_s, width)
+        _, attn = edge_attention(p, heads, proj, count, bias, tab_s, width)
         vv = stack_heads(tab_s[:, vcols], head_dim)
         agg = dot_nn(jnp.concatenate([a.astype(BF16) for a in attn], axis=1), vv)
         elu = jnp.where(agg > 0, agg, jnp.exp(jnp.minimum(agg, 0.0)) - 1.0)
-        hidden_ref[:, cols] = (x_ref[:, cols].astype(F32) + elu).astype(BF16)
+        hidden_ref[:, cols] = (x[:, cols].astype(F32) + elu).astype(BF16)
 
 
 def each(lo, hi, unroll, body):
@@ -175,25 +185,19 @@
         lax.fori_loop(lo, hi, lambda i, c: (body(i), c)[1], 0)
 
 
-def temporal_kernel(snaps, heads, me_ref, pos_ref, w_hbm, *refs):
-    hid_hbm = refs[:snaps]
-    cot_hbm = refs[snaps : 2 * snaps]
+def temporal_kernel(snaps, heads, me_ref, pos_ref, w_s, *refs):
+    hid = refs[:snaps]
+    cot = refs[snaps : 2 * snaps]
     (
-        terms_ref, dt_own_ref, cot_own_ref,
-        w_s, hid, cot, z_s, ct_s, tp_s, dt_s, act_s, s_s, d_s, a_s, ds_s, dk_s, dv_s, sems,
+        terms_hbm, dt_own_hbm, cot_own_hbm,
+        terms_s, own_s, z_s, ct_s, tp_s, dt_s, act_s, s_s, d_s, a_s, ds_s, dk_s, dv_s, sems,
     ) = refs[2 * snaps :]
-    _, local, width = hid.shape
-    ents = cot.shape[2]
+    local, width = hid[0].shape
+    ents = cot[0].shape[1]
     head_dim = width // heads
     scale = head_dim ** (-0.5)
     unroll = snaps <= 4
     me = me_ref[0]
-    fetch = Fetch(
-        sems,
-        *[(hid_hbm[n], hid.at[n]) for n in range(snaps)],
-        (w_hbm, w_s),
-        *[(cot_hbm[n], cot.at[n]) for n in range(snaps)],
-    )
     pos = pos_ref[...].astype(F32)
     which = lax.broadcasted_iota(jnp.int32, pos.shape, 0)
 
@@ -203,18 +207,15 @@
     for n in range(snaps):
         t = lax.bitwise_xor(me, n)
         shift = jnp.sum(jnp.where(which == t, pos, 0.0), axis=0, keepdims=True)
-        fetch.wait(n)
-        z_s[rows_of(t), :] = (hid[n].astype(F32) + shift).astype(BF16)
-    fetch.wait(snaps)
+        z_s[rows_of(t), :] = (hid[n][...].astype(F32) + shift).astype(BF16)
     for part in range(3):
         cols = slice(part * width, (part + 1) * width)
         tp_s[:, cols] = dot_nn(z_s[...], w_s[:, cols]).astype(BF16)
-    fetch.wait(*range(snaps + 1, 2 * snaps + 1))
     for m in range(snaps):
         at = pl.multiple_of(lax.bitwise_xor(me, m) * ents, ents)
         for t in range(snaps):
-            ct_s[pl.ds(t * local + at, ents), :] = cot[m, t].astype(ct_s.dtype)
-        act_s[pl.ds(at, ents), :] = cot[m, snaps][:, :LANES].astype(F32)
+            ct_s[pl.ds(t * local + at, ents), :] = cot[m][t].astype(ct_s.dtype)
+        act_s[pl.ds(at, ents), :] = cot[m][snaps][:, :LANES].astype(F32)
     lane_head = lax.broadcasted_iota(jnp.int32, (width, LANES), 0) // head_dim
     fold = (lane_head == lax.broadcasted_iota(jnp.int32, (width, LANES), 1)).astype(F32).astype(BF16)
     head_lane = lax.broadcasted_iota(jnp.int32, (LANES, width), 1) // head_dim
@@ -303,6 +304,10 @@
     each(0, snaps, unroll, scores)
     dt_s[:, width : 2 * width] = dk_s[...].astype(BF16)
     dt_s[:, 2 * width :] = dv_s[...].astype(BF16)
+    own_s[...] = ct_s[rows_of(me), :].astype(BF16)
+    store = Fetch(
+        sems, (dt_s.at[rows_of(me), :], dt_own_hbm), (own_s, cot_own_hbm)
+    )
     share = width // snaps
     pick = (
         lax.broadcasted_iota(jnp.int32, (width, share), 0)
@@ -311,14 +316,15 @@
     z_mine = dot_nn(z_s[...], jnp.where(pick, 1.0, 0.0).astype(BF16)).astype(BF16)
     for part in range(3):
         cols = slice(part * width, (part + 1) * width)
-        terms_ref[:, cols] = dot_tn(z_mine, dt_s[:, cols]).astype(BF16)
-    dt_own_ref[...] = dt_s[rows_of(me), :]
-    cot_own_ref[...] = ct_s[rows_of(me), :].astype(BF16)
+        terms_s[:, cols] = dot_tn(z_mine, dt_s[:, cols]).astype(BF16)
+    last = Fetch(sems.at[2:], (terms_s, terms_hbm))
+    store.wait(0, 1)
+    last.wait(0)
 
 
 def backward_kernel(
-    heads, bias_ref, halo_hbm, proj_hbm, count_hbm, ws_hbm, wt_hbm, dt_hbm, cot_hbm, back_ref, part_ref,
-    halo, proj, count, ws, wt, dt, cot, tab_s, dq_s, dtab_s, sems,
+    heads, bias_hbm, halo_hbm, proj_hbm, count_hbm, ws_hbm, wt_hbm, dt_hbm, cot_hbm, back_hbm, part_hbm,
+    bias, back_s, part_s, halo, proj, count, ws, wt, dt, cot, tab_s, dq_s, dtab_s, sems,
 ):
     rows, width = cot.shape
     halo_rows = halo.shape[0]
@@ -335,19 +341,20 @@
         (dt_hbm, dt),
         (cot_hbm, cot),
         (wt_hbm, wt),
+        (bias_hbm, bias),
     )
-    fetch.wait(*range(7))
+    fetch.wait(*range(8))
     fill_table(tab_s, proj, halo, ws.at[:, width:])
     dh = cot[...].astype(F32) + dot_nt(dt[...], wt[...])
-    part_ref[...] = dh.astype(BF16).astype(F32)
+    part_s[...] = dh.astype(BF16).astype(F32)
     for p in range(width // LANES):
         cols = slice(p * LANES, (p + 1) * LANES)
         vcols = slice(width + p * LANES, width + (p + 1) * LANES)
-        kk, attn = edge_attention(p, heads, proj, count, bias_ref, tab_s, width)
+        kk, attn = edge_attention(p, heads, proj, count, bias, tab_s, width)
         vv = stack_heads(tab_s[:, vcols], head_dim)
         attn_b = jnp.concatenate([a.astype(BF16) for a in attn], axis=1)
         agg = dot_nn(attn_b, vv)
-        da = part_ref[:, cols] * jnp.where(agg > 0, 1.0, jnp.exp(jnp.minimum(agg, 0.0)))
+        da = part_s[:, cols] * jnp.where(agg > 0, 1.0, jnp.exp(jnp.minimum(agg, 0.0)))
         da = da.astype(BF16)
         dattn = dot_nt(da, vv).astype(BF16).astype(F32)
         ds = []
@@ -358,11 +365,16 @@
         dq_s[:, cols] = (dot_nn(ds, kk) * scale).astype(BF16)
         dtab_s[:, cols] = (unstack_heads(dot_tn(ds, proj[:, cols]), head_dim) * scale).astype(BF16)
         dtab_s[:, vcols] = unstack_heads(dot_tn(attn_b, da), head_dim).astype(BF16)
-    back_ref[...] = dot_nt(dtab_s[rows : rows + halo_rows, :], ws[:, width:])
-    part_ref[...] += dot_nt(dq_s[...], ws[:, :width]) + dot_nt(dtab_s[:rows, :], ws[:, width:])
-
-
-def sum_kernel(parts_ref, back_ref, out_ref):
+    back_s[...] = dot_nt(dtab_s[rows : rows + halo_rows, :], ws[:, width:])
+    first = Fetch(sems.at[8:], (back_s, back_hbm))
+    part_s[...] += dot_nt(dq_s[...], ws[:, :width]) + dot_nt(dtab_s[:rows, :], ws[:, width:])
+    last = Fetch(sems.at[9:], (part_s, part_hbm))
+    first.wait(0)
+    last.wait(0)
+
+
+def sum_kernel(parts_ref, back_hbm, out_ref, back_ref, sems):
+    fetch = Fetch(sems, (back_hbm, back_ref))
     doms, rows, wide = parts_ref.shape
     per = back_ref.shape[0] // doms
     half = back_ref.shape[1] * per // rows
@@ -370,6 +382,7 @@
     for d in range(1, doms):
         total = total + parts_ref[d].astype(F32)
     total = total.astype(BF16)
+    fetch.wait(0)
     for d in range(doms):
         out_ref[d, :, :wide] = total
         tile = back_ref[d * per : (d + 1) * per, :]
@@ -377,21 +390,29 @@
         out_ref[d, :, wide:] = jnp.concatenate(folded, axis=0).astype(BF16)
 
 
-def last_kernel(route_ref, got_ref, part_ref, feat_ref, wtemp_ref, came_s):
+def last_kernel(
+    route_hbm, got_ref, part_hbm, feat_hbm, wtemp_hbm, route, part, feat, wtemp, came_s, sems
+):
+    fetch = Fetch(sems, (route_hbm, route), (part_hbm, part))
     doms, rows, wide = got_ref.shape
     per = came_s.shape[0] // doms
     half = came_s.shape[1] * per // rows
     wide -= half
     for d in range(doms):
-        wtemp_ref[d * rows : (d + 1) * rows, :] = got_ref[d, :, :wide].astype(F32)
+        wtemp[d * rows : (d + 1) * rows, :] = got_ref[d, :, :wide].astype(F32)
         folded = got_ref[d, :, wide:].astype(F32)
         for i in range(rows // per):
             came_s[d * per : (d + 1) * per, i * half : (i + 1) * half] = folded[
                 i * per : (i + 1) * per
             ]
-    picks = pick_rows(route_ref, part_ref.shape[0])
+    first = Fetch(sems.at[2:], (wtemp, wtemp_hbm))
+    fetch.wait(0, 1)
+    picks = pick_rows(route, part.shape[0])
     back = dot_tn(picks, came_s[...].astype(BF16))
-    feat_ref[...] = (part_ref[...] + back).astype(BF16)
+    feat[...] = (part[...] + back).astype(BF16)
+    last = Fetch(sems.at[3:], (feat, feat_hbm))
+    first.wait(0)
+    last.wait(0)
 
 
 def params(mib):
@@ -408,6 +429,10 @@
             held[m ^ bit] = lax.ppermute(held[m], axis, pairs)
         bit //= 2
     return [held[m] for m in range(count)]
+
+
+def in_hbm(*arrays):
+    return [pltpu.with_memory_space_constraint(a, pltpu.HBM) for a in arrays]
 
 
 def exchange(tiles, axis):
@@ -435,60 +460,75 @@
     def shape(*dims, dtype=BF16):
         return jax.ShapeDtypeStruct(dims, dtype)
 
+    def hbm(*dims, dtype=BF16):
+        return pltpu.HBM(dims, dtype)
+
     tiles = pl.pallas_call(
         tiles_kernel,
         out_shape=shape(halo_rows, width),
-        in_specs=[SMEM, VMEM],
+        in_specs=[HBM, HBM],
         out_specs=VMEM,
+        scratch_shapes=[
+            pltpu.SMEM(route.shape, jnp.int32),
+            pltpu.VMEM((local, width), BF16),
+            pltpu.SemaphoreType.DMA((2,)),
+        ],
         compiler_params=params(8),
         name="halo_tiles",
-    )(route, x)
+    )(*in_hbm(route, x))
     halo = exchange(tiles.reshape(doms, halo_per, width), "dom").reshape(halo_rows, width)
 
     proj, count, load = pl.pallas_call(
         own_kernel,
         out_shape=(
-            shape(local, 3 * width),
-            shape(kinds, local, keys),
-            shape(snaps + 1, ents, width),
+            hbm(local, 3 * width),
+            hbm(kinds, local, keys),
+            hbm(snaps + 1, ents, width),
         ),
-        in_specs=[VMEM, ANY, VMEM, VMEM, VMEM, VMEM],
-        out_specs=(VMEM,) * 3,
-        scratch_shapes=[pltpu.VMEM(w_struct.shape, BF16), pltpu.SemaphoreType.DMA((1,))],
+        in_specs=[HBM] * 6,
+        out_specs=(HBM,) * 3,
+        scratch_shapes=[
+            pltpu.VMEM((local, width), BF16),
+            pltpu.VMEM(w_struct.shape, BF16),
+            pltpu.VMEM((slots, local), jnp.int32),
+            pltpu.VMEM((slots, local), jnp.int32),
+            pltpu.VMEM((snaps, ents), jnp.int32),
+            pltpu.VMEM((local, 3 * width), BF16),
+            pltpu.VMEM((kinds, local, keys), BF16),
+            pltpu.VMEM((ents, width), BF16),
+            pltpu.SemaphoreType.DMA((9,)),
+        ],
         compiler_params=params(16),
         cost_estimate=pl.CostEstimate(flops=10**9, bytes_accessed=4 * 10**6, transcendentals=0),
         name="own_rows",
-    )(x, w_struct, nbr[0].T, rel_type[0].T, active, cotangent)
+    )(*in_hbm(x, w_struct, nbr[0].T, rel_type[0].T, active, cotangent))
     cots = gather_blocks(load, "snap")
 
     hidden = pl.pallas_call(
         functools.partial(forward_kernel, heads),
         out_shape=shape(local, width),
-        in_specs=[VMEM, VMEM] + [ANY] * 4,
+        in_specs=[VMEM] * 4 + [HBM],
         out_specs=VMEM,
         scratch_shapes=[
-            pltpu.VMEM((halo_rows, width), BF16),
+            pltpu.VMEM((kinds, local, keys), BF16),
             pltpu.VMEM((local, 3 * width), BF16),
-            pltpu.VMEM((kinds, local, keys), BF16),
-            pltpu.VMEM((width, 2 * width), BF16),
             pltpu.VMEM((keys, 2 * width), BF16),
-            pltpu.SemaphoreType.DMA((4,)),
+            pltpu.SemaphoreType.DMA((1,)),
         ],
-        compiler_params=params(16),
+        compiler_params=params(8),
         name="struct_forward",
-    )(x, rel_bias, halo, proj, count, w_struct)
+    )(x, rel_bias, halo, w_struct, *in_hbm(count))
 
     hids = gather_blocks(hidden, "snap")
     every = snaps * local
     terms, dt_own, cot_own = pl.pallas_call(
         functools.partial(temporal_kernel, snaps, heads),
-        out_shape=(shape(share, 3 * width), shape(local, 3 * width), shape(local, width)),
-        in_specs=[SMEM, VMEM] + [ANY] * (1 + 2 * snaps),
-        out_specs=(VMEM,) * 3,
+        out_shape=(hbm(share, 3 * width), hbm(local, 3 * width), hbm(local, width)),
+        in_specs=[SMEM] + [VMEM] * (2 + 2 * snaps),
+        out_specs=(HBM,) * 3,
         scratch_shapes=[
-            pltpu.VMEM(w_temp.shape, BF16),
-            pltpu.VMEM((snaps, local, width), BF16),
-            pltpu.VMEM((snaps, snaps + 1, ents, width), BF16),
+            pltpu.VMEM((share, 3 * width), BF16),
+            pltpu.VMEM((local, width), BF16),
             pltpu.VMEM((every, width), BF16),
             pltpu.VMEM((every, width), F32 if ents % 16 else BF16),
             pltpu.VMEM((every, 3 * width), BF16),
@@ -500,7 +540,7 @@
             pltpu.VMEM((snaps, local, LANES), BF16),
             pltpu.VMEM((every, width), F32),
             pltpu.VMEM((every, width), F32),
-            pltpu.SemaphoreType.DMA((2 * snaps + 1,)),
+            pltpu.SemaphoreType.DMA((3,)),
         ],
         compiler_params=params(24 if snaps <= 4 else 56),
         name="temporal",
@@ -509,10 +549,13 @@
     parts = exchange(terms.reshape(doms, piece, 3 * width), "dom")
     back, partial = pl.pallas_call(
         functools.partial(backward_kernel, heads),
-        out_shape=(shape(halo_rows, width, dtype=F32), shape(local, width, dtype=F32)),
-        in_specs=[VMEM] + [ANY] * 7,
-        out_specs=(VMEM, VMEM),
+        out_shape=(hbm(halo_rows, width, dtype=F32), hbm(local, width, dtype=F32)),
+        in_specs=[HBM] * 8,
+        out_specs=(HBM, HBM),
         scratch_shapes=[
+            pltpu.VMEM(rel_bias.shape, F32),
+            pltpu.VMEM((halo_rows, width), F32),
+            pltpu.VMEM((local, width), F32),
             pltpu.VMEM((halo_rows, width), BF16),
             pltpu.VMEM((local, 3 * width), BF16),
             pltpu.VMEM((kinds, local, keys), BF16),
@@ -523,33 +566,44 @@
             pltpu.VMEM((keys, 2 * width), BF16),
             pltpu.VMEM((local, width), BF16),
             pltpu.VMEM((keys, 2 * width), BF16),
-            pltpu.SemaphoreType.DMA((7,)),
+            pltpu.SemaphoreType.DMA((10,)),
         ],
         compiler_params=params(24),
         cost_estimate=pl.CostEstimate(flops=2 * 10**9, bytes_accessed=8 * 10**6, transcendentals=0),
         name="struct_backward",
-    )(rel_bias, halo, proj, count, w_struct, w_temp, dt_own, cot_own)
+    )(*in_hbm(rel_bias, halo, proj, count, w_struct, w_temp, dt_own, cot_own))
 
     if piece % 16 == 0 and (halo_per * width) % (piece * LANES) == 0:
         side = halo_per * width // piece
         mixed = pl.pallas_call(
             sum_kernel,
             out_shape=shape(doms, piece, 3 * width + side),
-            in_specs=[VMEM, VMEM],
+            in_specs=[VMEM, HBM],
             out_specs=VMEM,
+            scratch_shapes=[
+                pltpu.VMEM((halo_rows, width), F32),
+                pltpu.SemaphoreType.DMA((1,)),
+            ],
             compiler_params=params(8),
             name="sum_parts",
-        )(parts, back)
+        )(parts, *in_hbm(back))
         got = exchange(mixed, "dom")
         grad_feat, grad_wtemp = pl.pallas_call(
             last_kernel,
-            out_shape=(shape(local, width), shape(share, 3 * width, dtype=F32)),
-            in_specs=[SMEM, VMEM, VMEM],
-            out_specs=(VMEM, VMEM),
-            scratch_shapes=[pltpu.VMEM((halo_rows, width), F32)],
+            out_shape=(hbm(local, width), hbm(share, 3 * width, dtype=F32)),
+            in_specs=[HBM, VMEM, HBM],
+            out_specs=(HBM, HBM),
+            scratch_shapes=[
+                pltpu.SMEM(route.shape, jnp.int32),
+                pltpu.VMEM((local, width), F32),
+                pltpu.VMEM((local, width), BF16),
+                pltpu.VMEM((share, 3 * width), F32),
+                pltpu.VMEM((halo_rows, width), F32),
+                pltpu.SemaphoreType.DMA((4,)),
+            ],
             compiler_params=params(8),
             name="last_sums",
-        )(route, got, partial)
+        )(*in_hbm(route), got, *in_hbm(partial))
         return (grad_feat[None], grad_wtemp)
     total = jnp.sum(parts.astype(F32), axis=0).astype(BF16)
     got = exchange(jnp.broadcast_to(total[None], (doms,) + total.shape), "dom")

time: 79.4 us -> 69.8 us (0.88)
  local copies, waits for them, and re-layouts: 19.4 us -> 0.03 us
  Pallas kernels: 18.3 us -> 26.6 us
  waiting for transfers between devices: 5.5 us -> 8.34 us
  blocking collectives: 18.7 us -> 16.8 us
  starting transfers between devices: 15.9 us -> 16.8 us
    unnamed x62 -> x12, local copies, waits for them, and re-layouts: 19.4 us -> 0.03 us
    pallas_call x3, Pallas kernels: 8.96 us -> 15.1 us  [the longest x1 8.01 us: per_device(): pl.pallas_call(functools.partial(backward_kernel, heads), out_shape=(hbm(...]
    all_to_all x2, waiting for transfers between devices: 0.09 us -> 4.07 us  [exchange(): return lax.all_to_all(tiles, axis, split_axis=0, concat_axis=0, tiled=True)]
    all_to_all x1, blocking collectives: 18.7 us -> 16.8 us  [exchange(): return lax.all_to_all(tiles, axis, split_axis=0, concat_axis=0, tiled=True)]
    ppermute x6, waiting for transfers between devices: 5.41 us -> 4.27 us  [gather_blocks(): held[m ^ bit] = lax.ppermute(held[m], axis, pairs)]
    ppermute x6, starting transfers between devices: 2.61 us -> 3.68 us  [gather_blocks(): held[m ^ bit] = lax.ppermute(held[m], axis, pairs)]
    pallas_call x1, Pallas kernels: 0.06 us -> 0.94 us  [per_device(): pl.pallas_call(sum_kernel, out_shape=shape(doms, piece, 3 * width + side)...]
  transfers between devices with their start and end apart: 8 -> 8, of which waited for: 3 -> 4; matrix products, arithmetic and copies ran while one was open for 0% -> 0% of each run, Pallas kernels for 12% -> 23%
where the time goes in v3:
time: 69.8 us; the launch traced here: 69.4 us
  Pallas kernels  26.6 us (38%)
  starting transfers between devices  16.8 us (24%)
  blocking collectives  16.8 us (24%)
  waiting for transfers between devices  8.34 us (12%)
  between operations  0.74 us (1%)
    all_to_all x1, blocking collectives, exchange(): return lax.all_to_all(tiles, axis, split_axis=0, concat_axis=0, tiled=True)  16.8 us
    all_to_all x2, starting transfers between devices, exchange(): return lax.all_to_all(tiles, axis, split_axis=0, concat_axis=0, tiled=True)  13.2 us
    pallas_call x1, Pallas kernels, per_device(): pl.pallas_call(functools.partial(backward_kernel, heads), out_shape=(hbm(...  8.01 us
    pallas_call x1, Pallas kernels, per_device(): pl.pallas_call(functools.partial(temporal_kernel, snaps, heads), out_shap...  5.85 us
    pallas_call x1, Pallas kernels, per_device(): pl.pallas_call(own_kernel, out_shape=(hbm(local, 3 * width), hbm(kinds, l...  5.16 us
    ppermute x6, waiting for transfers between devices, gather_blocks(): held[m ^ bit] = lax.ppermute(held[m], axis, pairs)  4.27 us
    all_to_all x2, waiting for transfers between devices, exchange(): return lax.all_to_all(tiles, axis, split_axis=0, concat_axis=0, tiled=True)  4.07 us
    ppermute x6, starting transfers between devices, gather_blocks(): held[m ^ bit] = lax.ppermute(held[m], axis, pairs)  3.68 us
  transfers between devices with their start and end apart: 8, of which 4 were waited for; matrix products, arithmetic and copies ran while one was open for 0% of the time, Pallas kernels for 23%

profile of v3, /device:TPU:0, one launch (start us, length us, event | category | flops | bytes accessed | tf_op | source)
XLA Modules:
  0.0 69.4 jit_solution(8146930142360136795)
XLA Ops:
  0.6 1.7 %halo_tiles.1 = bf16[64,512]{1,0:T(8,128)(2,1)} custom-call(s32[8,8]{1,0:T(8,128)} %bitcast.19, bf16[128,512]{1,0:T(8,128)(2,1)} %bitcast.13), custom_call_target="tpu_custom_call" | custom-call | tf_op jit(solution)/shard_map/halo_tiles/pallas_call | solution.py:466
  2.3 7.3 %all-to-all-start = ((bf16[8,8,512]{2,1,0:T(8,128)(2,1)}), bf16[8,8,512]{2,1,0:T(8,128)(2,1)S(1)}, u32[]{:S(2)}, u32[]{:S(2)}) async-start(bf16[8,8,512]{2,1,0:T(8,128)(2,1)} %bitcast.3), calls=%async_computation | async-start | bytes 131072 | tf_op jit(solution)/shard_map/all_to_all | solution.py:439
  9.6 0.0 copy-start.2
  9.6 0.0 copy-start.5
  9.6 5.2 %own_rows.1 = (bf16[128,1536]{1,0:T(8,128)(2,1)}, bf16[4,128,256]{2,1,0:T(8,128)(2,1)}, bf16[5,32,512]{2,1,0:T(8,128)(2,1)}) custom-call(bf16[128,512]{1,0:T(8,128)(2,1)} %bitcast.14, bf16[512,1536]{1,0:T(8,128)(2,1)} %ws_hbm.1, s32[8,128]{1,0:T(8,128)} %bitcast.22, s32[8,128]{1,0:T(8,128)} %bitcast.23, s32[4,32]{1,0:T(4,128)} %act_hbm.1, ...), custom_call_target="tpu_custom_call" | custom-call | flops 1000000000 | bytes 4000000 | tf_op jit(solution)/shard_map/own_rows/pallas_call | solution.py:481
  14.8 0.0 copy-start
  14.8 0.0 copy-start.4
  14.8 1.6 %collective-permute-start.4 = (bf16[5,32,512]{2,1,0:T(8,128)(2,1)}, bf16[5,32,512]{2,1,0:T(8,128)(2,1)}, u32[]{:S(2)}, u32[]{:S(2)}) collective-permute-start(bf16[5,32,512]{2,1,0:T(8,128)(2,1)} %get-tuple-element.13.refs_4_), channel_id=1, source_target_pairs={{0,2},{1,3},{2,0},{3,1},{4,6},{5,7},{6,4},{7,5},{8,10},{9,11},{10,... | collective-permute-start | bytes 491528 | tf_op jit(solution)/shard_map/ppermute | solution.py:429
  16.4 0.1 all-to-all-done
  16.5 0.0 copy-done.1
  16.5 0.0 copy-done.2
  16.5 3.0 %struct_forward.1.refs_0_ = bf16[128,512]{1,0:T(8,128)(2,1)S(1)} custom-call(bf16[128,512]{1,0:T(8,128)(2,1)S(1)} %bitcast.15, f32[4,8]{1,0:T(4,128)S(1)} %copy-done.5, bf16[64,512]{1,0:T(8,128)(2,1)S(1)} %bitcast.16, bf16[512,1536]{1,0:T(8,128)(2,1)S(1)} %copy-done.1, bf16[4,128,256]{2,1,0:T(8,128)(2,1)} %get-tuple-element.12.count_hbm), custom_call_target="tpu_custom_call" | custom-call | tf_op jit(solution)/shard_map/struct_forward/pallas_call | solution.py:507
  19.6 1.6 %collective-permute-start.1 = (bf16[128,512]{1,0:T(8,128)(2,1)S(1)}, bf16[128,512]{1,0:T(8,128)(2,1)S(1)}, u32[]{:S(2)}, u32[]{:S(2)}) collective-permute-start(bf16[128,512]{1,0:T(8,128)(2,1)S(1)} %struct_forward.1.refs_0_), channel_id=1, source_target_pairs={{0,2},{1,3},{2,0},{3,1},{4,6},{5,7},{6,4},{7,5},{8,10},{9,11},{10,... | collective-permute-start | bytes 393224 | tf_op jit(solution)/shard_map/ppermute | solution.py:429
  21.2 0.0 collective-permute-start.3
  21.2 0.0 collective-permute-done.4.refs_6_
  21.2 0.5 collective-permute-start.5
  21.7 0.0 collective-permute-start
  21.7 2.9 %collective-permute-done.1.refs_2_ = bf16[128,512]{1,0:T(8,128)(2,1)S(1)} collective-permute-done((bf16[128,512]{1,0:T(8,128)(2,1)S(1)}, bf16[128,512]{1,0:T(8,128)(2,1)S(1)}, u32[]{:S(2)}, u32[]{:S(2)}) %collective-permute-start.1) | collective-permute-done | bytes 131104 | tf_op jit(solution)/shard_map/ppermute | solution.py:429
  24.6 0.0 collective-permute-start.2
  24.6 0.0 collective-permute-done.3.refs_5_
  24.6 0.0 collective-permute-done.refs_1_
  24.6 0.0 collective-permute-done.5.refs_7_
  24.6 1.3 %collective-permute-done.2.refs_3_ = bf16[128,512]{1,0:T(8,128)(2,1)S(1)} collective-permute-done((bf16[128,512]{1,0:T(8,128)(2,1)S(1)}, bf16[128,512]{1,0:T(8,128)(2,1)S(1)}, u32[]{:S(2)}, u32[]{:S(2)}) %collective-permute-start.2) | collective-permute-done | bytes 131104 | tf_op jit(solution)/shard_map/ppermute | solution.py:429
  26.0 0.0 copy-done
  26.0 5.9 %temporal.1 = (bf16[128,1536]{1,0:T(8,128)(2,1)}, bf16[128,1536]{1,0:T(8,128)(2,1)}, bf16[128,512]{1,0:T(8,128)(2,1)}) custom-call(s32[1]{0:T(128)} %bitcast.1.me_ref, bf16[4,512]{1,0:T(4,128)(2,1)S(1)} %copy-done.4, bf16[512,1536]{1,0:T(8,128)(2,1)S(1)} %copy-done, bf16[128,512]{1,0:T(8,128)(2,1)S(1)} %struct_forward.1.refs_0_, ...), custom_call_target="tpu_custom_call" | custom-call | tf_op jit(solution)/shard_map/temporal/pallas_call | solution.py:524
  31.8 0.0 copy-done.3
  31.8 5.9 %all-to-all-start.1 = ((bf16[8,16,1536]{2,1,0:T(8,128)(2,1)}), bf16[8,16,1536]{2,1,0:T(8,128)(2,1)S(1)}, u32[]{:S(2)}, u32[]{:S(2)}) async-start(bf16[8,16,1536]{2,1,0:T(8,128)(2,1)} %bitcast.18), calls=%async_computation.1 | async-start | bytes 786432 | tf_op jit(solution)/shard_map/all_to_all | solution.py:439
  37.7 8.0 %struct_backward.1 = (f32[64,512]{1,0:T(8,128)}, f32[128,512]{1,0:T(8,128)}) custom-call(f32[4,8]{1,0:T(4,128)} %bias_hbm.1, bf16[64,512]{1,0:T(8,128)(2,1)} %bitcast.17, bf16[128,1536]{1,0:T(8,128)(2,1)} %get-tuple-element.15.proj_hbm, bf16[4,128,256]{2,1,0:T(8,128)(2,1)} %get-tuple-element.12.count_hbm, bf16[512,1536]{1,0:T(8,128)(2,1)} %ws_hbm.1, ...), custom_call_target="tpu_custom_call" | custom-call | flops 2000000000 | bytes 8000000 | tf_op jit(solution)/shard_map/struct_backward/pallas_call | solution.py:550
  45.8 4.0 %all-to-all-done.1.parts_ref = bf16[8,16,1536]{2,1,0:T(8,128)(2,1)S(1)} async-done(((bf16[8,16,1536]{2,1,0:T(8,128)(2,1)}), bf16[8,16,1536]{2,1,0:T(8,128)(2,1)S(1)}, u32[]{:S(2)}, u32[]{:S(2)}) %all-to-all-start.1) | async-done | bytes 393248 | tf_op jit(solution)/shard_map/all_to_all | solution.py:439
  49.7 0.9 %sum_parts.1 = bf16[8,16,1792]{2,1,0:T(8,128)(2,1)S(1)} custom-call(bf16[8,16,1536]{2,1,0:T(8,128)(2,1)S(1)} %all-to-all-done.1.parts_ref, f32[64,512]{1,0:T(8,128)} %get-tuple-element.18.back_hbm), custom_call_target="tpu_custom_call" | custom-call | tf_op jit(solution)/shard_map/sum_parts/pallas_call | solution.py:578
  50.7 16.8 %all_to_all.15.got_ref = bf16[8,16,1792]{2,1,0:T(8,128)(2,1)S(1)} all-to-all(bf16[8,16,1792]{2,1,0:T(8,128)(2,1)S(1)} %sum_parts.1), channel_id=1, replica_groups=mesh['dom'=8,'snap'=4] {'dom'}, dimensions={0} | all-to-all | bytes 917504 | tf_op jit(solution)/shard_map/all_to_all | solution.py:439
  67.5 1.9 %last_sums.1 = (bf16[128,512]{1,0:T(8,128)(2,1)}, f32[128,1536]{1,0:T(8,128)}) custom-call(s32[8,8]{1,0:T(8,128)} %bitcast.20, bf16[8,16,1792]{2,1,0:T(8,128)(2,1)S(1)} %all_to_all.15.got_ref, f32[128,512]{1,0:T(8,128)} %get-tuple-element.19.part_hbm), custom_call_target="tpu_custom_call" | custom-call | tf_op jit(solution)/shard_map/last_sums/pallas_call | solution.py:591
  (4 shorter events, 0.0 us)
Async XLA Ops:
  2.3 14.2 %all-to-all-start = ((bf16[8,8,512]{2,1,0:T(8,128)(2,1)}), bf16[8,8,512]{2,1,0:T(8,128)(2,1)S(1)}, u32[]{:S(2)}, u32[]{:S(2)}) async-start(bf16[8,8,512]{2,1,0:T(8,128)(2,1)} %bitcast.3), calls=%async_computation | async-start | bytes 131072 | tf_op jit(solution)/shard_map/all_to_all | solution.py:439
  9.6 6.9 %copy-start.1 = (bf16[512,1536]{1,0:T(8,128)(2,1)S(1)}, bf16[512,1536]{1,0:T(8,128)(2,1)}, u32[]{:S(2)}) copy-start(bf16[512,1536]{1,0:T(8,128)(2,1)} %ws_hbm.1) | copy-start | bytes 4718596
  9.6 6.9 %copy-start.2 = (bf16[1,128,512]{2,1,0:T(8,128)(2,1)S(1)}, bf16[1,128,512]{2,1,0:T(8,128)(2,1)}, u32[]{:S(2)}) copy-start(bf16[1,128,512]{2,1,0:T(8,128)(2,1)} %param.10) | copy-start | bytes 393220
  9.6 6.9 %copy-start.5 = (f32[4,8]{1,0:T(4,128)S(1)}, f32[4,8]{1,0:T(4,128)}, u32[]{:S(2)}) copy-start(f32[4,8]{1,0:T(4,128)} %bias_hbm.1) | copy-start | bytes 388
  14.8 11.2 %copy-start = (bf16[512,1536]{1,0:T(8,128)(2,1)S(1)}, bf16[512,1536]{1,0:T(8,128)(2,1)}, u32[]{:S(2)}) copy-start(bf16[512,1536]{1,0:T(8,128)(2,1)} %wt_hbm.1) | copy-start | bytes 4718596
  14.8 11.1 %copy-start.4 = (bf16[4,512]{1,0:T(4,128)(2,1)S(1)}, bf16[4,512]{1,0:T(4,128)(2,1)}, u32[]{:S(2)}) copy-start(bf16[4,512]{1,0:T(4,128)(2,1)} %pos_ref.1) | copy-start | bytes 12292
  14.8 6.3 %collective-permute-start.4 = (bf16[5,32,512]{2,1,0:T(8,128)(2,1)}, bf16[5,32,512]{2,1,0:T(8,128)(2,1)}, u32[]{:S(2)}, u32[]{:S(2)}) collective-permute-start(bf16[5,32,512]{2,1,0:T(8,128)(2,1)} %get-tuple-element.13.refs_4_), channel_id=1, source_target_pairs={{0,2},{1,3},{2,0},{3,1},{4,6},{5,7},{6,4},{7,5},{8,10},{9,11},{10,... | collective-permute-start | bytes 491528 | tf_op jit(solution)/shard_map/ppermute | solution.py:429
  16.5 15.3 %copy-start.3 = (bf16[8,8,512]{2,1,0:T(8,128)(2,1)}, bf16[8,8,512]{2,1,0:T(8,128)(2,1)S(1)}, u32[]{:S(2)}) copy-start(bf16[8,8,512]{2,1,0:T(8,128)(2,1)S(1)} %all-to-all-done) | copy-start | bytes 196612
  19.6 5.0 %collective-permute-start.1 = (bf16[128,512]{1,0:T(8,128)(2,1)S(1)}, bf16[128,512]{1,0:T(8,128)(2,1)S(1)}, u32[]{:S(2)}, u32[]{:S(2)}) collective-permute-start(bf16[128,512]{1,0:T(8,128)(2,1)S(1)} %struct_forward.1.refs_0_), channel_id=1, source_target_pairs={{0,2},{1,3},{2,0},{3,1},{4,6},{5,7},{6,4},{7,5},{8,10},{9,11},{10,... | collective-permute-start | bytes 393224 | tf_op jit(solution)/shard_map/ppermute | solution.py:429
  21.2 3.5 %collective-permute-start.3 = (bf16[5,32,512]{2,1,0:T(8,128)(2,1)}, bf16[5,32,512]{2,1,0:T(8,128)(2,1)S(1)}, u32[]{:S(2)}, u32[]{:S(2)}) collective-permute-start(bf16[5,32,512]{2,1,0:T(8,128)(2,1)} %get-tuple-element.13.refs_4_), channel_id=1, source_target_pairs={{0,1},{1,0},{2,3},{3,2},{4,5},{5,4},{6,7},{7,6},{8,9},{9,8},{10,11... | collective-permute-start | bytes 491528 | tf_op jit(solution)/shard_map/ppermute | solution.py:429
  21.2 3.5 %collective-permute-start.5 = (bf16[5,32,512]{2,1,0:T(8,128)(2,1)}, bf16[5,32,512]{2,1,0:T(8,128)(2,1)S(1)}, u32[]{:S(2)}, u32[]{:S(2)}) collective-permute-start(bf16[5,32,512]{2,1,0:T(8,128)(2,1)} %collective-permute-done.4.refs_6_), channel_id=1, source_target_pairs={{0,1},{1,0},{2,3},{3,2},{4,5},{5,4},{6,7},{7,6},{8,9},{9,8},{10,11... | collective-permute-start | bytes 491528 | tf_op jit(solution)/shard_map/ppermute | solution.py:429
  21.7 2.9 %collective-permute-start = (bf16[128,512]{1,0:T(8,128)(2,1)S(1)}, bf16[128,512]{1,0:T(8,128)(2,1)S(1)}, u32[]{:S(2)}, u32[]{:S(2)}) collective-permute-start(bf16[128,512]{1,0:T(8,128)(2,1)S(1)} %struct_forward.1.refs_0_), channel_id=1, source_target_pairs={{0,1},{1,0},{2,3},{3,2},{4,5},{5,4},{6,7},{7,6},{8,9},{9,8},{10,11... | collective-permute-start | bytes 393224 | tf_op jit(solution)/shard_map/ppermute | solution.py:429
  24.6 1.3 %collective-permute-start.2 = (bf16[128,512]{1,0:T(8,128)(2,1)S(1)}, bf16[128,512]{1,0:T(8,128)(2,1)S(1)}, u32[]{:S(2)}, u32[]{:S(2)}) collective-permute-start(bf16[128,512]{1,0:T(8,128)(2,1)S(1)} %collective-permute-done.1.refs_2_), channel_id=1, source_target_pairs={{0,1},{1,0},{2,3},{3,2},{4,5},{5,4},{6,7},{7,6},{8,9},{9,8},{10,11... | collective-permute-start | bytes 393224 | tf_op jit(solution)/shard_map/ppermute | solution.py:429
  31.8 17.9 %all-to-all-start.1 = ((bf16[8,16,1536]{2,1,0:T(8,128)(2,1)}), bf16[8,16,1536]{2,1,0:T(8,128)(2,1)S(1)}, u32[]{:S(2)}, u32[]{:S(2)}) async-start(bf16[8,16,1536]{2,1,0:T(8,128)(2,1)} %bitcast.18), calls=%async_computation.1 | async-start | bytes 786432 | tf_op jit(solution)/shard_map/all_to_all | solution.py:439

commit v4 on v3

v4 whole, which is shorter than its diff:
```python
import functools

import jax
import jax.numpy as jnp
from jax import lax
from jax.experimental import pallas as pl
from jax.experimental.pallas import tpu as pltpu
from jax.sharding import PartitionSpec as P

F32 = jnp.float32
BF16 = jnp.bfloat16
LANES = 128
NEG = -1e30
VMEM = pl.BlockSpec(memory_space=pltpu.VMEM)
SMEM = pl.BlockSpec(memory_space=pltpu.SMEM)
HBM = pl.BlockSpec(memory_space=pltpu.HBM)


def dot_nn(a, b):
    return lax.dot_general(a, b, (((1,), (0,)), ((), ())), preferred_element_type=F32)


def dot_nt(a, b):
    return lax.dot_general(a, b, (((1,), (1,)), ((), ())), preferred_element_type=F32)


def dot_tn(a, b):
    return lax.dot_general(a, b, (((0,), (0,)), ((), ())), preferred_element_type=F32)


def stack_heads(block, head_dim):
    rows, lanes = block.shape
    head = lax.broadcasted_iota(jnp.int32, (rows, lanes), 1) // head_dim
    zero = jnp.zeros_like(block)
    return jnp.concatenate(
        [jnp.where(head == g, block, zero) for g in range(lanes // head_dim)], axis=0
    )


def unstack_heads(stacked, head_dim):
    lanes = stacked.shape[1]
    groups = lanes // head_dim
    rows = stacked.shape[0] // groups
    head = lax.broadcasted_iota(jnp.int32, (rows, lanes), 1) // head_dim
    out = stacked[:rows]
    for g in range(1, groups):
        out = jnp.where(head == g, stacked[g * rows : (g + 1) * rows], out)
    return out


class Fetch:

    def __init__(self, sems, *pairs):
        self.copies = [
            pltpu.make_async_copy(src, dst, sems.at[i]) for i, (src, dst) in enumerate(pairs)
        ]
        for copy in self.copies:
            copy.start()

    def wait(self, *which):
        for i in which:
            self.copies[i].wait()


def pick_rows(route_ref, local):
    doms, per = route_ref.shape
    lane = lax.broadcasted_iota(jnp.int32, (per, local), 1)
    sub = lax.broadcasted_iota(jnp.int32, (per, local), 0)
    tiles = []
    for r in range(doms):
        spot = jnp.zeros((per, local), jnp.int32)
        for j in range(per):
            spot = jnp.where(sub == j, route_ref[r, j], spot)
        tiles.append(jnp.where(lane == spot, 1.0, 0.0))
    return jnp.concatenate(tiles, axis=0).astype(BF16)


def tiles_kernel(route_hbm, x_hbm, out_ref, route, x, sems):
    fetch = Fetch(sems, (route_hbm, route), (x_hbm, x))
    fetch.wait(0, 1)
    out_ref[...] = dot_nn(pick_rows(route, x.shape[0]), x[...]).astype(BF16)


def own_kernel(
    nbr_hbm, rel_hbm, bias_hbm, act_hbm, cot_hbm, edge_hbm, load_ref,
    nbr, rel, bias, act, cot, edge, sems,
):
    heads, rows, keys = edge.shape
    kinds = bias.shape[0]
    slots = nbr.shape[0]
    snaps, ents, width = cot.shape
    fetch = Fetch(
        sems, (nbr_hbm, nbr), (rel_hbm, rel), (bias_hbm, bias), (act_hbm, act), (cot_hbm, cot)
    )
    row = lax.broadcasted_iota(jnp.int32, (ents, ents), 0)
    col = lax.broadcasted_iota(jnp.int32, (ents, ents), 1)
    lane = lax.broadcasted_iota(jnp.int32, (ents, width), 1)
    flags = jnp.zeros((ents, width), F32)
    fetch.wait(0, 1, 2, 3)
    on = act[...].astype(F32)
    for t in range(snaps):
        column = jnp.sum(jnp.where(row == col, on[t : t + 1, :], 0.0), axis=1, keepdims=True)
        flags = jnp.where(lane == t, column, flags)
    load_ref[snaps] = flags.astype(BF16)
    code = jnp.transpose((nbr[...] * kinds + rel[...]).astype(F32))
    spot = (lax.broadcasted_iota(jnp.int32, (rows, keys), 1) * kinds).astype(F32)
    counts = []
    for r in range(kinds):
        here = spot + float(r)
        total = jnp.zeros((rows, keys), F32)
        for k in range(slots):
            total = total + jnp.where(code[:, k : k + 1] == here, 1.0, 0.0)
        counts.append(total)
    gain = jnp.exp(bias[...])
    stores = []
    for h in range(heads):
        total = counts[0] * gain[0:1, h : h + 1]
        for r in range(1, kinds):
            total = total + counts[r] * gain[r : r + 1, h : h + 1]
        edge[h] = jnp.where(total > 0, jnp.log(total), NEG)
        stores.append(Fetch(sems.at[5 + h :], (edge.at[h], edge_hbm.at[h])))
    fetch.wait(4)
    for t in range(snaps):
        load_ref[t] = cot[t]
    for store in stores:
        store.wait(0)


def fill_table(tab_s, proj, halo, w_kv):
    rows, width = proj.shape[0], halo.shape[1]
    used = rows + halo.shape[0]
    tab_s[:rows, :] = proj[:, width:]
    for part in range(2):
        cols = slice(part * width, (part + 1) * width)
        tab_s[rows:used, cols] = dot_nn(halo[...], w_kv[:, cols]).astype(BF16)
    if tab_s.shape[0] > used:
        tab_s[used:, :] = jnp.zeros((tab_s.shape[0] - used, 2 * width), BF16)


def edge_attention(p, heads, proj, edge, tab_s, width):
    keys = tab_s.shape[0]
    head_dim = width // heads
    group = LANES // head_dim
    cols = slice(p * LANES, (p + 1) * LANES)
    kk = stack_heads(tab_s[:, cols], head_dim)
    score = dot_nt(proj[:, cols], kk)
    parts = []
    for g in range(group):
        s = score[:, g * keys : (g + 1) * keys] * head_dim ** (-0.5) + edge[p * group + g]
        e = jnp.exp(s - jnp.max(s, axis=1, keepdims=True))
        parts.append(e * (1.0 / jnp.sum(e, axis=1, keepdims=True)))
    return kk, parts


def forward_kernel(heads, x, halo, w, edge_hbm, hidden_ref, edge, proj, tab_s, sems):
    width = x.shape[1]
    head_dim = width // heads
    group = LANES // head_dim
    fetch = Fetch(sems, *[(edge_hbm.at[h], edge.at[h]) for h in range(heads)])
    for part in range(3):
        cols = slice(part * width, (part + 1) * width)
        proj[:, cols] = dot_nn(x[...], w[:, cols]).astype(BF16)
    fill_table(tab_s, proj, halo, w.at[:, width:])
    for p in range(width // LANES):
        cols = slice(p * LANES, (p + 1) * LANES)
        vcols = slice(width + p * LANES, width + (p + 1) * LANES)
        fetch.wait(*range(p * group, (p + 1) * group))
        _, attn = edge_attention(p, heads, proj, edge, tab_s, width)
        vv = stack_heads(tab_s[:, vcols], head_dim)
        agg = dot_nn(jnp.concatenate([a.astype(BF16) for a in attn], axis=1), vv)
        elu = jnp.where(agg > 0, agg, jnp.exp(jnp.minimum(agg, 0.0)) - 1.0)
        hidden_ref[:, cols] = (x[:, cols].astype(F32) + elu).astype(BF16)


def each(lo, hi, unroll, body):
    if unroll:
        for i in range(lo, hi):
            body(i)
    else:
        lax.fori_loop(lo, hi, lambda i, c: (body(i), c)[1], 0)


def temporal_kernel(snaps, heads, pieces, place_ref, pos_ref, w_s, *refs):
    hid = refs[:snaps]
    cot = refs[snaps : 2 * snaps]
    terms_ref = refs[2 * snaps : 2 * snaps + pieces]
    (
        dt_own_ref, cot_own_ref,
        z_s, ct_s, tp_s, dt_s, act_s, prod_s, s_s, d_s, a_s, ds_s, wa_s, wd_s, dk_s, dv_s, terms_s,
    ) = refs[2 * snaps + pieces :]
    local, width = hid[0].shape
    ents = cot[0].shape[1]
    head_dim = width // heads
    scale = head_dim ** (-0.5)
    unroll = snaps <= 4
    me, outer = place_ref[0], place_ref[1]
    pos = pos_ref[...].astype(F32)
    which = lax.broadcasted_iota(jnp.int32, pos.shape, 0)

    def rows_of(t):
        return pl.ds(t * local if isinstance(t, int) else pl.multiple_of(t * local, local), local)

    for n in range(snaps):
        t = lax.bitwise_xor(me, n)
        shift = jnp.sum(jnp.where(which == t, pos, 0.0), axis=0, keepdims=True)
        z_s[rows_of(t), :] = (hid[n][...].astype(F32) + shift).astype(BF16)
    for part in range(3):
        cols = slice(part * width, (part + 1) * width)
        tp_s[:, cols] = dot_nn(z_s[...], w_s[:, cols]).astype(BF16)
    for m in range(snaps):
        at = pl.multiple_of(lax.bitwise_xor(me, m) * ents, ents)
        for t in range(snaps):
            ct_s[pl.ds(t * local + at, ents), :] = cot[m][t].astype(ct_s.dtype)
        act_s[pl.ds(at, ents), :] = cot[m][snaps][:, :LANES].astype(F32)
    lane_head = lax.broadcasted_iota(jnp.int32, (width, LANES), 0) // head_dim
    fold = (lane_head == lax.broadcasted_iota(jnp.int32, (width, LANES), 1)).astype(F32)
    fold = fold.astype(BF16)
    head_lane = lax.broadcasted_iota(jnp.int32, (LANES, width), 1) // head_dim
    spread = (head_lane == lax.broadcasted_iota(jnp.int32, (LANES, width), 0)).astype(F32)
    spread_scaled = (spread * scale).astype(BF16)
    spread = spread.astype(BF16)
    act = act_s[...]
    snap_lane = lax.broadcasted_iota(jnp.int32, act.shape, 1)
    if not unroll:
        dk_s[...] = jnp.zeros_like(dk_s)
        dv_s[...] = jnp.zeros_like(dv_s)

    def one_snap(t):
        used = (t + 1 if unroll else snaps) * local
        half = snaps * local

        def product(u):
            q, k, v = (
                tp_s[rows_of(i), part * width : (part + 1) * width]
                for part, i in ((0, t), (1, u), (2, u))
            )
            prod_s[rows_of(u), :] = q * k
            prod_s[rows_of(snaps + u), :] = ct_s[rows_of(t), :].astype(BF16) * v

        each(0, t + 1, unroll, product)
        s_s[:used, :] = dot_nn(prod_s[:used, :], fold)
        d_s[:used, :] = dot_nn(prod_s[half : half + used, :], fold).astype(BF16).astype(F32)

        def mask(u):
            on = jnp.sum(jnp.where(snap_lane == u, act, 0.0), axis=1, keepdims=True)
            s_s[rows_of(u), :] = jnp.where((on > 0.5) | (u == t), s_s[rows_of(u), :] * scale, NEG)

        each(0, t + 1, unroll, mask)

        def reduced(fn, start):
            if unroll:
                for u in range(t + 1):
                    start = fn(u, start)
                return start
            return lax.fori_loop(0, t + 1, fn, start)

        top = reduced(
            lambda u, c: jnp.maximum(c, s_s[rows_of(u), :]), jnp.full((local, LANES), NEG, F32)
        )

        def expo(u, total):
            e = jnp.exp(s_s[rows_of(u), :] - top)
            s_s[rows_of(u), :] = e
            return total + e

        inv = 1.0 / reduced(expo, jnp.zeros((local, LANES), F32))

        def weigh(u, total):
            a = s_s[rows_of(u), :] * inv
            s_s[rows_of(u), :] = a
            return total + a * d_s[rows_of(u), :]

        dot = reduced(weigh, jnp.zeros((local, LANES), F32))

        def keep(u):
            a = s_s[rows_of(u), :]
            a_s[rows_of(u), :] = a.astype(BF16)
            ds_s[rows_of(u), :] = (a * (d_s[rows_of(u), :] - dot)).astype(BF16)

        each(0, t + 1, unroll, keep)
        wa_s[:used, :] = dot_nn(a_s[:used, :], spread)
        wd_s[:used, :] = dot_nn(ds_s[:used, :], spread_scaled)

        for p in range(width // LANES):
            c0 = p * LANES
            cols = slice(c0, c0 + LANES)
            q = tp_s[rows_of(t), cols].astype(F32)
            ct = ct_s[rows_of(t), cols].astype(F32)

            def back(u, dq):
                k = tp_s[rows_of(u), width + c0 : width + c0 + LANES].astype(F32)
                wide_ds = wd_s[rows_of(u), cols]
                dk, dv = wide_ds * q, wa_s[rows_of(u), cols] * ct
                if unroll and u == t:
                    dk_s[rows_of(u), cols] = dk
                    dv_s[rows_of(u), cols] = dv
                else:
                    dk_s[rows_of(u), cols] += dk
                    dv_s[rows_of(u), cols] += dv
                return dq + wide_ds * k

            dt_s[rows_of(t), cols] = reduced(back, jnp.zeros_like(q)).astype(BF16)

    each(0, snaps, unroll, one_snap)
    dt_s[:, width : 2 * width] = dk_s[...].astype(BF16)
    dt_s[:, 2 * width :] = dv_s[...].astype(BF16)
    share = width // snaps
    pick = (
        lax.broadcasted_iota(jnp.int32, (width, share), 0)
        == lax.broadcasted_iota(jnp.int32, (width, share), 1) + me * share
    )
    z_mine = dot_nn(z_s[...], pick.astype(F32).astype(BF16)).astype(BF16)
    for part in range(3):
        cols = slice(part * width, (part + 1) * width)
        terms_s[:, cols] = dot_tn(z_mine, dt_s[:, cols]).astype(BF16)
    piece = share // pieces
    for k in range(pieces):
        if pieces == 1:
            terms_ref[k][...] = terms_s[...]
        else:
            at = pl.multiple_of(lax.bitwise_xor(outer, k) * piece, piece)
            terms_ref[k][...] = terms_s[pl.ds(at, piece), :]
    dt_own_ref[...] = dt_s[rows_of(me), :]
    cot_own_ref[...] = ct_s[rows_of(me), :].astype(BF16)


def backward_kernel(
    heads, dt, cot, x_hbm, halo_hbm, edge_hbm, ws_hbm, wt_hbm, back_ref, part_ref,
    x, halo, edge, ws, wt, proj, tab_s, dq_s, dtab_s, sems,
):
    rows, width = cot.shape
    halo_rows = halo.shape[0]
    keys = tab_s.shape[0]
    head_dim = width // heads
    group = LANES // head_dim
    scale = head_dim ** (-0.5)
    fetch = Fetch(
        sems, (wt_hbm, wt), (x_hbm, x), (ws_hbm, ws), (halo_hbm, halo), (edge_hbm, edge)
    )
    fetch.wait(0)
    dh = cot[...].astype(F32) + dot_nt(dt[...], wt[...])
    part_ref[...] = dh.astype(BF16).astype(F32)
    fetch.wait(1, 2, 3)
    for part in range(3):
        cols = slice(part * width, (part + 1) * width)
        proj[:, cols] = dot_nn(x[...], ws[:, cols]).astype(BF16)
    fill_table(tab_s, proj, halo, ws.at[:, width:])
    fetch.wait(4)
    for p in range(width // LANES):
        cols = slice(p * LANES, (p + 1) * LANES)
        vcols = slice(width + p * LANES, width + (p + 1) * LANES)
        kk, attn = edge_attention(p, heads, proj, edge, tab_s, width)
        vv = stack_heads(tab_s[:, vcols], head_dim)
        attn_b = jnp.concatenate([a.astype(BF16) for a in attn], axis=1)
        agg = dot_nn(attn_b, vv)
        da = part_ref[:, cols] * jnp.where(agg > 0, 1.0, jnp.exp(jnp.minimum(agg, 0.0)))
        da = da.astype(BF16)
        dattn = dot_nt(da, vv).astype(BF16).astype(F32)
        ds = []
        for g in range(group):
            ad = attn[g] * dattn[:, g * keys : (g + 1) * keys]
            ds.append((ad - attn[g] * jnp.sum(ad, axis=1, keepdims=True)).astype(BF16))
        ds = jnp.concatenate(ds, axis=1)
        dq_s[:, cols] = (dot_nn(ds, kk) * scale).astype(BF16)
        dtab_s[:, cols] = (unstack_heads(dot_tn(ds, proj[:, cols]), head_dim) * scale).astype(BF16)
        dtab_s[:, vcols] = unstack_heads(dot_tn(attn_b, da), head_dim).astype(BF16)
    back_ref[...] = dot_nt(dtab_s[rows : rows + halo_rows, :], ws[:, width:])
    part_ref[...] += dot_nt(dq_s[...], ws[:, :width]) + dot_nt(dtab_s[:rows, :], ws[:, width:])


def tile_of(place_ref, flip, back_ref, per):
    at = lax.bitwise_xor(place_ref[2], flip) * per
    return back_ref[pl.ds(pl.multiple_of(at, per), per), :]


def outer_sum_kernel(per, place_ref, back_ref, *refs):
    *terms, out_ref = refs
    wide = terms[0].shape[1]
    total = terms[0][...].astype(F32)
    for term in terms[1:]:
        total = total + term[...].astype(F32)
    out_ref[:, :wide] = total.astype(BF16)
    tiles = [tile_of(place_ref, 2 * k + 1, back_ref, per) for k in range(len(terms))]
    out_ref[:, wide:] = jnp.concatenate(tiles, axis=0).astype(BF16)


def inner_sum_kernel(per, place_ref, back_ref, mine_ref, other_ref, *out):
    rows = mine_ref.shape[0]
    wide = mine_ref.shape[1] - back_ref.shape[1]
    lanes = out[0].shape[1] - wide
    total = (mine_ref[:, :wide].astype(F32) + other_ref[:, :wide].astype(F32)).astype(BF16)
    passing = other_ref[:, wide:].astype(F32)
    for k in range(len(out)):
        out[k][:, :wide] = total
        both = [tile_of(place_ref, 2 * k, back_ref, per), passing[k * per : (k + 1) * per]]
        folds = [
            tile[:, i * lanes : (i + 1) * lanes]
            for tile in both
            for i in range(rows // (2 * per))
        ]
        out[k][:, wide:] = jnp.concatenate(folds, axis=0).astype(BF16)


def last_kernel(per, place_ref, route_ref, part_ref, *refs):
    got = refs[:-6]
    feat_hbm, wtemp_hbm, feat, wtemp, came_s, sems = refs[-6:]
    pieces = len(got)
    rows = got[0].shape[0]
    wide = wtemp.shape[2]
    lanes = got[0].shape[1] - wide
    stores = []
    for k in range(pieces):
        wtemp[k] = got[k][:, :wide].astype(F32)
        at = pl.multiple_of(lax.bitwise_xor(place_ref[1], k) * rows, rows)
        stores.append(Fetch(sems.at[k:], (wtemp.at[k], wtemp_hbm.at[pl.ds(at, rows), :])))
        folded = got[k][:, wide:].astype(F32)
        folds = rows // (2 * per)
        for j in range(2):
            d = lax.bitwise_xor(place_ref[2], 2 * k + j) * per
            for i in range(folds):
                f = (j * folds + i) * per
                came_s[pl.ds(pl.multiple_of(d, per), per), i * lanes : (i + 1) * lanes] = folded[
                    f : f + per
                ]
    back = dot_tn(pick_rows(route_ref, part_ref.shape[0]), came_s[...].astype(BF16))
    feat[...] = (part_ref[...] + back).astype(BF16)
    stores.append(Fetch(sems.at[pieces:], (feat, feat_hbm)))
    for store in stores:
        store.wait(0)


def params(mib):
    return pltpu.CompilerParams(vmem_limit_bytes=mib * 1024 * 1024)


def gather_blocks(block, axis):
    count = lax.axis_size(axis)
    held = {0: block}
    bit = count // 2
    while bit:
        for m in sorted(held):
            pairs = [(i, i ^ bit) for i in range(count)]
            held[m ^ bit] = lax.ppermute(held[m], axis, pairs)
        bit //= 2
    return [held[m] for m in range(count)]


def in_hbm(*arrays):
    return [pltpu.with_memory_space_constraint(a, pltpu.HBM) for a in arrays]


def exchange(tiles, axis):
    return lax.all_to_all(tiles, axis, split_axis=0, concat_axis=0, tiled=True)


def flipped(block, axis, flip):
    count = lax.axis_size(axis)
    return lax.ppermute(block, axis, [(i, i ^ flip) for i in range(count)])


def per_device(
    feat, w_struct, w_temp, pos_embed, rel_bias, nbr, rel_type, send_idx, active, cotangent
):
    x = feat[0]
    local, width = x.shape
    heads = rel_bias.shape[1]
    slots = nbr.shape[2]
    doms = lax.axis_size("dom")
    snaps = lax.axis_size("snap")
    ents = local // snaps
    route = send_idx[0, 0]
    halo_per = route.shape[1]
    halo_rows = doms * halo_per
    keys = -(-(local + halo_rows) // LANES) * LANES
    share = width // snaps
    pieces = doms // 2
    piece = share // pieces
    lanes = 2 * halo_per * width // piece if piece else 0
    paired = (
        doms % 2 == 0
        and doms & (doms - 1) == 0
        and piece == pieces * halo_per
        and piece % 16 == 0
        and lanes % LANES == 0
        and lanes > 0
    )
    if not paired:
        pieces = 1
    dom = lax.axis_index("dom").astype(jnp.int32)
    snap = lax.axis_index("snap").astype(jnp.int32)
    place = jnp.stack([snap, dom // 2, dom])

    def shape(*dims, dtype=BF16):
        return jax.ShapeDtypeStruct(dims, dtype)

    def hbm(*dims, dtype=BF16):
        return pltpu.HBM(dims, dtype)

    tiles = pl.pallas_call(
        tiles_kernel,
        out_shape=shape(halo_rows, width),
        in_specs=[HBM, HBM],
        out_specs=VMEM,
        scratch_shapes=[
            pltpu.SMEM(route.shape, jnp.int32),
            pltpu.VMEM((local, width), BF16),
            pltpu.SemaphoreType.DMA((2,)),
        ],
        compiler_params=params(8),
        name="halo_tiles",
    )(*in_hbm(route, x))
    halo = exchange(tiles.reshape(doms, halo_per, width), "dom").reshape(halo_rows, width)

    edge, load = pl.pallas_call(
        own_kernel,
        out_shape=(hbm(heads, local, keys, dtype=F32), shape(snaps + 1, ents, width)),
        in_specs=[HBM] * 5,
        out_specs=(HBM, VMEM),
        scratch_shapes=[
            pltpu.VMEM((slots, local), jnp.int32),
            pltpu.VMEM((slots, local), jnp.int32),
            pltpu.VMEM(rel_bias.shape, F32),
            pltpu.VMEM((snaps, ents), jnp.int32),
            pltpu.VMEM((snaps, ents, width), BF16),
            pltpu.VMEM((heads, local, keys), F32),
            pltpu.SemaphoreType.DMA((5 + heads,)),
        ],
        compiler_params=params(16),
        cost_estimate=pl.CostEstimate(flops=10**9, bytes_accessed=4 * 10**6, transcendentals=0),
        name="own_edges",
    )(*in_hbm(nbr[0].T, rel_type[0].T, rel_bias, active, cotangent))
    cots = gather_blocks(load, "snap")

    hidden = pl.pallas_call(
        functools.partial(forward_kernel, heads),
        out_shape=shape(local, width),
        in_specs=[VMEM] * 3 + [HBM],
        out_specs=VMEM,
        scratch_shapes=[
            pltpu.VMEM((heads, local, keys), F32),
            pltpu.VMEM((local, 3 * width), BF16),
            pltpu.VMEM((keys, 2 * width), BF16),
            pltpu.SemaphoreType.DMA((heads,)),
        ],
        compiler_params=params(8),
        name="struct_forward",
    )(x, halo, w_struct, *in_hbm(edge))

    hids = gather_blocks(hidden, "snap")
    every = snaps * local
    *terms, dt_own, cot_own = pl.pallas_call(
        functools.partial(temporal_kernel, snaps, heads, pieces),
        out_shape=(shape(share // pieces, 3 * width),) * pieces
        + (shape(local, 3 * width), shape(local, width)),
        in_specs=[SMEM] + [VMEM] * (2 + 2 * snaps),
        out_specs=(VMEM,) * (pieces + 2),
        scratch_shapes=[
            pltpu.VMEM((every, width), BF16),
            pltpu.VMEM((every, width), F32 if ents % 16 else BF16),
            pltpu.VMEM((every, 3 * width), BF16),
            pltpu.VMEM((every, 3 * width), BF16),
            pltpu.VMEM((local, LANES), F32),
            pltpu.VMEM((2 * every, width), BF16),
            pltpu.VMEM((every, LANES), F32),
            pltpu.VMEM((every, LANES), F32),
            pltpu.VMEM((every, LANES), BF16),
            pltpu.VMEM((every, LANES), BF16),
            pltpu.VMEM((every, width), F32),
            pltpu.VMEM((every, width), F32),
            pltpu.VMEM((every, width), F32),
            pltpu.VMEM((every, width), F32),
            pltpu.VMEM((share, 3 * width), BF16),
        ],
        compiler_params=params(24 if snaps <= 4 else 56),
        name="temporal",
    )(place, pos_embed, w_temp, *hids, *cots)

    if paired:
        got = [terms[0]] + [flipped(terms[k], "dom", 2 * k) for k in range(1, pieces)]
    else:
        got = exchange(terms[0].reshape(doms, share // doms, 3 * width), "dom")
    back, partial = pl.pallas_call(
        functools.partial(backward_kernel, heads),
        out_shape=(shape(halo_rows, width, dtype=F32), shape(local, width, dtype=F32)),
        in_specs=[VMEM] * 2 + [HBM] * 5,
        out_specs=(VMEM, VMEM),
        scratch_shapes=[
            pltpu.VMEM((local, width), BF16),
            pltpu.VMEM((halo_rows, width), BF16),
            pltpu.VMEM((heads, local, keys), F32),
            pltpu.VMEM(w_struct.shape, BF16),
            pltpu.VMEM(w_temp.shape, BF16),
            pltpu.VMEM((local, 3 * width), BF16),
            pltpu.VMEM((keys, 2 * width), BF16),
            pltpu.VMEM((local, width), BF16),
            pltpu.VMEM((keys, 2 * width), BF16),
            pltpu.SemaphoreType.DMA((5,)),
        ],
        compiler_params=params(24),
        cost_estimate=pl.CostEstimate(flops=2 * 10**9, bytes_accessed=8 * 10**6, transcendentals=0),
        name="struct_backward",
    )(dt_own, cot_own, *in_hbm(x, halo, edge, w_struct, w_temp))

    if not paired:
        total = jnp.sum(got.astype(F32), axis=0).astype(BF16)
        full = exchange(jnp.broadcast_to(total[None], (doms,) + total.shape), "dom")
        grad_wtemp = full.astype(F32).reshape(share, 3 * width)
        came = exchange(back.astype(BF16).reshape(doms, halo_per, width), "dom")
        picks = (route.reshape(-1)[:, None] == jnp.arange(local, dtype=jnp.int32)).astype(BF16)
        sums = dot_tn(picks, came.reshape(halo_rows, width))
        return ((partial + sums).astype(BF16)[None], grad_wtemp)

    mine = pl.pallas_call(
        functools.partial(outer_sum_kernel, halo_per),
        out_shape=shape(piece, 4 * width),
        in_specs=[SMEM] + [VMEM] * (1 + pieces),
        out_specs=VMEM,
        compiler_params=params(8),
        name="outer_sum",
    )(place, back, *got)
    other = flipped(mine, "dom", 1)
    sums = pl.pallas_call(
        functools.partial(inner_sum_kernel, halo_per),
        out_shape=(shape(piece, 3 * width + lanes),) * pieces,
        in_specs=[SMEM] + [VMEM] * 3,
        out_specs=(VMEM,) * pieces,
        compiler_params=params(8),
        name="inner_sum",
    )(place, back, mine, other)
    sums = [sums[0]] + [flipped(sums[k], "dom", 2 * k) for k in range(1, pieces)]
    grad_feat, grad_wtemp = pl.pallas_call(
        functools.partial(last_kernel, halo_per),
        out_shape=(hbm(local, width), hbm(share, 3 * width, dtype=F32)),
        in_specs=[SMEM, SMEM] + [VMEM] * (1 + pieces),
        out_specs=(HBM, HBM),
        scratch_shapes=[
            pltpu.VMEM((local, width), BF16),
            pltpu.VMEM((pieces, piece, 3 * width), F32),
            pltpu.VMEM((halo_rows, width), F32),
            pltpu.SemaphoreType.DMA((pieces + 1,)),
        ],
        compiler_params=params(8),
        name="last_sums",
    )(place, route, partial, *sums)
    return (grad_feat[None], grad_wtemp)


def solution(mesh):
    return jax.shard_map(
        per_device,
        mesh=mesh,
        in_specs=(
            P("snap", "dom", None),
            P(),
            P(),
            P(),
            P(),
            P("snap", "dom", None),
            P("snap", "dom", None),
            P("snap", "dom", None, None),
            P(None, ("dom", "snap")),
            P(None, ("dom", "snap"), None),
        ),
        out_specs=(P("snap", "dom", None), P("snap", None)),
        check_vma=False,
    )
```

time: 69.8 us -> 62.4 us (0.89)
  blocking collectives: 16.8 us -> 0 us
  waiting for transfers between devices: 8.34 us -> 16.4 us
  starting transfers between devices: 16.8 us -> 21.3 us
  Pallas kernels: 26.6 us -> 23.6 us
    all_to_all x1 -> x0, blocking collectives: 16.8 us -> none  [exchange(): return lax.all_to_all(tiles, axis, split_axis=0, concat_axis=0, tiled=True)]
    ppermute x0 -> x7, waiting for transfers between devices: none -> 10.6 us  [flipped(): return lax.ppermute(block, axis, [(i, i ^ flip) for i in range(count)])]
    ppermute x0 -> x7, starting transfers between devices: none -> 10.3 us  [flipped(): return lax.ppermute(block, axis, [(i, i ^ flip) for i in range(count)])]
    all_to_all x2 -> x1, starting transfers between devices: 13.2 us -> 7.27 us  [exchange(): return lax.all_to_all(tiles, axis, split_axis=0, concat_axis=0, tiled=True)]
    pallas_call x5 -> x6, Pallas kernels: 21.9 us -> 18.4 us  [the longest x1 6.78 us: per_device(): pl.pallas_call(functools.partial(backward_kernel, heads), out_shape=(shap...]
    all_to_all x2 -> x1, waiting for transfers between devices: 4.07 us -> 1.61 us  [exchange(): return lax.all_to_all(tiles, axis, split_axis=0, concat_axis=0, tiled=True)]
  transfers between devices with their start and end apart: 8 -> 14, of which waited for: 4 -> 6; matrix products, arithmetic and copies ran while one was open for 0% -> 0% of each run, Pallas kernels for 23% -> 22%
where the time goes in v4:
time: 62.4 us; the launch traced here: 62.1 us
  Pallas kernels  23.6 us (38%)
  starting transfers between devices  21.3 us (34%)
  waiting for transfers between devices  16.4 us (26%)
  between operations  0.76 us (1%)
    ppermute x7, waiting for transfers between devices, flipped(): return lax.ppermute(block, axis, [(i, i ^ flip) for i in range(count)])  10.6 us
    ppermute x7, starting transfers between devices, flipped(): return lax.ppermute(block, axis, [(i, i ^ flip) for i in range(count)])  10.3 us
    all_to_all x1, starting transfers between devices, exchange(): return lax.all_to_all(tiles, axis, split_axis=0, concat_axis=0, tiled=True)  7.27 us
    pallas_call x1, Pallas kernels, per_device(): pl.pallas_call(functools.partial(backward_kernel, heads), out_shape=(shap...  6.78 us
    pallas_call x1, Pallas kernels, per_device(): pl.pallas_call(functools.partial(temporal_kernel, snaps, heads, pieces),...  5.11 us
    ppermute x6, waiting for transfers between devices, gather_blocks(): held[m ^ bit] = lax.ppermute(held[m], axis, pairs)  4.2 us
    ppermute x6, starting transfers between devices, gather_blocks(): held[m ^ bit] = lax.ppermute(held[m], axis, pairs)  3.68 us
    pallas_call x1, Pallas kernels, per_device(): pl.pallas_call(own_kernel, out_shape=(hbm(heads, local, keys, dtype=F32),...  3.66 us
  transfers between devices with their start and end apart: 14, of which 6 were waited for; matrix products, arithmetic and copies ran while one was open for 0% of the time, Pallas kernels for 22%

profile of v4, /device:TPU:0, one launch (start us, length us, event | category | flops | bytes accessed | tf_op | source)
XLA Modules:
  0.0 62.1 jit_solution(523551704350928630)
XLA Ops:
  0.6 1.7 %halo_tiles.1 = bf16[64,512]{1,0:T(8,128)(2,1)} custom-call(s32[8,8]{1,0:T(8,128)} %bitcast.19, bf16[128,512]{1,0:T(8,128)(2,1)} %bitcast.14), custom_call_target="tpu_custom_call" | custom-call | tf_op jit(solution)/shard_map/halo_tiles/pallas_call | solution.py:499
  2.3 7.3 %all-to-all-start = ((bf16[8,8,512]{2,1,0:T(8,128)(2,1)}), bf16[8,8,512]{2,1,0:T(8,128)(2,1)S(1)}, u32[]{:S(2)}, u32[]{:S(2)}) async-start(bf16[8,8,512]{2,1,0:T(8,128)(2,1)} %bitcast.5), calls=%async_computation | async-start | bytes 131072 | tf_op jit(solution)/shard_map/all_to_all | solution.py:453
  9.6 0.0 copy-start.2
  9.6 3.7 %own_edges.1 = (f32[8,128,256]{2,1,0:T(8,128)}, bf16[5,32,512]{2,1,0:T(8,128)(2,1)}) custom-call(s32[8,128]{1,0:T(8,128)} %bitcast.22, s32[8,128]{1,0:T(8,128)} %bitcast.23, f32[4,8]{1,0:T(4,128)} %bias_hbm.1, s32[4,32]{1,0:T(4,128)} %act_hbm.1, bf16[4,32,512]{2,1,0:T(8,128)(2,1)} %cot_hbm.1), custom_call_target="tpu_custom_call" | custom-call | flops 1000000000 | bytes 4000000 | tf_op jit(solution)/shard_map/own_edges/pallas_call | solution.py:514
  13.3 0.0 copy-start
  13.3 0.0 copy-start.5
  13.3 1.6 %collective-permute-start.4 = (bf16[5,32,512]{2,1,0:T(8,128)(2,1)}, bf16[5,32,512]{2,1,0:T(8,128)(2,1)}, u32[]{:S(2)}, u32[]{:S(2)}) collective-permute-start(bf16[5,32,512]{2,1,0:T(8,128)(2,1)} %get-tuple-element.19.refs_4_), channel_id=1, source_target_pairs={{0,2},{1,3},{2,0},{3,1},{4,6},{5,7},{6,4},{7,5},{8,10},{9,11},{10,... | collective-permute-start | bytes 491528 | tf_op jit(solution)/shard_map/ppermute | solution.py:443
  14.9 1.6 %all-to-all-done = bf16[8,8,512]{2,1,0:T(8,128)(2,1)S(1)} async-done(((bf16[8,8,512]{2,1,0:T(8,128)(2,1)}), bf16[8,8,512]{2,1,0:T(8,128)(2,1)S(1)}, u32[]{:S(2)}, u32[]{:S(2)}) %all-to-all-start) | async-done | bytes 65568 | tf_op jit(solution)/shard_map/all_to_all | solution.py:453
  16.5 3.5 %struct_forward.1.refs_0_ = bf16[128,512]{1,0:T(8,128)(2,1)S(1)} custom-call(bf16[128,512]{1,0:T(8,128)(2,1)S(1)} %bitcast.16, bf16[64,512]{1,0:T(8,128)(2,1)S(1)} %bitcast.17, bf16[512,1536]{1,0:T(8,128)(2,1)S(1)} %copy-done.1, f32[8,128,256]{2,1,0:T(8,128)} %get-tuple-element.18.edge_hbm), custom_call_target="tpu_custom_call" | custom-call | tf_op jit(solution)/shard_map/struct_forward/pallas_call | solution.py:534
  20.0 1.6 %collective-permute-start.1 = (bf16[128,512]{1,0:T(8,128)(2,1)S(1)}, bf16[128,512]{1,0:T(8,128)(2,1)S(1)}, u32[]{:S(2)}, u32[]{:S(2)}) collective-permute-start(bf16[128,512]{1,0:T(8,128)(2,1)S(1)} %struct_forward.1.refs_0_), channel_id=1, source_target_pairs={{0,2},{1,3},{2,0},{3,1},{4,6},{5,7},{6,4},{7,5},{8,10},{9,11},{10,... | collective-permute-start | bytes 393224 | tf_op jit(solution)/shard_map/ppermute | solution.py:443
  21.6 0.0 collective-permute-start.3
  21.6 0.0 collective-permute-done.4.refs_6_
  21.6 0.5 collective-permute-start.5
  22.1 0.0 collective-permute-start
  22.1 2.9 %collective-permute-done.1.refs_2_ = bf16[128,512]{1,0:T(8,128)(2,1)S(1)} collective-permute-done((bf16[128,512]{1,0:T(8,128)(2,1)S(1)}, bf16[128,512]{1,0:T(8,128)(2,1)S(1)}, u32[]{:S(2)}, u32[]{:S(2)}) %collective-permute-start.1) | collective-permute-done | bytes 131104 | tf_op jit(solution)/shard_map/ppermute | solution.py:443
  25.0 0.1 pad_add_fusion.place_ref
  25.1 1.3 %collective-permute-done.2.refs_3_ = bf16[128,512]{1,0:T(8,128)(2,1)S(1)} collective-permute-done((bf16[128,512]{1,0:T(8,128)(2,1)S(1)}, bf16[128,512]{1,0:T(8,128)(2,1)S(1)}, u32[]{:S(2)}, u32[]{:S(2)}) %collective-permute-start.2) | collective-permute-done | bytes 131104 | tf_op jit(solution)/shard_map/ppermute | solution.py:443
  26.4 5.1 %temporal.1 = (bf16[32,1536]{1,0:T(8,128)(2,1)S(1)}, bf16[32,1536]{1,0:T(8,128)(2,1)S(1)}, bf16[32,1536]{1,0:T(8,128)(2,1)S(1)}, bf16[32,1536]{1,0:T(8,128)(2,1)...) custom-call(s32[3]{0:T(128)S(1)} %pad_add_fusion.place_ref, bf16[4,512]{1,0:T(4,128)(2,1)S(1)} %copy-done.5, ...), custom_call_target="tpu_custom_call" | custom-call | tf_op jit(solution)/shard_map/temporal/pallas_call | solution.py:551
  31.5 0.5 collective-permute-start.6
  32.0 2.4 %collective-permute-start.7 = (bf16[32,1536]{1,0:T(8,128)(2,1)S(1)}, bf16[32,1536]{1,0:T(8,128)(2,1)S(1)}, u32[]{:S(2)}, u32[]{:S(2)}) collective-permute-start(bf16[32,1536]{1,0:T(8,128)(2,1)S(1)} %get-tuple-element.26), channel_id=1, source_target_pairs={{0,16},{4,20},{8,24},{12,28},{16,0},{20,4},{24,8},{28,12},{1,17},{... | collective-permute-start | bytes 294920 | tf_op jit(solution)/shard_map/ppermute | solution.py:458
  34.4 1.6 %collective-permute-start.8 = (bf16[32,1536]{1,0:T(8,128)(2,1)S(1)}, bf16[32,1536]{1,0:T(8,128)(2,1)S(1)}, u32[]{:S(2)}, u32[]{:S(2)}) collective-permute-start(bf16[32,1536]{1,0:T(8,128)(2,1)S(1)} %get-tuple-element.27), channel_id=1, source_target_pairs={{0,24},{4,28},{8,16},{12,20},{16,8},{20,12},{24,0},{28,4},{1,25},{... | collective-permute-start | bytes 294920 | tf_op jit(solution)/shard_map/ppermute | solution.py:458
  36.0 6.8 %struct_backward.1 = (f32[64,512]{1,0:T(8,128)S(1)}, f32[128,512]{1,0:T(8,128)S(1)}) custom-call(bf16[128,1536]{1,0:T(8,128)(2,1)S(1)} %get-tuple-element.20.dt, bf16[128,512]{1,0:T(8,128)(2,1)S(1)} %get-tuple-element.21.cot, bf16[128,512]{1,0:T(8,128)(2,1)} %bitcast.15, bf16[64,512]{1,0:T(8,128)(2,1)} %bitcast.18, ...), custom_call_target="tpu_custom_call" | custom-call | flops 2000000000 | bytes 8000000 | tf_op jit(solution)/shard_map/struct_backward/pallas_call | solution.py:582
  42.8 0.6 outer_sum.1.mine_ref
  43.4 1.4 %collective-permute-start.9 = (bf16[32,2048]{1,0:T(8,128)(2,1)S(1)}, bf16[32,2048]{1,0:T(8,128)(2,1)S(1)}, u32[]{:S(2)}, u32[]{:S(2)}) collective-permute-start(bf16[32,2048]{1,0:T(8,128)(2,1)S(1)} %outer_sum.1.mine_ref), channel_id=1, source_target_pairs={{0,4},{4,0},{8,12},{12,8},{16,20},{20,16},{24,28},{28,24},{1,5},{5... | collective-permute-start | bytes 393224 | tf_op jit(solution)/shard_map/ppermute | solution.py:458
  44.8 3.6 %collective-permute-done.9.other_ref = bf16[32,2048]{1,0:T(8,128)(2,1)S(1)} collective-permute-done((bf16[32,2048]{1,0:T(8,128)(2,1)S(1)}, bf16[32,2048]{1,0:T(8,128)(2,1)S(1)}, u32[]{:S(2)}, u32[]{:S(2)}) %collective-permute-start.9) | collective-permute-done | bytes 131104 | tf_op jit(solution)/shard_map/ppermute | solution.py:458
  48.4 0.6 inner_sum.1
  49.0 1.7 %collective-permute-start.10 = (bf16[32,1792]{1,0:T(8,128)(2,1)S(1)}, bf16[32,1792]{1,0:T(8,128)(2,1)S(1)}, u32[]{:S(2)}, u32[]{:S(2)}) collective-permute-start(bf16[32,1792]{1,0:T(8,128)(2,1)S(1)} %get-tuple-element.29), channel_id=1, source_target_pairs={{0,8},{4,12},{8,0},{12,4},{16,24},{20,28},{24,16},{28,20},{1,9},{5... | collective-permute-start | bytes 344072 | tf_op jit(solution)/shard_map/ppermute | solution.py:458
  50.7 1.2 %collective-permute-start.11 = (bf16[32,1792]{1,0:T(8,128)(2,1)S(1)}, bf16[32,1792]{1,0:T(8,128)(2,1)S(1)}, u32[]{:S(2)}, u32[]{:S(2)}) collective-permute-start(bf16[32,1792]{1,0:T(8,128)(2,1)S(1)} %get-tuple-element.30), channel_id=1, source_target_pairs={{0,16},{4,20},{8,24},{12,28},{16,0},{20,4},{24,8},{28,12},{1,17},{... | collective-permute-start | bytes 344072 | tf_op jit(solution)/shard_map/ppermute | solution.py:458
  51.9 1.5 %collective-permute-start.12 = (bf16[32,1792]{1,0:T(8,128)(2,1)S(1)}, bf16[32,1792]{1,0:T(8,128)(2,1)S(1)}, u32[]{:S(2)}, u32[]{:S(2)}) collective-permute-start(bf16[32,1792]{1,0:T(8,128)(2,1)S(1)} %get-tuple-element.31), channel_id=1, source_target_pairs={{0,24},{4,28},{8,16},{12,20},{16,8},{20,12},{24,0},{28,4},{1,25},{... | collective-permute-start | bytes 344072 | tf_op jit(solution)/shard_map/ppermute | solution.py:458
  53.5 0.6 collective-permute-done.10.refs_1_
  54.0 6.4 %collective-permute-done.11.refs_2_ = bf16[32,1792]{1,0:T(8,128)(2,1)S(1)} collective-permute-done((bf16[32,1792]{1,0:T(8,128)(2,1)S(1)}, bf16[32,1792]{1,0:T(8,128)(2,1)S(1)}, u32[]{:S(2)}, u32[]{:S(2)}) %collective-permute-start.11) | collective-permute-done | bytes 114720 | tf_op jit(solution)/shard_map/ppermute | solution.py:458
  60.4 1.7 %last_sums.1 = (bf16[128,512]{1,0:T(8,128)(2,1)}, f32[128,1536]{1,0:T(8,128)}) custom-call(s32[3]{0:T(128)S(1)} %pad_add_fusion.place_ref, s32[8,8]{1,0:T(8,128)S(1)} %bitcast.20, f32[128,512]{1,0:T(8,128)S(1)} %get-tuple-element.22.part_ref, bf16[32,1792]{1,0:T(8,128)(2,1)S(1)} %get-tuple-element.28.refs_0_, ...), custom_call_target="tpu_custom_call" | custom-call | tf_op jit(solution)/shard_map/last_sums/pallas_call | solution.py:631
  (17 shorter events, 0.0 us)
Async XLA Ops:
  2.3 14.2 %all-to-all-start = ((bf16[8,8,512]{2,1,0:T(8,128)(2,1)}), bf16[8,8,512]{2,1,0:T(8,128)(2,1)S(1)}, u32[]{:S(2)}, u32[]{:S(2)}) async-start(bf16[8,8,512]{2,1,0:T(8,128)(2,1)} %bitcast.5), calls=%async_computation | async-start | bytes 131072 | tf_op jit(solution)/shard_map/all_to_all | solution.py:453
  9.6 6.9 %copy-start.1 = (bf16[512,1536]{1,0:T(8,128)(2,1)S(1)}, bf16[512,1536]{1,0:T(8,128)(2,1)}, u32[]{:S(2)}) copy-start(bf16[512,1536]{1,0:T(8,128)(2,1)} %ws_hbm.1) | copy-start | bytes 4718596
  9.6 6.9 %copy-start.2 = (bf16[1,128,512]{2,1,0:T(8,128)(2,1)S(1)}, bf16[1,128,512]{2,1,0:T(8,128)(2,1)}, u32[]{:S(2)}) copy-start(bf16[1,128,512]{2,1,0:T(8,128)(2,1)} %param.10) | copy-start | bytes 393220
  13.3 13.1 %copy-start = (bf16[512,1536]{1,0:T(8,128)(2,1)S(1)}, bf16[512,1536]{1,0:T(8,128)(2,1)}, u32[]{:S(2)}) copy-start(bf16[512,1536]{1,0:T(8,128)(2,1)} %wt_hbm.1) | copy-start | bytes 4718596
  13.3 13.1 %copy-start.5 = (bf16[4,512]{1,0:T(4,128)(2,1)S(1)}, bf16[4,512]{1,0:T(4,128)(2,1)}, u32[]{:S(2)}) copy-start(bf16[4,512]{1,0:T(4,128)(2,1)} %pos_ref.1) | copy-start | bytes 12292
  13.3 8.3 %collective-permute-start.4 = (bf16[5,32,512]{2,1,0:T(8,128)(2,1)}, bf16[5,32,512]{2,1,0:T(8,128)(2,1)}, u32[]{:S(2)}, u32[]{:S(2)}) collective-permute-start(bf16[5,32,512]{2,1,0:T(8,128)(2,1)} %get-tuple-element.19.refs_4_), channel_id=1, source_target_pairs={{0,2},{1,3},{2,0},{3,1},{4,6},{5,7},{6,4},{7,5},{8,10},{9,11},{10,... | collective-permute-start | bytes 491528 | tf_op jit(solution)/shard_map/ppermute | solution.py:443
  16.5 15.0 %copy-start.3 = (bf16[8,8,512]{2,1,0:T(8,128)(2,1)}, bf16[8,8,512]{2,1,0:T(8,128)(2,1)S(1)}, u32[]{:S(2)}) copy-start(bf16[8,8,512]{2,1,0:T(8,128)(2,1)S(1)} %all-to-all-done) | copy-start | bytes 196612
  20.0 5.0 %collective-permute-start.1 = (bf16[128,512]{1,0:T(8,128)(2,1)S(1)}, bf16[128,512]{1,0:T(8,128)(2,1)S(1)}, u32[]{:S(2)}, u32[]{:S(2)}) collective-permute-start(bf16[128,512]{1,0:T(8,128)(2,1)S(1)} %struct_forward.1.refs_0_), channel_id=1, source_target_pairs={{0,2},{1,3},{2,0},{3,1},{4,6},{5,7},{6,4},{7,5},{8,10},{9,11},{10,... | collective-permute-start | bytes 393224 | tf_op jit(solution)/shard_map/ppermute | solution.py:443
  21.6 3.5 %collective-permute-start.3 = (bf16[5,32,512]{2,1,0:T(8,128)(2,1)}, bf16[5,32,512]{2,1,0:T(8,128)(2,1)S(1)}, u32[]{:S(2)}, u32[]{:S(2)}) collective-permute-start(bf16[5,32,512]{2,1,0:T(8,128)(2,1)} %get-tuple-element.19.refs_4_), channel_id=1, source_target_pairs={{0,1},{1,0},{2,3},{3,2},{4,5},{5,4},{6,7},{7,6},{8,9},{9,8},{10,11... | collective-permute-start | bytes 491528 | tf_op jit(solution)/shard_map/ppermute | solution.py:443
  21.6 3.5 %collective-permute-start.5 = (bf16[5,32,512]{2,1,0:T(8,128)(2,1)}, bf16[5,32,512]{2,1,0:T(8,128)(2,1)S(1)}, u32[]{:S(2)}, u32[]{:S(2)}) collective-permute-start(bf16[5,32,512]{2,1,0:T(8,128)(2,1)} %collective-permute-done.4.refs_6_), channel_id=1, source_target_pairs={{0,1},{1,0},{2,3},{3,2},{4,5},{5,4},{6,7},{7,6},{8,9},{9,8},{10,11... | collective-permute-start | bytes 491528 | tf_op jit(solution)/shard_map/ppermute | solution.py:443
  22.1 3.0 %collective-permute-start = (bf16[128,512]{1,0:T(8,128)(2,1)S(1)}, bf16[128,512]{1,0:T(8,128)(2,1)S(1)}, u32[]{:S(2)}, u32[]{:S(2)}) collective-permute-start(bf16[128,512]{1,0:T(8,128)(2,1)S(1)} %struct_forward.1.refs_0_), channel_id=1, source_target_pairs={{0,1},{1,0},{2,3},{3,2},{4,5},{5,4},{6,7},{7,6},{8,9},{9,8},{10,11... | collective-permute-start | bytes 393224 | tf_op jit(solution)/shard_map/ppermute | solution.py:443
  25.0 1.3 %collective-permute-start.2 = (bf16[128,512]{1,0:T(8,128)(2,1)S(1)}, bf16[128,512]{1,0:T(8,128)(2,1)S(1)}, u32[]{:S(2)}, u32[]{:S(2)}) collective-permute-start(bf16[128,512]{1,0:T(8,128)(2,1)S(1)} %collective-permute-done.1.refs_2_), channel_id=1, source_target_pairs={{0,1},{1,0},{2,3},{3,2},{4,5},{5,4},{6,7},{7,6},{8,9},{9,8},{10,11... | collective-permute-start | bytes 393224 | tf_op jit(solution)/shard_map/ppermute | solution.py:443
  31.5 11.3 %collective-permute-start.6 = (bf16[32,1536]{1,0:T(8,128)(2,1)S(1)}, bf16[32,1536]{1,0:T(8,128)(2,1)S(1)}, u32[]{:S(2)}, u32[]{:S(2)}) collective-permute-start(bf16[32,1536]{1,0:T(8,128)(2,1)S(1)} %get-tuple-element.25), channel_id=1, source_target_pairs={{0,8},{4,12},{8,0},{12,4},{16,24},{20,28},{24,16},{28,20},{1,9},{5... | collective-permute-start | bytes 294920 | tf_op jit(solution)/shard_map/ppermute | solution.py:458
  32.0 10.8 %collective-permute-start.7 = (bf16[32,1536]{1,0:T(8,128)(2,1)S(1)}, bf16[32,1536]{1,0:T(8,128)(2,1)S(1)}, u32[]{:S(2)}, u32[]{:S(2)}) collective-permute-start(bf16[32,1536]{1,0:T(8,128)(2,1)S(1)} %get-tuple-element.26), channel_id=1, source_target_pairs={{0,16},{4,20},{8,24},{12,28},{16,0},{20,4},{24,8},{28,12},{1,17},{... | collective-permute-start | bytes 294920 | tf_op jit(solution)/shard_map/ppermute | solution.py:458
  34.4 8.4 %collective-permute-start.8 = (bf16[32,1536]{1,0:T(8,128)(2,1)S(1)}, bf16[32,1536]{1,0:T(8,128)(2,1)S(1)}, u32[]{:S(2)}, u32[]{:S(2)}) collective-permute-start(bf16[32,1536]{1,0:T(8,128)(2,1)S(1)} %get-tuple-element.27), channel_id=1, source_target_pairs={{0,24},{4,28},{8,16},{12,20},{16,8},{20,12},{24,0},{28,4},{1,25},{... | collective-permute-start | bytes 294920 | tf_op jit(solution)/shard_map/ppermute | solution.py:458
  36.0 24.4 %copy-start.4 = (s32[1,1,8,8]{3,2,1,0:T(8,128)S(1)}, s32[1,1,8,8]{3,2,1,0:T(8,128)}, u32[]{:S(2)}) copy-start(s32[1,1,8,8]{3,2,1,0:T(8,128)} %param.17) | copy-start | bytes 772
  43.4 5.0 %collective-permute-start.9 = (bf16[32,2048]{1,0:T(8,128)(2,1)S(1)}, bf16[32,2048]{1,0:T(8,128)(2,1)S(1)}, u32[]{:S(2)}, u32[]{:S(2)}) collective-permute-start(bf16[32,2048]{1,0:T(8,128)(2,1)S(1)} %outer_sum.1.mine_ref), channel_id=1, source_target_pairs={{0,4},{4,0},{8,12},{12,8},{16,20},{20,16},{24,28},{28,24},{1,5},{5... | collective-permute-start | bytes 393224 | tf_op jit(solution)/shard_map/ppermute | solution.py:458
  49.0 5.0 %collective-permute-start.10 = (bf16[32,1792]{1,0:T(8,128)(2,1)S(1)}, bf16[32,1792]{1,0:T(8,128)(2,1)S(1)}, u32[]{:S(2)}, u32[]{:S(2)}) collective-permute-start(bf16[32,1792]{1,0:T(8,128)(2,1)S(1)} %get-tuple-element.29), channel_id=1, source_target_pairs={{0,8},{4,12},{8,0},{12,4},{16,24},{20,28},{24,16},{28,20},{1,9},{5... | collective-permute-start | bytes 344072 | tf_op jit(solution)/shard_map/ppermute | solution.py:458
  50.7 9.7 %collective-permute-start.11 = (bf16[32,1792]{1,0:T(8,128)(2,1)S(1)}, bf16[32,1792]{1,0:T(8,128)(2,1)S(1)}, u32[]{:S(2)}, u32[]{:S(2)}) collective-permute-start(bf16[32,1792]{1,0:T(8,128)(2,1)S(1)} %get-tuple-element.30), channel_id=1, source_target_pairs={{0,16},{4,20},{8,24},{12,28},{16,0},{20,4},{24,8},{28,12},{1,17},{... | collective-permute-start | bytes 344072 | tf_op jit(solution)/shard_map/ppermute | solution.py:458
  51.9 8.5 %collective-permute-start.12 = (bf16[32,1792]{1,0:T(8,128)(2,1)S(1)}, bf16[32,1792]{1,0:T(8,128)(2,1)S(1)}, u32[]{:S(2)}, u32[]{:S(2)}) collective-permute-start(bf16[32,1792]{1,0:T(8,128)(2,1)S(1)} %get-tuple-element.31), channel_id=1, source_target_pairs={{0,24},{4,28},{8,16},{12,20},{16,8},{20,12},{24,0},{28,4},{1,25},{... | collective-permute-start | bytes 344072 | tf_op jit(solution)/shard_map/ppermute | solution.py:458

commit v5 on v4

--- a/solution.py
+++ b/solution.py
@@ -81,49 +81,22 @@
     out_ref[...] = dot_nn(pick_rows(route, x.shape[0]), x[...]).astype(BF16)
 
 
-def own_kernel(
-    nbr_hbm, rel_hbm, bias_hbm, act_hbm, cot_hbm, edge_hbm, load_ref,
-    nbr, rel, bias, act, cot, edge, sems,
-):
-    heads, rows, keys = edge.shape
-    kinds = bias.shape[0]
-    slots = nbr.shape[0]
+def load_kernel(_, act_hbm, cot_hbm, load_hbm, act, cot, flags_s, sems):
     snaps, ents, width = cot.shape
-    fetch = Fetch(
-        sems, (nbr_hbm, nbr), (rel_hbm, rel), (bias_hbm, bias), (act_hbm, act), (cot_hbm, cot)
-    )
+    fetch = Fetch(sems, (cot_hbm, cot), (act_hbm, act))
     row = lax.broadcasted_iota(jnp.int32, (ents, ents), 0)
     col = lax.broadcasted_iota(jnp.int32, (ents, ents), 1)
     lane = lax.broadcasted_iota(jnp.int32, (ents, width), 1)
     flags = jnp.zeros((ents, width), F32)
-    fetch.wait(0, 1, 2, 3)
+    fetch.wait(1)
     on = act[...].astype(F32)
     for t in range(snaps):
         column = jnp.sum(jnp.where(row == col, on[t : t + 1, :], 0.0), axis=1, keepdims=True)
         flags = jnp.where(lane == t, column, flags)
-    load_ref[snaps] = flags.astype(BF16)
-    code = jnp.transpose((nbr[...] * kinds + rel[...]).astype(F32))
-    spot = (lax.broadcasted_iota(jnp.int32, (rows, keys), 1) * kinds).astype(F32)
-    counts = []
-    for r in range(kinds):
-        here = spot + float(r)
-        total = jnp.zeros((rows, keys), F32)
-        for k in range(slots):
-            total = total + jnp.where(code[:, k : k + 1] == here, 1.0, 0.0)
-        counts.append(total)
-    gain = jnp.exp(bias[...])
-    stores = []
-    for h in range(heads):
-        total = counts[0] * gain[0:1, h : h + 1]
-        for r in range(1, kinds):
-            total = total + counts[r] * gain[r : r + 1, h : h + 1]
-        edge[h] = jnp.where(total > 0, jnp.log(total), NEG)
-        stores.append(Fetch(sems.at[5 + h :], (edge.at[h], edge_hbm.at[h])))
-    fetch.wait(4)
-    for t in range(snaps):
-        load_ref[t] = cot[t]
-    for store in stores:
-        store.wait(0)
+    flags_s[...] = flags.astype(BF16)
+    fetch.wait(0)
+    store = Fetch(sems.at[2:], (flags_s, load_hbm.at[snaps]), (cot, load_hbm.at[:snaps]))
+    store.wait(0, 1)
 
 
 def fill_table(tab_s, proj, halo, w_kv):
@@ -137,7 +110,25 @@
         tab_s[used:, :] = jnp.zeros((tab_s.shape[0] - used, 2 * width), BF16)
 
 
-def edge_attention(p, heads, proj, edge, tab_s, width):
+def edge_counts(nbr, rel, kinds, keys):
+    bits = 4
+    slots, rows = nbr.shape
+    target = jnp.transpose(nbr[...].astype(F32))
+    one = jnp.transpose(lax.shift_left(jnp.ones_like(rel[...]), bits * rel[...]).astype(F32))
+    spot = lax.broadcasted_iota(jnp.int32, (rows, keys), 1).astype(F32)
+    packed = jnp.zeros((rows, keys), F32)
+    for k in range(slots):
+        packed = packed + jnp.where(target[:, k : k + 1] == spot, one[:, k : k + 1], 0.0)
+    packed = packed.astype(jnp.int32)
+    low = (1 << bits) - 1
+    counts = [
+        lax.bitwise_and(lax.shift_right_logical(packed, bits * r), low).astype(F32)
+        for r in range(kinds)
+    ]
+    return counts, jnp.where(packed > 0, 0.0, NEG)
+
+
+def edge_attention(p, heads, proj, counts, closed, gain, tab_s, width):
     keys = tab_s.shape[0]
     head_dim = width // heads
     group = LANES // head_dim
@@ -146,26 +137,29 @@
     score = dot_nt(proj[:, cols], kk)
     parts = []
     for g in range(group):
-        s = score[:, g * keys : (g + 1) * keys] * head_dim ** (-0.5) + edge[p * group + g]
-        e = jnp.exp(s - jnp.max(s, axis=1, keepdims=True))
+        h = p * group + g
+        weight = counts[0] * gain[0:1, h : h + 1]
+        for r in range(1, len(counts)):
+            weight = weight + counts[r] * gain[r : r + 1, h : h + 1]
+        s = score[:, g * keys : (g + 1) * keys] * head_dim ** (-0.5) + closed
+        e = jnp.exp(s - jnp.max(s, axis=1, keepdims=True)) * weight
         parts.append(e * (1.0 / jnp.sum(e, axis=1, keepdims=True)))
     return kk, parts
 
 
-def forward_kernel(heads, x, halo, w, edge_hbm, hidden_ref, edge, proj, tab_s, sems):
+def forward_kernel(heads, x, halo, w, nbr, rel, bias, hidden_ref, proj, tab_s):
     width = x.shape[1]
     head_dim = width // heads
-    group = LANES // head_dim
-    fetch = Fetch(sems, *[(edge_hbm.at[h], edge.at[h]) for h in range(heads)])
     for part in range(3):
         cols = slice(part * width, (part + 1) * width)
         proj[:, cols] = dot_nn(x[...], w[:, cols]).astype(BF16)
     fill_table(tab_s, proj, halo, w.at[:, width:])
+    counts, closed = edge_counts(nbr, rel, bias.shape[0], tab_s.shape[0])
+    gain = jnp.exp(bias[...])
     for p in range(width // LANES):
         cols = slice(p * LANES, (p + 1) * LANES)
         vcols = slice(width + p * LANES, width + (p + 1) * LANES)
-        fetch.wait(*range(p * group, (p + 1) * group))
-        _, attn = edge_attention(p, heads, proj, edge, tab_s, width)
+        _, attn = edge_attention(p, heads, proj, counts, closed, gain, tab_s, width)
         vv = stack_heads(tab_s[:, vcols], head_dim)
         agg = dot_nn(jnp.concatenate([a.astype(BF16) for a in attn], axis=1), vv)
         elu = jnp.where(agg > 0, agg, jnp.exp(jnp.minimum(agg, 0.0)) - 1.0)
@@ -180,16 +174,26 @@
         lax.fori_loop(lo, hi, lambda i, c: (body(i), c)[1], 0)
 
 
-def temporal_kernel(snaps, heads, pieces, place_ref, pos_ref, w_s, *refs):
+def cotangent_kernel(place_ref, *refs):
+    *cot, ct_ref, act_ref = refs
+    snaps = len(cot)
+    ents = cot[0].shape[1]
+    local = snaps * ents
+    for m in range(snaps):
+        at = pl.multiple_of(lax.bitwise_xor(place_ref[0], m) * ents, ents)
+        for t in range(snaps):
+            ct_ref[pl.ds(t * local + at, ents), :] = cot[m][t].astype(ct_ref.dtype)
+        act_ref[pl.ds(at, ents), :] = cot[m][snaps][:, :LANES].astype(F32)
+
+
+def temporal_kernel(snaps, heads, pieces, place_ref, pos_ref, w_s, ct_s, act_s, *refs):
     hid = refs[:snaps]
-    cot = refs[snaps : 2 * snaps]
-    terms_ref = refs[2 * snaps : 2 * snaps + pieces]
+    terms_ref = refs[snaps : snaps + pieces]
     (
         dt_own_ref, cot_own_ref,
-        z_s, ct_s, tp_s, dt_s, act_s, prod_s, s_s, d_s, a_s, ds_s, wa_s, wd_s, dk_s, dv_s, terms_s,
-    ) = refs[2 * snaps + pieces :]
+        z_s, tp_s, dt_s, prod_s, s_s, d_s, a_s, ds_s, wa_s, wd_s, dk_s, dv_s, terms_s,
+    ) = refs[snaps + pieces :]
     local, width = hid[0].shape
-    ents = cot[0].shape[1]
     head_dim = width // heads
     scale = head_dim ** (-0.5)
     unroll = snaps <= 4
@@ -207,11 +211,6 @@
     for part in range(3):
         cols = slice(part * width, (part + 1) * width)
         tp_s[:, cols] = dot_nn(z_s[...], w_s[:, cols]).astype(BF16)
-    for m in range(snaps):
-        at = pl.multiple_of(lax.bitwise_xor(me, m) * ents, ents)
-        for t in range(snaps):
-            ct_s[pl.ds(t * local + at, ents), :] = cot[m][t].astype(ct_s.dtype)
-        act_s[pl.ds(at, ents), :] = cot[m][snaps][:, :LANES].astype(F32)
     lane_head = lax.broadcasted_iota(jnp.int32, (width, LANES), 0) // head_dim
     fold = (lane_head == lax.broadcasted_iota(jnp.int32, (width, LANES), 1)).astype(F32)
     fold = fold.astype(BF16)
@@ -325,8 +324,8 @@
 
 
 def backward_kernel(
-    heads, dt, cot, x_hbm, halo_hbm, edge_hbm, ws_hbm, wt_hbm, back_ref, part_ref,
-    x, halo, edge, ws, wt, proj, tab_s, dq_s, dtab_s, sems,
+    heads, dt, cot, x, halo, nbr, rel, bias, ws, wt, back_ref, part_ref,
+    proj, tab_s, dq_s, dtab_s,
 ):
     rows, width = cot.shape
     halo_rows = halo.shape[0]
@@ -334,22 +333,18 @@
     head_dim = width // heads
     group = LANES // head_dim
     scale = head_dim ** (-0.5)
-    fetch = Fetch(
-        sems, (wt_hbm, wt), (x_hbm, x), (ws_hbm, ws), (halo_hbm, halo), (edge_hbm, edge)
-    )
-    fetch.wait(0)
     dh = cot[...].astype(F32) + dot_nt(dt[...], wt[...])
     part_ref[...] = dh.astype(BF16).astype(F32)
-    fetch.wait(1, 2, 3)
     for part in range(3):
         cols = slice(part * width, (part + 1) * width)
         proj[:, cols] = dot_nn(x[...], ws[:, cols]).astype(BF16)
     fill_table(tab_s, proj, halo, ws.at[:, width:])
-    fetch.wait(4)
+    counts, closed = edge_counts(nbr, rel, bias.shape[0], tab_s.shape[0])
+    gain = jnp.exp(bias[...])
     for p in range(width // LANES):
         cols = slice(p * LANES, (p + 1) * LANES)
         vcols = slice(width + p * LANES, width + (p + 1) * LANES)
-        kk, attn = edge_attention(p, heads, proj, edge, tab_s, width)
+        kk, attn = edge_attention(p, heads, proj, counts, closed, gain, tab_s, width)
         vv = stack_heads(tab_s[:, vcols], head_dim)
         attn_b = jnp.concatenate([a.astype(BF16) for a in attn], axis=1)
         agg = dot_nn(attn_b, vv)
@@ -401,48 +396,57 @@
         out[k][:, wide:] = jnp.concatenate(folds, axis=0).astype(BF16)
 
 
-def last_kernel(per, place_ref, route_ref, part_ref, *refs):
-    got = refs[:-6]
-    feat_hbm, wtemp_hbm, feat, wtemp, came_s, sems = refs[-6:]
-    pieces = len(got)
+def unpack_sums(flips, per, place_ref, got, wtemp, wtemp_hbm, came_s, sems):
     rows = got[0].shape[0]
-    wide = wtemp.shape[2]
-    lanes = got[0].shape[1] - wide
+    lanes = got[0].shape[1] - wtemp.shape[2]
+    folds = rows // (2 * per)
     stores = []
-    for k in range(pieces):
-        wtemp[k] = got[k][:, :wide].astype(F32)
+    came_s[...] = jnp.zeros_like(came_s)
+    for i, k in enumerate(flips):
+        wtemp[i] = got[i][:, : wtemp.shape[2]].astype(F32)
         at = pl.multiple_of(lax.bitwise_xor(place_ref[1], k) * rows, rows)
-        stores.append(Fetch(sems.at[k:], (wtemp.at[k], wtemp_hbm.at[pl.ds(at, rows), :])))
-        folded = got[k][:, wide:].astype(F32)
-        folds = rows // (2 * per)
+        stores.append(Fetch(sems.at[i:], (wtemp.at[i], wtemp_hbm.at[pl.ds(at, rows), :])))
+        folded = got[i][:, wtemp.shape[2] :].astype(F32)
         for j in range(2):
-            d = lax.bitwise_xor(place_ref[2], 2 * k + j) * per
-            for i in range(folds):
-                f = (j * folds + i) * per
-                came_s[pl.ds(pl.multiple_of(d, per), per), i * lanes : (i + 1) * lanes] = folded[
-                    f : f + per
-                ]
-    back = dot_tn(pick_rows(route_ref, part_ref.shape[0]), came_s[...].astype(BF16))
-    feat[...] = (part_ref[...] + back).astype(BF16)
-    stores.append(Fetch(sems.at[pieces:], (feat, feat_hbm)))
+            d = pl.multiple_of(lax.bitwise_xor(place_ref[2], 2 * k + j) * per, per)
+            for f in range(folds):
+                row = (j * folds + f) * per
+                came_s[pl.ds(d, per), f * lanes : (f + 1) * lanes] = folded[row : row + per]
+    return stores
+
+
+def early_kernel(flips, per, place_ref, route_ref, part_ref, *refs):
+    got = refs[: len(flips)]
+    sum_ref, picks_ref, wtemp_hbm, wtemp, came_s, sems = refs[len(flips) :]
+    stores = unpack_sums(flips, per, place_ref, got, wtemp, wtemp_hbm, came_s, sems)
+    picks = pick_rows(route_ref, part_ref.shape[0])
+    picks_ref[...] = picks
+    sum_ref[...] = part_ref[...] + dot_tn(picks, came_s[...].astype(BF16))
     for store in stores:
         store.wait(0)
 
 
+def last_kernel(flips, per, place_ref, picks_ref, sum_ref, _, *refs):
+    got = refs[: len(flips)]
+    feat_hbm, wtemp_hbm, feat, wtemp, came_s, sems = refs[len(flips) :]
+    stores = unpack_sums(flips, per, place_ref, got, wtemp, wtemp_hbm, came_s, sems)
+    feat[...] = (sum_ref[...] + dot_tn(picks_ref[...], came_s[...].astype(BF16))).astype(BF16)
+    stores.append(Fetch(sems.at[len(flips) :], (feat, feat_hbm)))
+    for store in stores:
+        store.wait(0)
+
+
 def params(mib):
     return pltpu.CompilerParams(vmem_limit_bytes=mib * 1024 * 1024)
 
 
-def gather_blocks(block, axis):
-    count = lax.axis_size(axis)
-    held = {0: block}
-    bit = count // 2
-    while bit:
+def gather_blocks(held, axis, bit, last):
+    held = dict(held)
+    while bit >= last:
         for m in sorted(held):
-            pairs = [(i, i ^ bit) for i in range(count)]
-            held[m ^ bit] = lax.ppermute(held[m], axis, pairs)
+            held[m ^ bit] = flipped(held[m], axis, bit)
         bit //= 2
-    return [held[m] for m in range(count)]
+    return held
 
 
 def in_hbm(*arrays):
@@ -464,7 +468,6 @@
     x = feat[0]
     local, width = x.shape
     heads = rel_bias.shape[1]
-    slots = nbr.shape[2]
     doms = lax.axis_size("dom")
     snaps = lax.axis_size("snap")
     ents = local // snaps
@@ -511,55 +514,62 @@
     )(*in_hbm(route, x))
     halo = exchange(tiles.reshape(doms, halo_per, width), "dom").reshape(halo_rows, width)
 
-    edge, load = pl.pallas_call(
-        own_kernel,
-        out_shape=(hbm(heads, local, keys, dtype=F32), shape(snaps + 1, ents, width)),
-        in_specs=[HBM] * 5,
-        out_specs=(HBM, VMEM),
+    load = pl.pallas_call(
+        load_kernel,
+        out_shape=hbm(snaps + 1, ents, width),
+        in_specs=[SMEM, HBM, HBM],
+        out_specs=HBM,
         scratch_shapes=[
-            pltpu.VMEM((slots, local), jnp.int32),
-            pltpu.VMEM((slots, local), jnp.int32),
-            pltpu.VMEM(rel_bias.shape, F32),
             pltpu.VMEM((snaps, ents), jnp.int32),
             pltpu.VMEM((snaps, ents, width), BF16),
-            pltpu.VMEM((heads, local, keys), F32),
-            pltpu.SemaphoreType.DMA((5 + heads,)),
+            pltpu.VMEM((ents, width), BF16),
+            pltpu.SemaphoreType.DMA((4,)),
         ],
-        compiler_params=params(16),
+        compiler_params=params(8),
         cost_estimate=pl.CostEstimate(flops=10**9, bytes_accessed=4 * 10**6, transcendentals=0),
-        name="own_edges",
-    )(*in_hbm(nbr[0].T, rel_type[0].T, rel_bias, active, cotangent))
-    cots = gather_blocks(load, "snap")
+        name="own_load",
+    )(place, *in_hbm(active, cotangent))
+    edges = (nbr[0].T, rel_type[0].T, rel_bias)
+    cots = gather_blocks({0: load}, "snap", snaps // 2, 1)
+    cots = [cots[m] for m in range(snaps)]
 
     hidden = pl.pallas_call(
         functools.partial(forward_kernel, heads),
         out_shape=shape(local, width),
-        in_specs=[VMEM] * 3 + [HBM],
+        in_specs=[VMEM] * 6,
         out_specs=VMEM,
         scratch_shapes=[
-            pltpu.VMEM((heads, local, keys), F32),
             pltpu.VMEM((local, 3 * width), BF16),
             pltpu.VMEM((keys, 2 * width), BF16),
-            pltpu.SemaphoreType.DMA((heads,)),
         ],
         compiler_params=params(8),
         name="struct_forward",
-    )(x, halo, w_struct, *in_hbm(edge))
-
-    hids = gather_blocks(hidden, "snap")
+    )(x, halo, w_struct, *edges)
+
+    hids = gather_blocks({0: hidden}, "snap", snaps // 2, 1)
+    hids = [hids[m] for m in range(snaps)]
     every = snaps * local
+    ct, act = pl.pallas_call(
+        cotangent_kernel,
+        out_shape=(
+            shape(every, width, dtype=F32 if ents % 16 else BF16),
+            shape(local, LANES, dtype=F32),
+        ),
+        in_specs=[SMEM] + [VMEM] * snaps,
+        out_specs=(VMEM, VMEM),
+        compiler_params=params(8),
+        name="cotangents",
+    )(place, *cots)
     *terms, dt_own, cot_own = pl.pallas_call(
         functools.partial(temporal_kernel, snaps, heads, pieces),
         out_shape=(shape(share // pieces, 3 * width),) * pieces
         + (shape(local, 3 * width), shape(local, width)),
-        in_specs=[SMEM] + [VMEM] * (2 + 2 * snaps),
+        in_specs=[SMEM] + [VMEM] * (4 + snaps),
         out_specs=(VMEM,) * (pieces + 2),
         scratch_shapes=[
             pltpu.VMEM((every, width), BF16),
-            pltpu.VMEM((every, width), F32 if ents % 16 else BF16),
             pltpu.VMEM((every, 3 * width), BF16),
             pltpu.VMEM((every, 3 * width), BF16),
-            pltpu.VMEM((local, LANES), F32),
             pltpu.VMEM((2 * every, width), BF16),
             pltpu.VMEM((every, LANES), F32),
             pltpu.VMEM((every, LANES), F32),
@@ -573,7 +583,7 @@
         ],
         compiler_params=params(24 if snaps <= 4 else 56),
         name="temporal",
-    )(place, pos_embed, w_temp, *hids, *cots)
+    )(place, pos_embed, w_temp, ct, act, *hids)
 
     if paired:
         got = [terms[0]] + [flipped(terms[k], "dom", 2 * k) for k in range(1, pieces)]
@@ -582,24 +592,18 @@
     back, partial = pl.pallas_call(
         functools.partial(backward_kernel, heads),
         out_shape=(shape(halo_rows, width, dtype=F32), shape(local, width, dtype=F32)),
-        in_specs=[VMEM] * 2 + [HBM] * 5,
+        in_specs=[VMEM] * 9,
         out_specs=(VMEM, VMEM),
         scratch_shapes=[
-            pltpu.VMEM((local, width), BF16),
-            pltpu.VMEM((halo_rows, width), BF16),
-            pltpu.VMEM((heads, local, keys), F32),
-            pltpu.VMEM(w_struct.shape, BF16),
-            pltpu.VMEM(w_temp.shape, BF16),
             pltpu.VMEM((local, 3 * width), BF16),
             pltpu.VMEM((keys, 2 * width), BF16),
             pltpu.VMEM((local, width), BF16),
             pltpu.VMEM((keys, 2 * width), BF16),
-            pltpu.SemaphoreType.DMA((5,)),
         ],
-        compiler_params=params(24),
+        compiler_params=params(16),
         cost_estimate=pl.CostEstimate(flops=2 * 10**9, bytes_accessed=8 * 10**6, transcendentals=0),
         name="struct_backward",
-    )(dt_own, cot_own, *in_hbm(x, halo, edge, w_struct, w_temp))
+    )(dt_own, cot_own, x, halo, *edges, w_struct, w_temp)
 
     if not paired:
         total = jnp.sum(got.astype(F32), axis=0).astype(BF16)
@@ -628,20 +632,39 @@
         name="inner_sum",
     )(place, back, mine, other)
     sums = [sums[0]] + [flipped(sums[k], "dom", 2 * k) for k in range(1, pieces)]
+    soon, late = list(range(pieces // 2)), list(range(pieces // 2, pieces))
+    partial, picks, grad_wtemp = pl.pallas_call(
+        functools.partial(early_kernel, soon, halo_per),
+        out_shape=(
+            shape(local, width, dtype=F32),
+            shape(halo_rows, local),
+            hbm(share, 3 * width, dtype=F32),
+        ),
+        in_specs=[SMEM, SMEM] + [VMEM] * (1 + len(soon)),
+        out_specs=(VMEM, VMEM, HBM),
+        scratch_shapes=[
+            pltpu.VMEM((len(soon), piece, 3 * width), F32),
+            pltpu.VMEM((halo_rows, width), F32),
+            pltpu.SemaphoreType.DMA((len(soon),)),
+        ],
+        compiler_params=params(8),
+        name="early_sums",
+    )(place, route, partial, *[sums[k] for k in soon])
     grad_feat, grad_wtemp = pl.pallas_call(
-        functools.partial(last_kernel, halo_per),
+        functools.partial(last_kernel, late, halo_per),
         out_shape=(hbm(local, width), hbm(share, 3 * width, dtype=F32)),
-        in_specs=[SMEM, SMEM] + [VMEM] * (1 + pieces),
+        in_specs=[SMEM] + [VMEM] * 2 + [HBM] + [VMEM] * len(late),
         out_specs=(HBM, HBM),
         scratch_shapes=[
             pltpu.VMEM((local, width), BF16),
-            pltpu.VMEM((pieces, piece, 3 * width), F32),
+            pltpu.VMEM((len(late), piece, 3 * width), F32),
             pltpu.VMEM((halo_rows, width), F32),
-            pltpu.SemaphoreType.DMA((pieces + 1,)),
+            pltpu.SemaphoreType.DMA((len(late) + 1,)),
         ],
+        input_output_aliases={3: 1},
         compiler_params=params(8),
         name="last_sums",
-    )(place, route, partial, *sums)
+    )(place, picks, partial, *in_hbm(grad_wtemp), *[sums[k] for k in late])
     return (grad_feat[None], grad_wtemp)
 
 

time: 62.4 us -> 60 us (0.962)
  Pallas kernels: 23.6 us -> 20.8 us
  waiting for transfers between devices: 16.4 us -> 17.2 us
    ppermute x6 -> x0, waiting for transfers between devices: 4.2 us -> none  [gather_blocks(): held[m ^ bit] = lax.ppermute(held[m], axis, pairs)]
    ppermute x6 -> x0, starting transfers between devices: 3.68 us -> none  [gather_blocks(): held[m ^ bit] = lax.ppermute(held[m], axis, pairs)]
    ppermute x7 -> x13, waiting for transfers between devices: 10.6 us -> 14.2 us  [flipped(): return lax.ppermute(block, axis, [(i, i ^ flip) for i in range(count)])]
    ppermute x7 -> x13, starting transfers between devices: 10.3 us -> 13.5 us  [flipped(): return lax.ppermute(block, axis, [(i, i ^ flip) for i in range(count)])]
    pallas_call x1, Pallas kernels: 6.78 us -> 5.18 us  [per_device(): pl.pallas_call(functools.partial(backward_kernel, heads), out_shape=(shap...]
    all_to_all x1, waiting for transfers between devices: 1.61 us -> 3.03 us  [exchange(): return lax.all_to_all(tiles, axis, split_axis=0, concat_axis=0, tiled=True)]
    pallas_call x1, Pallas kernels: 3.46 us -> 2.13 us  [per_device(): pl.pallas_call(functools.partial(forward_kernel, heads), out_shape=shape(...]
    pallas_call x2 -> x4, Pallas kernels: 5.33 us -> 6.04 us  [the longest x1 2.15 us: per_device(): pl.pallas_call(load_kernel, out_shape=hbm(snaps + 1, ents, width), in_spe...]
  transfers between devices with their start and end apart: 14 -> 14, of which waited for: 6 -> 7; matrix products, arithmetic and copies ran while one was open for 0% -> 0% of each run, Pallas kernels for 22% -> 20%
where the time goes in v5:
time: 60 us; the launch traced here: 59.7 us
  Pallas kernels  20.8 us (35%)
  starting transfers between devices  20.7 us (34%)
  waiting for transfers between devices  17.2 us (29%)
  between operations  0.8 us (1%)
    ppermute x13, waiting for transfers between devices, flipped(): return lax.ppermute(block, axis, [(i, i ^ flip) for i in range(count)])  14.2 us
    ppermute x13, starting transfers between devices, flipped(): return lax.ppermute(block, axis, [(i, i ^ flip) for i in range(count)])  13.5 us
    all_to_all x1, starting transfers between devices, exchange(): return lax.all_to_all(tiles, axis, split_axis=0, concat_axis=0, tiled=True)  7.27 us
    pallas_call x1, Pallas kernels, per_device(): pl.pallas_call(functools.partial(backward_kernel, heads), out_shape=(shap...  5.18 us
    pallas_call x1, Pallas kernels, per_device(): pl.pallas_call(functools.partial(temporal_kernel, snaps, heads, pieces),...  4.62 us
    all_to_all x1, waiting for transfers between devices, exchange(): return lax.all_to_all(tiles, axis, split_axis=0, concat_axis=0, tiled=True)  3.03 us
    pallas_call x1, Pallas kernels, per_device(): pl.pallas_call(load_kernel, out_shape=hbm(snaps + 1, ents, width), in_spe...  2.15 us
    pallas_call x1, Pallas kernels, per_device(): pl.pallas_call(functools.partial(forward_kernel, heads), out_shape=shape(...  2.13 us
  transfers between devices with their start and end apart: 14, of which 7 were waited for; matrix products, arithmetic and copies ran while one was open for 0% of the time, Pallas kernels for 20%

profile of v5, /device:TPU:0, one launch (start us, length us, event | category | flops | bytes accessed | tf_op | source)
XLA Modules:
  0.0 59.7 jit_solution(16069479339847517488)
XLA Ops:
  0.6 1.7 %halo_tiles.1 = bf16[64,512]{1,0:T(8,128)(2,1)} custom-call(s32[8,8]{1,0:T(8,128)} %bitcast.19, bf16[128,512]{1,0:T(8,128)(2,1)} %bitcast.14), custom_call_target="tpu_custom_call" | custom-call | tf_op jit(solution)/shard_map/halo_tiles/pallas_call | solution.py:502
  2.3 7.3 %all-to-all-start = ((bf16[8,8,512]{2,1,0:T(8,128)(2,1)}), bf16[8,8,512]{2,1,0:T(8,128)(2,1)S(1)}, u32[]{:S(2)}, u32[]{:S(2)}) async-start(bf16[8,8,512]{2,1,0:T(8,128)(2,1)} %bitcast.5), calls=%async_computation | async-start | bytes 131072 | tf_op jit(solution)/shard_map/all_to_all | solution.py:457
  9.6 0.1 pad_add_fusion._.place_ref
  9.7 2.1 %own_load.1.refs_0_ = bf16[5,32,512]{2,1,0:T(8,128)(2,1)} custom-call(s32[3]{0:T(128)S(1)} %pad_add_fusion._.place_ref, s32[4,32]{1,0:T(4,128)} %act_hbm.1, bf16[4,32,512]{2,1,0:T(8,128)(2,1)} %cot_hbm.1), custom_call_target="tpu_custom_call" | custom-call | flops 1000000000 | bytes 4000000 | tf_op jit(solution)/shard_map/own_load/pallas_call | solution.py:517
  11.9 0.0 copy-start
  11.9 0.0 copy-start.5
  11.9 1.6 %collective-permute-start.1 = (bf16[5,32,512]{2,1,0:T(8,128)(2,1)}, bf16[5,32,512]{2,1,0:T(8,128)(2,1)}, u32[]{:S(2)}, u32[]{:S(2)}) collective-permute-start(bf16[5,32,512]{2,1,0:T(8,128)(2,1)} %own_load.1.refs_0_), channel_id=1, source_target_pairs={{0,2},{1,3},{2,0},{3,1},{4,6},{5,7},{6,4},{7,5},{8,10},{9,11},{10,... | collective-permute-start | bytes 491528 | tf_op jit(solution)/shard_map/ppermute | solution.py:462
  13.5 3.0 %all-to-all-done = bf16[8,8,512]{2,1,0:T(8,128)(2,1)S(1)} async-done(((bf16[8,8,512]{2,1,0:T(8,128)(2,1)}), bf16[8,8,512]{2,1,0:T(8,128)(2,1)S(1)}, u32[]{:S(2)}, u32[]{:S(2)}) %all-to-all-start) | async-done | bytes 65568 | tf_op jit(solution)/shard_map/all_to_all | solution.py:457
  16.5 2.1 %struct_forward.1.refs_0_ = bf16[128,512]{1,0:T(8,128)(2,1)S(1)} custom-call(bf16[128,512]{1,0:T(8,128)(2,1)S(1)} %bitcast.15, bf16[64,512]{1,0:T(8,128)(2,1)S(1)} %bitcast.17, bf16[512,1536]{1,0:T(8,128)(2,1)S(1)} %copy-done.1, s32[8,128]{1,0:T(8,128)S(1)} %bitcast.21, s32[8,128]{1,0:T(8,128)S(1)} %bitcast.23, f32[4,8]{1,0:T(4,128)S(1)} %copy-done.8), custom_call_target="tpu_custom_call" | custom-call | tf_op jit(solution)/shard_map/struct_forward/pallas_call | solution.py:536
  18.7 1.6 %collective-permute-start.4 = (bf16[128,512]{1,0:T(8,128)(2,1)S(1)}, bf16[128,512]{1,0:T(8,128)(2,1)S(1)}, u32[]{:S(2)}, u32[]{:S(2)}) collective-permute-start(bf16[128,512]{1,0:T(8,128)(2,1)S(1)} %struct_forward.1.refs_0_), channel_id=1, source_target_pairs={{0,2},{1,3},{2,0},{3,1},{4,6},{5,7},{6,4},{7,5},{8,10},{9,11},{10,... | collective-permute-start | bytes 393224 | tf_op jit(solution)/shard_map/ppermute | solution.py:462
  20.3 0.5 collective-permute-start.2
  20.8 0.1 collective-permute-start.3
  20.9 2.9 %collective-permute-done.4.refs_2_ = bf16[128,512]{1,0:T(8,128)(2,1)S(1)} collective-permute-done((bf16[128,512]{1,0:T(8,128)(2,1)S(1)}, bf16[128,512]{1,0:T(8,128)(2,1)S(1)}, u32[]{:S(2)}, u32[]{:S(2)}) %collective-permute-start.4) | collective-permute-done | bytes 131104 | tf_op jit(solution)/shard_map/ppermute | solution.py:462
  23.7 1.0 %cotangents.1 = (bf16[512,512]{1,0:T(8,128)(2,1)S(1)}, f32[128,128]{1,0:T(8,128)S(1)}) custom-call(s32[3]{0:T(128)S(1)} %pad_add_fusion._.place_ref, bf16[5,32,512]{2,1,0:T(8,128)(2,1)S(1)} %copy-done.3, bf16[5,32,512]{2,1,0:T(8,128)(2,1)S(1)} %collective-permute-done.refs_1_, bf16[5,32,512]{2,1,0:T(8,128)(2,1)} %collective-permute-done.1.refs_2_, ...), custom_call_target="tpu_custom_call" | custom-call | tf_op jit(solution)/shard_map/cotangents/pallas_call | solution.py:552
  24.7 0.3 collective-permute-done.5.refs_3_
  25.1 4.6 %temporal.1 = (bf16[32,1536]{1,0:T(8,128)(2,1)S(1)}, bf16[32,1536]{1,0:T(8,128)(2,1)S(1)}, bf16[32,1536]{1,0:T(8,128)(2,1)S(1)}, bf16[32,1536]{1,0:T(8,128)(2,1)...) custom-call(s32[3]{0:T(128)S(1)} %pad_add_fusion._.place_ref, bf16[4,512]{1,0:T(4,128)(2,1)S(1)} %copy-done.5, ...), custom_call_target="tpu_custom_call" | custom-call | tf_op jit(solution)/shard_map/temporal/pallas_call | solution.py:563
  29.7 0.3 collective-permute-start.6
  30.0 1.2 %collective-permute-start.7 = (bf16[32,1536]{1,0:T(8,128)(2,1)S(1)}, bf16[32,1536]{1,0:T(8,128)(2,1)S(1)}, u32[]{:S(2)}, u32[]{:S(2)}) collective-permute-start(bf16[32,1536]{1,0:T(8,128)(2,1)S(1)} %get-tuple-element.29), channel_id=1, source_target_pairs={{0,16},{4,20},{8,24},{12,28},{16,0},{20,4},{24,8},{28,12},{1,17},{... | collective-permute-start | bytes 294920 | tf_op jit(solution)/shard_map/ppermute | solution.py:462
  31.1 3.0 %collective-permute-start.8 = (bf16[32,1536]{1,0:T(8,128)(2,1)S(1)}, bf16[32,1536]{1,0:T(8,128)(2,1)S(1)}, u32[]{:S(2)}, u32[]{:S(2)}) collective-permute-start(bf16[32,1536]{1,0:T(8,128)(2,1)S(1)} %get-tuple-element.30), channel_id=1, source_target_pairs={{0,24},{4,28},{8,16},{12,20},{16,8},{20,12},{24,0},{28,4},{1,25},{... | collective-permute-start | bytes 294920 | tf_op jit(solution)/shard_map/ppermute | solution.py:462
  34.2 5.2 %struct_backward.1 = (f32[64,512]{1,0:T(8,128)S(1)}, f32[128,512]{1,0:T(8,128)S(1)}) custom-call(bf16[128,1536]{1,0:T(8,128)(2,1)S(1)} %get-tuple-element.23.dt, bf16[128,512]{1,0:T(8,128)(2,1)S(1)} %get-tuple-element.24.cot, bf16[128,512]{1,0:T(8,128)(2,1)S(1)} %bitcast.16, bf16[64,512]{1,0:T(8,128)(2,1)S(1)} %bitcast.18, s32[8,128]{1,0:T(8,128)S(1)} %bitcast.22, ...), custom_call_target="tpu_custom_call" | custom-call | flops 2000000000 | bytes 8000000 | tf_op jit(solution)/shard_map/struct_backward/pallas_call | solution.py:592
  39.4 1.4 %collective-permute-done.7.refs_2_ = bf16[32,1536]{1,0:T(8,128)(2,1)S(1)} collective-permute-done((bf16[32,1536]{1,0:T(8,128)(2,1)S(1)}, bf16[32,1536]{1,0:T(8,128)(2,1)S(1)}, u32[]{:S(2)}, u32[]{:S(2)}) %collective-permute-start.7) | collective-permute-done | bytes 98336 | tf_op jit(solution)/shard_map/ppermute | solution.py:462
  40.8 0.6 outer_sum.1.mine_ref
  41.4 0.8 %collective-permute-start.9 = (bf16[32,2048]{1,0:T(8,128)(2,1)S(1)}, bf16[32,2048]{1,0:T(8,128)(2,1)S(1)}, u32[]{:S(2)}, u32[]{:S(2)}) collective-permute-start(bf16[32,2048]{1,0:T(8,128)(2,1)S(1)} %outer_sum.1.mine_ref), channel_id=1, source_target_pairs={{0,4},{4,0},{8,12},{12,8},{16,20},{20,16},{24,28},{28,24},{1,5},{5... | collective-permute-start | bytes 393224 | tf_op jit(solution)/shard_map/ppermute | solution.py:462
  42.2 4.2 %collective-permute-done.9.other_ref = bf16[32,2048]{1,0:T(8,128)(2,1)S(1)} collective-permute-done((bf16[32,2048]{1,0:T(8,128)(2,1)S(1)}, bf16[32,2048]{1,0:T(8,128)(2,1)S(1)}, u32[]{:S(2)}, u32[]{:S(2)}) %collective-permute-start.9) | collective-permute-done | bytes 131104 | tf_op jit(solution)/shard_map/ppermute | solution.py:462
  46.4 0.6 inner_sum.1
  47.0 1.8 %collective-permute-start.10 = (bf16[32,1792]{1,0:T(8,128)(2,1)S(1)}, bf16[32,1792]{1,0:T(8,128)(2,1)S(1)}, u32[]{:S(2)}, u32[]{:S(2)}) collective-permute-start(bf16[32,1792]{1,0:T(8,128)(2,1)S(1)} %get-tuple-element.32), channel_id=1, source_target_pairs={{0,8},{4,12},{8,0},{12,4},{16,24},{20,28},{24,16},{28,20},{1,9},{5... | collective-permute-start | bytes 344072 | tf_op jit(solution)/shard_map/ppermute | solution.py:462
  48.8 0.5 collective-permute-start.11
  49.3 2.1 %collective-permute-start.12 = (bf16[32,1792]{1,0:T(8,128)(2,1)S(1)}, bf16[32,1792]{1,0:T(8,128)(2,1)S(1)}, u32[]{:S(2)}, u32[]{:S(2)}) collective-permute-start(bf16[32,1792]{1,0:T(8,128)(2,1)S(1)} %get-tuple-element.37), channel_id=1, source_target_pairs={{0,24},{4,28},{8,16},{12,20},{16,8},{20,12},{24,0},{28,4},{1,25},{... | collective-permute-start | bytes 344072 | tf_op jit(solution)/shard_map/ppermute | solution.py:462
  51.5 2.9 %collective-permute-done.10.refs_1_ = bf16[32,1792]{1,0:T(8,128)(2,1)S(1)} collective-permute-done((bf16[32,1792]{1,0:T(8,128)(2,1)S(1)}, bf16[32,1792]{1,0:T(8,128)(2,1)S(1)}, u32[]{:S(2)}, u32[]{:S(2)}) %collective-permute-start.10) | collective-permute-done | bytes 114720 | tf_op jit(solution)/shard_map/ppermute | solution.py:462
  54.3 1.5 %early_sums.1 = (f32[128,512]{1,0:T(8,128)S(1)}, bf16[64,128]{1,0:T(8,128)(2,1)S(1)}, f32[128,1536]{1,0:T(8,128)}) custom-call(s32[3]{0:T(128)S(1)} %pad_add_fusion._.place_ref, s32[8,8]{1,0:T(8,128)S(1)} %bitcast.20, f32[128,512]{1,0:T(8,128)S(1)} %get-tuple-element.25.part_ref, bf16[32,1792]{1,0:T(8,128)(2,1)S(1)} %get-tuple-element.31.refs_0_, ...), custom_call_target="tpu_custom_call" | custom-call | tf_op jit(solution)/shard_map/early_sums/pallas_call | solution.py:636
  55.8 2.5 %collective-permute-done.11.refs_0_ = bf16[32,1792]{1,0:T(8,128)(2,1)S(1)} collective-permute-done((bf16[32,1792]{1,0:T(8,128)(2,1)S(1)}, bf16[32,1792]{1,0:T(8,128)(2,1)S(1)}, u32[]{:S(2)}, u32[]{:S(2)}) %collective-permute-start.11) | collective-permute-done | bytes 114720 | tf_op jit(solution)/shard_map/ppermute | solution.py:462
  58.3 1.4 %last_sums.1 = (bf16[128,512]{1,0:T(8,128)(2,1)}, f32[128,1536]{1,0:T(8,128)}) custom-call(s32[3]{0:T(128)S(1)} %pad_add_fusion._.place_ref, bf16[64,128]{1,0:T(8,128)(2,1)S(1)} %get-tuple-element.33.picks_ref, f32[128,512]{1,0:T(8,128)S(1)} %get-tuple-element.34.sum_ref, f32[128,1536]{1,0:T(8,128)} %get-tuple-element.35._, ...), custom_call_target="tpu_custom_call", output_to_operand_aliasing={{1}: (3, {})} | custom-call | tf_op jit(solution)/shard_map/last_sums/pallas_call | solution.py:653
  (25 shorter events, 0.1 us)
Async XLA Ops:
  2.3 14.2 %all-to-all-start = ((bf16[8,8,512]{2,1,0:T(8,128)(2,1)}), bf16[8,8,512]{2,1,0:T(8,128)(2,1)S(1)}, u32[]{:S(2)}, u32[]{:S(2)}) async-start(bf16[8,8,512]{2,1,0:T(8,128)(2,1)} %bitcast.5), calls=%async_computation | async-start | bytes 131072 | tf_op jit(solution)/shard_map/all_to_all | solution.py:457
  9.7 6.8 %copy-start.1 = (bf16[512,1536]{1,0:T(8,128)(2,1)S(1)}, bf16[512,1536]{1,0:T(8,128)(2,1)}, u32[]{:S(2)}) copy-start(bf16[512,1536]{1,0:T(8,128)(2,1)} %ws.1) | copy-start | bytes 4718596
  9.7 6.8 %copy-start.2 = (bf16[1,128,512]{2,1,0:T(8,128)(2,1)S(1)}, bf16[1,128,512]{2,1,0:T(8,128)(2,1)}, u32[]{:S(2)}) copy-start(bf16[1,128,512]{2,1,0:T(8,128)(2,1)} %param.10) | copy-start | bytes 393220
  9.7 6.8 %copy-start.6 = (s32[1,128,8]{1,2,0:T(8,128)S(1)}, s32[1,128,8]{1,2,0:T(8,128)}, u32[]{:S(2)}) copy-start(s32[1,128,8]{1,2,0:T(8,128)} %param.15) | copy-start | bytes 12292
  9.7 6.8 %copy-start.7 = (s32[1,128,8]{1,2,0:T(8,128)S(1)}, s32[1,128,8]{1,2,0:T(8,128)}, u32[]{:S(2)}) copy-start(s32[1,128,8]{1,2,0:T(8,128)} %param.16) | copy-start | bytes 12292
  9.7 6.8 %copy-start.8 = (f32[4,8]{1,0:T(4,128)S(1)}, f32[4,8]{1,0:T(4,128)}, u32[]{:S(2)}) copy-start(f32[4,8]{1,0:T(4,128)} %bias.3) | copy-start | bytes 388
  11.9 8.4 %copy-start.3 = (bf16[5,32,512]{2,1,0:T(8,128)(2,1)S(1)}, bf16[5,32,512]{2,1,0:T(8,128)(2,1)}, u32[]{:S(2)}) copy-start(bf16[5,32,512]{2,1,0:T(8,128)(2,1)} %own_load.1.refs_0_) | copy-start | bytes 491524
  11.9 13.2 %copy-start = (bf16[512,1536]{1,0:T(8,128)(2,1)S(1)}, bf16[512,1536]{1,0:T(8,128)(2,1)}, u32[]{:S(2)}) copy-start(bf16[512,1536]{1,0:T(8,128)(2,1)} %wt.1) | copy-start | bytes 4718596
  11.9 13.2 %copy-start.5 = (bf16[4,512]{1,0:T(4,128)(2,1)S(1)}, bf16[4,512]{1,0:T(4,128)(2,1)}, u32[]{:S(2)}) copy-start(bf16[4,512]{1,0:T(4,128)(2,1)} %pos_ref.1) | copy-start | bytes 12292
  11.9 8.4 %collective-permute-start.1 = (bf16[5,32,512]{2,1,0:T(8,128)(2,1)}, bf16[5,32,512]{2,1,0:T(8,128)(2,1)}, u32[]{:S(2)}, u32[]{:S(2)}) collective-permute-start(bf16[5,32,512]{2,1,0:T(8,128)(2,1)} %own_load.1.refs_0_), channel_id=1, source_target_pairs={{0,2},{1,3},{2,0},{3,1},{4,6},{5,7},{6,4},{7,5},{8,10},{9,11},{10,... | collective-permute-start | bytes 491528 | tf_op jit(solution)/shard_map/ppermute | solution.py:462
  18.7 5.0 %collective-permute-start.4 = (bf16[128,512]{1,0:T(8,128)(2,1)S(1)}, bf16[128,512]{1,0:T(8,128)(2,1)S(1)}, u32[]{:S(2)}, u32[]{:S(2)}) collective-permute-start(bf16[128,512]{1,0:T(8,128)(2,1)S(1)} %struct_forward.1.refs_0_), channel_id=1, source_target_pairs={{0,2},{1,3},{2,0},{3,1},{4,6},{5,7},{6,4},{7,5},{8,10},{9,11},{10,... | collective-permute-start | bytes 393224 | tf_op jit(solution)/shard_map/ppermute | solution.py:462
  20.3 3.5 %collective-permute-start = (bf16[5,32,512]{2,1,0:T(8,128)(2,1)S(1)}, bf16[5,32,512]{2,1,0:T(8,128)(2,1)S(1)}, u32[]{:S(2)}, u32[]{:S(2)}) collective-permute-start(bf16[5,32,512]{2,1,0:T(8,128)(2,1)S(1)} %copy-done.3), channel_id=1, source_target_pairs={{0,1},{1,0},{2,3},{3,2},{4,5},{5,4},{6,7},{7,6},{8,9},{9,8},{10,11... | collective-permute-start | bytes 491528 | tf_op jit(solution)/shard_map/ppermute | solution.py:462
  20.3 3.4 %collective-permute-start.2 = (bf16[5,32,512]{2,1,0:T(8,128)(2,1)}, bf16[5,32,512]{2,1,0:T(8,128)(2,1)S(1)}, u32[]{:S(2)}, u32[]{:S(2)}) collective-permute-start(bf16[5,32,512]{2,1,0:T(8,128)(2,1)} %collective-permute-done.1.refs_2_), channel_id=1, source_target_pairs={{0,1},{1,0},{2,3},{3,2},{4,5},{5,4},{6,7},{7,6},{8,9},{9,8},{10,11... | collective-permute-start | bytes 491528 | tf_op jit(solution)/shard_map/ppermute | solution.py:462
  20.8 3.9 %collective-permute-start.3 = (bf16[128,512]{1,0:T(8,128)(2,1)S(1)}, bf16[128,512]{1,0:T(8,128)(2,1)S(1)}, u32[]{:S(2)}, u32[]{:S(2)}) collective-permute-start(bf16[128,512]{1,0:T(8,128)(2,1)S(1)} %struct_forward.1.refs_0_), channel_id=1, source_target_pairs={{0,1},{1,0},{2,3},{3,2},{4,5},{5,4},{6,7},{7,6},{8,9},{9,8},{10,11... | collective-permute-start | bytes 393224 | tf_op jit(solution)/shard_map/ppermute | solution.py:462
  23.7 1.3 %collective-permute-start.5 = (bf16[128,512]{1,0:T(8,128)(2,1)S(1)}, bf16[128,512]{1,0:T(8,128)(2,1)S(1)}, u32[]{:S(2)}, u32[]{:S(2)}) collective-permute-start(bf16[128,512]{1,0:T(8,128)(2,1)S(1)} %collective-permute-done.4.refs_2_), channel_id=1, source_target_pairs={{0,1},{1,0},{2,3},{3,2},{4,5},{5,4},{6,7},{7,6},{8,9},{9,8},{10,11... | collective-permute-start | bytes 393224 | tf_op jit(solution)/shard_map/ppermute | solution.py:462
  29.7 9.6 %collective-permute-start.6 = (bf16[32,1536]{1,0:T(8,128)(2,1)S(1)}, bf16[32,1536]{1,0:T(8,128)(2,1)S(1)}, u32[]{:S(2)}, u32[]{:S(2)}) collective-permute-start(bf16[32,1536]{1,0:T(8,128)(2,1)S(1)} %get-tuple-element.28), channel_id=1, source_target_pairs={{0,8},{4,12},{8,0},{12,4},{16,24},{20,28},{24,16},{28,20},{1,9},{5... | collective-permute-start | bytes 294920 | tf_op jit(solution)/shard_map/ppermute | solution.py:462
  30.0 10.8 %collective-permute-start.7 = (bf16[32,1536]{1,0:T(8,128)(2,1)S(1)}, bf16[32,1536]{1,0:T(8,128)(2,1)S(1)}, u32[]{:S(2)}, u32[]{:S(2)}) collective-permute-start(bf16[32,1536]{1,0:T(8,128)(2,1)S(1)} %get-tuple-element.29), channel_id=1, source_target_pairs={{0,16},{4,20},{8,24},{12,28},{16,0},{20,4},{24,8},{28,12},{1,17},{... | collective-permute-start | bytes 294920 | tf_op jit(solution)/shard_map/ppermute | solution.py:462
  31.1 9.7 %collective-permute-start.8 = (bf16[32,1536]{1,0:T(8,128)(2,1)S(1)}, bf16[32,1536]{1,0:T(8,128)(2,1)S(1)}, u32[]{:S(2)}, u32[]{:S(2)}) collective-permute-start(bf16[32,1536]{1,0:T(8,128)(2,1)S(1)} %get-tuple-element.30), channel_id=1, source_target_pairs={{0,24},{4,28},{8,16},{12,20},{16,8},{20,12},{24,0},{28,4},{1,25},{... | collective-permute-start | bytes 294920 | tf_op jit(solution)/shard_map/ppermute | solution.py:462
  34.2 20.2 %copy-start.4 = (s32[1,1,8,8]{3,2,1,0:T(8,128)S(1)}, s32[1,1,8,8]{3,2,1,0:T(8,128)}, u32[]{:S(2)}) copy-start(s32[1,1,8,8]{3,2,1,0:T(8,128)} %param.17) | copy-start | bytes 772
  41.4 5.0 %collective-permute-start.9 = (bf16[32,2048]{1,0:T(8,128)(2,1)S(1)}, bf16[32,2048]{1,0:T(8,128)(2,1)S(1)}, u32[]{:S(2)}, u32[]{:S(2)}) collective-permute-start(bf16[32,2048]{1,0:T(8,128)(2,1)S(1)} %outer_sum.1.mine_ref), channel_id=1, source_target_pairs={{0,4},{4,0},{8,12},{12,8},{16,20},{20,16},{24,28},{28,24},{1,5},{5... | collective-permute-start | bytes 393224 | tf_op jit(solution)/shard_map/ppermute | solution.py:462
  47.0 7.3 %collective-permute-start.10 = (bf16[32,1792]{1,0:T(8,128)(2,1)S(1)}, bf16[32,1792]{1,0:T(8,128)(2,1)S(1)}, u32[]{:S(2)}, u32[]{:S(2)}) collective-permute-start(bf16[32,1792]{1,0:T(8,128)(2,1)S(1)} %get-tuple-element.32), channel_id=1, source_target_pairs={{0,8},{4,12},{8,0},{12,4},{16,24},{20,28},{24,16},{28,20},{1,9},{5... | collective-permute-start | bytes 344072 | tf_op jit(solution)/shard_map/ppermute | solution.py:462
  48.8 9.4 %collective-permute-start.11 = (bf16[32,1792]{1,0:T(8,128)(2,1)S(1)}, bf16[32,1792]{1,0:T(8,128)(2,1)S(1)}, u32[]{:S(2)}, u32[]{:S(2)}) collective-permute-start(bf16[32,1792]{1,0:T(8,128)(2,1)S(1)} %get-tuple-element.36), channel_id=1, source_target_pairs={{0,16},{4,20},{8,24},{12,28},{16,0},{20,4},{24,8},{28,12},{1,17},{... | collective-permute-start | bytes 344072 | tf_op jit(solution)/shard_map/ppermute | solution.py:462
  49.3 9.0 %collective-permute-start.12 = (bf16[32,1792]{1,0:T(8,128)(2,1)S(1)}, bf16[32,1792]{1,0:T(8,128)(2,1)S(1)}, u32[]{:S(2)}, u32[]{:S(2)}) collective-permute-start(bf16[32,1792]{1,0:T(8,128)(2,1)S(1)} %get-tuple-element.37), channel_id=1, source_target_pairs={{0,24},{4,28},{8,16},{12,20},{16,8},{20,12},{24,0},{28,4},{1,25},{... | collective-permute-start | bytes 344072 | tf_op jit(solution)/shard_map/ppermute | solution.py:462

commit v6 on v5

--- a/solution.py
+++ b/solution.py
@@ -14,6 +14,14 @@
 VMEM = pl.BlockSpec(memory_space=pltpu.VMEM)
 SMEM = pl.BlockSpec(memory_space=pltpu.SMEM)
 HBM = pl.BlockSpec(memory_space=pltpu.HBM)
+
+
+def snap_index():
+    return lax.axis_index("snap")
+
+
+def dom_index():
+    return lax.axis_index("dom")
 
 
 def dot_nn(a, b):
@@ -81,9 +89,23 @@
     out_ref[...] = dot_nn(pick_rows(route, x.shape[0]), x[...]).astype(BF16)
 
 
-def load_kernel(_, act_hbm, cot_hbm, load_hbm, act, cot, flags_s, sems):
+def own_kernel(
+    nbr_hbm, rel_hbm, bias_hbm, act_hbm, cot_hbm, x_hbm, w_hbm,
+    edge_ref, proj, x, w, load_hbm, nbr, rel, bias, act, cot, flags_s, sems,
+):
+    heads, rows, keys = edge_ref.shape
+    kinds = bias.shape[0]
     snaps, ents, width = cot.shape
-    fetch = Fetch(sems, (cot_hbm, cot), (act_hbm, act))
+    fetch = Fetch(
+        sems,
+        (cot_hbm, cot),
+        (act_hbm, act),
+        (nbr_hbm, nbr),
+        (rel_hbm, rel),
+        (bias_hbm, bias),
+        (x_hbm, x),
+        (w_hbm, w),
+    )
     row = lax.broadcasted_iota(jnp.int32, (ents, ents), 0)
     col = lax.broadcasted_iota(jnp.int32, (ents, ents), 1)
     lane = lax.broadcasted_iota(jnp.int32, (ents, width), 1)
@@ -95,7 +117,19 @@
         flags = jnp.where(lane == t, column, flags)
     flags_s[...] = flags.astype(BF16)
     fetch.wait(0)
-    store = Fetch(sems.at[2:], (flags_s, load_hbm.at[snaps]), (cot, load_hbm.at[:snaps]))
+    store = Fetch(sems.at[7:], (flags_s, load_hbm.at[snaps]), (cot, load_hbm.at[:snaps]))
+    fetch.wait(2, 3, 4)
+    counts = edge_counts(nbr, rel, kinds, keys)
+    gain = jnp.exp(bias[...])
+    for h in range(heads):
+        weight = counts[0] * gain[0:1, h : h + 1]
+        for r in range(1, kinds):
+            weight = weight + counts[r] * gain[r : r + 1, h : h + 1]
+        edge_ref[h] = jnp.where(weight > 0, jnp.log(weight), NEG)
+    fetch.wait(5, 6)
+    for part in range(3):
+        cols = slice(part * width, (part + 1) * width)
+        proj[:, cols] = dot_nn(x[...], w[:, cols]).astype(BF16)
     store.wait(0, 1)
 
 
@@ -125,10 +159,10 @@
         lax.bitwise_and(lax.shift_right_logical(packed, bits * r), low).astype(F32)
         for r in range(kinds)
     ]
-    return counts, jnp.where(packed > 0, 0.0, NEG)
-
-
-def edge_attention(p, heads, proj, counts, closed, gain, tab_s, width):
+    return counts
+
+
+def edge_attention(p, heads, proj, edge, tab_s, width):
     keys = tab_s.shape[0]
     head_dim = width // heads
     group = LANES // head_dim
@@ -137,29 +171,20 @@
     score = dot_nt(proj[:, cols], kk)
     parts = []
     for g in range(group):
-        h = p * group + g
-        weight = counts[0] * gain[0:1, h : h + 1]
-        for r in range(1, len(counts)):
-            weight = weight + counts[r] * gain[r : r + 1, h : h + 1]
-        s = score[:, g * keys : (g + 1) * keys] * head_dim ** (-0.5) + closed
-        e = jnp.exp(s - jnp.max(s, axis=1, keepdims=True)) * weight
+        s = score[:, g * keys : (g + 1) * keys] * head_dim ** (-0.5) + edge[p * group + g]
+        e = jnp.exp(s - jnp.max(s, axis=1, keepdims=True))
         parts.append(e * (1.0 / jnp.sum(e, axis=1, keepdims=True)))
     return kk, parts
 
 
-def forward_kernel(heads, x, halo, w, nbr, rel, bias, hidden_ref, proj, tab_s):
+def forward_kernel(heads, x, halo, w, proj, edge, hidden_ref, tab_s):
     width = x.shape[1]
     head_dim = width // heads
-    for part in range(3):
-        cols = slice(part * width, (part + 1) * width)
-        proj[:, cols] = dot_nn(x[...], w[:, cols]).astype(BF16)
     fill_table(tab_s, proj, halo, w.at[:, width:])
-    counts, closed = edge_counts(nbr, rel, bias.shape[0], tab_s.shape[0])
-    gain = jnp.exp(bias[...])
     for p in range(width // LANES):
         cols = slice(p * LANES, (p + 1) * LANES)
         vcols = slice(width + p * LANES, width + (p + 1) * LANES)
-        _, attn = edge_attention(p, heads, proj, counts, closed, gain, tab_s, width)
+        _, attn = edge_attention(p, heads, proj, edge, tab_s, width)
         vv = stack_heads(tab_s[:, vcols], head_dim)
         agg = dot_nn(jnp.concatenate([a.astype(BF16) for a in attn], axis=1), vv)
         elu = jnp.where(agg > 0, agg, jnp.exp(jnp.minimum(agg, 0.0)) - 1.0)
@@ -174,19 +199,19 @@
         lax.fori_loop(lo, hi, lambda i, c: (body(i), c)[1], 0)
 
 
-def cotangent_kernel(place_ref, *refs):
+def cotangent_kernel(*refs):
     *cot, ct_ref, act_ref = refs
     snaps = len(cot)
     ents = cot[0].shape[1]
     local = snaps * ents
     for m in range(snaps):
-        at = pl.multiple_of(lax.bitwise_xor(place_ref[0], m) * ents, ents)
+        at = pl.multiple_of(lax.bitwise_xor(snap_index(), m) * ents, ents)
         for t in range(snaps):
             ct_ref[pl.ds(t * local + at, ents), :] = cot[m][t].astype(ct_ref.dtype)
         act_ref[pl.ds(at, ents), :] = cot[m][snaps][:, :LANES].astype(F32)
 
 
-def temporal_kernel(snaps, heads, pieces, place_ref, pos_ref, w_s, ct_s, act_s, *refs):
+def temporal_kernel(snaps, heads, pieces, pos_ref, w_s, ct_s, act_s, *refs):
     hid = refs[:snaps]
     terms_ref = refs[snaps : snaps + pieces]
     (
@@ -197,7 +222,7 @@
     head_dim = width // heads
     scale = head_dim ** (-0.5)
     unroll = snaps <= 4
-    me, outer = place_ref[0], place_ref[1]
+    me, outer = snap_index(), dom_index() // 2
     pos = pos_ref[...].astype(F32)
     which = lax.broadcasted_iota(jnp.int32, pos.shape, 0)
 
@@ -324,8 +349,7 @@
 
 
 def backward_kernel(
-    heads, dt, cot, x, halo, nbr, rel, bias, ws, wt, back_ref, part_ref,
-    proj, tab_s, dq_s, dtab_s,
+    heads, dt, cot, proj, halo, edge, ws, wt, back_ref, part_ref, tab_s, dq_s, dtab_s,
 ):
     rows, width = cot.shape
     halo_rows = halo.shape[0]
@@ -335,16 +359,11 @@
     scale = head_dim ** (-0.5)
     dh = cot[...].astype(F32) + dot_nt(dt[...], wt[...])
     part_ref[...] = dh.astype(BF16).astype(F32)
-    for part in range(3):
-        cols = slice(part * width, (part + 1) * width)
-        proj[:, cols] = dot_nn(x[...], ws[:, cols]).astype(BF16)
     fill_table(tab_s, proj, halo, ws.at[:, width:])
-    counts, closed = edge_counts(nbr, rel, bias.shape[0], tab_s.shape[0])
-    gain = jnp.exp(bias[...])
     for p in range(width // LANES):
         cols = slice(p * LANES, (p + 1) * LANES)
         vcols = slice(width + p * LANES, width + (p + 1) * LANES)
-        kk, attn = edge_attention(p, heads, proj, counts, closed, gain, tab_s, width)
+        kk, attn = edge_attention(p, heads, proj, edge, tab_s, width)
         vv = stack_heads(tab_s[:, vcols], head_dim)
         attn_b = jnp.concatenate([a.astype(BF16) for a in attn], axis=1)
         agg = dot_nn(attn_b, vv)
@@ -363,23 +382,23 @@
     part_ref[...] += dot_nt(dq_s[...], ws[:, :width]) + dot_nt(dtab_s[:rows, :], ws[:, width:])
 
 
-def tile_of(place_ref, flip, back_ref, per):
-    at = lax.bitwise_xor(place_ref[2], flip) * per
+def tile_of(flip, back_ref, per):
+    at = lax.bitwise_xor(dom_index(), flip) * per
     return back_ref[pl.ds(pl.multiple_of(at, per), per), :]
 
 
-def outer_sum_kernel(per, place_ref, back_ref, *refs):
+def outer_sum_kernel(per, back_ref, *refs):
     *terms, out_ref = refs
     wide = terms[0].shape[1]
     total = terms[0][...].astype(F32)
     for term in terms[1:]:
         total = total + term[...].astype(F32)
     out_ref[:, :wide] = total.astype(BF16)
-    tiles = [tile_of(place_ref, 2 * k + 1, back_ref, per) for k in range(len(terms))]
+    tiles = [tile_of(2 * k + 1, back_ref, per) for k in range(len(terms))]
     out_ref[:, wide:] = jnp.concatenate(tiles, axis=0).astype(BF16)
 
 
-def inner_sum_kernel(per, place_ref, back_ref, mine_ref, other_ref, *out):
+def inner_sum_kernel(per, back_ref, mine_ref, other_ref, *out):
     rows = mine_ref.shape[0]
     wide = mine_ref.shape[1] - back_ref.shape[1]
     lanes = out[0].shape[1] - wide
@@ -387,7 +406,7 @@
     passing = other_ref[:, wide:].astype(F32)
     for k in range(len(out)):
         out[k][:, :wide] = total
-        both = [tile_of(place_ref, 2 * k, back_ref, per), passing[k * per : (k + 1) * per]]
+        both = [tile_of(2 * k, back_ref, per), passing[k * per : (k + 1) * per]]
         folds = [
             tile[:, i * lanes : (i + 1) * lanes]
             for tile in both
@@ -396,7 +415,7 @@
         out[k][:, wide:] = jnp.concatenate(folds, axis=0).astype(BF16)
 
 
-def unpack_sums(flips, per, place_ref, got, wtemp, wtemp_hbm, came_s, sems):
+def unpack_sums(flips, per, got, wtemp, wtemp_hbm, came_s, sems):
     rows = got[0].shape[0]
     lanes = got[0].shape[1] - wtemp.shape[2]
     folds = rows // (2 * per)
@@ -404,21 +423,21 @@
     came_s[...] = jnp.zeros_like(came_s)
     for i, k in enumerate(flips):
         wtemp[i] = got[i][:, : wtemp.shape[2]].astype(F32)
-        at = pl.multiple_of(lax.bitwise_xor(place_ref[1], k) * rows, rows)
+        at = pl.multiple_of(lax.bitwise_xor(dom_index() // 2, k) * rows, rows)
         stores.append(Fetch(sems.at[i:], (wtemp.at[i], wtemp_hbm.at[pl.ds(at, rows), :])))
         folded = got[i][:, wtemp.shape[2] :].astype(F32)
         for j in range(2):
-            d = pl.multiple_of(lax.bitwise_xor(place_ref[2], 2 * k + j) * per, per)
+            d = pl.multiple_of(lax.bitwise_xor(dom_index(), 2 * k + j) * per, per)
             for f in range(folds):
                 row = (j * folds + f) * per
                 came_s[pl.ds(d, per), f * lanes : (f + 1) * lanes] = folded[row : row + per]
     return stores
 
 
-def early_kernel(flips, per, place_ref, route_ref, part_ref, *refs):
+def early_kernel(flips, per, route_ref, part_ref, *refs):
     got = refs[: len(flips)]
     sum_ref, picks_ref, wtemp_hbm, wtemp, came_s, sems = refs[len(flips) :]
-    stores = unpack_sums(flips, per, place_ref, got, wtemp, wtemp_hbm, came_s, sems)
+    stores = unpack_sums(flips, per, got, wtemp, wtemp_hbm, came_s, sems)
     picks = pick_rows(route_ref, part_ref.shape[0])
     picks_ref[...] = picks
     sum_ref[...] = part_ref[...] + dot_tn(picks, came_s[...].astype(BF16))
@@ -426,10 +445,10 @@
         store.wait(0)
 
 
-def last_kernel(flips, per, place_ref, picks_ref, sum_ref, _, *refs):
+def last_kernel(flips, per, picks_ref, sum_ref, _, *refs):
     got = refs[: len(flips)]
     feat_hbm, wtemp_hbm, feat, wtemp, came_s, sems = refs[len(flips) :]
-    stores = unpack_sums(flips, per, place_ref, got, wtemp, wtemp_hbm, came_s, sems)
+    stores = unpack_sums(flips, per, got, wtemp, wtemp_hbm, came_s, sems)
     feat[...] = (sum_ref[...] + dot_tn(picks_ref[...], came_s[...].astype(BF16))).astype(BF16)
     stores.append(Fetch(sems.at[len(flips) :], (feat, feat_hbm)))
     for store in stores:
@@ -468,6 +487,7 @@
     x = feat[0]
     local, width = x.shape
     heads = rel_bias.shape[1]
+    slots = nbr.shape[2]
     doms = lax.axis_size("dom")
     snaps = lax.axis_size("snap")
     ents = local // snaps
@@ -489,12 +509,12 @@
     )
     if not paired:
         pieces = 1
-    dom = lax.axis_index("dom").astype(jnp.int32)
-    snap = lax.axis_index("snap").astype(jnp.int32)
-    place = jnp.stack([snap, dom // 2, dom])
 
     def shape(*dims, dtype=BF16):
         return jax.ShapeDtypeStruct(dims, dtype)
+
+    def vmem(*dims, dtype=BF16):
+        return pltpu.VMEM(dims, dtype)
 
     def hbm(*dims, dtype=BF16):
         return pltpu.HBM(dims, dtype)
@@ -514,37 +534,44 @@
     )(*in_hbm(route, x))
     halo = exchange(tiles.reshape(doms, halo_per, width), "dom").reshape(halo_rows, width)
 
-    load = pl.pallas_call(
-        load_kernel,
-        out_shape=hbm(snaps + 1, ents, width),
-        in_specs=[SMEM, HBM, HBM],
-        out_specs=HBM,
+    edge, proj, x_near, w_near, load = pl.pallas_call(
+        own_kernel,
+        out_shape=(
+            vmem(heads, local, keys, dtype=F32),
+            vmem(local, 3 * width),
+            vmem(local, width),
+            vmem(*w_struct.shape),
+            hbm(snaps + 1, ents, width),
+        ),
+        in_specs=[HBM] * 7,
+        out_specs=(VMEM,) * 4 + (HBM,),
         scratch_shapes=[
+            pltpu.VMEM((slots, local), jnp.int32),
+            pltpu.VMEM((slots, local), jnp.int32),
+            pltpu.VMEM(rel_bias.shape, F32),
             pltpu.VMEM((snaps, ents), jnp.int32),
             pltpu.VMEM((snaps, ents, width), BF16),
             pltpu.VMEM((ents, width), BF16),
-            pltpu.SemaphoreType.DMA((4,)),
+            pltpu.SemaphoreType.DMA((9,)),
         ],
         compiler_params=params(8),
         cost_estimate=pl.CostEstimate(flops=10**9, bytes_accessed=4 * 10**6, transcendentals=0),
-        name="own_load",
-    )(place, *in_hbm(active, cotangent))
-    edges = (nbr[0].T, rel_type[0].T, rel_bias)
+        name="own_rows",
+    )(
+        *in_hbm(nbr[0].T, rel_type[0].T, rel_bias, active, cotangent, x, w_struct),
+    )
     cots = gather_blocks({0: load}, "snap", snaps // 2, 1)
     cots = [cots[m] for m in range(snaps)]
 
     hidden = pl.pallas_call(
         functools.partial(forward_kernel, heads),
         out_shape=shape(local, width),
-        in_specs=[VMEM] * 6,
+        in_specs=[VMEM] * 5,
         out_specs=VMEM,
-        scratch_shapes=[
-            pltpu.VMEM((local, 3 * width), BF16),
-            pltpu.VMEM((keys, 2 * width), BF16),
-        ],
+        scratch_shapes=[pltpu.VMEM((keys, 2 * width), BF16)],
         compiler_params=params(8),
         name="struct_forward",
-    )(x, halo, w_struct, *edges)
+    )(x_near, halo, w_near, proj, edge)
 
     hids = gather_blocks({0: hidden}, "snap", snaps // 2, 1)
     hids = [hids[m] for m in range(snaps)]
@@ -555,16 +582,16 @@
             shape(every, width, dtype=F32 if ents % 16 else BF16),
             shape(local, LANES, dtype=F32),
         ),
-        in_specs=[SMEM] + [VMEM] * snaps,
+        in_specs=[VMEM] * snaps,
         out_specs=(VMEM, VMEM),
         compiler_params=params(8),
         name="cotangents",
-    )(place, *cots)
+    )(*cots)
     *terms, dt_own, cot_own = pl.pallas_call(
         functools.partial(temporal_kernel, snaps, heads, pieces),
         out_shape=(shape(share // pieces, 3 * width),) * pieces
         + (shape(local, 3 * width), shape(local, width)),
-        in_specs=[SMEM] + [VMEM] * (4 + snaps),
+        in_specs=[VMEM] * (4 + snaps),
         out_specs=(VMEM,) * (pieces + 2),
         scratch_shapes=[
             pltpu.VMEM((every, width), BF16),
@@ -583,7 +610,7 @@
         ],
         compiler_params=params(24 if snaps <= 4 else 56),
         name="temporal",
-    )(place, pos_embed, w_temp, ct, act, *hids)
+    )(pos_embed, w_temp, ct, act, *hids)
 
     if paired:
         got = [terms[0]] + [flipped(terms[k], "dom", 2 * k) for k in range(1, pieces)]
@@ -592,10 +619,9 @@
     back, partial = pl.pallas_call(
         functools.partial(backward_kernel, heads),
         out_shape=(shape(halo_rows, width, dtype=F32), shape(local, width, dtype=F32)),
-        in_specs=[VMEM] * 9,
+        in_specs=[VMEM] * 7,
         out_specs=(VMEM, VMEM),
         scratch_shapes=[
-            pltpu.VMEM((local, 3 * width), BF16),
             pltpu.VMEM((keys, 2 * width), BF16),
             pltpu.VMEM((local, width), BF16),
             pltpu.VMEM((keys, 2 * width), BF16),
@@ -603,7 +629,7 @@
         compiler_params=params(16),
         cost_estimate=pl.CostEstimate(flops=2 * 10**9, bytes_accessed=8 * 10**6, transcendentals=0),
         name="struct_backward",
-    )(dt_own, cot_own, x, halo, *edges, w_struct, w_temp)
+    )(dt_own, cot_own, proj, halo, edge, w_near, w_temp)
 
     if not paired:
         total = jnp.sum(got.astype(F32), axis=0).astype(BF16)
@@ -617,20 +643,20 @@
     mine = pl.pallas_call(
         functools.partial(outer_sum_kernel, halo_per),
         out_shape=shape(piece, 4 * width),
-        in_specs=[SMEM] + [VMEM] * (1 + pieces),
+        in_specs=[VMEM] * (1 + pieces),
         out_specs=VMEM,
         compiler_params=params(8),
         name="outer_sum",
-    )(place, back, *got)
+    )(back, *got)
     other = flipped(mine, "dom", 1)
     sums = pl.pallas_call(
         functools.partial(inner_sum_kernel, halo_per),
         out_shape=(shape(piece, 3 * width + lanes),) * pieces,
-        in_specs=[SMEM] + [VMEM] * 3,
+        in_specs=[VMEM] * 3,
         out_specs=(VMEM,) * pieces,
         compiler_params=params(8),
         name="inner_sum",
-    )(place, back, mine, other)
+    )(back, mine, other)
     sums = [sums[0]] + [flipped(sums[k], "dom", 2 * k) for k in range(1, pieces)]
     soon, late = list(range(pieces // 2)), list(range(pieces // 2, pieces))
     partial, picks, grad_wtemp = pl.pallas_call(
@@ -640,7 +666,7 @@
             shape(halo_rows, local),
             hbm(share, 3 * width, dtype=F32),
         ),
-        in_specs=[SMEM, SMEM] + [VMEM] * (1 + len(soon)),
+        in_specs=[SMEM] + [VMEM] * (1 + len(soon)),
         out_specs=(VMEM, VMEM, HBM),
         scratch_shapes=[
             pltpu.VMEM((len(soon), piece, 3 * width), F32),
@@ -649,11 +675,11 @@
         ],
         compiler_params=params(8),
         name="early_sums",
-    )(place, route, partial, *[sums[k] for k in soon])
+    )(route, partial, *[sums[k] for k in soon])
     grad_feat, grad_wtemp = pl.pallas_call(
         functools.partial(last_kernel, late, halo_per),
         out_shape=(hbm(local, width), hbm(share, 3 * width, dtype=F32)),
-        in_specs=[SMEM] + [VMEM] * 2 + [HBM] + [VMEM] * len(late),
+        in_specs=[VMEM] * 2 + [HBM] + [VMEM] * len(late),
         out_specs=(HBM, HBM),
         scratch_shapes=[
             pltpu.VMEM((local, width), BF16),
@@ -661,10 +687,10 @@
             pltpu.VMEM((halo_rows, width), F32),
             pltpu.SemaphoreType.DMA((len(late) + 1,)),
         ],
-        input_output_aliases={3: 1},
+        input_output_aliases={2: 1},
         compiler_params=params(8),
         name="last_sums",
-    )(place, picks, partial, *in_hbm(grad_wtemp), *[sums[k] for k in late])
+    )(picks, partial, *in_hbm(grad_wtemp), *[sums[k] for k in late])
     return (grad_feat[None], grad_wtemp)
 
 

time: 60 us -> 57.5 us (0.958)
  Pallas kernels: 20.8 us -> 17.4 us
  waiting for transfers between devices: 17.2 us -> 18.4 us
    ppermute x13, waiting for transfers between devices: 14.2 us -> 15.4 us  [flipped(): return lax.ppermute(block, axis, [(i, i ^ flip) for i in range(count)])]
    pallas_call x1, Pallas kernels: 0.97 us -> 0.06 us  [per_device(): pl.pallas_call(cotangent_kernel, out_shape=(shape(every, width, dtype=F32...]
  transfers between devices with their start and end apart: 14 -> 14, of which waited for: 7 -> 7; matrix products, arithmetic and copies ran while one was open for 0% -> 0% of each run, Pallas kernels for 20% -> 18%
where the time goes in v6:
time: 57.5 us; the launch traced here: 57.3 us
  starting transfers between devices  20.7 us (36%)
  waiting for transfers between devices  18.4 us (32%)
  Pallas kernels  17.4 us (30%)
  between operations  0.73 us (1%)
    ppermute x13, waiting for transfers between devices, flipped(): return lax.ppermute(block, axis, [(i, i ^ flip) for i in range(count)])  15.4 us
    ppermute x13, starting transfers between devices, flipped(): return lax.ppermute(block, axis, [(i, i ^ flip) for i in range(count)])  13.4 us
    all_to_all x1, starting transfers between devices, exchange(): return lax.all_to_all(tiles, axis, split_axis=0, concat_axis=0, tiled=True)  7.27 us
    pallas_call x1, Pallas kernels, per_device(): pl.pallas_call(functools.partial(backward_kernel, heads), out_shape=(shap...  4.87 us
    pallas_call x1, Pallas kernels, per_device(): pl.pallas_call(functools.partial(temporal_kernel, snaps, heads, pieces),...  4.2 us
    all_to_all x1, waiting for transfers between devices, exchange(): return lax.all_to_all(tiles, axis, split_axis=0, concat_axis=0, tiled=True)  2.97 us
    pallas_call x1, Pallas kernels, per_device(): pl.pallas_call(own_kernel, out_shape=(vmem(heads, local, keys, dtype=F32)...  2.35 us
    pallas_call x1, Pallas kernels, per_device(): pl.pallas_call(functools.partial(forward_kernel, heads), out_shape=shape(...  1.76 us
  transfers between devices with their start and end apart: 14, of which 7 were waited for; matrix products, arithmetic and copies ran while one was open for 0% of the time, Pallas kernels for 18%

profile of v6, /device:TPU:0, one launch (start us, length us, event | category | flops | bytes accessed | tf_op | source)
XLA Modules:
  0.0 57.3 jit_solution(16678811855487545941)
XLA Ops:
  0.6 1.7 %halo_tiles.1 = bf16[64,512]{1,0:T(8,128)(2,1)} custom-call(s32[8,8]{1,0:T(8,128)} %bitcast.13, bf16[128,512]{1,0:T(8,128)(2,1)} %bitcast.15), custom_call_target="tpu_custom_call" | custom-call | tf_op jit(solution)/shard_map/halo_tiles/pallas_call | solution.py:522
  2.3 7.3 %all-to-all-start = ((bf16[8,8,512]{2,1,0:T(8,128)(2,1)}), bf16[8,8,512]{2,1,0:T(8,128)(2,1)S(1)}, u32[]{:S(2)}, u32[]{:S(2)}) async-start(bf16[8,8,512]{2,1,0:T(8,128)(2,1)} %bitcast.6), calls=%async_computation | async-start | bytes 131072 | tf_op jit(solution)/shard_map/all_to_all | solution.py:476
  9.6 2.4 %own_rows.1 = (f32[8,128,256]{2,1,0:T(8,128)S(1)}, bf16[128,1536]{1,0:T(8,128)(2,1)S(1)}, bf16[128,512]{1,0:T(8,128)(2,1)S(1)}, bf16[512,1536]{1,0:T(8,128)(2,1)S(1)}, bf16[5,32,512]{2,1,0:T(8,128)(2,1)}) custom-call(s32[8,128]{1,0:T(8,128)} %bitcast.18, s32[8,128]{1,0:T(8,128)} %bitcast.19, f32[4,8]{1,0:T(4,128)} %bias_hbm.1, s32[4,32]{1,0:T(4,128)} %act_hbm.1, ...), custom_call_target="tpu_custom_call" | custom-call | flops 1000000000 | bytes 4000000 | tf_op jit(solution)/shard_map/own_rows/pallas_call | solution.py:537
  12.0 1.6 %collective-permute-start.1 = (bf16[5,32,512]{2,1,0:T(8,128)(2,1)}, bf16[5,32,512]{2,1,0:T(8,128)(2,1)S(1)}, u32[]{:S(2)}, u32[]{:S(2)}) collective-permute-start(bf16[5,32,512]{2,1,0:T(8,128)(2,1)} %get-tuple-element.26.refs_0_), channel_id=1, source_target_pairs={{0,2},{1,3},{2,0},{3,1},{4,6},{5,7},{6,4},{7,5},{8,10},{9,11},{10,... | collective-permute-start | bytes 491528 | tf_op jit(solution)/shard_map/ppermute | solution.py:481
  13.5 3.0 %all-to-all-done = bf16[8,8,512]{2,1,0:T(8,128)(2,1)S(1)} async-done(((bf16[8,8,512]{2,1,0:T(8,128)(2,1)}), bf16[8,8,512]{2,1,0:T(8,128)(2,1)S(1)}, u32[]{:S(2)}, u32[]{:S(2)}) %all-to-all-start) | async-done | bytes 65568 | tf_op jit(solution)/shard_map/all_to_all | solution.py:476
  16.5 1.8 %struct_forward.1.refs_0_ = bf16[128,512]{1,0:T(8,128)(2,1)S(1)} custom-call(bf16[128,512]{1,0:T(8,128)(2,1)S(1)} %get-tuple-element.29.x, bf16[64,512]{1,0:T(8,128)(2,1)S(1)} %bitcast.11, bf16[512,1536]{1,0:T(8,128)(2,1)S(1)} %get-tuple-element.30.w.ws, bf16[128,1536]{1,0:T(8,128)(2,1)S(1)} %get-tuple-element.31.proj, f32[8,128,256]{2,1,0:T(8,128)S(1)} %get-tuple-element.32.edge), custom_call_target="tpu_custom_call" | custom-call | tf_op jit(solution)/shard_map/struct_forward/pallas_call | solution.py:566
  18.3 1.6 %collective-permute-start.4 = (bf16[128,512]{1,0:T(8,128)(2,1)S(1)}, bf16[128,512]{1,0:T(8,128)(2,1)S(1)}, u32[]{:S(2)}, u32[]{:S(2)}) collective-permute-start(bf16[128,512]{1,0:T(8,128)(2,1)S(1)} %struct_forward.1.refs_0_), channel_id=1, source_target_pairs={{0,2},{1,3},{2,0},{3,1},{4,6},{5,7},{6,4},{7,5},{8,10},{9,11},{10,... | collective-permute-start | bytes 393224 | tf_op jit(solution)/shard_map/ppermute | solution.py:481
  19.9 0.0 collective-permute-start
  19.9 0.0 collective-permute-done.1.refs_2_
  19.9 0.5 collective-permute-start.2
  20.4 0.1 collective-permute-start.3
  20.5 2.9 %collective-permute-done.4.refs_2_ = bf16[128,512]{1,0:T(8,128)(2,1)S(1)} collective-permute-done((bf16[128,512]{1,0:T(8,128)(2,1)S(1)}, bf16[128,512]{1,0:T(8,128)(2,1)S(1)}, u32[]{:S(2)}, u32[]{:S(2)}) %collective-permute-start.4) | collective-permute-done | bytes 131104 | tf_op jit(solution)/shard_map/ppermute | solution.py:481
  23.3 0.0 collective-permute-start.5
  23.3 0.0 collective-permute-done.2.refs_3_
  23.3 0.1 cotangents.1
  23.4 1.3 %collective-permute-done.5.refs_3_ = bf16[128,512]{1,0:T(8,128)(2,1)S(1)} collective-permute-done((bf16[128,512]{1,0:T(8,128)(2,1)S(1)}, bf16[128,512]{1,0:T(8,128)(2,1)S(1)}, u32[]{:S(2)}, u32[]{:S(2)}) %collective-permute-start.5) | collective-permute-done | bytes 131104 | tf_op jit(solution)/shard_map/ppermute | solution.py:481
  24.7 4.2 %temporal.1 = (bf16[32,1536]{1,0:T(8,128)(2,1)S(1)}, bf16[32,1536]{1,0:T(8,128)(2,1)S(1)}, bf16[32,1536]{1,0:T(8,128)(2,1)S(1)}, bf16[32,1536]{1,0:T(8,128)(2,1)...) custom-call(bf16[4,512]{1,0:T(4,128)(2,1)S(1)} %copy-done.3, bf16[512,1536]{1,0:T(8,128)(2,1)S(1)} %copy-done, ...), custom_call_target="tpu_custom_call" | custom-call | tf_op jit(solution)/shard_map/temporal/pallas_call | solution.py:590
  28.9 0.3 collective-permute-start.6
  29.2 1.3 %collective-permute-start.7 = (bf16[32,1536]{1,0:T(8,128)(2,1)S(1)}, bf16[32,1536]{1,0:T(8,128)(2,1)S(1)}, u32[]{:S(2)}, u32[]{:S(2)}) collective-permute-start(bf16[32,1536]{1,0:T(8,128)(2,1)S(1)} %get-tuple-element.39), channel_id=1, source_target_pairs={{0,16},{4,20},{8,24},{12,28},{16,0},{20,4},{24,8},{28,12},{1,17},{... | collective-permute-start | bytes 294920 | tf_op jit(solution)/shard_map/ppermute | solution.py:481
  30.4 2.9 %collective-permute-start.8 = (bf16[32,1536]{1,0:T(8,128)(2,1)S(1)}, bf16[32,1536]{1,0:T(8,128)(2,1)S(1)}, u32[]{:S(2)}, u32[]{:S(2)}) collective-permute-start(bf16[32,1536]{1,0:T(8,128)(2,1)S(1)} %get-tuple-element.40), channel_id=1, source_target_pairs={{0,24},{4,28},{8,16},{12,20},{16,8},{20,12},{24,0},{28,4},{1,25},{... | collective-permute-start | bytes 294920 | tf_op jit(solution)/shard_map/ppermute | solution.py:481
  33.3 4.9 %struct_backward.1 = (f32[64,512]{1,0:T(8,128)S(1)}, f32[128,512]{1,0:T(8,128)S(1)}) custom-call(bf16[128,1536]{1,0:T(8,128)(2,1)S(1)} %get-tuple-element.33.dt, bf16[128,512]{1,0:T(8,128)(2,1)S(1)} %get-tuple-element.34.cot, bf16[128,1536]{1,0:T(8,128)(2,1)S(1)} %get-tuple-element.31.proj, bf16[64,512]{1,0:T(8,128)(2,1)S(1)} %bitcast.12, ...), custom_call_target="tpu_custom_call" | custom-call | flops 2000000000 | bytes 8000000 | tf_op jit(solution)/shard_map/struct_backward/pallas_call | solution.py:619
  38.2 1.8 %collective-permute-done.7.refs_2_ = bf16[32,1536]{1,0:T(8,128)(2,1)S(1)} collective-permute-done((bf16[32,1536]{1,0:T(8,128)(2,1)S(1)}, bf16[32,1536]{1,0:T(8,128)(2,1)S(1)}, u32[]{:S(2)}, u32[]{:S(2)}) %collective-permute-start.7) | collective-permute-done | bytes 98336 | tf_op jit(solution)/shard_map/ppermute | solution.py:481
  40.0 0.1 outer_sum.1.mine_ref
  40.0 0.8 %collective-permute-start.9 = (bf16[32,2048]{1,0:T(8,128)(2,1)S(1)}, bf16[32,2048]{1,0:T(8,128)(2,1)S(1)}, u32[]{:S(2)}, u32[]{:S(2)}) collective-permute-start(bf16[32,2048]{1,0:T(8,128)(2,1)S(1)} %outer_sum.1.mine_ref), channel_id=1, source_target_pairs={{0,4},{4,0},{8,12},{12,8},{16,20},{20,16},{24,28},{28,24},{1,5},{5... | collective-permute-start | bytes 393224 | tf_op jit(solution)/shard_map/ppermute | solution.py:481
  40.8 4.2 %collective-permute-done.9.other_ref = bf16[32,2048]{1,0:T(8,128)(2,1)S(1)} collective-permute-done((bf16[32,2048]{1,0:T(8,128)(2,1)S(1)}, bf16[32,2048]{1,0:T(8,128)(2,1)S(1)}, u32[]{:S(2)}, u32[]{:S(2)}) %collective-permute-start.9) | collective-permute-done | bytes 131104 | tf_op jit(solution)/shard_map/ppermute | solution.py:481
  45.1 1.8 %collective-permute-start.10 = (bf16[32,1792]{1,0:T(8,128)(2,1)S(1)}, bf16[32,1792]{1,0:T(8,128)(2,1)S(1)}, u32[]{:S(2)}, u32[]{:S(2)}) collective-permute-start(bf16[32,1792]{1,0:T(8,128)(2,1)S(1)} %get-tuple-element.42), channel_id=1, source_target_pairs={{0,8},{4,12},{8,0},{12,4},{16,24},{20,28},{24,16},{28,20},{1,9},{5... | collective-permute-start | bytes 344072 | tf_op jit(solution)/shard_map/ppermute | solution.py:481
  46.9 0.5 collective-permute-start.11
  47.4 2.2 %collective-permute-start.12 = (bf16[32,1792]{1,0:T(8,128)(2,1)S(1)}, bf16[32,1792]{1,0:T(8,128)(2,1)S(1)}, u32[]{:S(2)}, u32[]{:S(2)}) collective-permute-start(bf16[32,1792]{1,0:T(8,128)(2,1)S(1)} %get-tuple-element.47), channel_id=1, source_target_pairs={{0,24},{4,28},{8,16},{12,20},{16,8},{20,12},{24,0},{28,4},{1,25},{... | collective-permute-start | bytes 344072 | tf_op jit(solution)/shard_map/ppermute | solution.py:481
  49.6 2.9 %collective-permute-done.10.refs_1_ = bf16[32,1792]{1,0:T(8,128)(2,1)S(1)} collective-permute-done((bf16[32,1792]{1,0:T(8,128)(2,1)S(1)}, bf16[32,1792]{1,0:T(8,128)(2,1)S(1)}, u32[]{:S(2)}, u32[]{:S(2)}) %collective-permute-start.10) | collective-permute-done | bytes 114720 | tf_op jit(solution)/shard_map/ppermute | solution.py:481
  52.5 1.5 %early_sums.1 = (f32[128,512]{1,0:T(8,128)S(1)}, bf16[64,128]{1,0:T(8,128)(2,1)S(1)}, f32[128,1536]{1,0:T(8,128)}) custom-call(s32[8,8]{1,0:T(8,128)S(1)} %bitcast.14, f32[128,512]{1,0:T(8,128)S(1)} %get-tuple-element.35.part_ref, bf16[32,1792]{1,0:T(8,128)(2,1)S(1)} %get-tuple-element.41.refs_0_, bf16[32,1792]{1,0:T(8,128)(2,1)S(1)} %collective-permute-done.10.refs_1_), custom_call_target="tpu_custom_call" | custom-call | tf_op jit(solution)/shard_map/early_sums/pallas_call | solution.py:662
  54.0 2.4 %collective-permute-done.11.refs_0_ = bf16[32,1792]{1,0:T(8,128)(2,1)S(1)} collective-permute-done((bf16[32,1792]{1,0:T(8,128)(2,1)S(1)}, bf16[32,1792]{1,0:T(8,128)(2,1)S(1)}, u32[]{:S(2)}, u32[]{:S(2)}) %collective-permute-start.11) | collective-permute-done | bytes 114720 | tf_op jit(solution)/shard_map/ppermute | solution.py:481
  56.3 0.9 %last_sums.1 = (bf16[128,512]{1,0:T(8,128)(2,1)}, f32[128,1536]{1,0:T(8,128)}) custom-call(bf16[64,128]{1,0:T(8,128)(2,1)S(1)} %get-tuple-element.43.picks_ref, f32[128,512]{1,0:T(8,128)S(1)} %get-tuple-element.44.sum_ref, f32[128,1536]{1,0:T(8,128)} %get-tuple-element.45._, ...), custom_call_target="tpu_custom_call", output_to_operand_aliasing={{1}: (2, {})} | custom-call | tf_op jit(solution)/shard_map/last_sums/pallas_call | solution.py:679
  (14 shorter events, 0.1 us)
Async XLA Ops:
  2.3 14.2 %all-to-all-start = ((bf16[8,8,512]{2,1,0:T(8,128)(2,1)}), bf16[8,8,512]{2,1,0:T(8,128)(2,1)S(1)}, u32[]{:S(2)}, u32[]{:S(2)}) async-start(bf16[8,8,512]{2,1,0:T(8,128)(2,1)} %bitcast.6), calls=%async_computation | async-start | bytes 131072 | tf_op jit(solution)/shard_map/all_to_all | solution.py:476
  12.0 7.9 %collective-permute-start.1 = (bf16[5,32,512]{2,1,0:T(8,128)(2,1)}, bf16[5,32,512]{2,1,0:T(8,128)(2,1)S(1)}, u32[]{:S(2)}, u32[]{:S(2)}) collective-permute-start(bf16[5,32,512]{2,1,0:T(8,128)(2,1)} %get-tuple-element.26.refs_0_), channel_id=1, source_target_pairs={{0,2},{1,3},{2,0},{3,1},{4,6},{5,7},{6,4},{7,5},{8,10},{9,11},{10,... | collective-permute-start | bytes 491528 | tf_op jit(solution)/shard_map/ppermute | solution.py:481
  16.5 3.4 %copy-start.1 = (bf16[5,32,512]{2,1,0:T(8,128)(2,1)S(1)}, bf16[5,32,512]{2,1,0:T(8,128)(2,1)}, u32[]{:S(2)}) copy-start(bf16[5,32,512]{2,1,0:T(8,128)(2,1)} %get-tuple-element.26.refs_0_) | copy-start | bytes 491524
  16.5 8.2 %copy-start = (bf16[512,1536]{1,0:T(8,128)(2,1)S(1)}, bf16[512,1536]{1,0:T(8,128)(2,1)}, u32[]{:S(2)}) copy-start(bf16[512,1536]{1,0:T(8,128)(2,1)} %wt.1) | copy-start | bytes 4718596
  16.5 8.2 %copy-start.3 = (bf16[4,512]{1,0:T(4,128)(2,1)S(1)}, bf16[4,512]{1,0:T(4,128)(2,1)}, u32[]{:S(2)}) copy-start(bf16[4,512]{1,0:T(4,128)(2,1)} %pos_ref.1) | copy-start | bytes 12292
  18.3 5.0 %collective-permute-start.4 = (bf16[128,512]{1,0:T(8,128)(2,1)S(1)}, bf16[128,512]{1,0:T(8,128)(2,1)S(1)}, u32[]{:S(2)}, u32[]{:S(2)}) collective-permute-start(bf16[128,512]{1,0:T(8,128)(2,1)S(1)} %struct_forward.1.refs_0_), channel_id=1, source_target_pairs={{0,2},{1,3},{2,0},{3,1},{4,6},{5,7},{6,4},{7,5},{8,10},{9,11},{10,... | collective-permute-start | bytes 393224 | tf_op jit(solution)/shard_map/ppermute | solution.py:481
  19.9 3.5 %collective-permute-start = (bf16[5,32,512]{2,1,0:T(8,128)(2,1)S(1)}, bf16[5,32,512]{2,1,0:T(8,128)(2,1)S(1)}, u32[]{:S(2)}, u32[]{:S(2)}) collective-permute-start(bf16[5,32,512]{2,1,0:T(8,128)(2,1)S(1)} %copy-done.1), channel_id=1, source_target_pairs={{0,1},{1,0},{2,3},{3,2},{4,5},{5,4},{6,7},{7,6},{8,9},{9,8},{10,11... | collective-permute-start | bytes 491528 | tf_op jit(solution)/shard_map/ppermute | solution.py:481
  19.9 3.4 %collective-permute-start.2 = (bf16[5,32,512]{2,1,0:T(8,128)(2,1)S(1)}, bf16[5,32,512]{2,1,0:T(8,128)(2,1)S(1)}, u32[]{:S(2)}, u32[]{:S(2)}) collective-permute-start(bf16[5,32,512]{2,1,0:T(8,128)(2,1)S(1)} %collective-permute-done.1.refs_2_), channel_id=1, source_target_pairs={{0,1},{1,0},{2,3},{3,2},{4,5},{5,4},{6,7},{7,6},{8,9},{9,8},{10,11... | collective-permute-start | bytes 491528 | tf_op jit(solution)/shard_map/ppermute | solution.py:481
  20.4 3.0 %collective-permute-start.3 = (bf16[128,512]{1,0:T(8,128)(2,1)S(1)}, bf16[128,512]{1,0:T(8,128)(2,1)S(1)}, u32[]{:S(2)}, u32[]{:S(2)}) collective-permute-start(bf16[128,512]{1,0:T(8,128)(2,1)S(1)} %struct_forward.1.refs_0_), channel_id=1, source_target_pairs={{0,1},{1,0},{2,3},{3,2},{4,5},{5,4},{6,7},{7,6},{8,9},{9,8},{10,11... | collective-permute-start | bytes 393224 | tf_op jit(solution)/shard_map/ppermute | solution.py:481
  23.3 1.3 %collective-permute-start.5 = (bf16[128,512]{1,0:T(8,128)(2,1)S(1)}, bf16[128,512]{1,0:T(8,128)(2,1)S(1)}, u32[]{:S(2)}, u32[]{:S(2)}) collective-permute-start(bf16[128,512]{1,0:T(8,128)(2,1)S(1)} %collective-permute-done.4.refs_2_), channel_id=1, source_target_pairs={{0,1},{1,0},{2,3},{3,2},{4,5},{5,4},{6,7},{7,6},{8,9},{9,8},{10,11... | collective-permute-start | bytes 393224 | tf_op jit(solution)/shard_map/ppermute | solution.py:481
  28.9 9.3 %collective-permute-start.6 = (bf16[32,1536]{1,0:T(8,128)(2,1)S(1)}, bf16[32,1536]{1,0:T(8,128)(2,1)S(1)}, u32[]{:S(2)}, u32[]{:S(2)}) collective-permute-start(bf16[32,1536]{1,0:T(8,128)(2,1)S(1)} %get-tuple-element.38), channel_id=1, source_target_pairs={{0,8},{4,12},{8,0},{12,4},{16,24},{20,28},{24,16},{28,20},{1,9},{5... | collective-permute-start | bytes 294920 | tf_op jit(solution)/shard_map/ppermute | solution.py:481
  29.2 10.8 %collective-permute-start.7 = (bf16[32,1536]{1,0:T(8,128)(2,1)S(1)}, bf16[32,1536]{1,0:T(8,128)(2,1)S(1)}, u32[]{:S(2)}, u32[]{:S(2)}) collective-permute-start(bf16[32,1536]{1,0:T(8,128)(2,1)S(1)} %get-tuple-element.39), channel_id=1, source_target_pairs={{0,16},{4,20},{8,24},{12,28},{16,0},{20,4},{24,8},{28,12},{1,17},{... | collective-permute-start | bytes 294920 | tf_op jit(solution)/shard_map/ppermute | solution.py:481
  30.4 9.5 %collective-permute-start.8 = (bf16[32,1536]{1,0:T(8,128)(2,1)S(1)}, bf16[32,1536]{1,0:T(8,128)(2,1)S(1)}, u32[]{:S(2)}, u32[]{:S(2)}) collective-permute-start(bf16[32,1536]{1,0:T(8,128)(2,1)S(1)} %get-tuple-element.40), channel_id=1, source_target_pairs={{0,24},{4,28},{8,16},{12,20},{16,8},{20,12},{24,0},{28,4},{1,25},{... | collective-permute-start | bytes 294920 | tf_op jit(solution)/shard_map/ppermute | solution.py:481
  33.3 19.1 %copy-start.2 = (s32[1,1,8,8]{3,2,1,0:T(8,128)S(1)}, s32[1,1,8,8]{3,2,1,0:T(8,128)}, u32[]{:S(2)}) copy-start(s32[1,1,8,8]{3,2,1,0:T(8,128)} %param.17) | copy-start | bytes 772
  40.0 5.0 %collective-permute-start.9 = (bf16[32,2048]{1,0:T(8,128)(2,1)S(1)}, bf16[32,2048]{1,0:T(8,128)(2,1)S(1)}, u32[]{:S(2)}, u32[]{:S(2)}) collective-permute-start(bf16[32,2048]{1,0:T(8,128)(2,1)S(1)} %outer_sum.1.mine_ref), channel_id=1, source_target_pairs={{0,4},{4,0},{8,12},{12,8},{16,20},{20,16},{24,28},{28,24},{1,5},{5... | collective-permute-start | bytes 393224 | tf_op jit(solution)/shard_map/ppermute | solution.py:481
  45.1 7.4 %collective-permute-start.10 = (bf16[32,1792]{1,0:T(8,128)(2,1)S(1)}, bf16[32,1792]{1,0:T(8,128)(2,1)S(1)}, u32[]{:S(2)}, u32[]{:S(2)}) collective-permute-start(bf16[32,1792]{1,0:T(8,128)(2,1)S(1)} %get-tuple-element.42), channel_id=1, source_target_pairs={{0,8},{4,12},{8,0},{12,4},{16,24},{20,28},{24,16},{28,20},{1,9},{5... | collective-permute-start | bytes 344072 | tf_op jit(solution)/shard_map/ppermute | solution.py:481
  46.9 9.4 %collective-permute-start.11 = (bf16[32,1792]{1,0:T(8,128)(2,1)S(1)}, bf16[32,1792]{1,0:T(8,128)(2,1)S(1)}, u32[]{:S(2)}, u32[]{:S(2)}) collective-permute-start(bf16[32,1792]{1,0:T(8,128)(2,1)S(1)} %get-tuple-element.46), channel_id=1, source_target_pairs={{0,16},{4,20},{8,24},{12,28},{16,0},{20,4},{24,8},{28,12},{1,17},{... | collective-permute-start | bytes 344072 | tf_op jit(solution)/shard_map/ppermute | solution.py:481
  47.4 9.0 %collective-permute-start.12 = (bf16[32,1792]{1,0:T(8,128)(2,1)S(1)}, bf16[32,1792]{1,0:T(8,128)(2,1)S(1)}, u32[]{:S(2)}, u32[]{:S(2)}) collective-permute-start(bf16[32,1792]{1,0:T(8,128)(2,1)S(1)} %get-tuple-element.47), channel_id=1, source_target_pairs={{0,24},{4,28},{8,16},{12,20},{16,8},{20,12},{24,0},{28,4},{1,25},{... | collective-permute-start | bytes 344072 | tf_op jit(solution)/shard_map/ppermute | solution.py:481

commit v7 on v6

--- a/solution.py
+++ b/solution.py
@@ -613,7 +613,7 @@
     )(pos_embed, w_temp, ct, act, *hids)
 
     if paired:
-        got = [terms[0]] + [flipped(terms[k], "dom", 2 * k) for k in range(1, pieces)]
+        got = [terms[0]] + [flipped(terms[k], "dom", 2 * k) for k in range(pieces - 1, 0, -1)]
     else:
         got = exchange(terms[0].reshape(doms, share // doms, 3 * width), "dom")
     back, partial = pl.pallas_call(
@@ -657,8 +657,9 @@
         compiler_params=params(8),
         name="inner_sum",
     )(back, mine, other)
-    sums = [sums[0]] + [flipped(sums[k], "dom", 2 * k) for k in range(1, pieces)]
-    soon, late = list(range(pieces // 2)), list(range(pieces // 2, pieces))
+    order = [*range(2, pieces), 1]
+    sums = {0: sums[0]} | {k: flipped(sums[k], "dom", 2 * k) for k in order}
+    soon, late = [0], order
     partial, picks, grad_wtemp = pl.pallas_call(
         functools.partial(early_kernel, soon, halo_per),
         out_shape=(

time: 57.5 us -> 56.5 us (0.983)
  starting transfers between devices: 20.7 us -> 20.1 us
    ppermute x13, starting transfers between devices: 13.4 us -> 12.8 us  [flipped(): return lax.ppermute(block, axis, [(i, i ^ flip) for i in range(count)])]
  transfers between devices with their start and end apart: 14 -> 14, of which waited for: 7 -> 7; matrix products, arithmetic and copies ran while one was open for 0% -> 0% of each run, Pallas kernels for 18% -> 19%
where the time goes in v7:
time: 56.5 us; the launch traced here: 56.2 us
  starting transfers between devices  20.1 us (36%)
  waiting for transfers between devices  18 us (32%)
  Pallas kernels  17.4 us (31%)
  between operations  0.73 us (1%)
    ppermute x13, waiting for transfers between devices, flipped(): return lax.ppermute(block, axis, [(i, i ^ flip) for i in range(count)])  15 us
    ppermute x13, starting transfers between devices, flipped(): return lax.ppermute(block, axis, [(i, i ^ flip) for i in range(count)])  12.8 us
    all_to_all x1, starting transfers between devices, exchange(): return lax.all_to_all(tiles, axis, split_axis=0, concat_axis=0, tiled=True)  7.27 us
    pallas_call x1, Pallas kernels, per_device(): pl.pallas_call(functools.partial(backward_kernel, heads), out_shape=(shap...  4.87 us
    pallas_call x1, Pallas kernels, per_device(): pl.pallas_call(functools.partial(temporal_kernel, snaps, heads, pieces),...  4.2 us
    all_to_all x1, waiting for transfers between devices, exchange(): return lax.all_to_all(tiles, axis, split_axis=0, concat_axis=0, tiled=True)  2.97 us
    pallas_call x1, Pallas kernels, per_device(): pl.pallas_call(own_kernel, out_shape=(vmem(heads, local, keys, dtype=F32)...  2.35 us
    pallas_call x1, Pallas kernels, per_device(): pl.pallas_call(functools.partial(forward_kernel, heads), out_shape=shape(...  1.76 us
  transfers between devices with their start and end apart: 14, of which 7 were waited for; matrix products, arithmetic and copies ran while one was open for 0% of the time, Pallas kernels for 19%

profile of v7, /device:TPU:0, one launch (start us, length us, event | category | flops | bytes accessed | tf_op | source)
XLA Modules:
  0.0 56.2 jit_solution(10108367869026194373)
XLA Ops:
  0.6 1.7 %halo_tiles.1 = bf16[64,512]{1,0:T(8,128)(2,1)} custom-call(s32[8,8]{1,0:T(8,128)} %bitcast.13, bf16[128,512]{1,0:T(8,128)(2,1)} %bitcast.15), custom_call_target="tpu_custom_call" | custom-call | tf_op jit(solution)/shard_map/halo_tiles/pallas_call | solution.py:522
  2.3 7.3 %all-to-all-start = ((bf16[8,8,512]{2,1,0:T(8,128)(2,1)}), bf16[8,8,512]{2,1,0:T(8,128)(2,1)S(1)}, u32[]{:S(2)}, u32[]{:S(2)}) async-start(bf16[8,8,512]{2,1,0:T(8,128)(2,1)} %bitcast.6), calls=%async_computation | async-start | bytes 131072 | tf_op jit(solution)/shard_map/all_to_all | solution.py:476
  9.6 2.4 %own_rows.1 = (f32[8,128,256]{2,1,0:T(8,128)S(1)}, bf16[128,1536]{1,0:T(8,128)(2,1)S(1)}, bf16[128,512]{1,0:T(8,128)(2,1)S(1)}, bf16[512,1536]{1,0:T(8,128)(2,1)S(1)}, bf16[5,32,512]{2,1,0:T(8,128)(2,1)}) custom-call(s32[8,128]{1,0:T(8,128)} %bitcast.18, s32[8,128]{1,0:T(8,128)} %bitcast.19, f32[4,8]{1,0:T(4,128)} %bias_hbm.1, s32[4,32]{1,0:T(4,128)} %act_hbm.1, ...), custom_call_target="tpu_custom_call" | custom-call | flops 1000000000 | bytes 4000000 | tf_op jit(solution)/shard_map/own_rows/pallas_call | solution.py:537
  12.0 1.6 %collective-permute-start.1 = (bf16[5,32,512]{2,1,0:T(8,128)(2,1)}, bf16[5,32,512]{2,1,0:T(8,128)(2,1)S(1)}, u32[]{:S(2)}, u32[]{:S(2)}) collective-permute-start(bf16[5,32,512]{2,1,0:T(8,128)(2,1)} %get-tuple-element.26.refs_0_), channel_id=1, source_target_pairs={{0,2},{1,3},{2,0},{3,1},{4,6},{5,7},{6,4},{7,5},{8,10},{9,11},{10,... | collective-permute-start | bytes 491528 | tf_op jit(solution)/shard_map/ppermute | solution.py:481
  13.5 3.0 %all-to-all-done = bf16[8,8,512]{2,1,0:T(8,128)(2,1)S(1)} async-done(((bf16[8,8,512]{2,1,0:T(8,128)(2,1)}), bf16[8,8,512]{2,1,0:T(8,128)(2,1)S(1)}, u32[]{:S(2)}, u32[]{:S(2)}) %all-to-all-start) | async-done | bytes 65568 | tf_op jit(solution)/shard_map/all_to_all | solution.py:476
  16.5 1.8 %struct_forward.1.refs_0_ = bf16[128,512]{1,0:T(8,128)(2,1)S(1)} custom-call(bf16[128,512]{1,0:T(8,128)(2,1)S(1)} %get-tuple-element.29.x, bf16[64,512]{1,0:T(8,128)(2,1)S(1)} %bitcast.11, bf16[512,1536]{1,0:T(8,128)(2,1)S(1)} %get-tuple-element.30.w.ws, bf16[128,1536]{1,0:T(8,128)(2,1)S(1)} %get-tuple-element.31.proj, f32[8,128,256]{2,1,0:T(8,128)S(1)} %get-tuple-element.32.edge), custom_call_target="tpu_custom_call" | custom-call | tf_op jit(solution)/shard_map/struct_forward/pallas_call | solution.py:566
  18.3 1.6 %collective-permute-start.4 = (bf16[128,512]{1,0:T(8,128)(2,1)S(1)}, bf16[128,512]{1,0:T(8,128)(2,1)S(1)}, u32[]{:S(2)}, u32[]{:S(2)}) collective-permute-start(bf16[128,512]{1,0:T(8,128)(2,1)S(1)} %struct_forward.1.refs_0_), channel_id=1, source_target_pairs={{0,2},{1,3},{2,0},{3,1},{4,6},{5,7},{6,4},{7,5},{8,10},{9,11},{10,... | collective-permute-start | bytes 393224 | tf_op jit(solution)/shard_map/ppermute | solution.py:481
  19.9 0.0 collective-permute-start
  19.9 0.0 collective-permute-done.1.refs_2_
  19.9 0.5 collective-permute-start.2
  20.4 0.1 collective-permute-start.3
  20.5 2.9 %collective-permute-done.4.refs_2_ = bf16[128,512]{1,0:T(8,128)(2,1)S(1)} collective-permute-done((bf16[128,512]{1,0:T(8,128)(2,1)S(1)}, bf16[128,512]{1,0:T(8,128)(2,1)S(1)}, u32[]{:S(2)}, u32[]{:S(2)}) %collective-permute-start.4) | collective-permute-done | bytes 131104 | tf_op jit(solution)/shard_map/ppermute | solution.py:481
  23.3 0.0 collective-permute-start.5
  23.3 0.0 collective-permute-done.refs_1_
  23.3 0.1 cotangents.1
  23.4 1.3 %collective-permute-done.5.refs_3_ = bf16[128,512]{1,0:T(8,128)(2,1)S(1)} collective-permute-done((bf16[128,512]{1,0:T(8,128)(2,1)S(1)}, bf16[128,512]{1,0:T(8,128)(2,1)S(1)}, u32[]{:S(2)}, u32[]{:S(2)}) %collective-permute-start.5) | collective-permute-done | bytes 131104 | tf_op jit(solution)/shard_map/ppermute | solution.py:481
  24.7 4.2 %temporal.1 = (bf16[32,1536]{1,0:T(8,128)(2,1)S(1)}, bf16[32,1536]{1,0:T(8,128)(2,1)S(1)}, bf16[32,1536]{1,0:T(8,128)(2,1)S(1)}, bf16[32,1536]{1,0:T(8,128)(2,1)...) custom-call(bf16[4,512]{1,0:T(4,128)(2,1)S(1)} %copy-done.3, bf16[512,1536]{1,0:T(8,128)(2,1)S(1)} %copy-done, ...), custom_call_target="tpu_custom_call" | custom-call | tf_op jit(solution)/shard_map/temporal/pallas_call | solution.py:590
  28.9 1.0 %collective-permute-start.6 = (bf16[32,1536]{1,0:T(8,128)(2,1)S(1)}, bf16[32,1536]{1,0:T(8,128)(2,1)S(1)}, u32[]{:S(2)}, u32[]{:S(2)}) collective-permute-start(bf16[32,1536]{1,0:T(8,128)(2,1)S(1)} %get-tuple-element.38), channel_id=1, source_target_pairs={{0,24},{4,28},{8,16},{12,20},{16,8},{20,12},{24,0},{28,4},{1,25},{... | collective-permute-start | bytes 294920 | tf_op jit(solution)/shard_map/ppermute | solution.py:481
  29.9 0.8 %collective-permute-start.7 = (bf16[32,1536]{1,0:T(8,128)(2,1)S(1)}, bf16[32,1536]{1,0:T(8,128)(2,1)S(1)}, u32[]{:S(2)}, u32[]{:S(2)}) collective-permute-start(bf16[32,1536]{1,0:T(8,128)(2,1)S(1)} %get-tuple-element.39), channel_id=1, source_target_pairs={{0,16},{4,20},{8,24},{12,28},{16,0},{20,4},{24,8},{28,12},{1,17},{... | collective-permute-start | bytes 294920 | tf_op jit(solution)/shard_map/ppermute | solution.py:481
  30.6 2.7 %collective-permute-start.8 = (bf16[32,1536]{1,0:T(8,128)(2,1)S(1)}, bf16[32,1536]{1,0:T(8,128)(2,1)S(1)}, u32[]{:S(2)}, u32[]{:S(2)}) collective-permute-start(bf16[32,1536]{1,0:T(8,128)(2,1)S(1)} %get-tuple-element.40), channel_id=1, source_target_pairs={{0,8},{4,12},{8,0},{12,4},{16,24},{20,28},{24,16},{28,20},{1,9},{5... | collective-permute-start | bytes 294920 | tf_op jit(solution)/shard_map/ppermute | solution.py:481
  33.3 4.9 %struct_backward.1 = (f32[64,512]{1,0:T(8,128)S(1)}, f32[128,512]{1,0:T(8,128)S(1)}) custom-call(bf16[128,1536]{1,0:T(8,128)(2,1)S(1)} %get-tuple-element.33.dt, bf16[128,512]{1,0:T(8,128)(2,1)S(1)} %get-tuple-element.34.cot, bf16[128,1536]{1,0:T(8,128)(2,1)S(1)} %get-tuple-element.31.proj, bf16[64,512]{1,0:T(8,128)(2,1)S(1)} %bitcast.12, ...), custom_call_target="tpu_custom_call" | custom-call | flops 2000000000 | bytes 8000000 | tf_op jit(solution)/shard_map/struct_backward/pallas_call | solution.py:619
  38.2 1.5 %collective-permute-done.7.refs_2_ = bf16[32,1536]{1,0:T(8,128)(2,1)S(1)} collective-permute-done((bf16[32,1536]{1,0:T(8,128)(2,1)S(1)}, bf16[32,1536]{1,0:T(8,128)(2,1)S(1)}, u32[]{:S(2)}, u32[]{:S(2)}) %collective-permute-start.7) | collective-permute-done | bytes 98336 | tf_op jit(solution)/shard_map/ppermute | solution.py:481
  39.8 0.1 outer_sum.1.mine_ref
  39.8 1.1 %collective-permute-start.9 = (bf16[32,2048]{1,0:T(8,128)(2,1)S(1)}, bf16[32,2048]{1,0:T(8,128)(2,1)S(1)}, u32[]{:S(2)}, u32[]{:S(2)}) collective-permute-start(bf16[32,2048]{1,0:T(8,128)(2,1)S(1)} %outer_sum.1.mine_ref), channel_id=1, source_target_pairs={{0,4},{4,0},{8,12},{12,8},{16,20},{20,16},{24,28},{28,24},{1,5},{5... | collective-permute-start | bytes 393224 | tf_op jit(solution)/shard_map/ppermute | solution.py:481
  40.9 4.3 %collective-permute-done.9.other_ref = bf16[32,2048]{1,0:T(8,128)(2,1)S(1)} collective-permute-done((bf16[32,2048]{1,0:T(8,128)(2,1)S(1)}, bf16[32,2048]{1,0:T(8,128)(2,1)S(1)}, u32[]{:S(2)}, u32[]{:S(2)}) %collective-permute-start.9) | collective-permute-done | bytes 131104 | tf_op jit(solution)/shard_map/ppermute | solution.py:481
  45.2 0.4 collective-permute-start.10
  45.6 1.2 %collective-permute-start.11 = (bf16[32,1792]{1,0:T(8,128)(2,1)S(1)}, bf16[32,1792]{1,0:T(8,128)(2,1)S(1)}, u32[]{:S(2)}, u32[]{:S(2)}) collective-permute-start(bf16[32,1792]{1,0:T(8,128)(2,1)S(1)} %get-tuple-element.46), channel_id=1, source_target_pairs={{0,24},{4,28},{8,16},{12,20},{16,8},{20,12},{24,0},{28,4},{1,25},{... | collective-permute-start | bytes 344072 | tf_op jit(solution)/shard_map/ppermute | solution.py:481
  46.8 2.0 %collective-permute-start.12 = (bf16[32,1792]{1,0:T(8,128)(2,1)S(1)}, bf16[32,1792]{1,0:T(8,128)(2,1)S(1)}, u32[]{:S(2)}, u32[]{:S(2)}) collective-permute-start(bf16[32,1792]{1,0:T(8,128)(2,1)S(1)} %get-tuple-element.47), channel_id=1, source_target_pairs={{0,8},{4,12},{8,0},{12,4},{16,24},{20,28},{24,16},{28,20},{1,9},{5... | collective-permute-start | bytes 344072 | tf_op jit(solution)/shard_map/ppermute | solution.py:481
  48.8 1.4 %early_sums.1 = (f32[128,512]{1,0:T(8,128)S(1)}, bf16[64,128]{1,0:T(8,128)(2,1)S(1)}, f32[128,1536]{1,0:T(8,128)}) custom-call(s32[8,8]{1,0:T(8,128)S(1)} %bitcast.14, f32[128,512]{1,0:T(8,128)S(1)} %get-tuple-element.35.part_ref, bf16[32,1792]{1,0:T(8,128)(2,1)S(1)} %get-tuple-element.41.refs_0_), custom_call_target="tpu_custom_call" | custom-call | tf_op jit(solution)/shard_map/early_sums/pallas_call | solution.py:663
  50.2 4.3 %collective-permute-done.10.refs_0_ = bf16[32,1792]{1,0:T(8,128)(2,1)S(1)} collective-permute-done((bf16[32,1792]{1,0:T(8,128)(2,1)S(1)}, bf16[32,1792]{1,0:T(8,128)(2,1)S(1)}, u32[]{:S(2)}, u32[]{:S(2)}) %collective-permute-start.10) | collective-permute-done | bytes 114720 | tf_op jit(solution)/shard_map/ppermute | solution.py:481
  54.5 0.7 %collective-permute-done.12.refs_2_ = bf16[32,1792]{1,0:T(8,128)(2,1)S(1)} collective-permute-done((bf16[32,1792]{1,0:T(8,128)(2,1)S(1)}, bf16[32,1792]{1,0:T(8,128)(2,1)S(1)}, u32[]{:S(2)}, u32[]{:S(2)}) %collective-permute-start.12) | collective-permute-done | bytes 114720 | tf_op jit(solution)/shard_map/ppermute | solution.py:481
  55.2 1.0 %last_sums.1 = (bf16[128,512]{1,0:T(8,128)(2,1)}, f32[128,1536]{1,0:T(8,128)}) custom-call(bf16[64,128]{1,0:T(8,128)(2,1)S(1)} %get-tuple-element.42.picks_ref, f32[128,512]{1,0:T(8,128)S(1)} %get-tuple-element.43.sum_ref, f32[128,1536]{1,0:T(8,128)} %get-tuple-element.44._, ...), custom_call_target="tpu_custom_call", output_to_operand_aliasing={{1}: (2, {})} | custom-call | tf_op jit(solution)/shard_map/last_sums/pallas_call | solution.py:680
  (14 shorter events, 0.1 us)
Async XLA Ops:
  2.3 14.2 %all-to-all-start = ((bf16[8,8,512]{2,1,0:T(8,128)(2,1)}), bf16[8,8,512]{2,1,0:T(8,128)(2,1)S(1)}, u32[]{:S(2)}, u32[]{:S(2)}) async-start(bf16[8,8,512]{2,1,0:T(8,128)(2,1)} %bitcast.6), calls=%async_computation | async-start | bytes 131072 | tf_op jit(solution)/shard_map/all_to_all | solution.py:476
  12.0 7.9 %collective-permute-start.1 = (bf16[5,32,512]{2,1,0:T(8,128)(2,1)}, bf16[5,32,512]{2,1,0:T(8,128)(2,1)S(1)}, u32[]{:S(2)}, u32[]{:S(2)}) collective-permute-start(bf16[5,32,512]{2,1,0:T(8,128)(2,1)} %get-tuple-element.26.refs_0_), channel_id=1, source_target_pairs={{0,2},{1,3},{2,0},{3,1},{4,6},{5,7},{6,4},{7,5},{8,10},{9,11},{10,... | collective-permute-start | bytes 491528 | tf_op jit(solution)/shard_map/ppermute | solution.py:481
  16.5 3.4 %copy-start.1 = (bf16[5,32,512]{2,1,0:T(8,128)(2,1)S(1)}, bf16[5,32,512]{2,1,0:T(8,128)(2,1)}, u32[]{:S(2)}) copy-start(bf16[5,32,512]{2,1,0:T(8,128)(2,1)} %get-tuple-element.26.refs_0_) | copy-start | bytes 491524
  16.5 8.2 %copy-start = (bf16[512,1536]{1,0:T(8,128)(2,1)S(1)}, bf16[512,1536]{1,0:T(8,128)(2,1)}, u32[]{:S(2)}) copy-start(bf16[512,1536]{1,0:T(8,128)(2,1)} %wt.1) | copy-start | bytes 4718596
  16.5 8.2 %copy-start.3 = (bf16[4,512]{1,0:T(4,128)(2,1)S(1)}, bf16[4,512]{1,0:T(4,128)(2,1)}, u32[]{:S(2)}) copy-start(bf16[4,512]{1,0:T(4,128)(2,1)} %pos_ref.1) | copy-start | bytes 12292
  18.3 5.0 %collective-permute-start.4 = (bf16[128,512]{1,0:T(8,128)(2,1)S(1)}, bf16[128,512]{1,0:T(8,128)(2,1)S(1)}, u32[]{:S(2)}, u32[]{:S(2)}) collective-permute-start(bf16[128,512]{1,0:T(8,128)(2,1)S(1)} %struct_forward.1.refs_0_), channel_id=1, source_target_pairs={{0,2},{1,3},{2,0},{3,1},{4,6},{5,7},{6,4},{7,5},{8,10},{9,11},{10,... | collective-permute-start | bytes 393224 | tf_op jit(solution)/shard_map/ppermute | solution.py:481
  19.9 3.5 %collective-permute-start = (bf16[5,32,512]{2,1,0:T(8,128)(2,1)S(1)}, bf16[5,32,512]{2,1,0:T(8,128)(2,1)S(1)}, u32[]{:S(2)}, u32[]{:S(2)}) collective-permute-start(bf16[5,32,512]{2,1,0:T(8,128)(2,1)S(1)} %copy-done.1), channel_id=1, source_target_pairs={{0,1},{1,0},{2,3},{3,2},{4,5},{5,4},{6,7},{7,6},{8,9},{9,8},{10,11... | collective-permute-start | bytes 491528 | tf_op jit(solution)/shard_map/ppermute | solution.py:481
  19.9 3.4 %collective-permute-start.2 = (bf16[5,32,512]{2,1,0:T(8,128)(2,1)S(1)}, bf16[5,32,512]{2,1,0:T(8,128)(2,1)S(1)}, u32[]{:S(2)}, u32[]{:S(2)}) collective-permute-start(bf16[5,32,512]{2,1,0:T(8,128)(2,1)S(1)} %collective-permute-done.1.refs_2_), channel_id=1, source_target_pairs={{0,1},{1,0},{2,3},{3,2},{4,5},{5,4},{6,7},{7,6},{8,9},{9,8},{10,11... | collective-permute-start | bytes 491528 | tf_op jit(solution)/shard_map/ppermute | solution.py:481
  20.4 3.0 %collective-permute-start.3 = (bf16[128,512]{1,0:T(8,128)(2,1)S(1)}, bf16[128,512]{1,0:T(8,128)(2,1)S(1)}, u32[]{:S(2)}, u32[]{:S(2)}) collective-permute-start(bf16[128,512]{1,0:T(8,128)(2,1)S(1)} %struct_forward.1.refs_0_), channel_id=1, source_target_pairs={{0,1},{1,0},{2,3},{3,2},{4,5},{5,4},{6,7},{7,6},{8,9},{9,8},{10,11... | collective-permute-start | bytes 393224 | tf_op jit(solution)/shard_map/ppermute | solution.py:481
  23.3 1.3 %collective-permute-start.5 = (bf16[128,512]{1,0:T(8,128)(2,1)S(1)}, bf16[128,512]{1,0:T(8,128)(2,1)S(1)}, u32[]{:S(2)}, u32[]{:S(2)}) collective-permute-start(bf16[128,512]{1,0:T(8,128)(2,1)S(1)} %collective-permute-done.4.refs_2_), channel_id=1, source_target_pairs={{0,1},{1,0},{2,3},{3,2},{4,5},{5,4},{6,7},{7,6},{8,9},{9,8},{10,11... | collective-permute-start | bytes 393224 | tf_op jit(solution)/shard_map/ppermute | solution.py:481
  28.9 9.3 %collective-permute-start.6 = (bf16[32,1536]{1,0:T(8,128)(2,1)S(1)}, bf16[32,1536]{1,0:T(8,128)(2,1)S(1)}, u32[]{:S(2)}, u32[]{:S(2)}) collective-permute-start(bf16[32,1536]{1,0:T(8,128)(2,1)S(1)} %get-tuple-element.38), channel_id=1, source_target_pairs={{0,24},{4,28},{8,16},{12,20},{16,8},{20,12},{24,0},{28,4},{1,25},{... | collective-permute-start | bytes 294920 | tf_op jit(solution)/shard_map/ppermute | solution.py:481
  29.9 9.9 %collective-permute-start.7 = (bf16[32,1536]{1,0:T(8,128)(2,1)S(1)}, bf16[32,1536]{1,0:T(8,128)(2,1)S(1)}, u32[]{:S(2)}, u32[]{:S(2)}) collective-permute-start(bf16[32,1536]{1,0:T(8,128)(2,1)S(1)} %get-tuple-element.39), channel_id=1, source_target_pairs={{0,16},{4,20},{8,24},{12,28},{16,0},{20,4},{24,8},{28,12},{1,17},{... | collective-permute-start | bytes 294920 | tf_op jit(solution)/shard_map/ppermute | solution.py:481
  30.6 9.1 %collective-permute-start.8 = (bf16[32,1536]{1,0:T(8,128)(2,1)S(1)}, bf16[32,1536]{1,0:T(8,128)(2,1)S(1)}, u32[]{:S(2)}, u32[]{:S(2)}) collective-permute-start(bf16[32,1536]{1,0:T(8,128)(2,1)S(1)} %get-tuple-element.40), channel_id=1, source_target_pairs={{0,8},{4,12},{8,0},{12,4},{16,24},{20,28},{24,16},{28,20},{1,9},{5... | collective-permute-start | bytes 294920 | tf_op jit(solution)/shard_map/ppermute | solution.py:481
  33.3 15.5 %copy-start.2 = (s32[1,1,8,8]{3,2,1,0:T(8,128)S(1)}, s32[1,1,8,8]{3,2,1,0:T(8,128)}, u32[]{:S(2)}) copy-start(s32[1,1,8,8]{3,2,1,0:T(8,128)} %param.17) | copy-start | bytes 772
  39.8 5.4 %collective-permute-start.9 = (bf16[32,2048]{1,0:T(8,128)(2,1)S(1)}, bf16[32,2048]{1,0:T(8,128)(2,1)S(1)}, u32[]{:S(2)}, u32[]{:S(2)}) collective-permute-start(bf16[32,2048]{1,0:T(8,128)(2,1)S(1)} %outer_sum.1.mine_ref), channel_id=1, source_target_pairs={{0,4},{4,0},{8,12},{12,8},{16,20},{20,16},{24,28},{28,24},{1,5},{5... | collective-permute-start | bytes 393224 | tf_op jit(solution)/shard_map/ppermute | solution.py:481
  45.2 9.3 %collective-permute-start.10 = (bf16[32,1792]{1,0:T(8,128)(2,1)S(1)}, bf16[32,1792]{1,0:T(8,128)(2,1)S(1)}, u32[]{:S(2)}, u32[]{:S(2)}) collective-permute-start(bf16[32,1792]{1,0:T(8,128)(2,1)S(1)} %get-tuple-element.45), channel_id=1, source_target_pairs={{0,16},{4,20},{8,24},{12,28},{16,0},{20,4},{24,8},{28,12},{1,17},{... | collective-permute-start | bytes 344072 | tf_op jit(solution)/shard_map/ppermute | solution.py:481
  45.6 8.9 %collective-permute-start.11 = (bf16[32,1792]{1,0:T(8,128)(2,1)S(1)}, bf16[32,1792]{1,0:T(8,128)(2,1)S(1)}, u32[]{:S(2)}, u32[]{:S(2)}) collective-permute-start(bf16[32,1792]{1,0:T(8,128)(2,1)S(1)} %get-tuple-element.46), channel_id=1, source_target_pairs={{0,24},{4,28},{8,16},{12,20},{16,8},{20,12},{24,0},{28,4},{1,25},{... | collective-permute-start | bytes 344072 | tf_op jit(solution)/shard_map/ppermute | solution.py:481
  46.8 8.4 %collective-permute-start.12 = (bf16[32,1792]{1,0:T(8,128)(2,1)S(1)}, bf16[32,1792]{1,0:T(8,128)(2,1)S(1)}, u32[]{:S(2)}, u32[]{:S(2)}) collective-permute-start(bf16[32,1792]{1,0:T(8,128)(2,1)S(1)} %get-tuple-element.47), channel_id=1, source_target_pairs={{0,8},{4,12},{8,0},{12,4},{16,24},{20,28},{24,16},{28,20},{1,9},{5... | collective-permute-start | bytes 344072 | tf_op jit(solution)/shard_map/ppermute | solution.py:481

commit v8 on v7

--- a/solution.py
+++ b/solution.py
@@ -216,7 +216,7 @@
     terms_ref = refs[snaps : snaps + pieces]
     (
         dt_own_ref, cot_own_ref,
-        z_s, tp_s, dt_s, prod_s, s_s, d_s, a_s, ds_s, wa_s, wd_s, dk_s, dv_s, terms_s,
+        z_s, tp_s, dt_s, prod_s, s_s, d_s, a_s, ds_s, terms_s,
     ) = refs[snaps + pieces :]
     local, width = hid[0].shape
     head_dim = width // heads
@@ -245,9 +245,15 @@
     spread = spread.astype(BF16)
     act = act_s[...]
     snap_lane = lax.broadcasted_iota(jnp.int32, act.shape, 1)
-    if not unroll:
-        dk_s[...] = jnp.zeros_like(dk_s)
-        dv_s[...] = jnp.zeros_like(dv_s)
+    def pair_rows(t, u):
+        return rows_of((t * t + t) // 2 + u)
+
+    def reduced(lo, hi, fn, start):
+        if unroll:
+            for i in range(lo, hi):
+                start = fn(i, start)
+            return start
+        return lax.fori_loop(lo, hi, fn, start)
 
     def one_snap(t):
         used = (t + 1 if unroll else snaps) * local
@@ -271,15 +277,11 @@
 
         each(0, t + 1, unroll, mask)
 
-        def reduced(fn, start):
-            if unroll:
-                for u in range(t + 1):
-                    start = fn(u, start)
-                return start
-            return lax.fori_loop(0, t + 1, fn, start)
-
         top = reduced(
-            lambda u, c: jnp.maximum(c, s_s[rows_of(u), :]), jnp.full((local, LANES), NEG, F32)
+            0,
+            t + 1,
+            lambda u, c: jnp.maximum(c, s_s[rows_of(u), :]),
+            jnp.full((local, LANES), NEG, F32),
         )
 
         def expo(u, total):
@@ -287,47 +289,51 @@
             s_s[rows_of(u), :] = e
             return total + e
 
-        inv = 1.0 / reduced(expo, jnp.zeros((local, LANES), F32))
+        inv = 1.0 / reduced(0, t + 1, expo, jnp.zeros((local, LANES), F32))
 
         def weigh(u, total):
             a = s_s[rows_of(u), :] * inv
             s_s[rows_of(u), :] = a
             return total + a * d_s[rows_of(u), :]
 
-        dot = reduced(weigh, jnp.zeros((local, LANES), F32))
+        dot = reduced(0, t + 1, weigh, jnp.zeros((local, LANES), F32))
 
         def keep(u):
             a = s_s[rows_of(u), :]
-            a_s[rows_of(u), :] = a.astype(BF16)
-            ds_s[rows_of(u), :] = (a * (d_s[rows_of(u), :] - dot)).astype(BF16)
+            a_s[pair_rows(t, u), :] = a.astype(BF16)
+            ds_s[pair_rows(t, u), :] = (a * (d_s[rows_of(u), :] - dot)).astype(BF16)
 
         each(0, t + 1, unroll, keep)
-        wa_s[:used, :] = dot_nn(a_s[:used, :], spread)
-        wd_s[:used, :] = dot_nn(ds_s[:used, :], spread_scaled)
-
-        for p in range(width // LANES):
-            c0 = p * LANES
-            cols = slice(c0, c0 + LANES)
-            q = tp_s[rows_of(t), cols].astype(F32)
-            ct = ct_s[rows_of(t), cols].astype(F32)
-
-            def back(u, dq):
-                k = tp_s[rows_of(u), width + c0 : width + c0 + LANES].astype(F32)
-                wide_ds = wd_s[rows_of(u), cols]
-                dk, dv = wide_ds * q, wa_s[rows_of(u), cols] * ct
-                if unroll and u == t:
-                    dk_s[rows_of(u), cols] = dk
-                    dv_s[rows_of(u), cols] = dv
-                else:
-                    dk_s[rows_of(u), cols] += dk
-                    dv_s[rows_of(u), cols] += dv
-                return dq + wide_ds * k
-
-            dt_s[rows_of(t), cols] = reduced(back, jnp.zeros_like(q)).astype(BF16)
 
     each(0, snaps, unroll, one_snap)
-    dt_s[:, width : 2 * width] = dk_s[...].astype(BF16)
-    dt_s[:, 2 * width :] = dv_s[...].astype(BF16)
+    for p in range(width // LANES):
+        c0 = p * LANES
+        cols = slice(c0, c0 + LANES)
+
+        def columns(part, i):
+            return tp_s[rows_of(i), part * width + c0 : part * width + c0 + LANES].astype(F32)
+
+        def query(t):
+            def add(u, dq):
+                return dq + dot_nn(ds_s[pair_rows(t, u), :], spread_scaled[:, cols]) * columns(1, u)
+
+            dq = reduced(0, t + 1, add, jnp.zeros((local, LANES), F32))
+            dt_s[rows_of(t), cols] = dq.astype(BF16)
+
+        def key_value(u):
+            def add(t, grads):
+                dk, dv = grads
+                dk = dk + dot_nn(ds_s[pair_rows(t, u), :], spread_scaled[:, cols]) * columns(0, t)
+                wide = dot_nn(a_s[pair_rows(t, u), :], spread[:, cols])
+                return dk, dv + wide * ct_s[rows_of(t), cols].astype(F32)
+
+            zero = jnp.zeros((local, LANES), F32)
+            dk, dv = reduced(u, snaps, add, (zero, zero))
+            dt_s[rows_of(u), width + c0 : width + c0 + LANES] = dk.astype(BF16)
+            dt_s[rows_of(u), 2 * width + c0 : 2 * width + c0 + LANES] = dv.astype(BF16)
+
+        each(0, snaps, unroll, query)
+        each(0, snaps, unroll, key_value)
     share = width // snaps
     pick = (
         lax.broadcasted_iota(jnp.int32, (width, share), 0)
@@ -576,6 +582,7 @@
     hids = gather_blocks({0: hidden}, "snap", snaps // 2, 1)
     hids = [hids[m] for m in range(snaps)]
     every = snaps * local
+    pairs = snaps * (snaps + 1) // 2
     ct, act = pl.pallas_call(
         cotangent_kernel,
         out_shape=(
@@ -600,12 +607,8 @@
             pltpu.VMEM((2 * every, width), BF16),
             pltpu.VMEM((every, LANES), F32),
             pltpu.VMEM((every, LANES), F32),
-            pltpu.VMEM((every, LANES), BF16),
-            pltpu.VMEM((every, LANES), BF16),
-            pltpu.VMEM((every, width), F32),
-            pltpu.VMEM((every, width), F32),
-            pltpu.VMEM((every, width), F32),
-            pltpu.VMEM((every, width), F32),
+            pltpu.VMEM((pairs * local, LANES), BF16),
+            pltpu.VMEM((pairs * local, LANES), BF16),
             pltpu.VMEM((share, 3 * width), BF16),
         ],
         compiler_params=params(24 if snaps <= 4 else 56),

time: 56.5 us -> 56.3 us (level)
  no operation moved by 1% of the time
where the time goes in v8:
time: 56.3 us; the launch traced here: 56 us
  starting transfers between devices  20.1 us (36%)
  waiting for transfers between devices  18 us (32%)
  Pallas kernels  17.2 us (31%)
  between operations  0.73 us (1%)
    ppermute x13, waiting for transfers between devices, flipped(): return lax.ppermute(block, axis, [(i, i ^ flip) for i in range(count)])  15 us
    ppermute x13, starting transfers between devices, flipped(): return lax.ppermute(block, axis, [(i, i ^ flip) for i in range(count)])  12.8 us
    all_to_all x1, starting transfers between devices, exchange(): return lax.all_to_all(tiles, axis, split_axis=0, concat_axis=0, tiled=True)  7.27 us
    pallas_call x1, Pallas kernels, per_device(): pl.pallas_call(functools.partial(backward_kernel, heads), out_shape=(shap...  4.86 us
    pallas_call x1, Pallas kernels, per_device(): pl.pallas_call(functools.partial(temporal_kernel, snaps, heads, pieces),...  3.99 us
    all_to_all x1, waiting for transfers between devices, exchange(): return lax.all_to_all(tiles, axis, split_axis=0, concat_axis=0, tiled=True)  2.97 us
    pallas_call x1, Pallas kernels, per_device(): pl.pallas_call(own_kernel, out_shape=(vmem(heads, local, keys, dtype=F32)...  2.35 us
    pallas_call x1, Pallas kernels, per_device(): pl.pallas_call(functools.partial(forward_kernel, heads), out_shape=shape(...  1.76 us
  transfers between devices with their start and end apart: 14, of which 7 were waited for; matrix products, arithmetic and copies ran while one was open for 0% of the time, Pallas kernels for 19%

profile of v8, /device:TPU:0, one launch (start us, length us, event | category | flops | bytes accessed | tf_op | source)
XLA Modules:
  0.0 56.0 jit_solution(3036618690408036080)
XLA Ops:
  0.6 1.7 %halo_tiles.1 = bf16[64,512]{1,0:T(8,128)(2,1)} custom-call(s32[8,8]{1,0:T(8,128)} %bitcast.13, bf16[128,512]{1,0:T(8,128)(2,1)} %bitcast.15), custom_call_target="tpu_custom_call" | custom-call | tf_op jit(solution)/shard_map/halo_tiles/pallas_call | solution.py:528
  2.3 7.3 %all-to-all-start = ((bf16[8,8,512]{2,1,0:T(8,128)(2,1)}), bf16[8,8,512]{2,1,0:T(8,128)(2,1)S(1)}, u32[]{:S(2)}, u32[]{:S(2)}) async-start(bf16[8,8,512]{2,1,0:T(8,128)(2,1)} %bitcast.6), calls=%async_computation | async-start | bytes 131072 | tf_op jit(solution)/shard_map/all_to_all | solution.py:482
  9.6 2.4 %own_rows.1 = (f32[8,128,256]{2,1,0:T(8,128)S(1)}, bf16[128,1536]{1,0:T(8,128)(2,1)S(1)}, bf16[128,512]{1,0:T(8,128)(2,1)S(1)}, bf16[512,1536]{1,0:T(8,128)(2,1)S(1)}, bf16[5,32,512]{2,1,0:T(8,128)(2,1)}) custom-call(s32[8,128]{1,0:T(8,128)} %bitcast.18, s32[8,128]{1,0:T(8,128)} %bitcast.19, f32[4,8]{1,0:T(4,128)} %bias_hbm.1, s32[4,32]{1,0:T(4,128)} %act_hbm.1, ...), custom_call_target="tpu_custom_call" | custom-call | flops 1000000000 | bytes 4000000 | tf_op jit(solution)/shard_map/own_rows/pallas_call | solution.py:543
  12.0 1.6 %collective-permute-start.1 = (bf16[5,32,512]{2,1,0:T(8,128)(2,1)}, bf16[5,32,512]{2,1,0:T(8,128)(2,1)S(1)}, u32[]{:S(2)}, u32[]{:S(2)}) collective-permute-start(bf16[5,32,512]{2,1,0:T(8,128)(2,1)} %get-tuple-element.26.refs_0_), channel_id=1, source_target_pairs={{0,2},{1,3},{2,0},{3,1},{4,6},{5,7},{6,4},{7,5},{8,10},{9,11},{10,... | collective-permute-start | bytes 491528 | tf_op jit(solution)/shard_map/ppermute | solution.py:487
  13.5 3.0 %all-to-all-done = bf16[8,8,512]{2,1,0:T(8,128)(2,1)S(1)} async-done(((bf16[8,8,512]{2,1,0:T(8,128)(2,1)}), bf16[8,8,512]{2,1,0:T(8,128)(2,1)S(1)}, u32[]{:S(2)}, u32[]{:S(2)}) %all-to-all-start) | async-done | bytes 65568 | tf_op jit(solution)/shard_map/all_to_all | solution.py:482
  16.5 1.8 %struct_forward.1.refs_0_ = bf16[128,512]{1,0:T(8,128)(2,1)S(1)} custom-call(bf16[128,512]{1,0:T(8,128)(2,1)S(1)} %get-tuple-element.29.x, bf16[64,512]{1,0:T(8,128)(2,1)S(1)} %bitcast.11, bf16[512,1536]{1,0:T(8,128)(2,1)S(1)} %get-tuple-element.30.w.ws, bf16[128,1536]{1,0:T(8,128)(2,1)S(1)} %get-tuple-element.31.proj, f32[8,128,256]{2,1,0:T(8,128)S(1)} %get-tuple-element.32.edge), custom_call_target="tpu_custom_call" | custom-call | tf_op jit(solution)/shard_map/struct_forward/pallas_call | solution.py:572
  18.3 1.6 %collective-permute-start.4 = (bf16[128,512]{1,0:T(8,128)(2,1)S(1)}, bf16[128,512]{1,0:T(8,128)(2,1)S(1)}, u32[]{:S(2)}, u32[]{:S(2)}) collective-permute-start(bf16[128,512]{1,0:T(8,128)(2,1)S(1)} %struct_forward.1.refs_0_), channel_id=1, source_target_pairs={{0,2},{1,3},{2,0},{3,1},{4,6},{5,7},{6,4},{7,5},{8,10},{9,11},{10,... | collective-permute-start | bytes 393224 | tf_op jit(solution)/shard_map/ppermute | solution.py:487
  19.9 0.0 collective-permute-start
  19.9 0.0 collective-permute-done.1.refs_2_
  19.9 0.5 collective-permute-start.2
  20.4 0.1 collective-permute-start.3
  20.5 2.9 %collective-permute-done.4.refs_2_ = bf16[128,512]{1,0:T(8,128)(2,1)S(1)} collective-permute-done((bf16[128,512]{1,0:T(8,128)(2,1)S(1)}, bf16[128,512]{1,0:T(8,128)(2,1)S(1)}, u32[]{:S(2)}, u32[]{:S(2)}) %collective-permute-start.4) | collective-permute-done | bytes 131104 | tf_op jit(solution)/shard_map/ppermute | solution.py:487
  23.3 0.0 collective-permute-start.5
  23.3 0.0 collective-permute-done.refs_1_
  23.3 0.1 cotangents.1
  23.4 1.3 %collective-permute-done.5.refs_3_ = bf16[128,512]{1,0:T(8,128)(2,1)S(1)} collective-permute-done((bf16[128,512]{1,0:T(8,128)(2,1)S(1)}, bf16[128,512]{1,0:T(8,128)(2,1)S(1)}, u32[]{:S(2)}, u32[]{:S(2)}) %collective-permute-start.5) | collective-permute-done | bytes 131104 | tf_op jit(solution)/shard_map/ppermute | solution.py:487
  24.7 4.0 %temporal.1 = (bf16[32,1536]{1,0:T(8,128)(2,1)S(1)}, bf16[32,1536]{1,0:T(8,128)(2,1)S(1)}, bf16[32,1536]{1,0:T(8,128)(2,1)S(1)}, bf16[32,1536]{1,0:T(8,128)(2,1)...) custom-call(bf16[4,512]{1,0:T(4,128)(2,1)S(1)} %copy-done.3, bf16[512,1536]{1,0:T(8,128)(2,1)S(1)} %copy-done, ...), custom_call_target="tpu_custom_call" | custom-call | tf_op jit(solution)/shard_map/temporal/pallas_call | solution.py:597
  28.7 1.0 %collective-permute-start.6 = (bf16[32,1536]{1,0:T(8,128)(2,1)S(1)}, bf16[32,1536]{1,0:T(8,128)(2,1)S(1)}, u32[]{:S(2)}, u32[]{:S(2)}) collective-permute-start(bf16[32,1536]{1,0:T(8,128)(2,1)S(1)} %get-tuple-element.38), channel_id=1, source_target_pairs={{0,24},{4,28},{8,16},{12,20},{16,8},{20,12},{24,0},{28,4},{1,25},{... | collective-permute-start | bytes 294920 | tf_op jit(solution)/shard_map/ppermute | solution.py:487
  29.7 0.8 %collective-permute-start.7 = (bf16[32,1536]{1,0:T(8,128)(2,1)S(1)}, bf16[32,1536]{1,0:T(8,128)(2,1)S(1)}, u32[]{:S(2)}, u32[]{:S(2)}) collective-permute-start(bf16[32,1536]{1,0:T(8,128)(2,1)S(1)} %get-tuple-element.39), channel_id=1, source_target_pairs={{0,16},{4,20},{8,24},{12,28},{16,0},{20,4},{24,8},{28,12},{1,17},{... | collective-permute-start | bytes 294920 | tf_op jit(solution)/shard_map/ppermute | solution.py:487
  30.4 2.7 %collective-permute-start.8 = (bf16[32,1536]{1,0:T(8,128)(2,1)S(1)}, bf16[32,1536]{1,0:T(8,128)(2,1)S(1)}, u32[]{:S(2)}, u32[]{:S(2)}) collective-permute-start(bf16[32,1536]{1,0:T(8,128)(2,1)S(1)} %get-tuple-element.40), channel_id=1, source_target_pairs={{0,8},{4,12},{8,0},{12,4},{16,24},{20,28},{24,16},{28,20},{1,9},{5... | collective-permute-start | bytes 294920 | tf_op jit(solution)/shard_map/ppermute | solution.py:487
  33.1 4.9 %struct_backward.1 = (f32[64,512]{1,0:T(8,128)S(1)}, f32[128,512]{1,0:T(8,128)S(1)}) custom-call(bf16[128,1536]{1,0:T(8,128)(2,1)S(1)} %get-tuple-element.33.dt, bf16[128,512]{1,0:T(8,128)(2,1)S(1)} %get-tuple-element.34.cot, bf16[128,1536]{1,0:T(8,128)(2,1)S(1)} %get-tuple-element.31.proj, bf16[64,512]{1,0:T(8,128)(2,1)S(1)} %bitcast.12, ...), custom_call_target="tpu_custom_call" | custom-call | flops 2000000000 | bytes 8000000 | tf_op jit(solution)/shard_map/struct_backward/pallas_call | solution.py:622
  38.0 1.5 %collective-permute-done.7.refs_2_ = bf16[32,1536]{1,0:T(8,128)(2,1)S(1)} collective-permute-done((bf16[32,1536]{1,0:T(8,128)(2,1)S(1)}, bf16[32,1536]{1,0:T(8,128)(2,1)S(1)}, u32[]{:S(2)}, u32[]{:S(2)}) %collective-permute-start.7) | collective-permute-done | bytes 98336 | tf_op jit(solution)/shard_map/ppermute | solution.py:487
  39.6 0.1 outer_sum.1.mine_ref
  39.6 1.1 %collective-permute-start.9 = (bf16[32,2048]{1,0:T(8,128)(2,1)S(1)}, bf16[32,2048]{1,0:T(8,128)(2,1)S(1)}, u32[]{:S(2)}, u32[]{:S(2)}) collective-permute-start(bf16[32,2048]{1,0:T(8,128)(2,1)S(1)} %outer_sum.1.mine_ref), channel_id=1, source_target_pairs={{0,4},{4,0},{8,12},{12,8},{16,20},{20,16},{24,28},{28,24},{1,5},{5... | collective-permute-start | bytes 393224 | tf_op jit(solution)/shard_map/ppermute | solution.py:487
  40.7 4.3 %collective-permute-done.9.other_ref = bf16[32,2048]{1,0:T(8,128)(2,1)S(1)} collective-permute-done((bf16[32,2048]{1,0:T(8,128)(2,1)S(1)}, bf16[32,2048]{1,0:T(8,128)(2,1)S(1)}, u32[]{:S(2)}, u32[]{:S(2)}) %collective-permute-start.9) | collective-permute-done | bytes 131104 | tf_op jit(solution)/shard_map/ppermute | solution.py:487
  45.0 0.4 collective-permute-start.10
  45.4 1.2 %collective-permute-start.11 = (bf16[32,1792]{1,0:T(8,128)(2,1)S(1)}, bf16[32,1792]{1,0:T(8,128)(2,1)S(1)}, u32[]{:S(2)}, u32[]{:S(2)}) collective-permute-start(bf16[32,1792]{1,0:T(8,128)(2,1)S(1)} %get-tuple-element.46), channel_id=1, source_target_pairs={{0,24},{4,28},{8,16},{12,20},{16,8},{20,12},{24,0},{28,4},{1,25},{... | collective-permute-start | bytes 344072 | tf_op jit(solution)/shard_map/ppermute | solution.py:487
  46.6 2.0 %collective-permute-start.12 = (bf16[32,1792]{1,0:T(8,128)(2,1)S(1)}, bf16[32,1792]{1,0:T(8,128)(2,1)S(1)}, u32[]{:S(2)}, u32[]{:S(2)}) collective-permute-start(bf16[32,1792]{1,0:T(8,128)(2,1)S(1)} %get-tuple-element.47), channel_id=1, source_target_pairs={{0,8},{4,12},{8,0},{12,4},{16,24},{20,28},{24,16},{28,20},{1,9},{5... | collective-permute-start | bytes 344072 | tf_op jit(solution)/shard_map/ppermute | solution.py:487
  48.6 1.4 %early_sums.1 = (f32[128,512]{1,0:T(8,128)S(1)}, bf16[64,128]{1,0:T(8,128)(2,1)S(1)}, f32[128,1536]{1,0:T(8,128)}) custom-call(s32[8,8]{1,0:T(8,128)S(1)} %bitcast.14, f32[128,512]{1,0:T(8,128)S(1)} %get-tuple-element.35.part_ref, bf16[32,1792]{1,0:T(8,128)(2,1)S(1)} %get-tuple-element.41.refs_0_), custom_call_target="tpu_custom_call" | custom-call | tf_op jit(solution)/shard_map/early_sums/pallas_call | solution.py:666
  50.0 4.3 %collective-permute-done.10.refs_0_ = bf16[32,1792]{1,0:T(8,128)(2,1)S(1)} collective-permute-done((bf16[32,1792]{1,0:T(8,128)(2,1)S(1)}, bf16[32,1792]{1,0:T(8,128)(2,1)S(1)}, u32[]{:S(2)}, u32[]{:S(2)}) %collective-permute-start.10) | collective-permute-done | bytes 114720 | tf_op jit(solution)/shard_map/ppermute | solution.py:487
  54.3 0.7 %collective-permute-done.12.refs_2_ = bf16[32,1792]{1,0:T(8,128)(2,1)S(1)} collective-permute-done((bf16[32,1792]{1,0:T(8,128)(2,1)S(1)}, bf16[32,1792]{1,0:T(8,128)(2,1)S(1)}, u32[]{:S(2)}, u32[]{:S(2)}) %collective-permute-start.12) | collective-permute-done | bytes 114720 | tf_op jit(solution)/shard_map/ppermute | solution.py:487
  55.0 1.0 %last_sums.1 = (bf16[128,512]{1,0:T(8,128)(2,1)}, f32[128,1536]{1,0:T(8,128)}) custom-call(bf16[64,128]{1,0:T(8,128)(2,1)S(1)} %get-tuple-element.42.picks_ref, f32[128,512]{1,0:T(8,128)S(1)} %get-tuple-element.43.sum_ref, f32[128,1536]{1,0:T(8,128)} %get-tuple-element.44._, ...), custom_call_target="tpu_custom_call", output_to_operand_aliasing={{1}: (2, {})} | custom-call | tf_op jit(solution)/shard_map/last_sums/pallas_call | solution.py:683
  (14 shorter events, 0.1 us)
Async XLA Ops:
  2.3 14.2 %all-to-all-start = ((bf16[8,8,512]{2,1,0:T(8,128)(2,1)}), bf16[8,8,512]{2,1,0:T(8,128)(2,1)S(1)}, u32[]{:S(2)}, u32[]{:S(2)}) async-start(bf16[8,8,512]{2,1,0:T(8,128)(2,1)} %bitcast.6), calls=%async_computation | async-start | bytes 131072 | tf_op jit(solution)/shard_map/all_to_all | solution.py:482
  12.0 7.9 %collective-permute-start.1 = (bf16[5,32,512]{2,1,0:T(8,128)(2,1)}, bf16[5,32,512]{2,1,0:T(8,128)(2,1)S(1)}, u32[]{:S(2)}, u32[]{:S(2)}) collective-permute-start(bf16[5,32,512]{2,1,0:T(8,128)(2,1)} %get-tuple-element.26.refs_0_), channel_id=1, source_target_pairs={{0,2},{1,3},{2,0},{3,1},{4,6},{5,7},{6,4},{7,5},{8,10},{9,11},{10,... | collective-permute-start | bytes 491528 | tf_op jit(solution)/shard_map/ppermute | solution.py:487
  16.5 3.4 %copy-start.1 = (bf16[5,32,512]{2,1,0:T(8,128)(2,1)S(1)}, bf16[5,32,512]{2,1,0:T(8,128)(2,1)}, u32[]{:S(2)}) copy-start(bf16[5,32,512]{2,1,0:T(8,128)(2,1)} %get-tuple-element.26.refs_0_) | copy-start | bytes 491524
  16.5 8.2 %copy-start = (bf16[512,1536]{1,0:T(8,128)(2,1)S(1)}, bf16[512,1536]{1,0:T(8,128)(2,1)}, u32[]{:S(2)}) copy-start(bf16[512,1536]{1,0:T(8,128)(2,1)} %wt.1) | copy-start | bytes 4718596
  16.5 8.2 %copy-start.3 = (bf16[4,512]{1,0:T(4,128)(2,1)S(1)}, bf16[4,512]{1,0:T(4,128)(2,1)}, u32[]{:S(2)}) copy-start(bf16[4,512]{1,0:T(4,128)(2,1)} %pos_ref.1) | copy-start | bytes 12292
  18.3 5.0 %collective-permute-start.4 = (bf16[128,512]{1,0:T(8,128)(2,1)S(1)}, bf16[128,512]{1,0:T(8,128)(2,1)S(1)}, u32[]{:S(2)}, u32[]{:S(2)}) collective-permute-start(bf16[128,512]{1,0:T(8,128)(2,1)S(1)} %struct_forward.1.refs_0_), channel_id=1, source_target_pairs={{0,2},{1,3},{2,0},{3,1},{4,6},{5,7},{6,4},{7,5},{8,10},{9,11},{10,... | collective-permute-start | bytes 393224 | tf_op jit(solution)/shard_map/ppermute | solution.py:487
  19.9 3.5 %collective-permute-start = (bf16[5,32,512]{2,1,0:T(8,128)(2,1)S(1)}, bf16[5,32,512]{2,1,0:T(8,128)(2,1)S(1)}, u32[]{:S(2)}, u32[]{:S(2)}) collective-permute-start(bf16[5,32,512]{2,1,0:T(8,128)(2,1)S(1)} %copy-done.1), channel_id=1, source_target_pairs={{0,1},{1,0},{2,3},{3,2},{4,5},{5,4},{6,7},{7,6},{8,9},{9,8},{10,11... | collective-permute-start | bytes 491528 | tf_op jit(solution)/shard_map/ppermute | solution.py:487
  19.9 3.4 %collective-permute-start.2 = (bf16[5,32,512]{2,1,0:T(8,128)(2,1)S(1)}, bf16[5,32,512]{2,1,0:T(8,128)(2,1)S(1)}, u32[]{:S(2)}, u32[]{:S(2)}) collective-permute-start(bf16[5,32,512]{2,1,0:T(8,128)(2,1)S(1)} %collective-permute-done.1.refs_2_), channel_id=1, source_target_pairs={{0,1},{1,0},{2,3},{3,2},{4,5},{5,4},{6,7},{7,6},{8,9},{9,8},{10,11... | collective-permute-start | bytes 491528 | tf_op jit(solution)/shard_map/ppermute | solution.py:487
  20.4 3.0 %collective-permute-start.3 = (bf16[128,512]{1,0:T(8,128)(2,1)S(1)}, bf16[128,512]{1,0:T(8,128)(2,1)S(1)}, u32[]{:S(2)}, u32[]{:S(2)}) collective-permute-start(bf16[128,512]{1,0:T(8,128)(2,1)S(1)} %struct_forward.1.refs_0_), channel_id=1, source_target_pairs={{0,1},{1,0},{2,3},{3,2},{4,5},{5,4},{6,7},{7,6},{8,9},{9,8},{10,11... | collective-permute-start | bytes 393224 | tf_op jit(solution)/shard_map/ppermute | solution.py:487
  23.3 1.3 %collective-permute-start.5 = (bf16[128,512]{1,0:T(8,128)(2,1)S(1)}, bf16[128,512]{1,0:T(8,128)(2,1)S(1)}, u32[]{:S(2)}, u32[]{:S(2)}) collective-permute-start(bf16[128,512]{1,0:T(8,128)(2,1)S(1)} %collective-permute-done.4.refs_2_), channel_id=1, source_target_pairs={{0,1},{1,0},{2,3},{3,2},{4,5},{5,4},{6,7},{7,6},{8,9},{9,8},{10,11... | collective-permute-start | bytes 393224 | tf_op jit(solution)/shard_map/ppermute | solution.py:487
  28.7 9.3 %collective-permute-start.6 = (bf16[32,1536]{1,0:T(8,128)(2,1)S(1)}, bf16[32,1536]{1,0:T(8,128)(2,1)S(1)}, u32[]{:S(2)}, u32[]{:S(2)}) collective-permute-start(bf16[32,1536]{1,0:T(8,128)(2,1)S(1)} %get-tuple-element.38), channel_id=1, source_target_pairs={{0,24},{4,28},{8,16},{12,20},{16,8},{20,12},{24,0},{28,4},{1,25},{... | collective-permute-start | bytes 294920 | tf_op jit(solution)/shard_map/ppermute | solution.py:487
  29.7 9.9 %collective-permute-start.7 = (bf16[32,1536]{1,0:T(8,128)(2,1)S(1)}, bf16[32,1536]{1,0:T(8,128)(2,1)S(1)}, u32[]{:S(2)}, u32[]{:S(2)}) collective-permute-start(bf16[32,1536]{1,0:T(8,128)(2,1)S(1)} %get-tuple-element.39), channel_id=1, source_target_pairs={{0,16},{4,20},{8,24},{12,28},{16,0},{20,4},{24,8},{28,12},{1,17},{... | collective-permute-start | bytes 294920 | tf_op jit(solution)/shard_map/ppermute | solution.py:487
  30.4 9.1 %collective-permute-start.8 = (bf16[32,1536]{1,0:T(8,128)(2,1)S(1)}, bf16[32,1536]{1,0:T(8,128)(2,1)S(1)}, u32[]{:S(2)}, u32[]{:S(2)}) collective-permute-start(bf16[32,1536]{1,0:T(8,128)(2,1)S(1)} %get-tuple-element.40), channel_id=1, source_target_pairs={{0,8},{4,12},{8,0},{12,4},{16,24},{20,28},{24,16},{28,20},{1,9},{5... | collective-permute-start | bytes 294920 | tf_op jit(solution)/shard_map/ppermute | solution.py:487
  33.1 15.5 %copy-start.2 = (s32[1,1,8,8]{3,2,1,0:T(8,128)S(1)}, s32[1,1,8,8]{3,2,1,0:T(8,128)}, u32[]{:S(2)}) copy-start(s32[1,1,8,8]{3,2,1,0:T(8,128)} %param.17) | copy-start | bytes 772
  39.6 5.4 %collective-permute-start.9 = (bf16[32,2048]{1,0:T(8,128)(2,1)S(1)}, bf16[32,2048]{1,0:T(8,128)(2,1)S(1)}, u32[]{:S(2)}, u32[]{:S(2)}) collective-permute-start(bf16[32,2048]{1,0:T(8,128)(2,1)S(1)} %outer_sum.1.mine_ref), channel_id=1, source_target_pairs={{0,4},{4,0},{8,12},{12,8},{16,20},{20,16},{24,28},{28,24},{1,5},{5... | collective-permute-start | bytes 393224 | tf_op jit(solution)/shard_map/ppermute | solution.py:487
  45.0 9.3 %collective-permute-start.10 = (bf16[32,1792]{1,0:T(8,128)(2,1)S(1)}, bf16[32,1792]{1,0:T(8,128)(2,1)S(1)}, u32[]{:S(2)}, u32[]{:S(2)}) collective-permute-start(bf16[32,1792]{1,0:T(8,128)(2,1)S(1)} %get-tuple-element.45), channel_id=1, source_target_pairs={{0,16},{4,20},{8,24},{12,28},{16,0},{20,4},{24,8},{28,12},{1,17},{... | collective-permute-start | bytes 344072 | tf_op jit(solution)/shard_map/ppermute | solution.py:487
  45.4 8.9 %collective-permute-start.11 = (bf16[32,1792]{1,0:T(8,128)(2,1)S(1)}, bf16[32,1792]{1,0:T(8,128)(2,1)S(1)}, u32[]{:S(2)}, u32[]{:S(2)}) collective-permute-start(bf16[32,1792]{1,0:T(8,128)(2,1)S(1)} %get-tuple-element.46), channel_id=1, source_target_pairs={{0,24},{4,28},{8,16},{12,20},{16,8},{20,12},{24,0},{28,4},{1,25},{... | collective-permute-start | bytes 344072 | tf_op jit(solution)/shard_map/ppermute | solution.py:487
  46.6 8.4 %collective-permute-start.12 = (bf16[32,1792]{1,0:T(8,128)(2,1)S(1)}, bf16[32,1792]{1,0:T(8,128)(2,1)S(1)}, u32[]{:S(2)}, u32[]{:S(2)}) collective-permute-start(bf16[32,1792]{1,0:T(8,128)(2,1)S(1)} %get-tuple-element.47), channel_id=1, source_target_pairs={{0,8},{4,12},{8,0},{12,4},{16,24},{20,28},{24,16},{28,20},{1,9},{5... | collective-permute-start | bytes 344072 | tf_op jit(solution)/shard_map/ppermute | solution.py:487

commit v9 on v8

--- a/solution.py
+++ b/solution.py
@@ -199,43 +199,59 @@
         lax.fori_loop(lo, hi, lambda i, c: (body(i), c)[1], 0)
 
 
-def cotangent_kernel(*refs):
-    *cot, ct_ref, act_ref = refs
-    snaps = len(cot)
+def position_of(pos_ref, t):
+    pos = pos_ref[...].astype(F32)
+    which = lax.broadcasted_iota(jnp.int32, pos.shape, 0)
+    return jnp.sum(jnp.where(which == t, pos, 0.0), axis=0, keepdims=True)
+
+
+def arrived_kernel(snaps, flips, pos_ref, w, *refs):
+    cot, hid = refs[:snaps], refs[snaps : snaps + len(flips)]
+    ct_ref, act_ref, z_ref, tp_ref = refs[snaps + len(flips) :]
     ents = cot[0].shape[1]
-    local = snaps * ents
+    local, width = hid[0].shape
+    me = snap_index()
     for m in range(snaps):
-        at = pl.multiple_of(lax.bitwise_xor(snap_index(), m) * ents, ents)
+        at = pl.multiple_of(lax.bitwise_xor(me, m) * ents, ents)
         for t in range(snaps):
             ct_ref[pl.ds(t * local + at, ents), :] = cot[m][t].astype(ct_ref.dtype)
         act_ref[pl.ds(at, ents), :] = cot[m][snaps][:, :LANES].astype(F32)
-
-
-def temporal_kernel(snaps, heads, pieces, pos_ref, w_s, ct_s, act_s, *refs):
-    hid = refs[:snaps]
-    terms_ref = refs[snaps : snaps + pieces]
+    for i, n in enumerate(flips):
+        shift = position_of(pos_ref, lax.bitwise_xor(me, n))
+        z_ref[i * local : (i + 1) * local, :] = (hid[i][...].astype(F32) + shift).astype(BF16)
+    for part in range(3):
+        cols = slice(part * width, (part + 1) * width)
+        tp_ref[:, cols] = dot_nn(z_ref[...], w[:, cols]).astype(BF16)
+
+
+def temporal_kernel(
+    snaps, heads, pieces, soon, late, pos_ref, w_s, ct_s, act_s, z_soon, tp_soon, *refs
+):
+    hid, refs = refs[: len(late)], refs[len(late) :]
+    terms_ref = refs[:pieces]
     (
         dt_own_ref, cot_own_ref,
-        z_s, tp_s, dt_s, prod_s, s_s, d_s, a_s, ds_s, terms_s,
-    ) = refs[snaps + pieces :]
+        z_s, tp_s, dt_s, prod_s, s_s, d_s, a_s, ds_s, terms_s, z_late, tp_late,
+    ) = refs[pieces:]
     local, width = hid[0].shape
     head_dim = width // heads
     scale = head_dim ** (-0.5)
     unroll = snaps <= 4
     me, outer = snap_index(), dom_index() // 2
-    pos = pos_ref[...].astype(F32)
-    which = lax.broadcasted_iota(jnp.int32, pos.shape, 0)
-
     def rows_of(t):
         return pl.ds(t * local if isinstance(t, int) else pl.multiple_of(t * local, local), local)
 
-    for n in range(snaps):
-        t = lax.bitwise_xor(me, n)
-        shift = jnp.sum(jnp.where(which == t, pos, 0.0), axis=0, keepdims=True)
-        z_s[rows_of(t), :] = (hid[n][...].astype(F32) + shift).astype(BF16)
+    for i, n in enumerate(late):
+        shift = position_of(pos_ref, lax.bitwise_xor(me, n))
+        z_late[i * local : (i + 1) * local, :] = (hid[i][...].astype(F32) + shift).astype(BF16)
     for part in range(3):
         cols = slice(part * width, (part + 1) * width)
-        tp_s[:, cols] = dot_nn(z_s[...], w_s[:, cols]).astype(BF16)
+        tp_late[:, cols] = dot_nn(z_late[...], w_s[:, cols]).astype(BF16)
+    for flips, z_ref, tp_ref in ((soon, z_soon, tp_soon), (late, z_late, tp_late)):
+        for i, n in enumerate(flips):
+            t = lax.bitwise_xor(me, n)
+            z_s[rows_of(t), :] = z_ref[i * local : (i + 1) * local, :]
+            tp_s[rows_of(t), :] = tp_ref[i * local : (i + 1) * local, :]
     lane_head = lax.broadcasted_iota(jnp.int32, (width, LANES), 0) // head_dim
     fold = (lane_head == lax.broadcasted_iota(jnp.int32, (width, LANES), 1)).astype(F32)
     fold = fold.astype(BF16)
@@ -583,22 +599,26 @@
     hids = [hids[m] for m in range(snaps)]
     every = snaps * local
     pairs = snaps * (snaps + 1) // 2
-    ct, act = pl.pallas_call(
-        cotangent_kernel,
+    ahead = min(3, snaps - 1)
+    soon, late = list(range(ahead)), list(range(ahead, snaps))
+    ct, act, *begun = pl.pallas_call(
+        functools.partial(arrived_kernel, snaps, soon),
         out_shape=(
             shape(every, width, dtype=F32 if ents % 16 else BF16),
             shape(local, LANES, dtype=F32),
+            shape(len(soon) * local, width),
+            shape(len(soon) * local, 3 * width),
         ),
-        in_specs=[VMEM] * snaps,
-        out_specs=(VMEM, VMEM),
+        in_specs=[VMEM] * (2 + snaps + len(soon)),
+        out_specs=(VMEM,) * 4,
         compiler_params=params(8),
-        name="cotangents",
-    )(*cots)
+        name="arrived",
+    )(pos_embed, w_temp, *cots, *[hids[n] for n in soon])
     *terms, dt_own, cot_own = pl.pallas_call(
-        functools.partial(temporal_kernel, snaps, heads, pieces),
+        functools.partial(temporal_kernel, snaps, heads, pieces, soon, late),
         out_shape=(shape(share // pieces, 3 * width),) * pieces
         + (shape(local, 3 * width), shape(local, width)),
-        in_specs=[VMEM] * (4 + snaps),
+        in_specs=[VMEM] * (6 + len(late)),
         out_specs=(VMEM,) * (pieces + 2),
         scratch_shapes=[
             pltpu.VMEM((every, width), BF16),
@@ -610,10 +630,12 @@
             pltpu.VMEM((pairs * local, LANES), BF16),
             pltpu.VMEM((pairs * local, LANES), BF16),
             pltpu.VMEM((share, 3 * width), BF16),
+            pltpu.VMEM((len(late) * local, width), BF16),
+            pltpu.VMEM((len(late) * local, 3 * width), BF16),
         ],
         compiler_params=params(24 if snaps <= 4 else 56),
         name="temporal",
-    )(pos_embed, w_temp, ct, act, *hids)
+    )(pos_embed, w_temp, ct, act, *begun, *[hids[n] for n in late])
 
     if paired:
         got = [terms[0]] + [flipped(terms[k], "dom", 2 * k) for k in range(pieces - 1, 0, -1)]

time: 56.3 us -> 55.8 us (level)
  waiting for transfers between devices: 18 us -> 17.2 us
    ppermute x13, waiting for transfers between devices: 15 us -> 14.2 us  [flipped(): return lax.ppermute(block, axis, [(i, i ^ flip) for i in range(count)])]
  transfers between devices with their start and end apart: 14 -> 14, of which waited for: 7 -> 7; matrix products, arithmetic and copies ran while one was open for 0% -> 0% of each run, Pallas kernels for 19% -> 20%
where the time goes in v9:
time: 55.8 us; the launch traced here: 55.5 us
  starting transfers between devices  20.1 us (36%)
  Pallas kernels  17.5 us (31%)
  waiting for transfers between devices  17.2 us (31%)
  between operations  0.75 us (1%)
    ppermute x13, waiting for transfers between devices, flipped(): return lax.ppermute(block, axis, [(i, i ^ flip) for i in range(count)])  14.2 us
    ppermute x13, starting transfers between devices, flipped(): return lax.ppermute(block, axis, [(i, i ^ flip) for i in range(count)])  12.8 us
    all_to_all x1, starting transfers between devices, exchange(): return lax.all_to_all(tiles, axis, split_axis=0, concat_axis=0, tiled=True)  7.27 us
    pallas_call x1, Pallas kernels, per_device(): pl.pallas_call(functools.partial(backward_kernel, heads), out_shape=(shap...  4.85 us
    pallas_call x1, Pallas kernels, per_device(): pl.pallas_call(functools.partial(temporal_kernel, snaps, heads, pieces, s...  3.51 us
    all_to_all x1, waiting for transfers between devices, exchange(): return lax.all_to_all(tiles, axis, split_axis=0, concat_axis=0, tiled=True)  2.97 us
    pallas_call x1, Pallas kernels, per_device(): pl.pallas_call(own_kernel, out_shape=(vmem(heads, local, keys, dtype=F32)...  2.35 us
    pallas_call x1, Pallas kernels, per_device(): pl.pallas_call(functools.partial(forward_kernel, heads), out_shape=shape(...  1.76 us
  transfers between devices with their start and end apart: 14, of which 7 were waited for; matrix products, arithmetic and copies ran while one was open for 0% of the time, Pallas kernels for 20%

profile of v9, /device:TPU:0, one launch (start us, length us, event | category | flops | bytes accessed | tf_op | source)
XLA Modules:
  0.0 55.5 jit_solution(5838147850811487341)
XLA Ops:
  0.6 1.7 %halo_tiles.1 = bf16[64,512]{1,0:T(8,128)(2,1)} custom-call(s32[8,8]{1,0:T(8,128)} %bitcast.13, bf16[128,512]{1,0:T(8,128)(2,1)} %bitcast.15), custom_call_target="tpu_custom_call" | custom-call | tf_op jit(solution)/shard_map/halo_tiles/pallas_call | solution.py:544
  2.3 7.3 %all-to-all-start = ((bf16[8,8,512]{2,1,0:T(8,128)(2,1)}), bf16[8,8,512]{2,1,0:T(8,128)(2,1)S(1)}, u32[]{:S(2)}, u32[]{:S(2)}) async-start(bf16[8,8,512]{2,1,0:T(8,128)(2,1)} %bitcast.6), calls=%async_computation | async-start | bytes 131072 | tf_op jit(solution)/shard_map/all_to_all | solution.py:498
  9.6 2.4 %own_rows.1 = (f32[8,128,256]{2,1,0:T(8,128)S(1)}, bf16[128,1536]{1,0:T(8,128)(2,1)S(1)}, bf16[128,512]{1,0:T(8,128)(2,1)S(1)}, bf16[512,1536]{1,0:T(8,128)(2,1)S(1)}, bf16[5,32,512]{2,1,0:T(8,128)(2,1)}) custom-call(s32[8,128]{1,0:T(8,128)} %bitcast.18, s32[8,128]{1,0:T(8,128)} %bitcast.19, f32[4,8]{1,0:T(4,128)} %bias_hbm.1, s32[4,32]{1,0:T(4,128)} %act_hbm.1, ...), custom_call_target="tpu_custom_call" | custom-call | flops 1000000000 | bytes 4000000 | tf_op jit(solution)/shard_map/own_rows/pallas_call | solution.py:559
  12.0 1.6 %collective-permute-start.1 = (bf16[5,32,512]{2,1,0:T(8,128)(2,1)}, bf16[5,32,512]{2,1,0:T(8,128)(2,1)S(1)}, u32[]{:S(2)}, u32[]{:S(2)}) collective-permute-start(bf16[5,32,512]{2,1,0:T(8,128)(2,1)} %get-tuple-element.28.refs_0_), channel_id=1, source_target_pairs={{0,2},{1,3},{2,0},{3,1},{4,6},{5,7},{6,4},{7,5},{8,10},{9,11},{10,... | collective-permute-start | bytes 491528 | tf_op jit(solution)/shard_map/ppermute | solution.py:503
  13.5 3.0 %all-to-all-done = bf16[8,8,512]{2,1,0:T(8,128)(2,1)S(1)} async-done(((bf16[8,8,512]{2,1,0:T(8,128)(2,1)}), bf16[8,8,512]{2,1,0:T(8,128)(2,1)S(1)}, u32[]{:S(2)}, u32[]{:S(2)}) %all-to-all-start) | async-done | bytes 65568 | tf_op jit(solution)/shard_map/all_to_all | solution.py:498
  16.5 1.8 %struct_forward.1.refs_4_ = bf16[128,512]{1,0:T(8,128)(2,1)S(1)} custom-call(bf16[128,512]{1,0:T(8,128)(2,1)S(1)} %get-tuple-element.29.x, bf16[64,512]{1,0:T(8,128)(2,1)S(1)} %bitcast.11, bf16[512,1536]{1,0:T(8,128)(2,1)S(1)} %get-tuple-element.30.w.ws, bf16[128,1536]{1,0:T(8,128)(2,1)S(1)} %get-tuple-element.31.proj, f32[8,128,256]{2,1,0:T(8,128)S(1)} %get-tuple-element.32.edge), custom_call_target="tpu_custom_call" | custom-call | tf_op jit(solution)/shard_map/struct_forward/pallas_call | solution.py:588
  18.3 1.6 %collective-permute-start.4 = (bf16[128,512]{1,0:T(8,128)(2,1)S(1)}, bf16[128,512]{1,0:T(8,128)(2,1)S(1)}, u32[]{:S(2)}, u32[]{:S(2)}) collective-permute-start(bf16[128,512]{1,0:T(8,128)(2,1)S(1)} %struct_forward.1.refs_4_), channel_id=1, source_target_pairs={{0,2},{1,3},{2,0},{3,1},{4,6},{5,7},{6,4},{7,5},{8,10},{9,11},{10,... | collective-permute-start | bytes 393224 | tf_op jit(solution)/shard_map/ppermute | solution.py:503
  19.9 0.0 collective-permute-done.1.refs_2_
  19.9 0.5 collective-permute-start.2
  20.4 0.1 collective-permute-start.3
  20.5 2.9 %collective-permute-done.4.refs_6_ = bf16[128,512]{1,0:T(8,128)(2,1)S(1)} collective-permute-done((bf16[128,512]{1,0:T(8,128)(2,1)S(1)}, bf16[128,512]{1,0:T(8,128)(2,1)S(1)}, u32[]{:S(2)}, u32[]{:S(2)}) %collective-permute-start.4) | collective-permute-done | bytes 131104 | tf_op jit(solution)/shard_map/ppermute | solution.py:503
  23.3 0.0 collective-permute-done.3.refs_5_
  23.3 0.0 collective-permute-done.2.refs_3_
  23.4 0.8 %arrived.1 = (bf16[512,512]{1,0:T(8,128)(2,1)S(1)}, f32[128,128]{1,0:T(8,128)S(1)}, bf16[384,512]{1,0:T(8,128)(2,1)S(1)}, bf16[384,1536]{1,0:T(8,128)(2,1)S(1)}) custom-call(bf16[4,512]{1,0:T(4,128)(2,1)S(1)} %copy-done.2, bf16[512,1536]{1,0:T(8,128)(2,1)S(1)} %copy-done, bf16[5,32,512]{2,1,0:T(8,128)(2,1)S(1)} %copy-done.1, ...), custom_call_target="tpu_custom_call" | custom-call | tf_op jit(solution)/shard_map/arrived/pallas_call | solution.py:604
  24.2 0.5 collective-permute-done.5.refs_0_
  24.7 3.5 %temporal.1 = (bf16[32,1536]{1,0:T(8,128)(2,1)S(1)}, bf16[32,1536]{1,0:T(8,128)(2,1)S(1)}, bf16[32,1536]{1,0:T(8,128)(2,1)S(1)}, bf16[32,1536]{1,0:T(8,128)(2,1)...) custom-call(bf16[4,512]{1,0:T(4,128)(2,1)S(1)} %copy-done.2, bf16[512,1536]{1,0:T(8,128)(2,1)S(1)} %copy-done, ...), custom_call_target="tpu_custom_call" | custom-call | tf_op jit(solution)/shard_map/temporal/pallas_call | solution.py:617
  28.2 1.0 %collective-permute-start.6 = (bf16[32,1536]{1,0:T(8,128)(2,1)S(1)}, bf16[32,1536]{1,0:T(8,128)(2,1)S(1)}, u32[]{:S(2)}, u32[]{:S(2)}) collective-permute-start(bf16[32,1536]{1,0:T(8,128)(2,1)S(1)} %get-tuple-element.42), channel_id=1, source_target_pairs={{0,24},{4,28},{8,16},{12,20},{16,8},{20,12},{24,0},{28,4},{1,25},{... | collective-permute-start | bytes 294920 | tf_op jit(solution)/shard_map/ppermute | solution.py:503
  29.2 0.8 %collective-permute-start.7 = (bf16[32,1536]{1,0:T(8,128)(2,1)S(1)}, bf16[32,1536]{1,0:T(8,128)(2,1)S(1)}, u32[]{:S(2)}, u32[]{:S(2)}) collective-permute-start(bf16[32,1536]{1,0:T(8,128)(2,1)S(1)} %get-tuple-element.43), channel_id=1, source_target_pairs={{0,16},{4,20},{8,24},{12,28},{16,0},{20,4},{24,8},{28,12},{1,17},{... | collective-permute-start | bytes 294920 | tf_op jit(solution)/shard_map/ppermute | solution.py:503
  29.9 2.7 %collective-permute-start.8 = (bf16[32,1536]{1,0:T(8,128)(2,1)S(1)}, bf16[32,1536]{1,0:T(8,128)(2,1)S(1)}, u32[]{:S(2)}, u32[]{:S(2)}) collective-permute-start(bf16[32,1536]{1,0:T(8,128)(2,1)S(1)} %get-tuple-element.44), channel_id=1, source_target_pairs={{0,8},{4,12},{8,0},{12,4},{16,24},{20,28},{24,16},{28,20},{1,9},{5... | collective-permute-start | bytes 294920 | tf_op jit(solution)/shard_map/ppermute | solution.py:503
  32.7 4.9 %struct_backward.1 = (f32[64,512]{1,0:T(8,128)S(1)}, f32[128,512]{1,0:T(8,128)S(1)}) custom-call(bf16[128,1536]{1,0:T(8,128)(2,1)S(1)} %get-tuple-element.37.dt, bf16[128,512]{1,0:T(8,128)(2,1)S(1)} %get-tuple-element.38.cot, bf16[128,1536]{1,0:T(8,128)(2,1)S(1)} %get-tuple-element.31.proj, bf16[64,512]{1,0:T(8,128)(2,1)S(1)} %bitcast.12, ...), custom_call_target="tpu_custom_call" | custom-call | flops 2000000000 | bytes 8000000 | tf_op jit(solution)/shard_map/struct_backward/pallas_call | solution.py:644
  37.5 0.0 collective-permute-done.6.refs_1_
  37.5 1.6 %collective-permute-done.7.refs_2_ = bf16[32,1536]{1,0:T(8,128)(2,1)S(1)} collective-permute-done((bf16[32,1536]{1,0:T(8,128)(2,1)S(1)}, bf16[32,1536]{1,0:T(8,128)(2,1)S(1)}, u32[]{:S(2)}, u32[]{:S(2)}) %collective-permute-start.7) | collective-permute-done | bytes 98336 | tf_op jit(solution)/shard_map/ppermute | solution.py:503
  39.1 0.1 outer_sum.1.mine_ref
  39.1 1.1 %collective-permute-start.9 = (bf16[32,2048]{1,0:T(8,128)(2,1)S(1)}, bf16[32,2048]{1,0:T(8,128)(2,1)S(1)}, u32[]{:S(2)}, u32[]{:S(2)}) collective-permute-start(bf16[32,2048]{1,0:T(8,128)(2,1)S(1)} %outer_sum.1.mine_ref), channel_id=1, source_target_pairs={{0,4},{4,0},{8,12},{12,8},{16,20},{20,16},{24,28},{28,24},{1,5},{5... | collective-permute-start | bytes 393224 | tf_op jit(solution)/shard_map/ppermute | solution.py:503
  40.2 4.3 %collective-permute-done.9.other_ref = bf16[32,2048]{1,0:T(8,128)(2,1)S(1)} collective-permute-done((bf16[32,2048]{1,0:T(8,128)(2,1)S(1)}, bf16[32,2048]{1,0:T(8,128)(2,1)S(1)}, u32[]{:S(2)}, u32[]{:S(2)}) %collective-permute-start.9) | collective-permute-done | bytes 131104 | tf_op jit(solution)/shard_map/ppermute | solution.py:503
  44.5 0.4 collective-permute-start.10
  44.9 1.2 %collective-permute-start.11 = (bf16[32,1792]{1,0:T(8,128)(2,1)S(1)}, bf16[32,1792]{1,0:T(8,128)(2,1)S(1)}, u32[]{:S(2)}, u32[]{:S(2)}) collective-permute-start(bf16[32,1792]{1,0:T(8,128)(2,1)S(1)} %get-tuple-element.50), channel_id=1, source_target_pairs={{0,24},{4,28},{8,16},{12,20},{16,8},{20,12},{24,0},{28,4},{1,25},{... | collective-permute-start | bytes 344072 | tf_op jit(solution)/shard_map/ppermute | solution.py:503
  46.1 2.0 %collective-permute-start.12 = (bf16[32,1792]{1,0:T(8,128)(2,1)S(1)}, bf16[32,1792]{1,0:T(8,128)(2,1)S(1)}, u32[]{:S(2)}, u32[]{:S(2)}) collective-permute-start(bf16[32,1792]{1,0:T(8,128)(2,1)S(1)} %get-tuple-element.51), channel_id=1, source_target_pairs={{0,8},{4,12},{8,0},{12,4},{16,24},{20,28},{24,16},{28,20},{1,9},{5... | collective-permute-start | bytes 344072 | tf_op jit(solution)/shard_map/ppermute | solution.py:503
  48.1 1.4 %early_sums.1 = (f32[128,512]{1,0:T(8,128)S(1)}, bf16[64,128]{1,0:T(8,128)(2,1)S(1)}, f32[128,1536]{1,0:T(8,128)}) custom-call(s32[8,8]{1,0:T(8,128)S(1)} %bitcast.14, f32[128,512]{1,0:T(8,128)S(1)} %get-tuple-element.39.part_ref, bf16[32,1792]{1,0:T(8,128)(2,1)S(1)} %get-tuple-element.45.refs_0_), custom_call_target="tpu_custom_call" | custom-call | tf_op jit(solution)/shard_map/early_sums/pallas_call | solution.py:688
  49.5 4.3 %collective-permute-done.10.refs_0_ = bf16[32,1792]{1,0:T(8,128)(2,1)S(1)} collective-permute-done((bf16[32,1792]{1,0:T(8,128)(2,1)S(1)}, bf16[32,1792]{1,0:T(8,128)(2,1)S(1)}, u32[]{:S(2)}, u32[]{:S(2)}) %collective-permute-start.10) | collective-permute-done | bytes 114720 | tf_op jit(solution)/shard_map/ppermute | solution.py:503
  53.8 0.7 %collective-permute-done.12.refs_2_ = bf16[32,1792]{1,0:T(8,128)(2,1)S(1)} collective-permute-done((bf16[32,1792]{1,0:T(8,128)(2,1)S(1)}, bf16[32,1792]{1,0:T(8,128)(2,1)S(1)}, u32[]{:S(2)}, u32[]{:S(2)}) %collective-permute-start.12) | collective-permute-done | bytes 114720 | tf_op jit(solution)/shard_map/ppermute | solution.py:503
  54.5 1.0 %last_sums.1 = (bf16[128,512]{1,0:T(8,128)(2,1)}, f32[128,1536]{1,0:T(8,128)}) custom-call(bf16[64,128]{1,0:T(8,128)(2,1)S(1)} %get-tuple-element.46.picks_ref, f32[128,512]{1,0:T(8,128)S(1)} %get-tuple-element.47.sum_ref, f32[128,1536]{1,0:T(8,128)} %get-tuple-element.48._, ...), custom_call_target="tpu_custom_call", output_to_operand_aliasing={{1}: (2, {})} | custom-call | tf_op jit(solution)/shard_map/last_sums/pallas_call | solution.py:705
  (14 shorter events, 0.1 us)
Async XLA Ops:
  2.3 14.2 %all-to-all-start = ((bf16[8,8,512]{2,1,0:T(8,128)(2,1)}), bf16[8,8,512]{2,1,0:T(8,128)(2,1)S(1)}, u32[]{:S(2)}, u32[]{:S(2)}) async-start(bf16[8,8,512]{2,1,0:T(8,128)(2,1)} %bitcast.6), calls=%async_computation | async-start | bytes 131072 | tf_op jit(solution)/shard_map/all_to_all | solution.py:498
  12.0 7.9 %collective-permute-start.1 = (bf16[5,32,512]{2,1,0:T(8,128)(2,1)}, bf16[5,32,512]{2,1,0:T(8,128)(2,1)S(1)}, u32[]{:S(2)}, u32[]{:S(2)}) collective-permute-start(bf16[5,32,512]{2,1,0:T(8,128)(2,1)} %get-tuple-element.28.refs_0_), channel_id=1, source_target_pairs={{0,2},{1,3},{2,0},{3,1},{4,6},{5,7},{6,4},{7,5},{8,10},{9,11},{10,... | collective-permute-start | bytes 491528 | tf_op jit(solution)/shard_map/ppermute | solution.py:503
  16.5 3.4 %copy-start.1 = (bf16[5,32,512]{2,1,0:T(8,128)(2,1)S(1)}, bf16[5,32,512]{2,1,0:T(8,128)(2,1)}, u32[]{:S(2)}) copy-start(bf16[5,32,512]{2,1,0:T(8,128)(2,1)} %get-tuple-element.28.refs_0_) | copy-start | bytes 491524
  16.5 6.8 %copy-start = (bf16[512,1536]{1,0:T(8,128)(2,1)S(1)}, bf16[512,1536]{1,0:T(8,128)(2,1)}, u32[]{:S(2)}) copy-start(bf16[512,1536]{1,0:T(8,128)(2,1)} %wt.1) | copy-start | bytes 4718596
  16.5 6.8 %copy-start.2 = (bf16[4,512]{1,0:T(4,128)(2,1)S(1)}, bf16[4,512]{1,0:T(4,128)(2,1)}, u32[]{:S(2)}) copy-start(bf16[4,512]{1,0:T(4,128)(2,1)} %pos_ref.3) | copy-start | bytes 12292
  18.3 5.0 %collective-permute-start.4 = (bf16[128,512]{1,0:T(8,128)(2,1)S(1)}, bf16[128,512]{1,0:T(8,128)(2,1)S(1)}, u32[]{:S(2)}, u32[]{:S(2)}) collective-permute-start(bf16[128,512]{1,0:T(8,128)(2,1)S(1)} %struct_forward.1.refs_4_), channel_id=1, source_target_pairs={{0,2},{1,3},{2,0},{3,1},{4,6},{5,7},{6,4},{7,5},{8,10},{9,11},{10,... | collective-permute-start | bytes 393224 | tf_op jit(solution)/shard_map/ppermute | solution.py:503
  19.9 3.5 %collective-permute-start = (bf16[5,32,512]{2,1,0:T(8,128)(2,1)S(1)}, bf16[5,32,512]{2,1,0:T(8,128)(2,1)S(1)}, u32[]{:S(2)}, u32[]{:S(2)}) collective-permute-start(bf16[5,32,512]{2,1,0:T(8,128)(2,1)S(1)} %copy-done.1), channel_id=1, source_target_pairs={{0,1},{1,0},{2,3},{3,2},{4,5},{5,4},{6,7},{7,6},{8,9},{9,8},{10,11... | collective-permute-start | bytes 491528 | tf_op jit(solution)/shard_map/ppermute | solution.py:503
  19.9 3.5 %collective-permute-start.2 = (bf16[5,32,512]{2,1,0:T(8,128)(2,1)S(1)}, bf16[5,32,512]{2,1,0:T(8,128)(2,1)S(1)}, u32[]{:S(2)}, u32[]{:S(2)}) collective-permute-start(bf16[5,32,512]{2,1,0:T(8,128)(2,1)S(1)} %collective-permute-done.1.refs_2_), channel_id=1, source_target_pairs={{0,1},{1,0},{2,3},{3,2},{4,5},{5,4},{6,7},{7,6},{8,9},{9,8},{10,11... | collective-permute-start | bytes 491528 | tf_op jit(solution)/shard_map/ppermute | solution.py:503
  20.4 2.9 %collective-permute-start.3 = (bf16[128,512]{1,0:T(8,128)(2,1)S(1)}, bf16[128,512]{1,0:T(8,128)(2,1)S(1)}, u32[]{:S(2)}, u32[]{:S(2)}) collective-permute-start(bf16[128,512]{1,0:T(8,128)(2,1)S(1)} %struct_forward.1.refs_4_), channel_id=1, source_target_pairs={{0,1},{1,0},{2,3},{3,2},{4,5},{5,4},{6,7},{7,6},{8,9},{9,8},{10,11... | collective-permute-start | bytes 393224 | tf_op jit(solution)/shard_map/ppermute | solution.py:503
  23.3 1.3 %collective-permute-start.5 = (bf16[128,512]{1,0:T(8,128)(2,1)S(1)}, bf16[128,512]{1,0:T(8,128)(2,1)S(1)}, u32[]{:S(2)}, u32[]{:S(2)}) collective-permute-start(bf16[128,512]{1,0:T(8,128)(2,1)S(1)} %collective-permute-done.4.refs_6_), channel_id=1, source_target_pairs={{0,1},{1,0},{2,3},{3,2},{4,5},{5,4},{6,7},{7,6},{8,9},{9,8},{10,11... | collective-permute-start | bytes 393224 | tf_op jit(solution)/shard_map/ppermute | solution.py:503
  28.2 9.3 %collective-permute-start.6 = (bf16[32,1536]{1,0:T(8,128)(2,1)S(1)}, bf16[32,1536]{1,0:T(8,128)(2,1)S(1)}, u32[]{:S(2)}, u32[]{:S(2)}) collective-permute-start(bf16[32,1536]{1,0:T(8,128)(2,1)S(1)} %get-tuple-element.42), channel_id=1, source_target_pairs={{0,24},{4,28},{8,16},{12,20},{16,8},{20,12},{24,0},{28,4},{1,25},{... | collective-permute-start | bytes 294920 | tf_op jit(solution)/shard_map/ppermute | solution.py:503
  29.2 9.9 %collective-permute-start.7 = (bf16[32,1536]{1,0:T(8,128)(2,1)S(1)}, bf16[32,1536]{1,0:T(8,128)(2,1)S(1)}, u32[]{:S(2)}, u32[]{:S(2)}) collective-permute-start(bf16[32,1536]{1,0:T(8,128)(2,1)S(1)} %get-tuple-element.43), channel_id=1, source_target_pairs={{0,16},{4,20},{8,24},{12,28},{16,0},{20,4},{24,8},{28,12},{1,17},{... | collective-permute-start | bytes 294920 | tf_op jit(solution)/shard_map/ppermute | solution.py:503
  29.9 9.1 %collective-permute-start.8 = (bf16[32,1536]{1,0:T(8,128)(2,1)S(1)}, bf16[32,1536]{1,0:T(8,128)(2,1)S(1)}, u32[]{:S(2)}, u32[]{:S(2)}) collective-permute-start(bf16[32,1536]{1,0:T(8,128)(2,1)S(1)} %get-tuple-element.44), channel_id=1, source_target_pairs={{0,8},{4,12},{8,0},{12,4},{16,24},{20,28},{24,16},{28,20},{1,9},{5... | collective-permute-start | bytes 294920 | tf_op jit(solution)/shard_map/ppermute | solution.py:503
  32.6 15.4 %copy-start.3 = (s32[1,1,8,8]{3,2,1,0:T(8,128)S(1)}, s32[1,1,8,8]{3,2,1,0:T(8,128)}, u32[]{:S(2)}) copy-start(s32[1,1,8,8]{3,2,1,0:T(8,128)} %param.17) | copy-start | bytes 772
  39.1 5.4 %collective-permute-start.9 = (bf16[32,2048]{1,0:T(8,128)(2,1)S(1)}, bf16[32,2048]{1,0:T(8,128)(2,1)S(1)}, u32[]{:S(2)}, u32[]{:S(2)}) collective-permute-start(bf16[32,2048]{1,0:T(8,128)(2,1)S(1)} %outer_sum.1.mine_ref), channel_id=1, source_target_pairs={{0,4},{4,0},{8,12},{12,8},{16,20},{20,16},{24,28},{28,24},{1,5},{5... | collective-permute-start | bytes 393224 | tf_op jit(solution)/shard_map/ppermute | solution.py:503
  44.5 9.3 %collective-permute-start.10 = (bf16[32,1792]{1,0:T(8,128)(2,1)S(1)}, bf16[32,1792]{1,0:T(8,128)(2,1)S(1)}, u32[]{:S(2)}, u32[]{:S(2)}) collective-permute-start(bf16[32,1792]{1,0:T(8,128)(2,1)S(1)} %get-tuple-element.49), channel_id=1, source_target_pairs={{0,16},{4,20},{8,24},{12,28},{16,0},{20,4},{24,8},{28,12},{1,17},{... | collective-permute-start | bytes 344072 | tf_op jit(solution)/shard_map/ppermute | solution.py:503
  44.9 8.9 %collective-permute-start.11 = (bf16[32,1792]{1,0:T(8,128)(2,1)S(1)}, bf16[32,1792]{1,0:T(8,128)(2,1)S(1)}, u32[]{:S(2)}, u32[]{:S(2)}) collective-permute-start(bf16[32,1792]{1,0:T(8,128)(2,1)S(1)} %get-tuple-element.50), channel_id=1, source_target_pairs={{0,24},{4,28},{8,16},{12,20},{16,8},{20,12},{24,0},{28,4},{1,25},{... | collective-permute-start | bytes 344072 | tf_op jit(solution)/shard_map/ppermute | solution.py:503
  46.1 8.4 %collective-permute-start.12 = (bf16[32,1792]{1,0:T(8,128)(2,1)S(1)}, bf16[32,1792]{1,0:T(8,128)(2,1)S(1)}, u32[]{:S(2)}, u32[]{:S(2)}) collective-permute-start(bf16[32,1792]{1,0:T(8,128)(2,1)S(1)} %get-tuple-element.51), channel_id=1, source_target_pairs={{0,8},{4,12},{8,0},{12,4},{16,24},{20,28},{24,16},{28,20},{1,9},{5... | collective-permute-start | bytes 344072 | tf_op jit(solution)/shard_map/ppermute | solution.py:503

commit v10 on v9

--- a/solution.py
+++ b/solution.py
@@ -351,11 +351,14 @@
         each(0, snaps, unroll, query)
         each(0, snaps, unroll, key_value)
     share = width // snaps
-    pick = (
-        lax.broadcasted_iota(jnp.int32, (width, share), 0)
-        == lax.broadcasted_iota(jnp.int32, (width, share), 1) + me * share
-    )
-    z_mine = dot_nn(z_s[...], pick.astype(F32).astype(BF16)).astype(BF16)
+    if share % LANES == 0:
+        z_mine = z_s[:, pl.ds(pl.multiple_of(me * share, LANES), share)]
+    else:
+        pick = (
+            lax.broadcasted_iota(jnp.int32, (width, share), 0)
+            == lax.broadcasted_iota(jnp.int32, (width, share), 1) + me * share
+        )
+        z_mine = dot_nn(z_s[...], pick.astype(F32).astype(BF16)).astype(BF16)
     for part in range(3):
         cols = slice(part * width, (part + 1) * width)
         terms_s[:, cols] = dot_tn(z_mine, dt_s[:, cols]).astype(BF16)

time: 55.8 us -> 55.3 us (level)
  no operation moved by 1% of the time
where the time goes in v10:
time: 55.3 us; the launch traced here: 55 us
  starting transfers between devices  20.1 us (36%)
  waiting for transfers between devices  17.2 us (31%)
  Pallas kernels  17 us (31%)
  between operations  0.75 us (1%)
    ppermute x13, waiting for transfers between devices, flipped(): return lax.ppermute(block, axis, [(i, i ^ flip) for i in range(count)])  14.2 us
    ppermute x13, starting transfers between devices, flipped(): return lax.ppermute(block, axis, [(i, i ^ flip) for i in range(count)])  12.8 us
    all_to_all x1, starting transfers between devices, exchange(): return lax.all_to_all(tiles, axis, split_axis=0, concat_axis=0, tiled=True)  7.27 us
    pallas_call x1, Pallas kernels, per_device(): pl.pallas_call(functools.partial(backward_kernel, heads), out_shape=(shap...  4.86 us
    pallas_call x1, Pallas kernels, per_device(): pl.pallas_call(functools.partial(temporal_kernel, snaps, heads, pieces, s...  3.03 us
    all_to_all x1, waiting for transfers between devices, exchange(): return lax.all_to_all(tiles, axis, split_axis=0, concat_axis=0, tiled=True)  2.97 us
    pallas_call x1, Pallas kernels, per_device(): pl.pallas_call(own_kernel, out_shape=(vmem(heads, local, keys, dtype=F32)...  2.35 us
    pallas_call x1, Pallas kernels, per_device(): pl.pallas_call(functools.partial(forward_kernel, heads), out_shape=shape(...  1.76 us
  transfers between devices with their start and end apart: 14, of which 7 were waited for; matrix products, arithmetic and copies ran while one was open for 0% of the time, Pallas kernels for 20%

profile of v10, /device:TPU:0, one launch (start us, length us, event | category | flops | bytes accessed | tf_op | source)
XLA Modules:
  0.0 55.0 jit_solution(4447598059527103305)
XLA Ops:
  0.6 1.7 %halo_tiles.1 = bf16[64,512]{1,0:T(8,128)(2,1)} custom-call(s32[8,8]{1,0:T(8,128)} %bitcast.13, bf16[128,512]{1,0:T(8,128)(2,1)} %bitcast.15), custom_call_target="tpu_custom_call" | custom-call | tf_op jit(solution)/shard_map/halo_tiles/pallas_call | solution.py:547
  2.3 7.3 %all-to-all-start = ((bf16[8,8,512]{2,1,0:T(8,128)(2,1)}), bf16[8,8,512]{2,1,0:T(8,128)(2,1)S(1)}, u32[]{:S(2)}, u32[]{:S(2)}) async-start(bf16[8,8,512]{2,1,0:T(8,128)(2,1)} %bitcast.6), calls=%async_computation | async-start | bytes 131072 | tf_op jit(solution)/shard_map/all_to_all | solution.py:501
  9.6 2.4 %own_rows.1 = (f32[8,128,256]{2,1,0:T(8,128)S(1)}, bf16[128,1536]{1,0:T(8,128)(2,1)S(1)}, bf16[128,512]{1,0:T(8,128)(2,1)S(1)}, bf16[512,1536]{1,0:T(8,128)(2,1)S(1)}, bf16[5,32,512]{2,1,0:T(8,128)(2,1)}) custom-call(s32[8,128]{1,0:T(8,128)} %bitcast.18, s32[8,128]{1,0:T(8,128)} %bitcast.19, f32[4,8]{1,0:T(4,128)} %bias_hbm.1, s32[4,32]{1,0:T(4,128)} %act_hbm.1, ...), custom_call_target="tpu_custom_call" | custom-call | flops 1000000000 | bytes 4000000 | tf_op jit(solution)/shard_map/own_rows/pallas_call | solution.py:562
  12.0 1.6 %collective-permute-start.1 = (bf16[5,32,512]{2,1,0:T(8,128)(2,1)}, bf16[5,32,512]{2,1,0:T(8,128)(2,1)S(1)}, u32[]{:S(2)}, u32[]{:S(2)}) collective-permute-start(bf16[5,32,512]{2,1,0:T(8,128)(2,1)} %get-tuple-element.28.refs_0_), channel_id=1, source_target_pairs={{0,2},{1,3},{2,0},{3,1},{4,6},{5,7},{6,4},{7,5},{8,10},{9,11},{10,... | collective-permute-start | bytes 491528 | tf_op jit(solution)/shard_map/ppermute | solution.py:506
  13.5 3.0 %all-to-all-done = bf16[8,8,512]{2,1,0:T(8,128)(2,1)S(1)} async-done(((bf16[8,8,512]{2,1,0:T(8,128)(2,1)}), bf16[8,8,512]{2,1,0:T(8,128)(2,1)S(1)}, u32[]{:S(2)}, u32[]{:S(2)}) %all-to-all-start) | async-done | bytes 65568 | tf_op jit(solution)/shard_map/all_to_all | solution.py:501
  16.5 1.8 %struct_forward.1.refs_4_ = bf16[128,512]{1,0:T(8,128)(2,1)S(1)} custom-call(bf16[128,512]{1,0:T(8,128)(2,1)S(1)} %get-tuple-element.29.x, bf16[64,512]{1,0:T(8,128)(2,1)S(1)} %bitcast.11, bf16[512,1536]{1,0:T(8,128)(2,1)S(1)} %get-tuple-element.30.w.ws, bf16[128,1536]{1,0:T(8,128)(2,1)S(1)} %get-tuple-element.31.proj, f32[8,128,256]{2,1,0:T(8,128)S(1)} %get-tuple-element.32.edge), custom_call_target="tpu_custom_call" | custom-call | tf_op jit(solution)/shard_map/struct_forward/pallas_call | solution.py:591
  18.3 1.6 %collective-permute-start.4 = (bf16[128,512]{1,0:T(8,128)(2,1)S(1)}, bf16[128,512]{1,0:T(8,128)(2,1)S(1)}, u32[]{:S(2)}, u32[]{:S(2)}) collective-permute-start(bf16[128,512]{1,0:T(8,128)(2,1)S(1)} %struct_forward.1.refs_4_), channel_id=1, source_target_pairs={{0,2},{1,3},{2,0},{3,1},{4,6},{5,7},{6,4},{7,5},{8,10},{9,11},{10,... | collective-permute-start | bytes 393224 | tf_op jit(solution)/shard_map/ppermute | solution.py:506
  19.9 0.0 collective-permute-start
  19.9 0.5 collective-permute-start.2
  20.4 0.1 collective-permute-start.3
  20.5 2.9 %collective-permute-done.4.refs_6_ = bf16[128,512]{1,0:T(8,128)(2,1)S(1)} collective-permute-done((bf16[128,512]{1,0:T(8,128)(2,1)S(1)}, bf16[128,512]{1,0:T(8,128)(2,1)S(1)}, u32[]{:S(2)}, u32[]{:S(2)}) %collective-permute-start.4) | collective-permute-done | bytes 131104 | tf_op jit(solution)/shard_map/ppermute | solution.py:506
  23.3 0.0 collective-permute-done.2.refs_3_
  23.4 0.8 %arrived.1 = (bf16[512,512]{1,0:T(8,128)(2,1)S(1)}, f32[128,128]{1,0:T(8,128)S(1)}, bf16[384,512]{1,0:T(8,128)(2,1)S(1)}, bf16[384,1536]{1,0:T(8,128)(2,1)S(1)}) custom-call(bf16[4,512]{1,0:T(4,128)(2,1)S(1)} %copy-done.2, bf16[512,1536]{1,0:T(8,128)(2,1)S(1)} %copy-done, bf16[5,32,512]{2,1,0:T(8,128)(2,1)S(1)} %copy-done.1, ...), custom_call_target="tpu_custom_call" | custom-call | tf_op jit(solution)/shard_map/arrived/pallas_call | solution.py:607
  24.2 0.5 collective-permute-done.5.refs_0_
  24.7 3.0 %temporal.1 = (bf16[32,1536]{1,0:T(8,128)(2,1)S(1)}, bf16[32,1536]{1,0:T(8,128)(2,1)S(1)}, bf16[32,1536]{1,0:T(8,128)(2,1)S(1)}, bf16[32,1536]{1,0:T(8,128)(2,1)...) custom-call(bf16[4,512]{1,0:T(4,128)(2,1)S(1)} %copy-done.2, bf16[512,1536]{1,0:T(8,128)(2,1)S(1)} %copy-done, ...), custom_call_target="tpu_custom_call" | custom-call | tf_op jit(solution)/shard_map/temporal/pallas_call | solution.py:620
  27.7 1.0 %collective-permute-start.6 = (bf16[32,1536]{1,0:T(8,128)(2,1)S(1)}, bf16[32,1536]{1,0:T(8,128)(2,1)S(1)}, u32[]{:S(2)}, u32[]{:S(2)}) collective-permute-start(bf16[32,1536]{1,0:T(8,128)(2,1)S(1)} %get-tuple-element.42), channel_id=1, source_target_pairs={{0,24},{4,28},{8,16},{12,20},{16,8},{20,12},{24,0},{28,4},{1,25},{... | collective-permute-start | bytes 294920 | tf_op jit(solution)/shard_map/ppermute | solution.py:506
  28.7 0.7 %collective-permute-start.7 = (bf16[32,1536]{1,0:T(8,128)(2,1)S(1)}, bf16[32,1536]{1,0:T(8,128)(2,1)S(1)}, u32[]{:S(2)}, u32[]{:S(2)}) collective-permute-start(bf16[32,1536]{1,0:T(8,128)(2,1)S(1)} %get-tuple-element.43), channel_id=1, source_target_pairs={{0,16},{4,20},{8,24},{12,28},{16,0},{20,4},{24,8},{28,12},{1,17},{... | collective-permute-start | bytes 294920 | tf_op jit(solution)/shard_map/ppermute | solution.py:506
  29.5 2.7 %collective-permute-start.8 = (bf16[32,1536]{1,0:T(8,128)(2,1)S(1)}, bf16[32,1536]{1,0:T(8,128)(2,1)S(1)}, u32[]{:S(2)}, u32[]{:S(2)}) collective-permute-start(bf16[32,1536]{1,0:T(8,128)(2,1)S(1)} %get-tuple-element.44), channel_id=1, source_target_pairs={{0,8},{4,12},{8,0},{12,4},{16,24},{20,28},{24,16},{28,20},{1,9},{5... | collective-permute-start | bytes 294920 | tf_op jit(solution)/shard_map/ppermute | solution.py:506
  32.2 4.9 %struct_backward.1 = (f32[64,512]{1,0:T(8,128)S(1)}, f32[128,512]{1,0:T(8,128)S(1)}) custom-call(bf16[128,1536]{1,0:T(8,128)(2,1)S(1)} %get-tuple-element.37.dt, bf16[128,512]{1,0:T(8,128)(2,1)S(1)} %get-tuple-element.38.cot, bf16[128,1536]{1,0:T(8,128)(2,1)S(1)} %get-tuple-element.31.proj, bf16[64,512]{1,0:T(8,128)(2,1)S(1)} %bitcast.12, ...), custom_call_target="tpu_custom_call" | custom-call | flops 2000000000 | bytes 8000000 | tf_op jit(solution)/shard_map/struct_backward/pallas_call | solution.py:647
  37.0 0.0 collective-permute-done.6.refs_1_
  37.0 1.5 %collective-permute-done.7.refs_2_ = bf16[32,1536]{1,0:T(8,128)(2,1)S(1)} collective-permute-done((bf16[32,1536]{1,0:T(8,128)(2,1)S(1)}, bf16[32,1536]{1,0:T(8,128)(2,1)S(1)}, u32[]{:S(2)}, u32[]{:S(2)}) %collective-permute-start.7) | collective-permute-done | bytes 98336 | tf_op jit(solution)/shard_map/ppermute | solution.py:506
  38.6 0.0 collective-permute-done.8.refs_3_
  38.6 0.1 outer_sum.1.mine_ref
  38.7 1.1 %collective-permute-start.9 = (bf16[32,2048]{1,0:T(8,128)(2,1)S(1)}, bf16[32,2048]{1,0:T(8,128)(2,1)S(1)}, u32[]{:S(2)}, u32[]{:S(2)}) collective-permute-start(bf16[32,2048]{1,0:T(8,128)(2,1)S(1)} %outer_sum.1.mine_ref), channel_id=1, source_target_pairs={{0,4},{4,0},{8,12},{12,8},{16,20},{20,16},{24,28},{28,24},{1,5},{5... | collective-permute-start | bytes 393224 | tf_op jit(solution)/shard_map/ppermute | solution.py:506
  39.7 4.3 %collective-permute-done.9.other_ref = bf16[32,2048]{1,0:T(8,128)(2,1)S(1)} collective-permute-done((bf16[32,2048]{1,0:T(8,128)(2,1)S(1)}, bf16[32,2048]{1,0:T(8,128)(2,1)S(1)}, u32[]{:S(2)}, u32[]{:S(2)}) %collective-permute-start.9) | collective-permute-done | bytes 131104 | tf_op jit(solution)/shard_map/ppermute | solution.py:506
  44.1 0.4 collective-permute-start.10
  44.4 1.2 %collective-permute-start.11 = (bf16[32,1792]{1,0:T(8,128)(2,1)S(1)}, bf16[32,1792]{1,0:T(8,128)(2,1)S(1)}, u32[]{:S(2)}, u32[]{:S(2)}) collective-permute-start(bf16[32,1792]{1,0:T(8,128)(2,1)S(1)} %get-tuple-element.50), channel_id=1, source_target_pairs={{0,24},{4,28},{8,16},{12,20},{16,8},{20,12},{24,0},{28,4},{1,25},{... | collective-permute-start | bytes 344072 | tf_op jit(solution)/shard_map/ppermute | solution.py:506
  45.6 2.0 %collective-permute-start.12 = (bf16[32,1792]{1,0:T(8,128)(2,1)S(1)}, bf16[32,1792]{1,0:T(8,128)(2,1)S(1)}, u32[]{:S(2)}, u32[]{:S(2)}) collective-permute-start(bf16[32,1792]{1,0:T(8,128)(2,1)S(1)} %get-tuple-element.51), channel_id=1, source_target_pairs={{0,8},{4,12},{8,0},{12,4},{16,24},{20,28},{24,16},{28,20},{1,9},{5... | collective-permute-start | bytes 344072 | tf_op jit(solution)/shard_map/ppermute | solution.py:506
  47.6 1.4 %early_sums.1 = (f32[128,512]{1,0:T(8,128)S(1)}, bf16[64,128]{1,0:T(8,128)(2,1)S(1)}, f32[128,1536]{1,0:T(8,128)}) custom-call(s32[8,8]{1,0:T(8,128)S(1)} %bitcast.14, f32[128,512]{1,0:T(8,128)S(1)} %get-tuple-element.39.part_ref, bf16[32,1792]{1,0:T(8,128)(2,1)S(1)} %get-tuple-element.45.refs_0_), custom_call_target="tpu_custom_call" | custom-call | tf_op jit(solution)/shard_map/early_sums/pallas_call | solution.py:691
  49.0 4.3 %collective-permute-done.10.refs_0_ = bf16[32,1792]{1,0:T(8,128)(2,1)S(1)} collective-permute-done((bf16[32,1792]{1,0:T(8,128)(2,1)S(1)}, bf16[32,1792]{1,0:T(8,128)(2,1)S(1)}, u32[]{:S(2)}, u32[]{:S(2)}) %collective-permute-start.10) | collective-permute-done | bytes 114720 | tf_op jit(solution)/shard_map/ppermute | solution.py:506
  53.4 0.7 %collective-permute-done.12.refs_2_ = bf16[32,1792]{1,0:T(8,128)(2,1)S(1)} collective-permute-done((bf16[32,1792]{1,0:T(8,128)(2,1)S(1)}, bf16[32,1792]{1,0:T(8,128)(2,1)S(1)}, u32[]{:S(2)}, u32[]{:S(2)}) %collective-permute-start.12) | collective-permute-done | bytes 114720 | tf_op jit(solution)/shard_map/ppermute | solution.py:506
  54.0 1.0 %last_sums.1 = (bf16[128,512]{1,0:T(8,128)(2,1)}, f32[128,1536]{1,0:T(8,128)}) custom-call(bf16[64,128]{1,0:T(8,128)(2,1)S(1)} %get-tuple-element.46.picks_ref, f32[128,512]{1,0:T(8,128)S(1)} %get-tuple-element.47.sum_ref, f32[128,1536]{1,0:T(8,128)} %get-tuple-element.48._, ...), custom_call_target="tpu_custom_call", output_to_operand_aliasing={{1}: (2, {})} | custom-call | tf_op jit(solution)/shard_map/last_sums/pallas_call | solution.py:708
  (14 shorter events, 0.1 us)
Async XLA Ops:
  2.3 14.2 %all-to-all-start = ((bf16[8,8,512]{2,1,0:T(8,128)(2,1)}), bf16[8,8,512]{2,1,0:T(8,128)(2,1)S(1)}, u32[]{:S(2)}, u32[]{:S(2)}) async-start(bf16[8,8,512]{2,1,0:T(8,128)(2,1)} %bitcast.6), calls=%async_computation | async-start | bytes 131072 | tf_op jit(solution)/shard_map/all_to_all | solution.py:501
  12.0 7.9 %collective-permute-start.1 = (bf16[5,32,512]{2,1,0:T(8,128)(2,1)}, bf16[5,32,512]{2,1,0:T(8,128)(2,1)S(1)}, u32[]{:S(2)}, u32[]{:S(2)}) collective-permute-start(bf16[5,32,512]{2,1,0:T(8,128)(2,1)} %get-tuple-element.28.refs_0_), channel_id=1, source_target_pairs={{0,2},{1,3},{2,0},{3,1},{4,6},{5,7},{6,4},{7,5},{8,10},{9,11},{10,... | collective-permute-start | bytes 491528 | tf_op jit(solution)/shard_map/ppermute | solution.py:506
  16.5 3.4 %copy-start.1 = (bf16[5,32,512]{2,1,0:T(8,128)(2,1)S(1)}, bf16[5,32,512]{2,1,0:T(8,128)(2,1)}, u32[]{:S(2)}) copy-start(bf16[5,32,512]{2,1,0:T(8,128)(2,1)} %get-tuple-element.28.refs_0_) | copy-start | bytes 491524
  16.5 6.8 %copy-start = (bf16[512,1536]{1,0:T(8,128)(2,1)S(1)}, bf16[512,1536]{1,0:T(8,128)(2,1)}, u32[]{:S(2)}) copy-start(bf16[512,1536]{1,0:T(8,128)(2,1)} %wt.1) | copy-start | bytes 4718596
  16.5 6.8 %copy-start.2 = (bf16[4,512]{1,0:T(4,128)(2,1)S(1)}, bf16[4,512]{1,0:T(4,128)(2,1)}, u32[]{:S(2)}) copy-start(bf16[4,512]{1,0:T(4,128)(2,1)} %pos_ref.3) | copy-start | bytes 12292
  18.3 5.0 %collective-permute-start.4 = (bf16[128,512]{1,0:T(8,128)(2,1)S(1)}, bf16[128,512]{1,0:T(8,128)(2,1)S(1)}, u32[]{:S(2)}, u32[]{:S(2)}) collective-permute-start(bf16[128,512]{1,0:T(8,128)(2,1)S(1)} %struct_forward.1.refs_4_), channel_id=1, source_target_pairs={{0,2},{1,3},{2,0},{3,1},{4,6},{5,7},{6,4},{7,5},{8,10},{9,11},{10,... | collective-permute-start | bytes 393224 | tf_op jit(solution)/shard_map/ppermute | solution.py:506
  19.9 3.5 %collective-permute-start = (bf16[5,32,512]{2,1,0:T(8,128)(2,1)S(1)}, bf16[5,32,512]{2,1,0:T(8,128)(2,1)S(1)}, u32[]{:S(2)}, u32[]{:S(2)}) collective-permute-start(bf16[5,32,512]{2,1,0:T(8,128)(2,1)S(1)} %copy-done.1), channel_id=1, source_target_pairs={{0,1},{1,0},{2,3},{3,2},{4,5},{5,4},{6,7},{7,6},{8,9},{9,8},{10,11... | collective-permute-start | bytes 491528 | tf_op jit(solution)/shard_map/ppermute | solution.py:506
  19.9 3.5 %collective-permute-start.2 = (bf16[5,32,512]{2,1,0:T(8,128)(2,1)S(1)}, bf16[5,32,512]{2,1,0:T(8,128)(2,1)S(1)}, u32[]{:S(2)}, u32[]{:S(2)}) collective-permute-start(bf16[5,32,512]{2,1,0:T(8,128)(2,1)S(1)} %collective-permute-done.1.refs_2_), channel_id=1, source_target_pairs={{0,1},{1,0},{2,3},{3,2},{4,5},{5,4},{6,7},{7,6},{8,9},{9,8},{10,11... | collective-permute-start | bytes 491528 | tf_op jit(solution)/shard_map/ppermute | solution.py:506
  20.4 2.9 %collective-permute-start.3 = (bf16[128,512]{1,0:T(8,128)(2,1)S(1)}, bf16[128,512]{1,0:T(8,128)(2,1)S(1)}, u32[]{:S(2)}, u32[]{:S(2)}) collective-permute-start(bf16[128,512]{1,0:T(8,128)(2,1)S(1)} %struct_forward.1.refs_4_), channel_id=1, source_target_pairs={{0,1},{1,0},{2,3},{3,2},{4,5},{5,4},{6,7},{7,6},{8,9},{9,8},{10,11... | collective-permute-start | bytes 393224 | tf_op jit(solution)/shard_map/ppermute | solution.py:506
  23.3 1.3 %collective-permute-start.5 = (bf16[128,512]{1,0:T(8,128)(2,1)S(1)}, bf16[128,512]{1,0:T(8,128)(2,1)S(1)}, u32[]{:S(2)}, u32[]{:S(2)}) collective-permute-start(bf16[128,512]{1,0:T(8,128)(2,1)S(1)} %collective-permute-done.4.refs_6_), channel_id=1, source_target_pairs={{0,1},{1,0},{2,3},{3,2},{4,5},{5,4},{6,7},{7,6},{8,9},{9,8},{10,11... | collective-permute-start | bytes 393224 | tf_op jit(solution)/shard_map/ppermute | solution.py:506
  27.7 9.3 %collective-permute-start.6 = (bf16[32,1536]{1,0:T(8,128)(2,1)S(1)}, bf16[32,1536]{1,0:T(8,128)(2,1)S(1)}, u32[]{:S(2)}, u32[]{:S(2)}) collective-permute-start(bf16[32,1536]{1,0:T(8,128)(2,1)S(1)} %get-tuple-element.42), channel_id=1, source_target_pairs={{0,24},{4,28},{8,16},{12,20},{16,8},{20,12},{24,0},{28,4},{1,25},{... | collective-permute-start | bytes 294920 | tf_op jit(solution)/shard_map/ppermute | solution.py:506
  28.7 9.9 %collective-permute-start.7 = (bf16[32,1536]{1,0:T(8,128)(2,1)S(1)}, bf16[32,1536]{1,0:T(8,128)(2,1)S(1)}, u32[]{:S(2)}, u32[]{:S(2)}) collective-permute-start(bf16[32,1536]{1,0:T(8,128)(2,1)S(1)} %get-tuple-element.43), channel_id=1, source_target_pairs={{0,16},{4,20},{8,24},{12,28},{16,0},{20,4},{24,8},{28,12},{1,17},{... | collective-permute-start | bytes 294920 | tf_op jit(solution)/shard_map/ppermute | solution.py:506
  29.5 9.1 %collective-permute-start.8 = (bf16[32,1536]{1,0:T(8,128)(2,1)S(1)}, bf16[32,1536]{1,0:T(8,128)(2,1)S(1)}, u32[]{:S(2)}, u32[]{:S(2)}) collective-permute-start(bf16[32,1536]{1,0:T(8,128)(2,1)S(1)} %get-tuple-element.44), channel_id=1, source_target_pairs={{0,8},{4,12},{8,0},{12,4},{16,24},{20,28},{24,16},{28,20},{1,9},{5... | collective-permute-start | bytes 294920 | tf_op jit(solution)/shard_map/ppermute | solution.py:506
  32.2 15.5 %copy-start.3 = (s32[1,1,8,8]{3,2,1,0:T(8,128)S(1)}, s32[1,1,8,8]{3,2,1,0:T(8,128)}, u32[]{:S(2)}) copy-start(s32[1,1,8,8]{3,2,1,0:T(8,128)} %param.17) | copy-start | bytes 772
  38.7 5.4 %collective-permute-start.9 = (bf16[32,2048]{1,0:T(8,128)(2,1)S(1)}, bf16[32,2048]{1,0:T(8,128)(2,1)S(1)}, u32[]{:S(2)}, u32[]{:S(2)}) collective-permute-start(bf16[32,2048]{1,0:T(8,128)(2,1)S(1)} %outer_sum.1.mine_ref), channel_id=1, source_target_pairs={{0,4},{4,0},{8,12},{12,8},{16,20},{20,16},{24,28},{28,24},{1,5},{5... | collective-permute-start | bytes 393224 | tf_op jit(solution)/shard_map/ppermute | solution.py:506
  44.1 9.3 %collective-permute-start.10 = (bf16[32,1792]{1,0:T(8,128)(2,1)S(1)}, bf16[32,1792]{1,0:T(8,128)(2,1)S(1)}, u32[]{:S(2)}, u32[]{:S(2)}) collective-permute-start(bf16[32,1792]{1,0:T(8,128)(2,1)S(1)} %get-tuple-element.49), channel_id=1, source_target_pairs={{0,16},{4,20},{8,24},{12,28},{16,0},{20,4},{24,8},{28,12},{1,17},{... | collective-permute-start | bytes 344072 | tf_op jit(solution)/shard_map/ppermute | solution.py:506
  44.4 8.9 %collective-permute-start.11 = (bf16[32,1792]{1,0:T(8,128)(2,1)S(1)}, bf16[32,1792]{1,0:T(8,128)(2,1)S(1)}, u32[]{:S(2)}, u32[]{:S(2)}) collective-permute-start(bf16[32,1792]{1,0:T(8,128)(2,1)S(1)} %get-tuple-element.50), channel_id=1, source_target_pairs={{0,24},{4,28},{8,16},{12,20},{16,8},{20,12},{24,0},{28,4},{1,25},{... | collective-permute-start | bytes 344072 | tf_op jit(solution)/shard_map/ppermute | solution.py:506
  45.6 8.5 %collective-permute-start.12 = (bf16[32,1792]{1,0:T(8,128)(2,1)S(1)}, bf16[32,1792]{1,0:T(8,128)(2,1)S(1)}, u32[]{:S(2)}, u32[]{:S(2)}) collective-permute-start(bf16[32,1792]{1,0:T(8,128)(2,1)S(1)} %get-tuple-element.51), channel_id=1, source_target_pairs={{0,8},{4,12},{8,0},{12,4},{16,24},{20,28},{24,16},{28,20},{1,9},{5... | collective-permute-start | bytes 344072 | tf_op jit(solution)/shard_map/ppermute | solution.py:506
